TPU v7x, 32 devices: a whole 2x2x4 slice. The times are simulated.
32 devices in a mesh: fsdp: 32 (over z, y, x, core).
Axes of the slice: x: 2, y: 2, z: 4, core: 2. Of those that a mesh axis runs over, the one named last changes fastest.
Arguments:
- tokens: bfloat16 [512, 16, 1024], P('fsdp'), may hold values from -6 to 6
- depth_count: int32 [512], P('fsdp'), may hold values from 8 to 16, as said below
- cotangent: bfloat16 [512, 16, 1024], P('fsdp'), may hold values from -6.5 to 6.5
- joint_weight: float32 [2048, 3072], P('fsdp'), may hold values from -0.1875 to 0.1875
- output_weight: float32 [2048, 1024], P('fsdp'), may hold values from -0.5 to 0.5
- expand_weight: float32 [2048, 8192], P('fsdp'), may hold values from -0.1875 to 0.1875
- shrink_weight: float32 [2, 4096, 1024], P(None, 'fsdp'), may hold values from -0.09375 to 0.09375
- norm_gains: float32 [2, 1024], P(None, 'fsdp'), may hold values from 0.25 to 2.05
- joint_mean: float32 [2048, 3072], P('fsdp'), may hold values from -0.00012207031 to 0.00012207031
- joint_square: float32 [2048, 3072], P('fsdp'), may hold values from 1.1920201e-10 to 1.9966337e-09
- output_mean: float32 [2048, 1024], P('fsdp'), may hold values from -0.00024414062 to 0.00024414062
- output_square: float32 [2048, 1024], P('fsdp'), may hold values from 7.748131e-10 to 1.2516211e-08
- expand_mean: float32 [2048, 8192], P('fsdp'), may hold values from -0.00024414062 to 0.00024414062
- expand_square: float32 [2048, 8192], P('fsdp'), may hold values from 7.748131e-10 to 1.2516211e-08
- shrink_mean: float32 [2, 4096, 1024], P(None, 'fsdp'), may hold values from -0.00024414062 to 0.00024414062
- shrink_square: float32 [2, 4096, 1024], P(None, 'fsdp'), may hold values from 7.748131e-10 to 1.2516211e-08
- gains_mean: float32 [2, 1024], P(None, 'fsdp'), may hold values from -0.0008544922 to 0.0008544922
- gains_square: float32 [2, 1024], P(None, 'fsdp'), may hold values from 7.1521207e-09 to 1.1324191e-07
Outputs:
- result: bfloat16 [512, 16, 1024], P('fsdp')
- tokens_grad: bfloat16 [512, 16, 1024], P('fsdp')
- grad_norm: float32 [], replicated
- joint_updated: float32 [2048, 3072], P('fsdp')
- joint_mean_out: float32 [2048, 3072], P('fsdp')
- joint_square_out: float32 [2048, 3072], P('fsdp')
- output_updated: float32 [2048, 1024], P('fsdp')
- output_mean_out: float32 [2048, 1024], P('fsdp')
- output_square_out: float32 [2048, 1024], P('fsdp')
- expand_updated: float32 [2048, 8192], P('fsdp')
- expand_mean_out: float32 [2048, 8192], P('fsdp')
- expand_square_out: float32 [2048, 8192], P('fsdp')
- shrink_updated: float32 [2, 4096, 1024], P(None, 'fsdp')
- shrink_mean_out: float32 [2, 4096, 1024], P(None, 'fsdp')
- shrink_square_out: float32 [2, 4096, 1024], P(None, 'fsdp')
- gains_updated: float32 [2, 1024], P(None, 'fsdp')
- gains_mean_out: float32 [2, 1024], P(None, 'fsdp')
- gains_square_out: float32 [2, 1024], P(None, 'fsdp')
Inputs may be any that keep to these rules, and one draw needn't show every extreme that they name: `depth_count`: each frame has either half of 16 or 16 live positions.
All inputs are finite; a program needn't handle non-finite values.
Results may differ from a plain program's by a relative error of at most 0.012.
The roundings to bfloat16 on the way count: a program that leaves them out, or rounds other values in their place, can miss the bound.
Values may be sent and summed in bfloat16 or wider, within the bound.
No kernel may reach another device: no remote copies, remote signals or barrier semaphores. Data moves between devices by JAX's collectives and lax.ppermute only.
A program may use at most 320 MiB of HBM per device.

v0:
```python
import jax
import jax.numpy as jnp
from jax import lax
from jax.sharding import PartitionSpec as P

HEADS = 16
SETS = 2
STEP = 10


NORM_EPS = 1e-05
BETA_ONE = 0.9
BETA_TWO = 0.95
ADAM_EPS = 1e-08
MATRIX_RATE = 0.08
GAIN_RATE = 1.0
MATRIX_DECAY = 0.1
CLIP_LIMIT = 1.0


def per_set(values, weight):
    frame_count, positions, features = values.shape
    grouped = values.reshape(frame_count, SETS, positions // SETS, features)
    product = jnp.einsum("fspd,sde->fspe", grouped, weight, preferred_element_type=jnp.float32)
    return product.reshape(frame_count, positions, weight.shape[2])


def per_set_back(values, grad_out, weight):
    frame_count, positions, features = values.shape
    grouped = values.reshape(frame_count, SETS, positions // SETS, features)
    grad_grouped = grad_out.reshape(frame_count, SETS, positions // SETS, grad_out.shape[2])
    grad_in = jnp.einsum("fspe,sde->fspd", grad_grouped, weight, preferred_element_type=jnp.float32)
    grad_weight = jnp.einsum(
        "fspd,fspe->sde", grouped, grad_grouped, preferred_element_type=jnp.float32
    )
    return (grad_in.reshape(frame_count, positions, features), grad_weight)


def normalize(values, gain_row):
    inverse = lax.rsqrt(jnp.mean(values * values, axis=-1, keepdims=True) + NORM_EPS)
    return (values * inverse * gain_row, inverse)


def normalize_back(values, inverse, gain_row, grad_out):
    scaled = grad_out * gain_row
    grad_in = inverse * scaled - values * inverse * inverse * inverse * jnp.mean(
        scaled * values, axis=-1, keepdims=True
    )
    grad_gain = jnp.sum(grad_out * values * inverse, axis=(0, 1))
    return (grad_in, grad_gain)


def split_heads(mixed):
    frame_count, positions, triple = mixed.shape
    head_dim = triple // 3 // HEADS
    split = mixed.reshape(frame_count, positions, 3, HEADS, head_dim)
    return (split[:, :, 0], split[:, :, 1], split[:, :, 2], head_dim ** (-0.5))


def attend(mixed):
    frame_count, positions, triple = mixed.shape
    queries, key_rows, value_rows, score_scale = split_heads(mixed)
    scores = (
        jnp.einsum("fphd,fkhd->fhpk", queries, key_rows, preferred_element_type=jnp.float32)
        * score_scale
    )
    index_row = jnp.arange(positions)
    scores = jnp.where(index_row[:, None] >= index_row[None, :], scores, -1e30)
    highest = jnp.max(scores, axis=-1, keepdims=True)
    exp_scores = jnp.exp(scores - highest)
    attention = exp_scores / jnp.sum(exp_scores, axis=-1, keepdims=True)
    context = jnp.einsum(
        "fhpk,fkhd->fphd",
        attention.astype(jnp.bfloat16),
        value_rows,
        preferred_element_type=jnp.float32,
    )
    return (attention, context.reshape(frame_count, positions, triple // 3).astype(jnp.bfloat16))


def attend_back(mixed, attention, grad_context):
    frame_count, positions, triple = mixed.shape
    queries, key_rows, value_rows, score_scale = split_heads(mixed)
    grad_heads = grad_context.reshape(queries.shape)
    grad_attention = jnp.einsum(
        "fphd,fkhd->fhpk", grad_heads, value_rows, preferred_element_type=jnp.float32
    )
    grad_value = jnp.einsum(
        "fhpk,fphd->fkhd",
        attention.astype(jnp.bfloat16),
        grad_heads,
        preferred_element_type=jnp.float32,
    )
    grad_scores = attention * (
        grad_attention - jnp.sum(grad_attention * attention, axis=-1, keepdims=True)
    )
    grad_scores = grad_scores.astype(jnp.bfloat16)
    grad_query = (
        jnp.einsum("fhpk,fkhd->fphd", grad_scores, key_rows, preferred_element_type=jnp.float32)
        * score_scale
    )
    grad_key = (
        jnp.einsum("fhpk,fphd->fkhd", grad_scores, queries, preferred_element_type=jnp.float32)
        * score_scale
    )
    stacked = jnp.stack([grad_query, grad_key, grad_value], axis=2)
    return stacked.reshape(frame_count, positions, triple).astype(jnp.bfloat16)


def forward(inputs, live_mask, weights):
    joint_low, output_low, expand_low, shrink_low, gains_low = weights
    gains_full = gains_low.astype(jnp.float32)
    normed_one, inverse_one = normalize(inputs, gains_full[0])
    first = normed_one.astype(jnp.bfloat16)
    mixed = per_set(first, joint_low).astype(jnp.bfloat16)
    attention, context = attend(mixed)
    branch = per_set(context, output_low)
    middle = inputs + live_mask * branch
    normed_two, inverse_two = normalize(middle, gains_full[1])
    second = normed_two.astype(jnp.bfloat16)
    gate_values = per_set(second, expand_low)
    half_width = gate_values.shape[2] // 2
    hidden = (jax.nn.silu(gate_values[..., :half_width]) * gate_values[..., half_width:]).astype(
        jnp.bfloat16
    )
    shrunk = per_set(hidden, shrink_low)
    result = middle + live_mask * shrunk
    return (
        result,
        (
            inverse_one,
            first,
            mixed,
            attention,
            context,
            middle,
            inverse_two,
            second,
            gate_values,
            hidden,
        ),
    )


def backward(inputs, live_mask, cotangent, weights, kept_values):
    joint_low, output_low, expand_low, shrink_low, gains_low = weights
    gains_full = gains_low.astype(jnp.float32)
    (
        inverse_one,
        first,
        mixed,
        attention,
        context,
        middle,
        inverse_two,
        second,
        gate_values,
        hidden,
    ) = kept_values
    grad_result = cotangent.astype(jnp.float32) * live_mask
    grad_hidden, grad_shrink = per_set_back(hidden, grad_result.astype(jnp.bfloat16), shrink_low)
    half_width = gate_values.shape[2] // 2
    gate_part = gate_values[..., :half_width]
    up_part = gate_values[..., half_width:]
    sigmoid_gate = jax.nn.sigmoid(gate_part)
    grad_gate = grad_hidden * up_part * sigmoid_gate * (1.0 + gate_part * (1.0 - sigmoid_gate))
    grad_up = grad_hidden * gate_part * sigmoid_gate
    grad_gates = jnp.concatenate([grad_gate, grad_up], axis=-1).astype(jnp.bfloat16)
    grad_second, grad_expand = per_set_back(second, grad_gates, expand_low)
    grad_mid_norm, grad_gain_two = normalize_back(middle, inverse_two, gains_full[1], grad_second)
    grad_middle = grad_result + grad_mid_norm
    grad_branch = (grad_middle * live_mask).astype(jnp.bfloat16)
    grad_context, grad_output = per_set_back(context, grad_branch, output_low)
    grad_mixed = attend_back(mixed, attention, grad_context.astype(jnp.bfloat16))
    grad_first, grad_joint = per_set_back(first, grad_mixed, joint_low)
    grad_in_norm, grad_gain_one = normalize_back(inputs, inverse_one, gains_full[0], grad_first)
    grad_inputs = grad_middle + grad_in_norm
    grad_gains = jnp.stack([grad_gain_one, grad_gain_two], axis=0)
    return (grad_inputs, (grad_joint, grad_output, grad_expand, grad_shrink, grad_gains))


def adam_step(weight, grad_value, mean_old, square_old, learn_rate, weight_decay):
    mean_new = BETA_ONE * mean_old + (1.0 - BETA_ONE) * grad_value
    square_new = BETA_TWO * square_old + (1.0 - BETA_TWO) * grad_value * grad_value
    mean_hat = mean_new / (1.0 - BETA_ONE**STEP)
    square_hat = square_new / (1.0 - BETA_TWO**STEP)
    weight_new = weight - learn_rate * (
        mean_hat / (jnp.sqrt(square_hat) + ADAM_EPS) + weight_decay * weight
    )
    return (weight_new, mean_new, square_new)


def stack_sets(whole):
    joint_all, output_all, expand_all, shrink_all, gains_all = whole
    joint_sets = joint_all.reshape(SETS, joint_all.shape[0] // SETS, joint_all.shape[1])
    output_sets = output_all.reshape(SETS, output_all.shape[0] // SETS, output_all.shape[1])
    expand_sets = expand_all.reshape(SETS, expand_all.shape[0] // SETS, expand_all.shape[1])
    return (joint_sets, output_sets, expand_sets, shrink_all, gains_all)


def local(
    tokens,
    depth_count,
    cotangent,
    joint_weight,
    output_weight,
    expand_weight,
    shrink_weight,
    norm_gains,
    joint_mean,
    joint_square,
    output_mean,
    output_square,
    expand_mean,
    expand_square,
    shrink_mean,
    shrink_square,
    gains_mean,
    gains_square,
):
    inputs = tokens.astype(jnp.float32)
    position_index = jnp.arange(tokens.shape[1])
    live_mask = (position_index[None, :] < depth_count[:, None]).astype(jnp.float32)[:, :, None]
    joint_low = joint_weight.astype(jnp.bfloat16)
    output_low = output_weight.astype(jnp.bfloat16)
    expand_low = expand_weight.astype(jnp.bfloat16)
    shrink_low = shrink_weight.astype(jnp.bfloat16)
    gains_low = norm_gains.astype(jnp.bfloat16)
    gathered = stack_sets(
        (
            lax.all_gather(joint_low, "fsdp", axis=0, tiled=True),
            lax.all_gather(output_low, "fsdp", axis=0, tiled=True),
            lax.all_gather(expand_low, "fsdp", axis=0, tiled=True),
            lax.all_gather(shrink_low, "fsdp", axis=1, tiled=True),
            lax.all_gather(gains_low, "fsdp", axis=1, tiled=True),
        )
    )
    result, kept_values = forward(inputs, live_mask, gathered)
    backward_weights = stack_sets(
        (
            lax.all_gather(joint_low, "fsdp", axis=0, tiled=True),
            lax.all_gather(output_low, "fsdp", axis=0, tiled=True),
            lax.all_gather(expand_low, "fsdp", axis=0, tiled=True),
            lax.all_gather(shrink_low, "fsdp", axis=1, tiled=True),
            lax.all_gather(gains_low, "fsdp", axis=1, tiled=True),
        )
    )
    unused_result, backward_values = forward(inputs, live_mask, backward_weights)
    grad_inputs, grad_terms = backward(
        inputs, live_mask, cotangent, backward_weights, backward_values
    )
    joint_term = grad_terms[0].reshape(
        grad_terms[0].shape[0] * grad_terms[0].shape[1], grad_terms[0].shape[2]
    )
    output_term = grad_terms[1].reshape(
        grad_terms[1].shape[0] * grad_terms[1].shape[1], grad_terms[1].shape[2]
    )
    expand_term = grad_terms[2].reshape(
        grad_terms[2].shape[0] * grad_terms[2].shape[1], grad_terms[2].shape[2]
    )
    reduced = (
        lax.psum_scatter(joint_term, "fsdp", scatter_dimension=0, tiled=True),
        lax.psum_scatter(output_term, "fsdp", scatter_dimension=0, tiled=True),
        lax.psum_scatter(expand_term, "fsdp", scatter_dimension=0, tiled=True),
        lax.psum_scatter(grad_terms[3], "fsdp", scatter_dimension=1, tiled=True),
        lax.psum_scatter(grad_terms[4], "fsdp", scatter_dimension=1, tiled=True),
    )
    local_sq = (
        jnp.sum(reduced[0] * reduced[0])
        + jnp.sum(reduced[1] * reduced[1])
        + jnp.sum(reduced[2] * reduced[2])
        + jnp.sum(reduced[3] * reduced[3])
        + jnp.sum(reduced[4] * reduced[4])
    )
    total_sq = lax.psum(local_sq, "fsdp")
    grad_norm_value = jnp.sqrt(total_sq)
    factor = CLIP_LIMIT / jnp.maximum(grad_norm_value, CLIP_LIMIT)
    joint_new = adam_step(
        joint_weight, factor * reduced[0], joint_mean, joint_square, MATRIX_RATE, MATRIX_DECAY
    )
    output_new = adam_step(
        output_weight, factor * reduced[1], output_mean, output_square, MATRIX_RATE, MATRIX_DECAY
    )
    expand_new = adam_step(
        expand_weight, factor * reduced[2], expand_mean, expand_square, MATRIX_RATE, MATRIX_DECAY
    )
    shrink_new = adam_step(
        shrink_weight, factor * reduced[3], shrink_mean, shrink_square, MATRIX_RATE, MATRIX_DECAY
    )
    gains_new = adam_step(norm_gains, factor * reduced[4], gains_mean, gains_square, GAIN_RATE, 0.0)
    return (
        result.astype(jnp.bfloat16),
        grad_inputs.astype(jnp.bfloat16),
        grad_norm_value,
        joint_new[0],
        joint_new[1],
        joint_new[2],
        output_new[0],
        output_new[1],
        output_new[2],
        expand_new[0],
        expand_new[1],
        expand_new[2],
        shrink_new[0],
        shrink_new[1],
        shrink_new[2],
        gains_new[0],
        gains_new[1],
        gains_new[2],
    )


def solution(mesh):
    placed = (
        P("fsdp", None, None),
        P("fsdp"),
        P("fsdp", None, None),
        P("fsdp", None),
        P("fsdp", None),
        P("fsdp", None),
        P(None, "fsdp", None),
        P(None, "fsdp"),
        P("fsdp", None),
        P("fsdp", None),
        P("fsdp", None),
        P("fsdp", None),
        P("fsdp", None),
        P("fsdp", None),
        P(None, "fsdp", None),
        P(None, "fsdp", None),
        P(None, "fsdp"),
        P(None, "fsdp"),
    )
    return jax.shard_map(
        local,
        mesh=mesh,
        in_specs=placed,
        out_specs=(
            P("fsdp", None, None),
            P("fsdp", None, None),
            P(),
            P("fsdp", None),
            P("fsdp", None),
            P("fsdp", None),
            P("fsdp", None),
            P("fsdp", None),
            P("fsdp", None),
            P("fsdp", None),
            P("fsdp", None),
            P("fsdp", None),
            P(None, "fsdp", None),
            P(None, "fsdp", None),
            P(None, "fsdp", None),
            P(None, "fsdp"),
            P(None, "fsdp"),
            P(None, "fsdp"),
        ),
        check_vma=False,
    )
```

profile of v0, /device:TPU:0, one launch (start us, length us, event | category | flops | bytes accessed | tf_op | source)
XLA Modules:
  0.0 2243.6 jit_solution(7027798747813648141)
XLA Ops:
  7.2 2.0 convert_element_type.109
  9.3 1.6 convert_element_type.117
  12.0 2.7 convert_element_type.119
  14.8 43.4 %all-gather = bf16[32,32,2]{1,2,0:T(2,128)(2,1)S(1)} all-gather(bf16[1,32,2]{1,2,0:T(2,128)(2,1)S(1)} %convert_bitcast_fusion), channel_id=1, replica_groups=mesh['fsdp'=32] {'fsdp'}, dimensions={0}, use_global_device_ids=true | all-gather | bytes 4224 | tf_op jit(solution)/shard_map/all_gather | solution.py:235
  58.7 51.5 %all-gather.6.cloned.1.call-done = bf16[2048,3072]{1,0:T(8,128)(2,1)} async-done(((bf16[64,3072]{1,0:T(8,128)(2,1)}), bf16[2048,3072]{1,0:T(8,128)(2,1)}) %all-gather.6.cloned.1.call-update) | async-done | bytes 12582928 | tf_op jit(solution)/shard_map/all_gather | solution.py:231
  110.2 6.4 fusion.15
  116.8 3.5 convert_element_type.112
  120.2 3.6 fusion.88
  123.9 2.7 fusion.90
  126.5 2.5 fusion.24
  130.1 43.9 %all-gather.8.cloned.1.call-done = bf16[2048,1024]{1,0:T(8,128)(2,1)} async-done(((bf16[64,1024]{1,0:T(8,128)(2,1)}), bf16[2048,1024]{1,0:T(8,128)(2,1)}) %all-gather.8.cloned.1.call-update) | async-done | bytes 4194320 | tf_op jit(solution)/shard_map/all_gather | solution.py:232
  174.0 3.0 convolution_bitcast_fusion.2
  177.4 113.4 %all-gather.12.cloned.1.call-done = bf16[2,4096,1024]{2,1,0:T(8,128)(2,1)} async-done(((bf16[2,128,1024]{2,1,0:T(8,128)(2,1)}), bf16[2,4096,1024]{2,1,0:T(8,128)(2,1)}) %all-gather.12.cloned.1.call-update) | async-done | bytes 16777232 | tf_op jit(solution)/shard_map/all_gather | solution.py:234
  290.8 13.3 fusion.5
  304.1 183.0 %all-gather.10.cloned.1.call-done = bf16[2048,8192]{1,0:T(8,128)(2,1)} async-done(((bf16[64,8192]{1,0:T(8,128)(2,1)}), bf16[2048,8192]{1,0:T(8,128)(2,1)}) %all-gather.10.cloned.1.call-update) | async-done | bytes 33554448 | tf_op jit(solution)/shard_map/all_gather | solution.py:233
  487.1 18.9 convolution_bitcast_fusion.1
  506.0 4.1 copy.221
  510.5 4.1 fusion.20
  514.7 18.5 fusion.36
  533.2 1.6 fusion.54
  535.5 1.8 fusion.68
  537.4 1.5 fusion.41
  538.9 1.6 convert_element_type.128
  540.6 2.7 fusion.25
  548.4 2.4 copy.137
  550.8 4.9 convert_element_type.130
  555.8 9.3 fusion.26
  568.2 5.6 fusion.92
  573.9 11.7 fusion.91
  586.6 13.2 convolution_bitcast_fusion
  599.9 1.1 copy-done.1
  601.8 24.8 %fusion.82 = f32[2,1024,8192,1]{2,1,0,3:T(8,128)} fusion(bf16[16,2,8,4096]{3,2,1,0:T(8,128)(2,1)} %get-tuple-element.40, bf16[16,2,8,4096]{3,2,1,0:T(8,128)(2,1)S(1)} %copy-done.24, f32[16,16,1024]{2,1,0:T(8,128)S(1)} %copy-done.1, f32[1024]{0:T(1024)S(1)} %bitcast.215, f32[16,16]{1,0:T(8,128)S(1)} %copy-done.38), kind=kOutput, calls=%fused_computation.141 | convolution fusion | flops 4304142336 | bytes 72356864 | tf_op jit(solution)/shard_map/fspd,fspe->sde/dot_general | solution.py:33
  628.2 9.1 fusion.31
  637.3 63.0 %reduce-scatter.16.cloned.1.call-done = f32[32,2]{1,0:T(8,128)} async-done(((f32[1024,2]{1,0:T(8,128)}), f32[32,2]{1,0:T(8,128)}) %reduce-scatter.16.cloned.1.call-update) | async-done | bytes 272
  701.8 145.7 %reduce-scatter.10.cloned.1.call-done = f32[64,1024]{1,0:T(8,128)} async-done(((f32[2048,1024]{1,0:T(8,128)}), f32[64,1024]{1,0:T(8,128)}) %reduce-scatter.10.cloned.1.call-update) | async-done | bytes 262160 | tf_op jit(solution)/shard_map/reduce_scatter | solution.py:263
  847.4 1.6 multiply_reduce_fusion.6
  849.1 247.4 %reduce-scatter.8.cloned.1.call-done = f32[64,3072]{1,0:T(8,128)} async-done(((f32[2048,3072]{1,0:T(8,128)}), f32[64,3072]{1,0:T(8,128)}) %reduce-scatter.8.cloned.1.call-update) | async-done | bytes 786448 | tf_op jit(solution)/shard_map/reduce_scatter | solution.py:262
  1096.4 1.9 multiply_reduce_fusion.5
  1099.7 353.0 %reduce-scatter.14.cloned.1.call-done = f32[2,128,1024]{2,1,0:T(8,128)} async-done(((f32[2,4096,1024]{2,1,0:T(8,128)}), f32[2,128,1024]{2,1,0:T(8,128)}) %reduce-scatter.14.cloned.1.call-update) | async-done | bytes 1048592 | tf_op jit(solution)/shard_map/reduce_scatter | solution.py:265
  1452.6 2.1 multiply_reduce_fusion.2
  1454.7 710.5 %reduce-scatter.12.cloned.1.call-done = f32[64,8192]{1,0:T(8,128)} async-done(((f32[2048,8192]{1,0:T(8,128)}), f32[64,8192]{1,0:T(8,128)}) %reduce-scatter.12.cloned.1.call-update) | async-done | bytes 2097168 | tf_op jit(solution)/shard_map/reduce_scatter | solution.py:264
  2165.2 2.7 multiply_reduce_fusion
  2170.0 3.4 fusion.47
  2173.4 47.1 %psum.7 = f32[]{:T(128)} all-reduce(f32[]{:T(128)S(6)} %add.150), channel_id=1, replica_groups=mesh['fsdp'=32] {'fsdp'}, use_global_device_ids=true, to_apply=%region_19.20 | all-reduce | flops 1 | bytes 8 | tf_op jit(solution)/shard_map/psum | solution.py:275
  2221.9 3.8 multiply_subtract_fusion.2
  2225.7 2.1 multiply_subtract_fusion.3
  2227.9 5.5 multiply_subtract_fusion
  2233.4 2.3 multiply_subtract_fusion.1
  (151 shorter events, 17.9 us)
Async XLA Ops:
  7.2 3.8 copy-start.21
  7.2 103.0 %all-gather.6.cloned.1.call-start = ((), (), s32[]{:S(2)}) async-start(), calls=%async_computation.5 | async-start | bytes 12976128 | tf_op jit(solution)/shard_map/all_gather | solution.py:231
  9.3 164.7 %all-gather.8.cloned.1.call-start = ((), (), s32[]{:S(2)}) async-start(), calls=%async_computation.6 | async-start | bytes 4325376 | tf_op jit(solution)/shard_map/all_gather | solution.py:232
  11.0 279.8 %all-gather.12.cloned.1.call-start = ((), (), s32[]{:S(2)}) async-start(), calls=%async_computation.8 | async-start | bytes 17301504 | tf_op jit(solution)/shard_map/all_gather | solution.py:234
  11.9 2.9 copy-start.48
  11.9 46.4 %copy-start.5 = (bf16[16,16,1024]{2,1,0:T(8,128)(2,1)S(1)}, bf16[16,16,1024]{2,1,0:T(8,128)(2,1)}, u32[]{:S(2)}) copy-start(bf16[16,16,1024]{2,1,0:T(8,128)(2,1)} %param.18) | copy-start | bytes 1572868
  11.9 46.6 %copy-start.52 = (s32[16]{0:T(128)S(1)}, s32[16]{0:T(128)}, u32[]{:S(2)}) copy-start(s32[16]{0:T(128)} %param.19) | copy-start | bytes 196
  12.0 475.1 %all-gather.10.cloned.1.call-start = ((), (), s32[]{:S(2)}) async-start(), calls=%async_computation.7 | async-start | bytes 34603008 | tf_op jit(solution)/shard_map/all_gather | solution.py:233
  14.7 685.6 %reduce-scatter.16.cloned.1.call-start = ((), (), s32[]{:S(2)}) async-start(), calls=%async_computation.13 | async-start | bytes 540672
  58.6 476.3 %copy-start.43 = (f32[16,16]{1,0:T(8,128)}, f32[16,16]{1,0:T(8,128)S(1)}, u32[]{:S(2)}) copy-start(f32[16,16]{1,0:T(8,128)S(1)} %fusion.78) | copy-start | bytes 3076
  58.6 476.3 %copy-start.35 = (f32[1,1024]{1,0:T(1,128)}, f32[1,1024]{1,0:T(1,128)S(1)}, u32[]{:S(2)}) copy-start(f32[1,1024]{1,0:T(1,128)S(1)} %get-tuple-element.48) | copy-start | bytes 12292
  58.6 515.2 %copy-start.39 = (f32[1,1024]{1,0:T(1,128)}, f32[1,1024]{1,0:T(1,128)S(1)}, u32[]{:S(2)}) copy-start(f32[1,1024]{1,0:T(1,128)S(1)} %get-tuple-element.49) | copy-start | bytes 12292
  58.7 515.2 %copy-start.41 = (f32[16,16]{1,0:T(8,128)}, f32[16,16]{1,0:T(8,128)S(1)}, u32[]{:S(2)}) copy-start(f32[16,16]{1,0:T(8,128)S(1)} %add_rsqrt_fusion.1) | copy-start | bytes 3076
  123.9 2.7 copy-start.19
  130.0 43.9 %copy-start.29 = (bf16[16,2,8,1024]{3,2,1,0:T(8,128)(2,1)}, bf16[16,2,8,1024]{3,2,1,0:T(8,128)(2,1)S(1)}, u32[]{:S(2)}) copy-start(bf16[16,2,8,1024]{3,2,1,0:T(8,128)(2,1)S(1)} %convert_element_type.116) | copy-start | bytes 1572868
  174.0 3.0 copy-start.13
  177.3 126.8 %copy-start.15 = (bf16[16,2,8,1024]{3,2,1,0:T(8,128)(2,1)}, bf16[16,2,8,1024]{3,2,1,0:T(8,128)(2,1)S(1)}, u32[]{:S(2)}) copy-start(bf16[16,2,8,1024]{3,2,1,0:T(8,128)(2,1)S(1)} %get-tuple-element.47) | copy-start | bytes 1572868
  177.4 357.6 %copy-start = (f32[16,16,1024]{2,1,0:T(8,128)}, f32[16,16,1024]{2,1,0:T(8,128)S(1)}, u32[]{:S(2)}) copy-start(f32[16,16,1024]{2,1,0:T(8,128)S(1)} %get-tuple-element.38) | copy-start | bytes 3145732
  177.4 357.5 %copy-start.37 = (f32[16,16]{1,0:T(8,128)}, f32[16,16]{1,0:T(8,128)S(1)}, u32[]{:S(2)}) copy-start(f32[16,16]{1,0:T(8,128)S(1)} %add_rsqrt_fusion) | copy-start | bytes 3076
  506.0 4.6 copy-start.2
  514.7 71.0 %copy-start.3 = (bf16[16,2,8,4096]{3,2,1,0:T(8,128)(2,1)}, bf16[16,2,8,4096]{3,2,1,0:T(8,128)(2,1)S(1)}, u32[]{:S(2)}) copy-start(bf16[16,2,8,4096]{3,2,1,0:T(8,128)(2,1)S(1)} %get-tuple-element.41) | copy-start | bytes 6291460
  533.2 4.1 copy-start.8
  540.6 2.7 copy-start.27
  540.6 2.8 copy-start.30
  540.6 3.1 copy-start.32
  555.8 10.3 copy-start.6
  568.0 279.4 %reduce-scatter.10.cloned.1.call-start = ((), (), s32[]{:S(2)}) async-start(), calls=%async_computation.10 | async-start | bytes 8650752 | tf_op jit(solution)/shard_map/reduce_scatter | solution.py:263
  573.8 522.6 %reduce-scatter.8.cloned.1.call-start = ((), (), s32[]{:S(2)}) async-start(), calls=%async_computation.9 | async-start | bytes 25952256 | tf_op jit(solution)/shard_map/reduce_scatter | solution.py:262
  585.6 867.0 %reduce-scatter.14.cloned.1.call-start = ((), (), s32[]{:S(2)}) async-start(), calls=%async_computation.12 | async-start | bytes 34603008 | tf_op jit(solution)/shard_map/reduce_scatter | solution.py:265
  599.9 1565.3 %reduce-scatter.12.cloned.1.call-start = ((), (), s32[]{:S(2)}) async-start(), calls=%async_computation.11 | async-start | bytes 69206016 | tf_op jit(solution)/shard_map/reduce_scatter | solution.py:264
  701.7 1468.2 %copy-start.7 = (bf16[16,16,1024]{2,1,0:T(8,128)(2,1)S(1)}, bf16[16,16,1024]{2,1,0:T(8,128)(2,1)}, u32[]{:S(2)}) copy-start(bf16[16,16,1024]{2,1,0:T(8,128)(2,1)} %param.18) | copy-start | bytes 1572868
  701.7 1468.2 %copy-start.9 = (f32[16,2,8,1024]{3,2,0,1:T(8,128)S(1)}, f32[16,2,8,1024]{3,2,0,1:T(8,128)}, u32[]{:S(2)}) copy-start(f32[16,2,8,1024]{3,2,0,1:T(8,128)} %fusion.36) | copy-start | bytes 3145732
  701.7 1468.2 %copy-start.14 = (bf16[16,16,1024]{2,1,0:T(8,128)(2,1)S(1)}, bf16[16,16,1024]{2,1,0:T(8,128)(2,1)}, u32[]{:S(2)}) copy-start(bf16[16,16,1024]{2,1,0:T(8,128)(2,1)} %param.20) | copy-start | bytes 1572868
  701.7 1468.2 %copy-start.40 = (f32[1,1024]{1,0:T(1,128)S(1)}, f32[1,1024]{1,0:T(1,128)}, u32[]{:S(2)}) copy-start(f32[1,1024]{1,0:T(1,128)} %copy-done.39) | copy-start | bytes 12292
  701.7 1468.2 %copy-start.42 = (f32[16,16]{1,0:T(8,128)S(1)}, f32[16,16]{1,0:T(8,128)}, u32[]{:S(2)}) copy-start(f32[16,16]{1,0:T(8,128)} %copy-done.41) | copy-start | bytes 3076
  701.7 1468.2 %copy-start.44 = (f32[16,16]{1,0:T(8,128)S(1)}, f32[16,16]{1,0:T(8,128)}, u32[]{:S(2)}) copy-start(f32[16,16]{1,0:T(8,128)} %copy-done.43) | copy-start | bytes 3076
  701.8 1468.2 %copy-start.46 = (f32[16,16]{1,0:T(8,128)S(1)}, f32[16,16]{1,0:T(8,128)}, u32[]{:S(2)}) copy-start(f32[16,16]{1,0:T(8,128)} %copy-done.45) | copy-start | bytes 3076
  2170.0 51.3 %copy-start.49 = (f32[2,32]{1,0:T(2,128)S(1)}, f32[2,32]{1,0:T(2,128)}, u32[]{:S(2)}) copy-start(f32[2,32]{1,0:T(2,128)} %param.25) | copy-start | bytes 772
  2170.0 51.3 %copy-start.50 = (f32[2,32]{1,0:T(2,128)S(1)}, f32[2,32]{1,0:T(2,128)}, u32[]{:S(2)}) copy-start(f32[2,32]{1,0:T(2,128)} %param.34) | copy-start | bytes 772
  2170.0 51.3 %copy-start.51 = (f32[2,32]{1,0:T(2,128)S(1)}, f32[2,32]{1,0:T(2,128)}, u32[]{:S(2)}) copy-start(f32[2,32]{1,0:T(2,128)} %param.35) | copy-start | bytes 772
  2170.0 55.7 %copy-start.31 = (f32[64,1024]{1,0:T(8,128)S(1)}, f32[64,1024]{1,0:T(8,128)}, u32[]{:S(2)}) copy-start(f32[64,1024]{1,0:T(8,128)} %param.22) | copy-start | bytes 786436
  2221.9 5.9 copy-start.11
  2221.9 5.9 copy-start.12
  2221.9 5.9 copy-start.28
  2227.8 5.6 copy-start.22
  2227.8 5.5 copy-start.23
  2227.8 5.5 copy-start.33
  2227.9 5.5 copy-start.34
  (14 other events, 20.7 us)
Sparse Core Ops, SparseCore 0:
  11.5 98.6 all-gather.5
  113.6 60.2 all-gather.7
  177.5 113.2 all-gather.11
  294.1 192.9 all-gather.9
  568.1 132.1 reduce-scatter.15
  702.6 144.8 reduce-scatter.9
  855.0 241.3 reduce-scatter.7
  1098.7 353.8 reduce-scatter.13
  1455.0 710.1 reduce-scatter.11
where the time goes:
time: 2250 us; the launch traced here: 2240 us
  waiting for transfers between devices  1910 us (85%)
  matrix products  145 us (6%)
  blocking collectives  90.6 us (4%)
  other arithmetic  44.5 us (2%)
  local copies, waits for them, and re-layouts  31.4 us (1%)
    reduce_scatter x1, waiting for transfers between devices, local(): lax.psum_scatter(expand_term, 'fsdp', scatter_dimension=0, tiled=True)  710 us
    reduce_scatter x1, waiting for transfers between devices, local(): lax.psum_scatter(grad_terms[3], 'fsdp', scatter_dimension=1, tiled=True)  353 us
    reduce_scatter x1, waiting for transfers between devices, local(): lax.psum_scatter(joint_term, 'fsdp', scatter_dimension=0, tiled=True)  247 us
    all_gather x1, waiting for transfers between devices, local(): lax.all_gather(expand_low, 'fsdp', axis=0, tiled=True)  183 us
    reduce_scatter x1, waiting for transfers between devices, local(): lax.psum_scatter(output_term, 'fsdp', scatter_dimension=0, tiled=True)  146 us
    all_gather x1, waiting for transfers between devices, local(): lax.all_gather(shrink_low, 'fsdp', axis=1, tiled=True)  113 us
    unnamed x10, waiting for transfers between devices  63.2 us
    dot_general x4, matrix products, per_set_back(): jnp.einsum('fspd,fspe->sde', grouped, grad_grouped, preferred_element_typ...  55.3 us
  transfers between devices with their start and end apart: 9, of which 9 were waited for; matrix products, arithmetic and copies ran while one was open for 5% of the time, Pallas kernels for 0%

commit v1 on v0

v1 whole, which is shorter than its diff:
```python
import jax
import jax.numpy as jnp
from jax import lax
from jax.sharding import PartitionSpec as P

HEADS = 16
SETS = 2
STEP = 10

NORM_EPS = 1e-05
BETA_ONE = 0.9
BETA_TWO = 0.95
ADAM_EPS = 1e-08
MATRIX_RATE = 0.08
GAIN_RATE = 1.0
MATRIX_DECAY = 0.1
CLIP_LIMIT = 1.0

BF = jnp.bfloat16
F32 = jnp.float32


def dot(a, b):
    return lax.dot_general(a, b, (((1,), (0,)), ((), ())), preferred_element_type=F32)


def dot_nt(a, b):
    return lax.dot_general(a, b, (((1,), (1,)), ((), ())), preferred_element_type=F32)


def dot_tn(a, b):
    return lax.dot_general(a, b, (((0,), (0,)), ((), ())), preferred_element_type=F32)


def adam_step(weight, grad_value, mean_old, square_old, learn_rate, weight_decay):
    mean_new = BETA_ONE * mean_old + (1.0 - BETA_ONE) * grad_value
    square_new = BETA_TWO * square_old + (1.0 - BETA_TWO) * grad_value * grad_value
    mean_hat = mean_new / (1.0 - BETA_ONE**STEP)
    square_hat = square_new / (1.0 - BETA_TWO**STEP)
    weight_new = weight - learn_rate * (
        mean_hat / (jnp.sqrt(square_hat) + ADAM_EPS) + weight_decay * weight
    )
    return (weight_new, mean_new, square_new)


class Cube:
    def __init__(self, count):
        self.count = count
        self.bits = count.bit_length() - 1
        self.top = self.bits - 1
        self.index = lax.axis_index("fsdp")
        chip = list(range(1, self.top))
        third = max(1, len(chip) // 3)
        self.orders = [chip[third * k :] + chip[: third * k] for k in range(3)]

    def bit(self, b):
        return (self.index >> b) & 1

    def swap(self, value, b):
        pairs = [(i, i ^ (1 << b)) for i in range(self.count)]
        return lax.ppermute(value, "fsdp", pairs)

    def gather(self, value, bits, lead=0):
        have = []
        for b in bits:
            other = self.swap(value, b)
            mine = self.bit(b) == 1
            axis = lead + sum(1 for h in have if h > b)
            low = jnp.where(mine, other, value)
            high = jnp.where(mine, value, other)
            value = jnp.stack([low, high], axis=axis)
            have.append(b)
        return value

    def reduce(self, value, have, bits, lead=0, last=F32):
        have = list(have)
        for step, b in enumerate(bits):
            axis = lead + sum(1 for h in have if h > b)
            mine = self.bit(b)
            send = lax.dynamic_index_in_dim(value, 1 - mine, axis, keepdims=False).astype(BF)
            keep = lax.dynamic_index_in_dim(value, mine, axis, keepdims=False)
            other = self.swap(send, b)
            value = keep.astype(F32) + other.astype(F32)
            if step < len(bits) - 1:
                value = value.astype(BF)
            have.remove(b)
        return value.astype(last)

    def total(self, value):
        for b in range(self.bits):
            value = value + self.swap(value, b)
        return value


def cuts(width, parts=3, unit=128):
    units = width // unit
    sizes = [units // parts + (1 if k < units % parts else 0) for k in range(parts)]
    edges = [0]
    for size in sizes:
        edges.append(edges[-1] + size * unit)
    return edges


def local(
    count,
    tokens,
    depth_count,
    cotangent,
    joint_weight,
    output_weight,
    expand_weight,
    shrink_weight,
    norm_gains,
    joint_mean,
    joint_square,
    output_mean,
    output_square,
    expand_mean,
    expand_square,
    shrink_mean,
    shrink_square,
    gains_mean,
    gains_square,
):
    cube = Cube(count)
    half = count // 2
    own_bits = cube.top
    frames, positions, width = tokens.shape
    run = positions // SETS
    in_set = cube.bit(cube.top)
    upper = in_set == 1
    all_frames = 2 * frames
    rows = all_frames * run
    hidden_width = expand_weight.shape[1] // 2
    head_dim = width // HEADS

    def to_sets(value):
        first, second = value[:, :run], value[:, run:]
        other = cube.swap(jnp.where(upper, first, second), cube.top)
        own = jnp.where(upper, second, first)
        low = jnp.where(upper, other, own)
        high = jnp.where(upper, own, other)
        return jnp.concatenate([low, high], axis=0)

    def from_sets(value):
        value = value.reshape(2, frames, run, value.shape[-1])
        own = jnp.where(upper, value[1], value[0])
        other = cube.swap(jnp.where(upper, value[0], value[1]), cube.top)
        first = jnp.where(upper, other, own)
        second = jnp.where(upper, own, other)
        return jnp.concatenate([first, second], axis=1)

    position_index = jnp.arange(positions)
    live_here = (position_index[None, :] < depth_count[:, None]).astype(F32)[:, :, None]
    masked = (cotangent.astype(F32) * live_here).astype(BF)

    gains_local = norm_gains.astype(BF)
    gains_all = cube.gather(gains_local, range(cube.bits), lead=1)
    gains_all = gains_all.reshape(2, width).astype(F32)

    def gather_matrix(shard, order, lead=0):
        return cube.gather(shard, list(order) + [0], lead=lead)

    joint_low = joint_weight.astype(BF)
    joint_parts = [
        gather_matrix(joint_low[:, k * width : (k + 1) * width], cube.orders[k]).reshape(width, width)
        for k in range(3)
    ]
    x_rows = to_sets(tokens).reshape(rows, width).astype(F32)
    live = to_sets(live_here).reshape(rows, 1)
    cot = to_sets(masked).reshape(rows, width)

    output_low = output_weight.astype(BF)
    expand_low = expand_weight.astype(BF)
    wide = hidden_width // 4
    edge = [0, wide, (wide + hidden_width) // 2, hidden_width]
    expand_shards = []
    for k in range(3):
        gate_cols = expand_low[:, edge[k] : edge[k + 1]]
        up_cols = expand_low[:, hidden_width + edge[k] : hidden_width + edge[k + 1]]
        parts = ([output_low] if k == 0 else []) + [gate_cols, up_cols]
        expand_shards.append(jnp.concatenate(parts, axis=1))
    expand_parts = [
        gather_matrix(expand_shards[k], cube.orders[k]).reshape(width, -1) for k in range(3)
    ]
    output_full = expand_parts[0][:, :width]
    gate_full = [expand_parts[0][:, width : 2 * width]] + [
        expand_parts[k][:, : edge[k + 1] - edge[k]] for k in (1, 2)
    ]
    up_full = [expand_parts[0][:, 2 * width :]] + [
        expand_parts[k][:, edge[k + 1] - edge[k] :] for k in (1, 2)
    ]

    shrink_low = shrink_weight.astype(BF)
    shrink_mine = jnp.where(upper, shrink_low[1], shrink_low[0])
    shrink_send = jnp.where(upper, shrink_low[0], shrink_low[1])
    shrink_other = cube.swap(shrink_send, cube.top)
    shrink_pair = jnp.stack(
        [jnp.where(upper, shrink_other, shrink_mine), jnp.where(upper, shrink_mine, shrink_other)]
    )
    col = cuts(width)
    shrink_parts = [
        gather_matrix(shrink_pair[:, :, col[k] : col[k + 1]], cube.orders[k], lead=1).reshape(
            hidden_width, -1
        )
        for k in range(3)
    ]

    inv_one = lax.rsqrt(jnp.mean(x_rows * x_rows, axis=-1, keepdims=True) + NORM_EPS)
    first = (x_rows * inv_one * gains_all[0]).astype(BF)
    query, key_own, value_own = [dot(first, joint_parts[k]).astype(BF) for k in range(3)]
    key_value = cube.swap(jnp.concatenate([key_own, value_own], axis=1), cube.top)

    def heads(value):
        return value.reshape(all_frames, run, HEADS, head_dim)

    q_h = heads(query)
    k_h = jnp.concatenate([heads(key_value[:, :width]), heads(key_own)], axis=1)
    v_h = jnp.concatenate([heads(key_value[:, width:]), heads(value_own)], axis=1)
    scale = head_dim ** (-0.5)
    scores = jnp.einsum("fphd,fkhd->fhpk", q_h, k_h, preferred_element_type=F32) * scale
    row = jnp.arange(run)[:, None]
    column = jnp.arange(2 * run)[None, :]
    seen = jnp.where(column < run, upper, row >= column - run)
    scores = jnp.where(seen, scores, -1e30)
    exp_scores = jnp.exp(scores - jnp.max(scores, axis=-1, keepdims=True))
    attention = exp_scores / jnp.sum(exp_scores, axis=-1, keepdims=True)
    attention_low = attention.astype(BF)
    context = (
        jnp.einsum("fhpk,fkhd->fphd", attention_low, v_h, preferred_element_type=F32)
        .reshape(rows, width)
        .astype(BF)
    )
    middle = x_rows + live * dot(context, output_full)
    inv_two = lax.rsqrt(jnp.mean(middle * middle, axis=-1, keepdims=True) + NORM_EPS)
    second = (middle * inv_two * gains_all[1]).astype(BF)
    gate = [dot(second, w) for w in gate_full]
    up = [dot(second, w) for w in up_full]
    hidden = jnp.concatenate(
        [(jax.nn.silu(g) * u).astype(BF) for g, u in zip(gate, up)], axis=1
    )
    shrunk = jnp.concatenate([dot(hidden, w) for w in shrink_parts], axis=1)
    result = from_sets((middle + live * shrunk).astype(BF))

    def reduce_matrix(grad, order, lead=0, block=None):
        bits = list(range(own_bits))
        shape = grad.shape
        if lead:
            grad = grad.reshape((2,) + (2,) * own_bits + (shape[0] // 2 // half, shape[1]))
        else:
            grad = grad.reshape((2,) * own_bits + (shape[0] // half, shape[1]))
        return cube.reduce(grad, bits, [0] + list(order), lead=lead)

    grad_shrink_parts = [
        reduce_matrix(dot_tn(hidden, cot[:, col[k] : col[k + 1]]).astype(BF), cube.orders[k], lead=1)
        for k in range(3)
    ]
    grad_shrink_pair = jnp.concatenate(grad_shrink_parts, axis=-1)
    shrink_keep = jnp.where(upper, grad_shrink_pair[1], grad_shrink_pair[0])
    shrink_give = jnp.where(upper, grad_shrink_pair[0], grad_shrink_pair[1]).astype(BF)
    shrink_got = cube.swap(shrink_give, cube.top).astype(F32)
    grad_shrink = jnp.stack(
        [jnp.where(upper, shrink_got, shrink_keep), jnp.where(upper, shrink_keep, shrink_got)]
    )

    grad_hidden = sum(dot_nt(cot[:, col[k] : col[k + 1]], shrink_parts[k]) for k in range(3))
    grad_second = 0.0
    grad_expand_parts = []
    for k in range(3):
        d_hid = grad_hidden[:, edge[k] : edge[k + 1]]
        sig = jax.nn.sigmoid(gate[k])
        d_gate = (d_hid * up[k] * sig * (1.0 + gate[k] * (1.0 - sig))).astype(BF)
        d_up = (d_hid * gate[k] * sig).astype(BF)
        both = jnp.concatenate([d_gate, d_up], axis=1)
        weight_pair = jnp.concatenate([gate_full[k], up_full[k]], axis=1)
        grad_second = grad_second + dot_nt(both, weight_pair)
        grad_expand_parts.append(
            reduce_matrix(dot_tn(second, both).astype(BF), cube.orders[k])
        )
    grad_expand = jnp.concatenate(
        [grad_expand_parts[k][:, : edge[k + 1] - edge[k]] for k in range(3)]
        + [grad_expand_parts[k][:, edge[k + 1] - edge[k] :] for k in range(3)],
        axis=1,
    )

    def normalize_back(values, inverse, gain_row, grad_out):
        scaled = grad_out * gain_row
        grad_in = inverse * scaled - values * inverse * inverse * inverse * jnp.mean(
            scaled * values, axis=-1, keepdims=True
        )
        return (grad_in, jnp.sum(grad_out * values * inverse, axis=0))

    grad_mid_norm, grad_gain_two = normalize_back(middle, inv_two, gains_all[1], grad_second)
    grad_middle = cot.astype(F32) + grad_mid_norm
    grad_branch = (grad_middle * live).astype(BF)
    grad_context = dot_nt(grad_branch, output_full).astype(BF)

    g_h = heads(grad_context)
    grad_attention = jnp.einsum("fphd,fkhd->fhpk", g_h, v_h, preferred_element_type=F32)
    grad_value = jnp.einsum("fhpk,fphd->fkhd", attention_low, g_h, preferred_element_type=F32)
    grad_scores = attention * (
        grad_attention - jnp.sum(grad_attention * attention, axis=-1, keepdims=True)
    )
    grad_scores = grad_scores.astype(BF)
    grad_query = (
        jnp.einsum("fhpk,fkhd->fphd", grad_scores, k_h, preferred_element_type=F32) * scale
    )
    grad_key = jnp.einsum("fhpk,fphd->fkhd", grad_scores, q_h, preferred_element_type=F32) * scale
    give = jnp.concatenate(
        [grad_key[:, :run].reshape(rows, width), grad_value[:, :run].reshape(rows, width)], axis=1
    ).astype(BF)
    got = cube.swap(give, cube.top).astype(F32)
    got = jnp.where(upper, 0.0, got)
    d_query = grad_query.reshape(rows, width).astype(BF)
    d_key = (grad_key[:, run:].reshape(rows, width) + got[:, :width]).astype(BF)
    d_value = (grad_value[:, run:].reshape(rows, width) + got[:, width:]).astype(BF)

    grad_output = reduce_matrix(dot_tn(context, grad_branch).astype(BF), cube.orders[0])
    joint_grads = [
        reduce_matrix(dot_tn(first, d).astype(BF), cube.orders[k])
        for k, d in enumerate((d_query, d_key, d_value))
    ]
    grad_joint = jnp.concatenate(joint_grads, axis=1)
    grad_first = sum(
        dot_nt(d, w) for d, w in zip((d_query, d_key, d_value), joint_parts)
    )
    grad_in_norm, grad_gain_one = normalize_back(x_rows, inv_one, gains_all[0], grad_first)
    grad_inputs = from_sets((grad_middle + grad_in_norm).astype(BF))

    gains_term = jnp.stack([grad_gain_one, grad_gain_two]).reshape((2,) + (2,) * cube.bits + (-1,))
    bits = list(range(cube.bits))
    have = list(bits)
    for b in bits:
        axis = 1 + sum(1 for h in have if h > b)
        mine = cube.bit(b)
        send = lax.dynamic_index_in_dim(gains_term, 1 - mine, axis, keepdims=False)
        keep = lax.dynamic_index_in_dim(gains_term, mine, axis, keepdims=False)
        gains_term = keep + cube.swap(send, b)
        have.remove(b)
    grad_gains = gains_term

    reduced = (grad_joint, grad_output, grad_expand, grad_shrink, grad_gains)
    local_sq = sum(jnp.sum(g * g) for g in reduced)
    total_sq = cube.total(jnp.broadcast_to(local_sq, (8, 128)))[0, 0]
    grad_norm_value = jnp.sqrt(total_sq)
    factor = CLIP_LIMIT / jnp.maximum(grad_norm_value, CLIP_LIMIT)
    joint_new = adam_step(
        joint_weight, factor * reduced[0], joint_mean, joint_square, MATRIX_RATE, MATRIX_DECAY
    )
    output_new = adam_step(
        output_weight, factor * reduced[1], output_mean, output_square, MATRIX_RATE, MATRIX_DECAY
    )
    expand_new = adam_step(
        expand_weight, factor * reduced[2], expand_mean, expand_square, MATRIX_RATE, MATRIX_DECAY
    )
    shrink_new = adam_step(
        shrink_weight, factor * reduced[3], shrink_mean, shrink_square, MATRIX_RATE, MATRIX_DECAY
    )
    gains_new = adam_step(norm_gains, factor * reduced[4], gains_mean, gains_square, GAIN_RATE, 0.0)
    return (
        result,
        grad_inputs,
        grad_norm_value,
        *joint_new,
        *output_new,
        *expand_new,
        *shrink_new,
        *gains_new,
    )


def solution(mesh):
    rows = P("fsdp", None)
    cube = P("fsdp", None, None)
    inner = P(None, "fsdp", None)
    gains = P(None, "fsdp")
    count = mesh.shape["fsdp"]

    def body(*args):
        return local(count, *args)

    return jax.shard_map(
        body,
        mesh=mesh,
        in_specs=(cube, P("fsdp"), cube, rows, rows, rows, inner, gains)
        + (rows,) * 6
        + (inner, inner, gains, gains),
        out_specs=(cube, cube, P()) + (rows,) * 9 + (inner,) * 3 + (gains,) * 3,
        check_vma=False,
    )
```

time: 2250 us -> 685 us (0.30)
  waiting for transfers between devices: 1910 us -> 278 us
  blocking collectives: 90.6 us -> 0 us
  other arithmetic: 44.5 us -> 123 us
  starting transfers between devices: 0.55 us -> 74.9 us
  local copies, waits for them, and re-layouts: 31.4 us -> 101 us
  matrix products: 145 us -> 88.4 us
    reduce_scatter x4 -> x0, waiting for transfers between devices: 1460 us -> none  [the longest x1 710 us: local(): lax.psum_scatter(expand_term, 'fsdp', scatter_dimension=0, tiled=True)]
    all_gather x4 -> x0, waiting for transfers between devices: 392 us -> none  [the longest x1 183 us: local(): lax.all_gather(expand_low, 'fsdp', axis=0, tiled=True)]
    ppermute x0 -> x100, waiting for transfers between devices: none -> 278 us  [swap(): return lax.ppermute(value, 'fsdp', pairs)]
    ppermute x0 -> x100, starting transfers between devices: none -> 74.9 us  [swap(): return lax.ppermute(value, 'fsdp', pairs)]
    unnamed x10 -> x0, waiting for transfers between devices: 63.2 us -> none
    dot_general x17 -> x38, matrix products: 143 us -> 83.1 us  [the longest x13 28.1 us: dot(): lax.dot_general(a, b, (((1,), (0,)), ((), ())), preferred_element_type=F32)]
    another operation x2 -> x80, other arithmetic: 0.77 us -> 57.3 us  [the longest x76 54.7 us: gather(): value = jnp.stack([low, high], axis=axis)]
    psum x1 -> x0, blocking collectives: 47.1 us -> none  [local(): total_sq = lax.psum(local_sq, 'fsdp')]
  transfers between devices with their start and end apart: 9 -> 100, of which waited for: 9 -> 47; matrix products, arithmetic and copies ran while one was open for 5% -> 32% of each run, Pallas kernels for 0% -> 0%
where the time goes in v1:
time: 685 us; the launch traced here: 675 us
  waiting for transfers between devices  278 us (41%)
  other arithmetic  123 us (18%)
  local copies, waits for them, and re-layouts  101 us (15%)
  matrix products  88.4 us (13%)
  starting transfers between devices  74.9 us (11%)
  between operations  9.27 us (1%)
    ppermute x100, waiting for transfers between devices, swap(): return lax.ppermute(value, 'fsdp', pairs)  278 us
    ppermute x100, starting transfers between devices, swap(): return lax.ppermute(value, 'fsdp', pairs)  74.9 us
    another operation x76, other arithmetic, gather(): value = jnp.stack([low, high], axis=axis)  54.7 us
    dot_general x13, matrix products, dot(): lax.dot_general(a, b, (((1,), (0,)), ((), ())), preferred_element_type=F32)  28.1 us
    dot_general x10, matrix products, dot_tn(): lax.dot_general(a, b, (((0,), (0,)), ((), ())), preferred_element_type=F32)  24.3 us
    unnamed x364, local copies, waits for them, and re-layouts  23.9 us
    convert_element_type x30, other arithmetic, reduce(): value = value.astype(BF)  22.6 us
    dot_general x10, matrix products, dot_nt(): lax.dot_general(a, b, (((1,), (1,)), ((), ())), preferred_element_type=F32)  18.2 us
  transfers between devices with their start and end apart: 100, of which 47 were waited for; matrix products, arithmetic and copies ran while one was open for 32% of the time, Pallas kernels for 0%

profile of v1, /device:TPU:0, one launch (start us, length us, event | category | flops | bytes accessed | tf_op | source)
XLA Modules:
  0.0 674.9 jit_solution(5873338750763757167)
XLA Ops:
  26.8 3.1 collective-permute-done.4
  30.2 4.1 collective-permute-done.1
  34.8 3.2 collective-permute-done.5
  39.2 3.6 collective-permute-done.6
  54.0 7.3 %collective-permute-done.32 = bf16[128,1024]{1,0:T(8,128)(2,1)S(1)} collective-permute-done((bf16[128,1024]{1,0:T(8,128)(2,1)}, bf16[128,1024]{1,0:T(8,128)(2,1)S(1)}, u32[]{:S(2)}, u32[]{:S(2)}) %collective-permute-start.32) | collective-permute-done | bytes 262176 | tf_op jit(solution)/shard_map/ppermute | solution.py:61
  62.7 3.2 collective-permute-done.46
  74.3 3.1 collective-permute-done.8
  85.3 4.4 collective-permute-start.42
  93.1 6.1 collective-permute-done.42
  102.7 8.6 %collective-permute-done.34 = bf16[2,2,128,384]{3,2,0,1:T(8,128)(2,1)S(1)} collective-permute-done((bf16[2,2,128,384]{3,2,0,1:T(8,128)(2,1)S(1)}, bf16[2,2,128,384]{3,2,0,1:T(8,128)(2,1)S(1)}, u32[]{:S(2)}, u32[]{:S(2)}) %collective-permute-start.34) | collective-permute-done | bytes 393248 | tf_op jit(solution)/shard_map/ppermute | solution.py:61
  116.6 17.0 %collective-permute-done.43 = bf16[2,2,2,128,256]{4,3,0,1,2:T(8,128)(2,1)S(1)} collective-permute-done((bf16[2,2,2,128,256]{4,3,0,1,2:T(8,128)(2,1)S(1)}, bf16[2,2,2,128,256]{4,3,0,1,2:T(8,128)(2,1)S(1)}, u32[]{:S(2)}, u32[]{:S(2)}) %collective-permute-start.43) | collective-permute-done | bytes 524320 | tf_op jit(solution)/shard_map/ppermute | solution.py:61
  142.9 6.3 collective-permute-done.35
  170.1 12.5 %collective-permute-done.22 = bf16[2,2,64,3072]{3,2,1,0:T(8,128)(2,1)} collective-permute-done((bf16[2,2,64,3072]{3,2,1,0:T(8,128)(2,1)}, bf16[2,2,64,3072]{3,2,1,0:T(8,128)(2,1)}, u32[]{:S(2)}, u32[]{:S(2)}) %collective-permute-start.22) | collective-permute-done | bytes 1572896 | tf_op jit(solution)/shard_map/ppermute | solution.py:61
  195.3 29.0 %collective-permute-done.15 = bf16[256,2048]{1,0:T(8,128)(2,1)S(1)} collective-permute-done((bf16[256,2048]{1,0:T(8,128)(2,1)S(1)}, bf16[256,2048]{1,0:T(8,128)(2,1)S(1)}, u32[]{:S(2)}, u32[]{:S(2)}) %collective-permute-start.15) | collective-permute-done | bytes 1048608 | tf_op jit(solution)/shard_map/ppermute | solution.py:61
  237.9 5.2 fusion.160
  250.1 3.4 select_bitcast_fusion.7
  261.6 3.3 select_bitcast_fusion.1
  267.4 3.1 copy.255
  272.7 3.2 pad_maximum_fusion
  278.7 3.5 fusion.19
  295.4 3.2 multiply_convert_fusion.10
  298.9 5.2 multiply_convert_fusion.5
  318.8 3.8 multiply_reduce_fusion.1
  337.7 3.3 convolution_convert_fusion.5
  341.0 4.5 convolution_convert_fusion.1
  345.5 4.5 convolution_convert_fusion
  372.5 3.3 reshape.539
  409.9 7.2 %collective-permute-done.47 = bf16[256,2048]{1,0:T(8,128)(2,1)} collective-permute-done((bf16[256,2048]{1,0:T(8,128)(2,1)}, bf16[256,2048]{1,0:T(8,128)(2,1)}, u32[]{:S(2)}, u32[]{:S(2)}) %collective-permute-start.47) | collective-permute-done | bytes 1048608 | tf_op jit(solution)/shard_map/ppermute | solution.py:61
  434.5 7.3 %collective-permute-done.91 = f32[2,2,2,2,32]{4,3,2,1,0:T(2,128)S(1)} collective-permute-done((f32[2,2,2,2,32]{4,3,2,1,0:T(2,128)S(1)}, f32[2,2,2,2,32]{4,3,2,1,0:T(2,128)S(1)}, u32[]{:S(2)}, u32[]{:S(2)}) %collective-permute-start.91) | collective-permute-done | bytes 2080 | tf_op jit(solution)/shard_map/ppermute | solution.py:61
  445.7 3.5 collective-permute-done.93
  449.5 4.3 collective-permute-done.94
  454.9 8.4 %collective-permute-done.62 = bf16[2,2,64,1024]{3,2,0,1:T(8,128)(2,1)S(1)} collective-permute-done((bf16[2,2,64,1024]{3,2,0,1:T(8,128)(2,1)S(1)}, bf16[2,2,64,1024]{3,2,0,1:T(8,128)(2,1)S(1)}, u32[]{:S(2)}, u32[]{:S(2)}) %collective-permute-start.62) | collective-permute-done | bytes 524320 | tf_op jit(solution)/shard_map/ppermute | solution.py:61
  469.3 4.3 collective-permute-done.51
  475.1 3.7 collective-permute-done.63
  481.5 3.7 collective-permute-done.52
  498.2 12.1 %collective-permute-done.82 = bf16[2,2,2,128,384]{4,3,0,2,1:T(8,128)(2,1)S(1)} collective-permute-done((bf16[2,2,2,128,384]{4,3,0,2,1:T(8,128)(2,1)S(1)}, bf16[2,2,2,128,384]{4,3,0,2,1:T(8,128)(2,1)S(1)}, u32[]{:S(2)}, u32[]{:S(2)}) %collective-permute-start.82) | collective-permute-done | bytes 786464 | tf_op jit(solution)/shard_map/ppermute | solution.py:61
  513.6 10.2 %collective-permute-done.54 = bf16[2,2,64,1024]{3,2,1,0:T(8,128)(2,1)S(1)} collective-permute-done((bf16[2,2,64,1024]{3,2,1,0:T(8,128)(2,1)S(1)}, bf16[2,2,64,1024]{3,2,1,0:T(8,128)(2,1)S(1)}, u32[]{:S(2)}, u32[]{:S(2)}) %collective-permute-start.54) | collective-permute-done | bytes 524320 | tf_op jit(solution)/shard_map/ppermute | solution.py:61
  526.6 7.2 %collective-permute-done.79 = bf16[2,2,128,384]{3,2,0,1:T(8,128)(2,1)S(1)} collective-permute-done((bf16[2,2,128,384]{3,2,0,1:T(8,128)(2,1)S(1)}, bf16[2,2,128,384]{3,2,0,1:T(8,128)(2,1)S(1)}, u32[]{:S(2)}, u32[]{:S(2)}) %collective-permute-start.79) | collective-permute-done | bytes 393248 | tf_op jit(solution)/shard_map/ppermute | solution.py:61
  534.2 7.3 %collective-permute-done.59 = bf16[2,64,1024]{2,1,0:T(8,128)(2,1)S(1)} collective-permute-done((bf16[2,64,1024]{2,1,0:T(8,128)(2,1)S(1)}, bf16[2,64,1024]{2,1,0:T(8,128)(2,1)S(1)}, u32[]{:S(2)}, u32[]{:S(2)}) %collective-permute-start.59) | collective-permute-done | bytes 262176 | tf_op jit(solution)/shard_map/ppermute | solution.py:61
  543.6 3.5 collective-permute-done.84
  568.3 5.6 collective-permute-done.67
  576.6 30.5 %collective-permute-done.68 = bf16[64,2048]{1,0:T(8,128)(2,1)S(1)} collective-permute-done((bf16[64,2048]{1,0:T(8,128)(2,1)S(1)}, bf16[64,2048]{1,0:T(8,128)(2,1)S(1)}, u32[]{:S(2)}, u32[]{:S(2)}) %collective-permute-start.68) | collective-permute-done | bytes 262176 | tf_op jit(solution)/shard_map/ppermute | solution.py:61
  610.9 11.3 %collective-permute-done.71 = bf16[2,64,3072]{2,1,0:T(8,128)(2,1)S(1)} collective-permute-done((bf16[2,64,3072]{2,1,0:T(8,128)(2,1)S(1)}, bf16[2,64,3072]{2,1,0:T(8,128)(2,1)S(1)}, u32[]{:S(2)}, u32[]{:S(2)}) %collective-permute-start.71) | collective-permute-done | bytes 786464 | tf_op jit(solution)/shard_map/ppermute | solution.py:61
  625.7 4.6 collective-permute-done.72
  647.1 7.5 %collective-permute-done.48 = bf16[16,8,1024]{2,1,0:T(8,128)(2,1)S(1)} collective-permute-done((bf16[16,8,1024]{2,1,0:T(8,128)(2,1)S(1)}, bf16[16,8,1024]{2,1,0:T(8,128)(2,1)S(1)}, u32[]{:S(2)}, u32[]{:S(2)}) %collective-permute-start.48) | collective-permute-done | bytes 262176 | tf_op jit(solution)/shard_map/ppermute | solution.py:61
  655.6 3.7 collective-permute-done.99
  660.5 3.4 multiply_subtract_fusion.2
  664.0 5.5 multiply_subtract_fusion
  (849 shorter events, 349.9 us)
Async XLA Ops:
  2.8 41.9 %collective-permute-start.16 = (bf16[64,1024]{1,0:T(8,128)(2,1)}, bf16[64,1024]{1,0:T(8,128)(2,1)}, u32[]{:S(2)}, u32[]{:S(2)}) collective-permute-start(bf16[64,1024]{1,0:T(8,128)(2,1)} %get-tuple-element.170), channel_id=1, source_target_pairs={{0,2},{1,3},{2,0},{3,1},{4,6},{5,7},{6,4},{7,5},{8,10},{9,11},{10,... | collective-permute-start | bytes 393224 | tf_op jit(solution)/shard_map/ppermute | solution.py:61
  5.7 39.4 %collective-permute-start.7 = (bf16[64,1024]{1,0:T(8,128)(2,1)}, bf16[64,1024]{1,0:T(8,128)(2,1)}, u32[]{:S(2)}, u32[]{:S(2)}) collective-permute-start(bf16[64,1024]{1,0:T(8,128)(2,1)} %get-tuple-element.172), channel_id=1, source_target_pairs={{0,4},{1,5},{2,6},{3,7},{4,0},{5,1},{6,2},{7,3},{8,12},{9,13},{10,... | collective-permute-start | bytes 393224 | tf_op jit(solution)/shard_map/ppermute | solution.py:61
  7.2 38.2 %collective-permute-start.11 = (bf16[64,1024]{1,0:T(8,128)(2,1)}, bf16[64,1024]{1,0:T(8,128)(2,1)}, u32[]{:S(2)}, u32[]{:S(2)}) collective-permute-start(bf16[64,1024]{1,0:T(8,128)(2,1)} %get-tuple-element.171), channel_id=1, source_target_pairs={{0,8},{1,9},{2,10},{3,11},{4,12},{5,13},{6,14},{7,15},{8,0},{9,1},... | collective-permute-start | bytes 393224 | tf_op jit(solution)/shard_map/ppermute | solution.py:61
  10.7 40.7 %collective-permute-start = (bf16[16,8,1024]{2,1,0:T(8,128)(2,1)}, bf16[16,8,1024]{2,1,0:T(8,128)(2,1)}, u32[]{:S(2)}, u32[]{:S(2)}) collective-permute-start(bf16[16,8,1024]{2,1,0:T(8,128)(2,1)} %broadcast_select_fusion.10), channel_id=1, source_target_pairs={{0,16},{1,17},{2,18},{3,19},{4,20},{5,21},{6,22},{7,23},{8,24},{9,... | collective-permute-start | bytes 786440 | tf_op jit(solution)/shard_map/ppermute | solution.py:61
  42.8 38.8 %collective-permute-start.20 = (bf16[64,3072]{1,0:T(8,128)(2,1)}, bf16[64,3072]{1,0:T(8,128)(2,1)}, u32[]{:S(2)}, u32[]{:S(2)}) collective-permute-start(bf16[64,3072]{1,0:T(8,128)(2,1)} %pad_maximum_fusion.48), channel_id=1, source_target_pairs={{0,2},{1,3},{2,0},{3,1},{4,6},{5,7},{6,4},{7,5},{8,10},{9,11},{10,... | collective-permute-start | bytes 1179656 | tf_op jit(solution)/shard_map/ppermute | solution.py:61
  44.7 38.8 %collective-permute-start.28 = (bf16[64,3072]{1,0:T(8,128)(2,1)}, bf16[64,3072]{1,0:T(8,128)(2,1)}, u32[]{:S(2)}, u32[]{:S(2)}) collective-permute-start(bf16[64,3072]{1,0:T(8,128)(2,1)} %pad_maximum_fusion.50), channel_id=1, source_target_pairs={{0,8},{1,9},{2,10},{3,11},{4,12},{5,13},{6,14},{7,15},{8,0},{9,1},... | collective-permute-start | bytes 1179656 | tf_op jit(solution)/shard_map/ppermute | solution.py:61
  45.4 20.5 %collective-permute-start.46 = (bf16[16,8,1024]{2,1,0:T(8,128)(2,1)}, bf16[16,8,1024]{2,1,0:T(8,128)(2,1)S(1)}, u32[]{:S(2)}, u32[]{:S(2)}) collective-permute-start(bf16[16,8,1024]{2,1,0:T(8,128)(2,1)} %broadcast_select_fusion.6), channel_id=1, source_target_pairs={{0,16},{1,17},{2,18},{3,19},{4,20},{5,21},{6,22},{7,23},{8,24},{9,... | collective-permute-start | bytes 786440 | tf_op jit(solution)/shard_map/ppermute | solution.py:61
  51.4 19.7 %collective-permute-start.12 = (bf16[2,64,1024]{2,1,0:T(8,128)(2,1)}, bf16[2,64,1024]{2,1,0:T(8,128)(2,1)}, u32[]{:S(2)}, u32[]{:S(2)}) collective-permute-start(bf16[2,64,1024]{2,1,0:T(8,128)(2,1)} %pad_maximum_fusion.54), channel_id=1, source_target_pairs={{0,2},{1,3},{2,0},{3,1},{4,6},{5,7},{6,4},{7,5},{8,10},{9,11},{10,... | collective-permute-start | bytes 786440 | tf_op jit(solution)/shard_map/ppermute | solution.py:61
  81.6 30.2 %collective-permute-start.13 = (bf16[2,2,64,1024]{3,2,1,0:T(8,128)(2,1)S(1)}, bf16[2,2,64,1024]{3,2,1,0:T(8,128)(2,1)S(1)}, u32[]{:S(2)}, u32[]{:S(2)}) collective-permute-start(bf16[2,2,64,1024]{3,2,1,0:T(8,128)(2,1)S(1)} %pad_maximum_fusion.43), channel_id=1, source_target_pairs={{0,4},{1,5},{2,6},{3,7},{4,0},{5,1},{6,2},{7,3},{8,12},{9,13},{10,... | collective-permute-start | bytes 1572872 | tf_op jit(solution)/shard_map/ppermute | solution.py:61
  83.5 28.9 %collective-permute-start.9 = (bf16[2,2,64,1024]{3,2,1,0:T(8,128)(2,1)S(1)}, bf16[2,2,64,1024]{3,2,1,0:T(8,128)(2,1)S(1)}, u32[]{:S(2)}, u32[]{:S(2)}) collective-permute-start(bf16[2,2,64,1024]{3,2,1,0:T(8,128)(2,1)S(1)} %pad_maximum_fusion.42), channel_id=1, source_target_pairs={{0,2},{1,3},{2,0},{3,1},{4,6},{5,7},{6,4},{7,5},{8,10},{9,11},{10,... | collective-permute-start | bytes 1572872 | tf_op jit(solution)/shard_map/ppermute | solution.py:61
  84.9 28.8 %collective-permute-start.18 = (bf16[2,2,64,1024]{3,2,1,0:T(8,128)(2,1)S(1)}, bf16[2,2,64,1024]{3,2,1,0:T(8,128)(2,1)S(1)}, u32[]{:S(2)}, u32[]{:S(2)}) collective-permute-start(bf16[2,2,64,1024]{3,2,1,0:T(8,128)(2,1)S(1)} %pad_maximum_fusion.44), channel_id=1, source_target_pairs={{0,8},{1,9},{2,10},{3,11},{4,12},{5,13},{6,14},{7,15},{8,0},{9,1},... | collective-permute-start | bytes 1572872 | tf_op jit(solution)/shard_map/ppermute | solution.py:61
  101.4 33.9 %collective-permute-start.21 = (bf16[2,64,3072]{2,1,0:T(8,128)(2,1)S(1)}, bf16[2,64,3072]{2,1,0:T(8,128)(2,1)S(1)}, u32[]{:S(2)}, u32[]{:S(2)}) collective-permute-start(bf16[2,64,3072]{2,1,0:T(8,128)(2,1)S(1)} %pad_maximum_fusion.33), channel_id=1, source_target_pairs={{0,4},{1,5},{2,6},{3,7},{4,0},{5,1},{6,2},{7,3},{8,12},{9,13},{10,... | collective-permute-start | bytes 2359304 | tf_op jit(solution)/shard_map/ppermute | solution.py:61
  111.3 24.2 %collective-permute-start.29 = (bf16[2,64,3072]{2,1,0:T(8,128)(2,1)S(1)}, bf16[2,64,3072]{2,1,0:T(8,128)(2,1)S(1)}, u32[]{:S(2)}, u32[]{:S(2)}) collective-permute-start(bf16[2,64,3072]{2,1,0:T(8,128)(2,1)S(1)} %pad_maximum_fusion.35), channel_id=1, source_target_pairs={{0,2},{1,3},{2,0},{3,1},{4,6},{5,7},{6,4},{7,5},{8,10},{9,11},{10,... | collective-permute-start | bytes 2359304 | tf_op jit(solution)/shard_map/ppermute | solution.py:61
  111.8 24.4 %collective-permute-start.25 = (bf16[2,64,3072]{2,1,0:T(8,128)(2,1)S(1)}, bf16[2,64,3072]{2,1,0:T(8,128)(2,1)S(1)}, u32[]{:S(2)}, u32[]{:S(2)}) collective-permute-start(bf16[2,64,3072]{2,1,0:T(8,128)(2,1)S(1)} %pad_maximum_fusion.34), channel_id=1, source_target_pairs={{0,8},{1,9},{2,10},{3,11},{4,12},{5,13},{6,14},{7,15},{8,0},{9,1},... | collective-permute-start | bytes 2359304 | tf_op jit(solution)/shard_map/ppermute | solution.py:61
  112.3 21.3 %collective-permute-start.43 = (bf16[2,2,2,128,256]{4,3,0,1,2:T(8,128)(2,1)S(1)}, bf16[2,2,2,128,256]{4,3,0,1,2:T(8,128)(2,1)S(1)}, u32[]{:S(2)}, u32[]{:S(2)}) collective-permute-start(bf16[2,2,2,128,256]{4,3,0,1,2:T(8,128)(2,1)S(1)} %pad_maximum_fusion.45), channel_id=1, source_target_pairs={{0,4},{1,5},{2,6},{3,7},{4,0},{5,1},{6,2},{7,3},{8,12},{9,13},{10,... | collective-permute-start | bytes 1572872 | tf_op jit(solution)/shard_map/ppermute | solution.py:61
  113.7 27.1 %collective-permute-start.39 = (bf16[2,2,2,128,384]{4,3,0,2,1:T(8,128)(2,1)S(1)}, bf16[2,2,2,128,384]{4,3,0,2,1:T(8,128)(2,1)S(1)}, u32[]{:S(2)}, u32[]{:S(2)}) collective-permute-start(bf16[2,2,2,128,384]{4,3,0,2,1:T(8,128)(2,1)S(1)} %pad_maximum_fusion.37), channel_id=1, source_target_pairs={{0,2},{1,3},{2,0},{3,1},{4,6},{5,7},{6,4},{7,5},{8,10},{9,11},{10,... | collective-permute-start | bytes 2359304 | tf_op jit(solution)/shard_map/ppermute | solution.py:61
  136.2 24.5 %collective-permute-start.19 = (bf16[2,2,2,64,1024]{4,3,2,1,0:T(8,128)(2,1)}, bf16[2,2,2,64,1024]{4,3,2,1,0:T(8,128)(2,1)}, u32[]{:S(2)}, u32[]{:S(2)}) collective-permute-start(bf16[2,2,2,64,1024]{4,3,2,1,0:T(8,128)(2,1)} %pad_maximum_fusion.23), channel_id=1, source_target_pairs={{0,1},{1,0},{2,3},{3,2},{4,5},{5,4},{6,7},{7,6},{8,9},{9,8},{10,11... | collective-permute-start | bytes 3145736 | tf_op jit(solution)/shard_map/ppermute | solution.py:61
  140.8 25.5 %collective-permute-start.44 = (bf16[2,2,2,2,128,256]{5,4,0,1,3,2:T(8,128)(2,1)}, bf16[2,2,2,2,128,256]{5,4,0,1,3,2:T(8,128)(2,1)}, u32[]{:S(2)}, u32[]{:S(2)}) collective-permute-start(bf16[2,2,2,2,128,256]{5,4,0,1,3,2:T(8,128)(2,1)} %pad_maximum_fusion.24), channel_id=1, source_target_pairs={{0,1},{1,0},{2,3},{3,2},{4,5},{5,4},{6,7},{7,6},{8,9},{9,8},{10,11... | collective-permute-start | bytes 3145736 | tf_op jit(solution)/shard_map/ppermute | solution.py:61
  149.2 33.4 %collective-permute-start.22 = (bf16[2,2,64,3072]{3,2,1,0:T(8,128)(2,1)}, bf16[2,2,64,3072]{3,2,1,0:T(8,128)(2,1)}, u32[]{:S(2)}, u32[]{:S(2)}) collective-permute-start(bf16[2,2,64,3072]{3,2,1,0:T(8,128)(2,1)} %pad_maximum_fusion.13), channel_id=1, source_target_pairs={{0,8},{1,9},{2,10},{3,11},{4,12},{5,13},{6,14},{7,15},{8,0},{9,1},... | collective-permute-start | bytes 4718600 | tf_op jit(solution)/shard_map/ppermute | solution.py:61
  151.7 34.5 %collective-permute-start.30 = (bf16[2,2,64,3072]{3,2,0,1:T(8,128)(2,1)}, bf16[2,2,64,3072]{3,2,0,1:T(8,128)(2,1)}, u32[]{:S(2)}, u32[]{:S(2)}) collective-permute-start(bf16[2,2,64,3072]{3,2,0,1:T(8,128)(2,1)} %pad_maximum_fusion.15), channel_id=1, source_target_pairs={{0,4},{1,5},{2,6},{3,7},{4,0},{5,1},{6,2},{7,3},{8,12},{9,13},{10,... | collective-permute-start | bytes 4718600 | tf_op jit(solution)/shard_map/ppermute | solution.py:61
  152.6 38.0 %collective-permute-start.26 = (bf16[2,2,64,3072]{3,2,0,1:T(8,128)(2,1)}, bf16[2,2,64,3072]{3,2,0,1:T(8,128)(2,1)}, u32[]{:S(2)}, u32[]{:S(2)}) collective-permute-start(bf16[2,2,64,3072]{3,2,0,1:T(8,128)(2,1)} %pad_maximum_fusion.14), channel_id=1, source_target_pairs={{0,2},{1,3},{2,0},{3,1},{4,6},{5,7},{6,4},{7,5},{8,10},{9,11},{10,... | collective-permute-start | bytes 4718600 | tf_op jit(solution)/shard_map/ppermute | solution.py:61
  160.7 89.4 %collective-permute-start.40 = (bf16[2,2,2,2,128,384]{5,4,0,2,1,3:T(8,128)(2,1)}, bf16[2,2,2,2,128,384]{5,4,0,2,1,3:T(8,128)(2,1)}, u32[]{:S(2)}, u32[]{:S(2)}) collective-permute-start(bf16[2,2,2,2,128,384]{5,4,0,2,1,3:T(8,128)(2,1)} %pad_maximum_fusion.17), channel_id=1, source_target_pairs={{0,1},{1,0},{2,3},{3,2},{4,5},{5,4},{6,7},{7,6},{8,9},{9,8},{10,11... | collective-permute-start | bytes 4718600 | tf_op jit(solution)/shard_map/ppermute | solution.py:61
  166.3 83.8 %collective-permute-start.36 = (bf16[2,2,2,2,128,384]{5,4,0,2,1,3:T(8,128)(2,1)}, bf16[2,2,2,2,128,384]{5,4,0,2,1,3:T(8,128)(2,1)}, u32[]{:S(2)}, u32[]{:S(2)}) collective-permute-start(bf16[2,2,2,2,128,384]{5,4,0,2,1,3:T(8,128)(2,1)} %pad_maximum_fusion.16), channel_id=1, source_target_pairs={{0,1},{1,0},{2,3},{3,2},{4,5},{5,4},{6,7},{7,6},{8,9},{9,8},{10,11... | collective-permute-start | bytes 4718600 | tf_op jit(solution)/shard_map/ppermute | solution.py:61
  182.6 41.8 %collective-permute-start.15 = (bf16[256,2048]{1,0:T(8,128)(2,1)S(1)}, bf16[256,2048]{1,0:T(8,128)(2,1)S(1)}, u32[]{:S(2)}, u32[]{:S(2)}) collective-permute-start(bf16[256,2048]{1,0:T(8,128)(2,1)S(1)} %pad_maximum_fusion.22), channel_id=1, source_target_pairs={{0,16},{1,17},{2,18},{3,19},{4,20},{5,21},{6,22},{7,23},{8,24},{9,... | collective-permute-start | bytes 3145736 | tf_op jit(solution)/shard_map/ppermute | solution.py:61
  186.2 84.3 %collective-permute-start.23 = (bf16[2,2,2,64,3072]{4,3,2,1,0:T(8,128)(2,1)}, bf16[2,2,2,64,3072]{4,3,2,1,0:T(8,128)(2,1)}, u32[]{:S(2)}, u32[]{:S(2)}) collective-permute-start(bf16[2,2,2,64,3072]{4,3,2,1,0:T(8,128)(2,1)} %pad_maximum_fusion.3), channel_id=1, source_target_pairs={{0,1},{1,0},{2,3},{3,2},{4,5},{5,4},{6,7},{7,6},{8,9},{9,8},{10,11... | collective-permute-start | bytes 9437192 | tf_op jit(solution)/shard_map/ppermute | solution.py:61
  190.6 71.0 %collective-permute-start.31 = (bf16[2,2,2,64,3072]{4,3,0,2,1:T(8,128)(2,1)}, bf16[2,2,2,64,3072]{4,3,0,2,1:T(8,128)(2,1)}, u32[]{:S(2)}, u32[]{:S(2)}) collective-permute-start(bf16[2,2,2,64,3072]{4,3,0,2,1:T(8,128)(2,1)} %pad_maximum_fusion.5), channel_id=1, source_target_pairs={{0,1},{1,0},{2,3},{3,2},{4,5},{5,4},{6,7},{7,6},{8,9},{9,8},{10,11... | collective-permute-start | bytes 9437192 | tf_op jit(solution)/shard_map/ppermute | solution.py:61
  224.4 62.1 %collective-permute-start.27 = (bf16[2,2,2,64,3072]{4,3,0,2,1:T(8,128)(2,1)}, bf16[2,2,2,64,3072]{4,3,0,2,1:T(8,128)(2,1)}, u32[]{:S(2)}, u32[]{:S(2)}) collective-permute-start(bf16[2,2,2,64,3072]{4,3,0,2,1:T(8,128)(2,1)} %pad_maximum_fusion.4), channel_id=1, source_target_pairs={{0,1},{1,0},{2,3},{3,2},{4,5},{5,4},{6,7},{7,6},{8,9},{9,8},{10,11... | collective-permute-start | bytes 9437192 | tf_op jit(solution)/shard_map/ppermute | solution.py:61
  355.8 51.3 %collective-permute-start.45 = (bf16[16,8,1024]{2,1,0:T(8,128)(2,1)}, bf16[16,8,1024]{2,1,0:T(8,128)(2,1)}, u32[]{:S(2)}, u32[]{:S(2)}) collective-permute-start(bf16[16,8,1024]{2,1,0:T(8,128)(2,1)} %select_bitcast_fusion.53), channel_id=1, source_target_pairs={{0,16},{1,17},{2,18},{3,19},{4,20},{5,21},{6,22},{7,23},{8,24},{9,... | collective-permute-start | bytes 786440 | tf_op jit(solution)/shard_map/ppermute | solution.py:61
  367.9 49.3 %collective-permute-start.47 = (bf16[256,2048]{1,0:T(8,128)(2,1)}, bf16[256,2048]{1,0:T(8,128)(2,1)}, u32[]{:S(2)}, u32[]{:S(2)}) collective-permute-start(bf16[256,2048]{1,0:T(8,128)(2,1)} %pad_maximum_fusion.26), channel_id=1, source_target_pairs={{0,16},{1,17},{2,18},{3,19},{4,20},{5,21},{6,22},{7,23},{8,24},{9,... | collective-permute-start | bytes 3145736 | tf_op jit(solution)/shard_map/ppermute | solution.py:61
  378.9 45.3 %collective-permute-start.49 = (bf16[2,2,2,64,1024]{4,3,0,1,2:T(8,128)(2,1)}, bf16[2,2,2,64,1024]{4,3,0,1,2:T(8,128)(2,1)}, u32[]{:S(2)}, u32[]{:S(2)}) collective-permute-start(bf16[2,2,2,64,1024]{4,3,0,1,2:T(8,128)(2,1)} %bitcast.584), channel_id=1, source_target_pairs={{0,1},{1,0},{2,3},{3,2},{4,5},{5,4},{6,7},{7,6},{8,9},{9,8},{10,11... | collective-permute-start | bytes 3145736 | tf_op jit(solution)/shard_map/ppermute | solution.py:61
  382.1 45.7 %collective-permute-start.61 = (bf16[2,2,2,64,1024]{4,3,0,1,2:T(8,128)(2,1)}, bf16[2,2,2,64,1024]{4,3,0,1,2:T(8,128)(2,1)}, u32[]{:S(2)}, u32[]{:S(2)}) collective-permute-start(bf16[2,2,2,64,1024]{4,3,0,1,2:T(8,128)(2,1)} %bitcast.581), channel_id=1, source_target_pairs={{0,1},{1,0},{2,3},{3,2},{4,5},{5,4},{6,7},{7,6},{8,9},{9,8},{10,11... | collective-permute-start | bytes 3145736 | tf_op jit(solution)/shard_map/ppermute | solution.py:61
  385.9 107.7 %collective-permute-start.65 = (bf16[2,2,2,64,2048]{4,3,0,1,2:T(8,128)(2,1)}, bf16[2,2,2,64,2048]{4,3,0,1,2:T(8,128)(2,1)}, u32[]{:S(2)}, u32[]{:S(2)}) collective-permute-start(bf16[2,2,2,64,2048]{4,3,0,1,2:T(8,128)(2,1)} %bitcast.577), channel_id=1, source_target_pairs={{0,1},{1,0},{2,3},{3,2},{4,5},{5,4},{6,7},{7,6},{8,9},{9,8},{10,11... | collective-permute-start | bytes 6291464 | tf_op jit(solution)/shard_map/ppermute | solution.py:61
  407.1 22.6 %collective-permute-start.85 = (bf16[2,2,2,2,128,256]{5,4,0,2,3,1:T(8,128)(2,1)}, bf16[2,2,2,2,128,256]{5,4,0,2,3,1:T(8,128)(2,1)}, u32[]{:S(2)}, u32[]{:S(2)}) collective-permute-start(bf16[2,2,2,2,128,256]{5,4,0,2,3,1:T(8,128)(2,1)} %bitcast.580), channel_id=1, source_target_pairs={{0,1},{1,0},{2,3},{3,2},{4,5},{5,4},{6,7},{7,6},{8,9},{9,8},{10,11... | collective-permute-start | bytes 3145736 | tf_op jit(solution)/shard_map/ppermute | solution.py:61
  417.1 47.3 %collective-permute-start.81 = (bf16[2,2,2,2,128,384]{5,4,0,3,1,2:T(8,128)(2,1)}, bf16[2,2,2,2,128,384]{5,4,0,3,1,2:T(8,128)(2,1)}, u32[]{:S(2)}, u32[]{:S(2)}) collective-permute-start(bf16[2,2,2,2,128,384]{5,4,0,3,1,2:T(8,128)(2,1)} %bitcast.578), channel_id=1, source_target_pairs={{0,1},{1,0},{2,3},{3,2},{4,5},{5,4},{6,7},{7,6},{8,9},{9,8},{10,11... | collective-permute-start | bytes 4718600 | tf_op jit(solution)/shard_map/ppermute | solution.py:61
  424.2 43.1 %collective-permute-start.77 = (bf16[2,2,2,2,128,384]{5,4,0,1,2,3:T(8,128)(2,1)}, bf16[2,2,2,2,128,384]{5,4,0,1,2,3:T(8,128)(2,1)S(1)}, u32[]{:S(2)}, u32[]{:S(2)}) collective-permute-start(bf16[2,2,2,2,128,384]{5,4,0,1,2,3:T(8,128)(2,1)} %bitcast.628), channel_id=1, source_target_pairs={{0,1},{1,0},{2,3},{3,2},{4,5},{5,4},{6,7},{7,6},{8,9},{9,8},{10,11... | collective-permute-start | bytes 4718600 | tf_op jit(solution)/shard_map/ppermute | solution.py:61
  427.7 26.9 %collective-permute-start.50 = (bf16[2,2,64,1024]{3,2,0,1:T(8,128)(2,1)S(1)}, bf16[2,2,64,1024]{3,2,0,1:T(8,128)(2,1)S(1)}, u32[]{:S(2)}, u32[]{:S(2)}) collective-permute-start(bf16[2,2,64,1024]{3,2,0,1:T(8,128)(2,1)S(1)} %dynamic-slice_bitcast_fusion.12), channel_id=1, source_target_pairs={{0,2},{1,3},{2,0},{3,1},{4,6},{5,7},{6,4},{7,5},{8,10},{9,11},{10,... | collective-permute-start | bytes 1572872 | tf_op jit(solution)/shard_map/ppermute | solution.py:61
  463.3 26.9 %collective-permute-start.57 = (bf16[2,2,2,64,1024]{4,3,1,2,0:T(8,128)(2,1)S(1)}, bf16[2,2,2,64,1024]{4,3,1,2,0:T(8,128)(2,1)S(1)}, u32[]{:S(2)}, u32[]{:S(2)}) collective-permute-start(bf16[2,2,2,64,1024]{4,3,1,2,0:T(8,128)(2,1)S(1)} %bitcast.630), channel_id=1, source_target_pairs={{0,1},{1,0},{2,3},{3,2},{4,5},{5,4},{6,7},{7,6},{8,9},{9,8},{10,11... | collective-permute-start | bytes 3145736 | tf_op jit(solution)/shard_map/ppermute | solution.py:61
  464.3 27.1 %collective-permute-start.53 = (bf16[2,2,2,64,1024]{4,3,2,0,1:T(8,128)(2,1)S(1)}, bf16[2,2,2,64,1024]{4,3,2,0,1:T(8,128)(2,1)S(1)}, u32[]{:S(2)}, u32[]{:S(2)}) collective-permute-start(bf16[2,2,2,64,1024]{4,3,2,0,1:T(8,128)(2,1)S(1)} %bitcast.629), channel_id=1, source_target_pairs={{0,1},{1,0},{2,3},{3,2},{4,5},{5,4},{6,7},{7,6},{8,9},{9,8},{10,11... | collective-permute-start | bytes 3145736 | tf_op jit(solution)/shard_map/ppermute | solution.py:61
  486.8 73.4 %collective-permute-start.69 = (bf16[2,2,2,64,3072]{4,3,2,0,1:T(8,128)(2,1)}, bf16[2,2,2,64,3072]{4,3,2,0,1:T(8,128)(2,1)}, u32[]{:S(2)}, u32[]{:S(2)}) collective-permute-start(bf16[2,2,2,64,3072]{4,3,2,0,1:T(8,128)(2,1)} %bitcast.576), channel_id=1, source_target_pairs={{0,1},{1,0},{2,3},{3,2},{4,5},{5,4},{6,7},{7,6},{8,9},{9,8},{10,11... | collective-permute-start | bytes 9437192 | tf_op jit(solution)/shard_map/ppermute | solution.py:61
  490.2 74.1 %collective-permute-start.73 = (bf16[2,2,2,64,3072]{4,3,1,2,0:T(8,128)(2,1)}, bf16[2,2,2,64,3072]{4,3,1,2,0:T(8,128)(2,1)}, u32[]{:S(2)}, u32[]{:S(2)}) collective-permute-start(bf16[2,2,2,64,3072]{4,3,1,2,0:T(8,128)(2,1)} %bitcast.575), channel_id=1, source_target_pairs={{0,1},{1,0},{2,3},{3,2},{4,5},{5,4},{6,7},{7,6},{8,9},{9,8},{10,11... | collective-permute-start | bytes 9437192 | tf_op jit(solution)/shard_map/ppermute | solution.py:61
  490.3 20.0 %collective-permute-start.82 = (bf16[2,2,2,128,384]{4,3,0,2,1:T(8,128)(2,1)S(1)}, bf16[2,2,2,128,384]{4,3,0,2,1:T(8,128)(2,1)S(1)}, u32[]{:S(2)}, u32[]{:S(2)}) collective-permute-start(bf16[2,2,2,128,384]{4,3,0,2,1:T(8,128)(2,1)S(1)} %dynamic-slice_bitcast_fusion.3), channel_id=1, source_target_pairs={{0,4},{1,5},{2,6},{3,7},{4,0},{5,1},{6,2},{7,3},{8,12},{9,13},{10,... | collective-permute-start | bytes 2359304 | tf_op jit(solution)/shard_map/ppermute | solution.py:61
  491.3 19.8 %collective-permute-start.78 = (bf16[2,2,2,128,384]{4,3,0,1,2:T(8,128)(2,1)S(1)}, bf16[2,2,2,128,384]{4,3,0,1,2:T(8,128)(2,1)S(1)}, u32[]{:S(2)}, u32[]{:S(2)}) collective-permute-start(bf16[2,2,2,128,384]{4,3,0,1,2:T(8,128)(2,1)S(1)} %dynamic-slice_bitcast_fusion.4), channel_id=1, source_target_pairs={{0,2},{1,3},{2,0},{3,1},{4,6},{5,7},{6,4},{7,5},{8,10},{9,11},{10,... | collective-permute-start | bytes 2359304 | tf_op jit(solution)/shard_map/ppermute | solution.py:61
  493.6 19.5 %collective-permute-start.58 = (bf16[2,2,64,1024]{3,2,0,1:T(8,128)(2,1)S(1)}, bf16[2,2,64,1024]{3,2,0,1:T(8,128)(2,1)S(1)}, u32[]{:S(2)}, u32[]{:S(2)}) collective-permute-start(bf16[2,2,64,1024]{3,2,0,1:T(8,128)(2,1)S(1)} %dynamic-slice_bitcast_fusion.10), channel_id=1, source_target_pairs={{0,8},{1,9},{2,10},{3,11},{4,12},{5,13},{6,14},{7,15},{8,0},{9,1},... | collective-permute-start | bytes 1572872 | tf_op jit(solution)/shard_map/ppermute | solution.py:61
  511.1 45.7 %collective-permute-start.66 = (bf16[2,2,64,2048]{3,2,0,1:T(8,128)(2,1)}, bf16[2,2,64,2048]{3,2,0,1:T(8,128)(2,1)}, u32[]{:S(2)}, u32[]{:S(2)}) collective-permute-start(bf16[2,2,64,2048]{3,2,0,1:T(8,128)(2,1)} %dynamic-slice_bitcast_fusion.2), channel_id=1, source_target_pairs={{0,2},{1,3},{2,0},{3,1},{4,6},{5,7},{6,4},{7,5},{8,10},{9,11},{10,... | collective-permute-start | bytes 3145736 | tf_op jit(solution)/shard_map/ppermute | solution.py:61
  552.1 22.6 %collective-permute-start.89 = (bf16[128,1024]{1,0:T(8,128)(2,1)}, bf16[128,1024]{1,0:T(8,128)(2,1)}, u32[]{:S(2)}, u32[]{:S(2)}) collective-permute-start(bf16[128,1024]{1,0:T(8,128)(2,1)} %fusion.108), channel_id=1, source_target_pairs={{0,16},{1,17},{2,18},{3,19},{4,20},{5,21},{6,22},{7,23},{8,24},{9,... | collective-permute-start | bytes 786440 | tf_op jit(solution)/shard_map/ppermute | solution.py:61
  563.4 43.8 %collective-permute-start.70 = (bf16[2,2,64,3072]{3,2,1,0:T(8,128)(2,1)S(1)}, bf16[2,2,64,3072]{3,2,1,0:T(8,128)(2,1)S(1)}, u32[]{:S(2)}, u32[]{:S(2)}) collective-permute-start(bf16[2,2,64,3072]{3,2,1,0:T(8,128)(2,1)S(1)} %dynamic-slice_bitcast_fusion.1), channel_id=1, source_target_pairs={{0,4},{1,5},{2,6},{3,7},{4,0},{5,1},{6,2},{7,3},{8,12},{9,13},{10,... | collective-permute-start | bytes 4718600 | tf_op jit(solution)/shard_map/ppermute | solution.py:61
  567.7 40.8 %collective-permute-start.74 = (bf16[2,2,64,3072]{3,2,0,1:T(8,128)(2,1)S(1)}, bf16[2,2,64,3072]{3,2,0,1:T(8,128)(2,1)S(1)}, u32[]{:S(2)}, u32[]{:S(2)}) collective-permute-start(bf16[2,2,64,3072]{3,2,0,1:T(8,128)(2,1)S(1)} %dynamic-slice_bitcast_fusion), channel_id=1, source_target_pairs={{0,8},{1,9},{2,10},{3,11},{4,12},{5,13},{6,14},{7,15},{8,0},{9,1},... | collective-permute-start | bytes 4718600 | tf_op jit(solution)/shard_map/ppermute | solution.py:61
  574.1 33.0 %collective-permute-start.68 = (bf16[64,2048]{1,0:T(8,128)(2,1)S(1)}, bf16[64,2048]{1,0:T(8,128)(2,1)S(1)}, u32[]{:S(2)}, u32[]{:S(2)}) collective-permute-start(bf16[64,2048]{1,0:T(8,128)(2,1)S(1)} %dynamic-slice_bitcast_fusion.18), channel_id=1, source_target_pairs={{0,8},{1,9},{2,10},{3,11},{4,12},{5,13},{6,14},{7,15},{8,0},{9,1},... | collective-permute-start | bytes 786440 | tf_op jit(solution)/shard_map/ppermute | solution.py:61
  (232 other events, 1720.2 us)

commit v2 on v1

--- a/solution.py
+++ b/solution.py
@@ -1,6 +1,10 @@
+import functools
+
 import jax
 import jax.numpy as jnp
 from jax import lax
+from jax.experimental import pallas as pl
+from jax.experimental.pallas import tpu as pltpu
 from jax.sharding import PartitionSpec as P
 
 HEADS = 16
@@ -101,7 +105,7 @@
     return edges
 
 
-def local(
+def local_general(
     count,
     tokens,
     depth_count,
@@ -369,6 +373,1343 @@
     )
 
 
+CHIPS = 8
+CHAIN_BITS = [[(k + t) % 3 for t in range(3)] for k in range(3)]
+CHAIN_MASKS = [
+    [sum(((j >> t) & 1) << bits[t] for t in range(3)) for j in range(CHIPS)] for bits in CHAIN_BITS
+]
+VM = pl.BlockSpec(memory_space=pltpu.VMEM)
+HB = pl.BlockSpec(memory_space=pltpu.HBM)
+SM = pl.BlockSpec(memory_space=pltpu.SMEM)
+MIB = 1 << 20
+SMALL = pl.CostEstimate(flops=1, bytes_accessed=1, transcendentals=0)
+
+
+def aligned(index, size):
+    return pl.ds(pl.multiple_of(index * size, size), size)
+
+
+def after(value, *earlier):
+    return lax.optimization_barrier((value, earlier))[0]
+
+
+def plus(a, b):
+    return (a.astype(F32) + b.astype(F32)).astype(BF)
+
+
+class Jobs:
+    def __init__(self, width):
+        self.width = width
+        self.inputs, self.outputs, self.work = [], [], []
+
+    def source(self, array):
+        for i, known in enumerate(self.inputs):
+            if known is array:
+                return i
+        self.inputs.append(array)
+        return len(self.inputs) - 1
+
+    def output(self, rows, dtype=BF):
+        self.outputs.append(jax.ShapeDtypeStruct((rows, self.width), dtype))
+        return len(self.outputs) - 1
+
+    def copy(self, array, row, target, target_row, count):
+        self.work.append((self.source(array), row, None, 0, target, target_row, count))
+
+    def add(self, a, a_row, b, b_row, target, target_row, count):
+        self.work.append((self.source(a), a_row, self.source(b), b_row, target, target_row, count))
+
+    def run(self, meta, name, *earlier, squares=False):
+        inputs = after(self.inputs, *earlier) if earlier else self.inputs
+        adds = [w for w in self.work if w[2] is not None]
+        rows = sum(w[6] for w in adds)
+        moved = sum(w[6] for w in self.work if w[2] is None)
+        scratch = [pltpu.SemaphoreType.DMA((3, len(self.work)))]
+        scratch += [pltpu.VMEM((max(moved, 16), self.width), BF)]
+        if adds:
+            scratch += [pltpu.VMEM((rows, self.width), BF)] * 3
+            scratch += [pltpu.VMEM((rows, self.width), F32)]
+        shapes = list(self.outputs)
+        if squares:
+            shapes.append(jax.ShapeDtypeStruct((8, self.width), F32))
+        return pl.pallas_call(
+            functools.partial(jobs_kernel, self.work, len(inputs), self.outputs, squares),
+            in_specs=[SM] + [HB] * len(inputs),
+            out_specs=[HB] * len(self.outputs) + ([VM] if squares else []),
+            out_shape=shapes,
+            scratch_shapes=scratch,
+            compiler_params=pltpu.CompilerParams(vmem_limit_bytes=60 * MIB),
+            cost_estimate=SMALL,
+            name=name,
+        )(meta, *inputs)
+
+
+def jobs_kernel(work, count, outputs, squares, meta, *refs):
+    sources, targets = refs[:count], refs[count : count + len(outputs)]
+    refs = refs[count + len(outputs) :]
+    if squares:
+        square_ref = refs[0]
+        refs = refs[1:]
+    sem = refs[0]
+    core = meta[1]
+
+    def part(ref, row, rows):
+        if isinstance(row, tuple):
+            start = pl.multiple_of(jnp.where(core == 0, row[0], row[1]), 16)
+            return ref.at[pl.ds(start, rows)]
+        return ref.at[row : row + rows]
+
+    coming, leaving = [], []
+    at, moved = 0, 0
+    transit = refs[1]
+    refs = refs[:1] + refs[2:]
+    for i, (a, a_row, b, b_row, target, target_row, rows) in enumerate(work):
+        if b is None:
+            spot = slice(moved, moved + rows)
+            copy = pltpu.make_async_copy(part(sources[a], a_row, rows), transit.at[spot], sem.at[0, i])
+            copy.start()
+            coming.append(((copy,), spot))
+            moved += rows
+            continue
+        spot = slice(at, at + rows)
+        pair = (
+            pltpu.make_async_copy(part(sources[a], a_row, rows), refs[1].at[spot], sem.at[0, i]),
+            pltpu.make_async_copy(part(sources[b], b_row, rows), refs[2].at[spot], sem.at[1, i]),
+        )
+        for copy in pair:
+            copy.start()
+        coming.append((pair, spot))
+        at += rows
+    if squares:
+        square_ref[...] = jnp.zeros_like(square_ref)
+    for i, (a, a_row, b, b_row, target, target_row, rows) in enumerate(work):
+        pair, spot = coming[i]
+        finish(pair)
+        if b is None:
+            copy = pltpu.make_async_copy(
+                transit.at[spot], part(targets[target], target_row, rows), sem.at[2, i]
+            )
+            copy.start()
+            leaving.append(copy)
+            continue
+        wide = outputs[target].dtype == F32
+        store = refs[4] if wide else refs[3]
+        if not wide and not squares:
+            store[spot] = plus(refs[1][spot], refs[2][spot])
+        else:
+            total = refs[1][spot].astype(F32) + refs[2][spot].astype(F32)
+            store[spot] = total.astype(store.dtype)
+            if wide:
+                square = (total * total).reshape(rows // 8, 8, total.shape[1])
+                square_ref[...] += jnp.sum(square, axis=0)
+        copy = pltpu.make_async_copy(
+            store.at[spot], part(targets[target], target_row, rows), sem.at[2, i]
+        )
+        copy.start()
+        leaving.append(copy)
+    finish(leaving)
+
+
+class Blocks:
+    def __init__(self, own=None, rows=None):
+        self.rows = own.shape[0] if rows is None else rows
+        self.held = [] if own is None else [(own, 0)]
+
+    def arrived(self, array, row, count):
+        for j in range(count):
+            self.held.append((array, row + j * self.rows))
+
+
+def place(jobs, held, rows, target, target_row):
+    start = 0
+    while start < len(held):
+        array, row = held[start]
+        stop = start + 1
+        while stop < len(held) and held[stop][0] is array and held[stop][1] == row + (stop - start) * rows:
+            stop += 1
+        jobs.copy(array, row, target, target_row + start * rows, (stop - start) * rows)
+        start = stop
+
+
+class Round:
+    def __init__(self, cube, meta, width, name):
+        self.cube, self.meta, self.name = cube, meta, name
+        self.jobs = Jobs(width)
+        self.axis_work = []
+        self.core_work = []
+
+    def gather(self, chains, level):
+        self.axis_work.append((chains, level))
+        return self
+
+    def core(self, chains, others, start, stop):
+        self.core_work.append((chains, others, start, stop))
+        return self
+
+    def run(self, *earlier, gate=()):
+        jobs = self.jobs
+        filled = []
+        for axis in range(3):
+            held = []
+            for chains, level in self.axis_work:
+                blocks = chains[(axis - level) % 3]
+                if blocks is not None:
+                    held.append((blocks, blocks.held[: 1 << level]))
+            filled.append(held)
+        core_held = []
+        for chains, others, start, stop in self.core_work:
+            for blocks, other in zip(chains, others):
+                if blocks is not None:
+                    core_held.append((blocks, other, blocks.held[start:stop]))
+        direct = not core_held and all(len(h) == 1 and len(h[0][1]) == 1 for h in filled)
+        if direct:
+            payloads = [h[0][1][0][0] for h in filled]
+            if earlier:
+                payloads = after(payloads, *earlier)
+        else:
+            for held in filled:
+                if held:
+                    target = jobs.output(sum(b.rows * len(h) for b, h in held))
+                    row = 0
+                    for blocks, part in held:
+                        place(jobs, part, blocks.rows, target, row)
+                        row += blocks.rows * len(part)
+            if core_held:
+                target = jobs.output(sum(b.rows * len(h) for b, _, h in core_held))
+                row = 0
+                for blocks, _, part in core_held:
+                    place(jobs, part, blocks.rows, target, row)
+                    row += blocks.rows * len(part)
+            payloads = jobs.run(self.meta, self.name, *earlier)
+            self.packed = payloads
+            if gate:
+                axes = sum(1 for held in filled if held)
+                payloads = after(list(payloads[:axes]), *gate) + list(payloads[axes:])
+        got = []
+        index = 0
+        for axis, held in enumerate(filled):
+            if not held:
+                continue
+            array = self.cube.swap(payloads[index], 1 + axis)
+            index += 1
+            row = 0
+            for blocks, part in held:
+                blocks.arrived(array, row, len(part))
+                row += blocks.rows * len(part)
+            got.append(array)
+        self.got = got
+        self.core_got = None
+        if core_held:
+            array = self.cube.swap(payloads[index], 0)
+            row = 0
+            for blocks, other, part in core_held:
+                other.arrived(array, row, len(part))
+                row += blocks.rows * len(part)
+            self.core_got = array
+        self.payloads = payloads
+        return self
+
+
+def operands(*chains):
+    arrays, tables = [], []
+    for blocks in chains:
+        table = []
+        for array, row in blocks.held:
+            found = [i for i, a in enumerate(arrays) if a is array]
+            if not found:
+                arrays.append(array)
+                found = [len(arrays) - 1]
+            table.append((found[0], row))
+        tables.append((blocks.rows, table))
+    return arrays, tables
+
+
+class Sums:
+    def __init__(self, keep, send, rows, final):
+        self.keep, self.send, self.rows, self.count, self.final = keep, send, rows, 4, final
+
+
+def reduce_round(cube, meta, width, name, work, *earlier, squares=False, gate=()):
+    jobs = Jobs(width)
+    filled = []
+    direct = all(step == 0 for _, step in work) and len(work) == 1
+    for axis in range(3):
+        parts = []
+        for chains, step in work:
+            if step < 3:
+                chain = chains[(axis - (2 - step)) % 3]
+                if chain is not None:
+                    parts.append((chain, step))
+        filled.append(parts)
+    if direct:
+        payloads = [parts[0][0].send[0] for parts in filled]
+        if earlier:
+            payloads = after(payloads, *earlier)
+    else:
+        layout = []
+        for parts in filled:
+            if not parts:
+                continue
+            rows = 0
+            target = None
+            sizes = []
+            for chain, step in parts:
+                size = chain.rows * (4 >> step)
+                sizes.append((chain, step, rows, size))
+                rows += size
+            layout.append((jobs.output(rows), sizes))
+        kept = {}
+        for target, sizes in layout:
+            for chain, step, row, size in sizes:
+                if step == 0:
+                    jobs.copy(chain.send[0], chain.send[1], target, row, size)
+                else:
+                    got, got_row = chain.got
+                    array, keep_row = chain.keep
+                    own = jobs.output(size)
+                    jobs.add(got, got_row + size, array, keep_row + size, target, row, size)
+                    jobs.add(got, got_row, array, keep_row, own, 0, size)
+                    kept[own] = chain
+        for chains, step in work:
+            if step == 3:
+                for chain in chains:
+                    if chain is not None:
+                        chain.final(jobs, chain.got, chain.keep, chain.rows)
+        out = jobs.run(meta, name, *earlier, squares=squares)
+        for own, chain in kept.items():
+            chain.keep = (out[own], 0)
+        payloads = [out[target] for target, _ in layout]
+        if gate and payloads:
+            payloads = after(payloads, *gate)
+    got = []
+    index = 0
+    for axis, parts in enumerate(filled):
+        if not parts:
+            continue
+        array = cube.swap(payloads[index], 1 + axis)
+        index += 1
+        row = 0
+        for chain, step in parts:
+            chain.got = (array, row)
+            row += chain.rows * (4 >> step)
+        got.append(array)
+    return (got, out) if not direct else (got, None)
+
+
+def first_kernel(joint, q, k, v):
+    width = q.shape[1]
+    q[...] = joint[:, :width].astype(BF)
+    k[...] = joint[:, width : 2 * width].astype(BF)
+    v[: joint.shape[0]] = joint[:, 2 * width :].astype(BF)
+
+
+def first_shards(joint):
+    rows, width = joint.shape[0], joint.shape[1] // 3
+    return pl.pallas_call(
+        first_kernel,
+        in_specs=[VM],
+        out_specs=[VM] * 3,
+        out_shape=[jax.ShapeDtypeStruct((r, width), BF) for r in (rows, rows, rows + 16)],
+        compiler_params=pltpu.CompilerParams(vmem_limit_bytes=60 * MIB),
+        name="first_shards",
+    )(joint)
+
+
+def split_kernel(meta, expand, shrink, output, own, give, shrink_own, shrink_give, out_a, out_b):
+    core, group = meta[1], meta[2]
+    rows = expand.shape[0]
+    block = expand.shape[1] // (2 * 2 * 2 * CHIPS)
+    for turn in range(2):
+        part = turn ^ (1 - group)
+        for kind in range(2):
+            for chip in range(CHIPS):
+                base = ((kind * 2 + part) * CHIPS + chip) * 2
+                cols = slice(chip * block, (chip + 1) * block)
+                r = slice((turn * 2 + kind) * rows, (turn * 2 + kind + 1) * rows)
+                own[r, cols] = expand[:, aligned(base + core, block)].astype(BF)
+                give[r, cols] = expand[:, aligned(base + 1 - core, block)].astype(BF)
+    shrink_own[...] = shrink[group].astype(BF)
+    shrink_give[...] = shrink[1 - group].astype(BF)
+    out_a[...] = output[: rows // 2].astype(BF)
+    out_b[...] = output[rows // 2 :].astype(BF)
+
+
+def split_weights(meta, expand, shrink, output):
+    rows, width = output.shape
+    four = jax.ShapeDtypeStruct((4 * rows, width), BF)
+    two = jax.ShapeDtypeStruct(shrink.shape[1:], BF)
+    half = jax.ShapeDtypeStruct((rows // 2, width), BF)
+    return pl.pallas_call(
+        split_kernel,
+        in_specs=[SM, VM, VM, VM],
+        out_specs=[VM] * 6,
+        out_shape=[four, four, two, two, half, half],
+        compiler_params=pltpu.CompilerParams(vmem_limit_bytes=60 * MIB),
+        name="split_weights",
+    )(meta, expand, shrink, output)
+
+
+def load_blocks(table, refs, w, k, chip, sem):
+    copies = []
+    rows, places = table
+    for j, (index, row) in enumerate(places):
+        target = w.at[aligned(chip ^ CHAIN_MASKS[k][j], rows), :]
+        copy = pltpu.make_async_copy(refs[index].at[row : row + rows], target, sem.at[j])
+        copy.start()
+        copies.append(copy)
+    return copies
+
+
+def store_blocks(w, pieces, rows, k, chip, sem):
+    copies = []
+    for j in range(CHIPS):
+        source = w.at[aligned(chip ^ CHAIN_MASKS[k][j], rows), :]
+        row = (j % 4) * rows
+        copy = pltpu.make_async_copy(source, pieces[j // 4].at[row : row + rows], sem.at[j])
+        copy.start()
+        copies.append(copy)
+    return copies
+
+
+def finish(copies):
+    for copy in copies:
+        copy.wait()
+
+
+TILE = 256
+
+
+def ffn_rows_kernel(first, count, tables, meta, n2m, n2o, cm, co, *refs):
+    pieces = refs[:count]
+    refs = refs[count:]
+    if not first:
+        dn_in = refs[0]
+        refs = refs[1:]
+    if first:
+        dn_out, hid, dg, du, n2, c, wg, wu, ws, sem = refs
+    else:
+        dn_out, dn_send, hid, dg, du, n2, c, wg, wu, ws, sem = refs
+    chip = meta[0]
+    mats = (wg, wu, ws)
+    coming = [load_blocks(tables[k], pieces, mats[k], k, chip, sem.at[k]) for k in range(3)]
+    rows = n2m.shape[0]
+    n2[:rows] = n2m[...]
+    n2[rows:] = n2o[...]
+    c[:rows] = cm[...]
+    c[rows:] = co[...]
+    for copies in coming:
+        finish(copies)
+    width = wg.shape[1]
+
+    def gates(t, _):
+        cols = aligned(t, TILE)
+        g = dot(n2[...], wg[:, cols])
+        u = dot(n2[...], wu[:, cols])
+        dh = dot_nt(c[...], ws[cols, :])
+        sig = jax.nn.sigmoid(g)
+        silu = g * sig
+        hid[:, cols] = (silu * u).astype(BF)
+        du[:, cols] = (dh * silu).astype(BF)
+        dg[:, cols] = (dh * u * sig * (1.0 + g * (1.0 - sig))).astype(BF)
+        return 0
+
+    lax.fori_loop(0, width // TILE, gates, 0)
+
+    def back(t, _):
+        cols = aligned(t, TILE)
+        d = dot_nt(dg[...], wg[cols, :]) + dot_nt(du[...], wu[cols, :])
+        if first:
+            dn_out[:, cols] = d
+        else:
+            d = d + dn_in[:, cols]
+            dn_out[:, cols] = d[:rows]
+            dn_send[:, cols] = d[rows:]
+        return 0
+
+    lax.fori_loop(0, width // TILE, back, 0)
+
+
+def ffn_rows(meta, n2m, n2o, cm, co, chains, carried):
+    first = carried is None
+    arrays, tables = operands(*chains)
+    rows, width = 2 * n2m.shape[0], n2m.shape[1]
+    low = jax.ShapeDtypeStruct((rows, width), BF)
+    return pl.pallas_call(
+        functools.partial(ffn_rows_kernel, first, len(arrays), tables),
+        in_specs=[SM] + [VM] * 4 + [HB] * len(arrays) + ([] if first else [VM]),
+        out_specs=[VM] * (4 if first else 5),
+        out_shape=(
+            [jax.ShapeDtypeStruct((rows, width), F32)]
+            if first
+            else [jax.ShapeDtypeStruct((rows // 2, width), F32)] * 2
+        )
+        + [low, low, low],
+        scratch_shapes=[pltpu.VMEM((rows, width), BF)] * 2
+        + [pltpu.VMEM((width, width), BF)] * 3
+        + [pltpu.SemaphoreType.DMA((3, CHIPS))],
+        compiler_params=pltpu.CompilerParams(vmem_limit_bytes=60 * MIB),
+        cost_estimate=SMALL,
+        name="ffn_rows",
+    )(meta, n2m, n2o, cm, co, *arrays, *(() if first else (carried,)))
+
+
+def ffn_weights_kernel(first, count, table, meta, n2m, n2o, cm, co, hid, dg, du, *refs):
+    pieces = refs[:count]
+    refs = refs[count:]
+    if not first:
+        f_in = refs[0]
+        refs = refs[1:]
+    f_out = refs[0]
+    if not first:
+        f_send = refs[1]
+        refs = refs[1:]
+    outs = refs[1:7]
+    n2, c, ws, dwg, dwu, dws, in_sem, out_sem = refs[7:]
+    chip = meta[0]
+    coming = load_blocks(table, pieces, ws, 2, chip, in_sem)
+    rows = n2m.shape[0]
+    n2[:rows] = n2m[...]
+    n2[rows:] = n2o[...]
+    c[:rows] = cm[...]
+    c[rows:] = co[...]
+    width = ws.shape[1]
+    leaving = []
+    for k, (lhs, rhs, dw) in enumerate(((n2, dg, dwg), (n2, du, dwu), (hid, c, dws))):
+
+        def step(t, _, lhs=lhs, rhs=rhs, dw=dw):
+            cols = aligned(t, TILE)
+            dw[cols, :] = dot_tn(lhs[:, cols], rhs[...]).astype(BF)
+            return 0
+
+        lax.fori_loop(0, width // TILE, step, 0)
+        leaving += store_blocks(dw, outs[2 * k : 2 * k + 2], table[0], k, chip, out_sem.at[k])
+    finish(coming)
+
+    def down(t, _):
+        cols = aligned(t, TILE)
+        f = dot(hid[...], ws[:, cols])
+        if first:
+            f_out[:, cols] = f
+        else:
+            f = f + f_in[:, cols]
+            f_out[:, cols] = f[:rows]
+            f_send[:, cols] = f[rows:].astype(BF)
+        return 0
+
+    lax.fori_loop(0, width // TILE, down, 0)
+    finish(leaving)
+
+
+def ffn_weights(meta, n2m, n2o, cm, co, hid, dg, du, chain, carried):
+    first = carried is None
+    arrays, tables = operands(chain)
+    rows, width = 2 * n2m.shape[0], n2m.shape[1]
+    piece = jax.ShapeDtypeStruct((4 * chain.rows, width), BF)
+    return pl.pallas_call(
+        functools.partial(ffn_weights_kernel, first, len(arrays), tables[0]),
+        in_specs=[SM] + [VM] * 7 + [HB] * len(arrays) + ([] if first else [VM]),
+        out_specs=[VM] * (1 if first else 2) + [HB] * 6,
+        out_shape=(
+            [jax.ShapeDtypeStruct((rows, width), F32)]
+            if first
+            else [
+                jax.ShapeDtypeStruct((rows // 2, width), F32),
+                jax.ShapeDtypeStruct((rows // 2, width), BF),
+            ]
+        )
+        + [piece] * 6,
+        scratch_shapes=[pltpu.VMEM((rows, width), BF)] * 2
+        + [pltpu.VMEM((width, width), BF)] * 4
+        + [pltpu.SemaphoreType.DMA((CHIPS,)), pltpu.SemaphoreType.DMA((3, CHIPS))],
+        compiler_params=pltpu.CompilerParams(vmem_limit_bytes=60 * MIB),
+        cost_estimate=SMALL,
+        name="ffn_weights",
+    )(meta, n2m, n2o, cm, co, hid, dg, du, *arrays, *(() if first else (carried,)))
+
+
+OUTPUT_CHAINS = (1, 2)
+
+
+def load_devices(table, refs, k, side, shard, row, count, target, lo, meta, sem, used):
+    chip, core = meta[0], meta[1]
+    copies = []
+    for j, (index, base) in enumerate(table[1]):
+        device = (chip ^ CHAIN_MASKS[k][j]) * 2 + (core if side == 0 else 1 - core)
+        start = pl.multiple_of(device * shard + row, 16)
+        copy = pltpu.make_async_copy(
+            refs[index].at[base : base + count],
+            target.at[pl.ds(start, count), lo : lo + target.shape[0]],
+            sem.at[used + j],
+        )
+        copy.start()
+        copies.append(copy)
+    return copies
+
+
+def load_joint(tables, refs, target, meta, sem):
+    width = target.shape[0]
+    shard = width // (2 * CHIPS)
+    copies = []
+    for k in range(3):
+        for side in range(2):
+            copies += load_devices(
+                tables[3 * side + k], refs, k, side, shard, 0, shard, target, k * width, meta, sem, len(copies)
+            )
+    return copies
+
+
+def load_output(tables, refs, target, meta, sem):
+    shard = target.shape[0] // (2 * CHIPS)
+    half = shard // 2
+    copies = []
+    for i, k in enumerate(OUTPUT_CHAINS):
+        for side in range(2):
+            copies += load_devices(
+                tables[2 * side + i], refs, k, side, shard, i * half, half, target, 0, meta, sem, len(copies)
+            )
+    return copies
+
+
+PAIR_COPIES = 128
+
+
+def joint_kernel(count, tables, meta, x, *refs):
+    pieces = refs[:count]
+    first, query, key, value_out, gains, w, gain_rows, sem, gain_sem = refs[count:]
+    width = x.shape[1]
+    coming = load_joint(tables, pieces, w, meta, sem)
+    shard = width // (2 * CHIPS)
+    gain_copies = []
+    for side in range(2):
+        for j, (index, base) in enumerate(tables[3 * side + 2][1]):
+            copy = pltpu.make_async_copy(
+                pieces[index].at[base + shard : base + shard + 16],
+                gain_rows.at[side * CHIPS + j],
+                gain_sem.at[side * CHIPS + j],
+            )
+            copy.start()
+            gain_copies.append(copy)
+    value = x[...].astype(F32)
+    inverse = lax.rsqrt(jnp.mean(value * value, axis=-1, keepdims=True) + NORM_EPS)
+    finish(gain_copies)
+    whole = jnp.sum(gain_rows[...].astype(F32), axis=0)
+    gains[...] = whole[:8]
+    first[...] = (value * inverse * whole[0:1]).astype(BF)
+    finish(coming)
+    tiles = width // TILE
+    for part, out in enumerate((query, key, value_out)):
+
+        def step(t, _, part=part, out=out):
+            weight = w[:, aligned(t + part * tiles, TILE)]
+            out[:, aligned(t, TILE)] = dot(first[...], weight).astype(BF)
+            return 0
+
+        lax.fori_loop(0, tiles, step, 0)
+
+
+def joint_forward(meta, x, chains):
+    rows, width = x.shape
+    arrays, tables = operands(*chains)
+    low = jax.ShapeDtypeStruct((rows, width), BF)
+    return pl.pallas_call(
+        functools.partial(joint_kernel, len(arrays), tables),
+        in_specs=[SM, VM] + [HB] * len(arrays),
+        out_specs=[VM] * 5,
+        out_shape=[
+            low,
+            low,
+            low,
+            low,
+            jax.ShapeDtypeStruct((8, width), F32),
+        ],
+        scratch_shapes=[
+            pltpu.VMEM((width, 3 * width), BF),
+            pltpu.VMEM((2 * CHIPS, 16, width), BF),
+            pltpu.SemaphoreType.DMA((PAIR_COPIES,)),
+            pltpu.SemaphoreType.DMA((2 * CHIPS,)),
+        ],
+        compiler_params=pltpu.CompilerParams(vmem_limit_bytes=60 * MIB),
+        cost_estimate=SMALL,
+        name="joint_forward",
+    )(meta, x, *arrays)
+
+
+CHUNK = 128
+
+
+def bias_into(bias, run, upper):
+    size = 2 * CHUNK
+    row = lax.broadcasted_iota(jnp.int32, (size, size), 0) & (CHUNK - 1)
+    column = lax.broadcasted_iota(jnp.int32, (size, size), 1)
+    own = column < CHUNK
+    column = column & (CHUNK - 1)
+    shift = run.bit_length() - 1
+    same = (row >> shift) == (column >> shift)
+    reach = jnp.where(upper, CHUNK, 0)
+    seen = same & ((own & (row >= column)) | (~own & (row < reach)))
+    bias[...] = jnp.where(seen, 0.0, -1e30)
+
+
+def stacked(value, left):
+    zero = jnp.zeros_like(value)
+    return jnp.concatenate([jnp.where(left, value, zero), jnp.where(left, zero, value)], axis=0)
+
+
+def probabilities(q_st, k_all, bias, scale):
+    scores = dot_nt(q_st, k_all) * scale + bias[...]
+    exp_scores = jnp.exp(scores - jnp.max(scores, axis=-1, keepdims=True))
+    return exp_scores / jnp.sum(exp_scores, axis=-1, keepdims=True)
+
+
+def context_kernel(run, head_dim, count, tables, meta, query, k_own, v_own, k_other, v_other, x, live, gains, *refs):
+    pieces = refs[:count]
+    ctx, h_out, n2, wo, bias, sem = refs[count:]
+    rows, width = x.shape
+    coming = load_output(tables, pieces, wo, meta, sem)
+    bias_into(bias, run, meta[2] == 1)
+    scale = head_dim ** (-0.5)
+    lanes = 2 * head_dim
+    left = lax.broadcasted_iota(jnp.int32, (CHUNK, lanes), 1) < head_dim
+
+    def pair(p, _):
+        cols = aligned(p, lanes)
+        for chunk in range(rows // CHUNK):
+            r = slice(chunk * CHUNK, (chunk + 1) * CHUNK)
+            q_st = stacked(query[r, cols], left)
+            k_all = jnp.concatenate([k_own[r, cols], k_other[r, cols]], axis=0)
+            v_all = jnp.concatenate([v_own[r, cols], v_other[r, cols]], axis=0)
+            prob = probabilities(q_st, k_all, bias, scale)
+            out = dot(prob.astype(BF), v_all)
+            ctx[r, cols] = jnp.where(left, out[:CHUNK], out[CHUNK:]).astype(BF)
+        return 0
+
+    lax.fori_loop(0, width // lanes, pair, 0)
+    finish(coming)
+
+    def project(t, _):
+        cols = aligned(t, TILE)
+        h_out[:, cols] = x[:, cols].astype(F32) + live[...] * dot(ctx[...], wo[:, cols])
+        return 0
+
+    lax.fori_loop(0, width // TILE, project, 0)
+    h = h_out[...]
+    inverse = lax.rsqrt(jnp.mean(h * h, axis=-1, keepdims=True) + NORM_EPS)
+    n2[...] = (h * inverse * gains[1:2, :]).astype(BF)
+
+
+def context_forward(
+    run, meta, query, k_own, v_own, k_other, v_other, x, live, gains, chains
+):
+    rows, width = x.shape
+    arrays, tables = operands(*chains)
+    low = jax.ShapeDtypeStruct((rows, width), BF)
+    return pl.pallas_call(
+        functools.partial(context_kernel, run, width // HEADS, len(arrays), tables),
+        in_specs=[SM] + [VM] * 8 + [HB] * len(arrays),
+        out_specs=[VM] * 3,
+        out_shape=[low, jax.ShapeDtypeStruct((rows, width), F32), low],
+        scratch_shapes=[
+            pltpu.VMEM((width, width), BF),
+            pltpu.VMEM((2 * CHUNK, 2 * CHUNK), F32),
+            pltpu.SemaphoreType.DMA((PAIR_COPIES,)),
+        ],
+        compiler_params=pltpu.CompilerParams(vmem_limit_bytes=60 * MIB),
+        cost_estimate=SMALL,
+        name="context_forward",
+    )(meta, query, k_own, v_own, k_other, v_other, x, live, gains, *arrays)
+
+
+def norm_back(value, gain, grad):
+    inverse = lax.rsqrt(jnp.mean(value * value, axis=-1, keepdims=True) + NORM_EPS)
+    scaled = grad * gain
+    mean = jnp.mean(scaled * value, axis=-1, keepdims=True)
+    grad_in = inverse * scaled - value * (inverse * inverse * inverse) * mean
+    return grad_in, jnp.sum(grad * value * inverse, axis=0, keepdims=True)
+
+
+def context_back_kernel(
+    run, head_dim, count, tables, meta, dn_own, dn_got, h, cot, live, gains, query, *refs
+):
+    k_own, v_own, k_other, v_other = refs[:4]
+    pieces = refs[4 : 4 + count]
+    dh, dg2, da, dq, dkv, k_give, v_give, wo, bias, dctx, sem = refs[4 + count :]
+    rows, width = h.shape
+    coming = load_output(tables, pieces, wo, meta, sem)
+    bias_into(bias, run, meta[2] == 1)
+    grad_in, dg2[...] = norm_back(h[...], gains[1:2, :], dn_own[...] + dn_got[...])
+    grad = cot[...].astype(F32) + grad_in
+    dh[...] = grad
+    da[...] = (grad * live[...]).astype(BF)
+    finish(coming)
+
+    def project(t, _):
+        cols = aligned(t, TILE)
+        dctx[:, cols] = dot_nt(da[...], wo[cols, :]).astype(BF)
+        return 0
+
+    lax.fori_loop(0, width // TILE, project, 0)
+    scale = head_dim ** (-0.5)
+    lanes = 2 * head_dim
+    pairs = width // lanes
+    left = lax.broadcasted_iota(jnp.int32, (CHUNK, lanes), 1) < head_dim
+
+    def pair(p, _):
+        cols = aligned(p, lanes)
+        v_cols = aligned(p + pairs, lanes)
+        for chunk in range(rows // CHUNK):
+            r = slice(chunk * CHUNK, (chunk + 1) * CHUNK)
+            q_st = stacked(query[r, cols], left)
+            g_st = stacked(dctx[r, cols], left)
+            k_all = jnp.concatenate([k_own[r, cols], k_other[r, cols]], axis=0)
+            v_all = jnp.concatenate([v_own[r, cols], v_other[r, cols]], axis=0)
+            prob = probabilities(q_st, k_all, bias, scale)
+            d_prob = dot_nt(g_st, v_all)
+            d_score = prob * (d_prob - jnp.sum(d_prob * prob, axis=-1, keepdims=True))
+            d_score = d_score.astype(BF)
+            d_query = dot(d_score, k_all) * scale
+            d_key = dot_tn(d_score, q_st) * scale
+            d_value = dot_tn(prob.astype(BF), g_st)
+            dq[r, cols] = jnp.where(left, d_query[:CHUNK], d_query[CHUNK:]).astype(BF)
+            dkv[r, cols] = d_key[:CHUNK]
+            dkv[r, v_cols] = d_value[:CHUNK]
+            k_give[r, cols] = d_key[CHUNK:].astype(BF)
+            v_give[r, cols] = d_value[CHUNK:].astype(BF)
+        return 0
+
+    lax.fori_loop(0, pairs, pair, 0)
+
+
+def context_back(
+    run, meta, dn_own, dn_got, h, cot, live, gains, query, k_own, v_own, k_other, v_other, chains
+):
+    rows, width = h.shape
+    arrays, tables = operands(*chains)
+    low = jax.ShapeDtypeStruct((rows, width), BF)
+    return pl.pallas_call(
+        functools.partial(context_back_kernel, run, width // HEADS, len(arrays), tables),
+        in_specs=[SM] + [VM] * 11 + [HB] * len(arrays),
+        out_specs=[VM] * 7,
+        out_shape=[
+            jax.ShapeDtypeStruct((rows, width), F32),
+            jax.ShapeDtypeStruct((1, width), F32),
+            low,
+            low,
+            jax.ShapeDtypeStruct((rows, 2 * width), F32),
+            low,
+            low,
+        ],
+        scratch_shapes=[
+            pltpu.VMEM((width, width), BF),
+            pltpu.VMEM((2 * CHUNK, 2 * CHUNK), F32),
+            pltpu.VMEM((rows, width), BF),
+            pltpu.SemaphoreType.DMA((PAIR_COPIES,)),
+        ],
+        compiler_params=pltpu.CompilerParams(vmem_limit_bytes=60 * MIB),
+        cost_estimate=SMALL,
+        name="context_back",
+    )(
+        meta,
+        dn_own,
+        dn_got,
+        h,
+        cot,
+        live,
+        gains,
+        query,
+        k_own,
+        v_own,
+        k_other,
+        v_other,
+        *arrays,
+    )
+
+
+def shard_grads(lhs, rhs_cols, dw):
+    width = lhs.shape[1]
+    for i, rhs in enumerate(rhs_cols):
+
+        def step(t, _, rhs=rhs, i=i):
+            cols = aligned(t, TILE)
+            dw[i, cols, :] = dot_tn(lhs[:, cols], rhs()).astype(BF)
+            return 0
+
+        lax.fori_loop(0, width // TILE, step, 0)
+
+
+def store_devices(dw, matrix, row, count, k, targets, base, meta, sem, used):
+    chip, core = meta[0], meta[1]
+    shard = dw.shape[1] // (2 * CHIPS)
+    copies = []
+    for side, target in enumerate(targets):
+        for j in range(CHIPS):
+            device = (chip ^ CHAIN_MASKS[k][j]) * 2 + (1 - core if side == 0 else core)
+            start = pl.multiple_of(device * shard + row, 16)
+            low = base + j * count
+            copy = pltpu.make_async_copy(
+                dw.at[matrix, pl.ds(start, count), :],
+                target.at[low : low + count],
+                sem.at[used + len(copies)],
+            )
+            copy.start()
+            copies.append(copy)
+    return copies
+
+
+def output_grad_kernel(meta, context, grad, give, keep, dw, sem):
+    shard_grads(context, (lambda: grad[...],), dw)
+    half = dw.shape[1] // (4 * CHIPS)
+    leaving = []
+    for i, k in enumerate(OUTPUT_CHAINS):
+        base = i * CHIPS * half
+        leaving += store_devices(
+            dw, 0, i * half, half, k, (give, keep), base, meta, sem, len(leaving)
+        )
+    finish(leaving)
+
+
+def output_grad(meta, context, grad):
+    rows, width = context.shape
+    part = jax.ShapeDtypeStruct((width // 2, width), BF)
+    return pl.pallas_call(
+        output_grad_kernel,
+        in_specs=[SM, VM, VM],
+        out_specs=[HB, HB],
+        out_shape=[part, part],
+        scratch_shapes=[
+            pltpu.VMEM((1, width, width), BF),
+            pltpu.SemaphoreType.DMA((PAIR_COPIES,)),
+        ],
+        compiler_params=pltpu.CompilerParams(vmem_limit_bytes=60 * MIB),
+        cost_estimate=SMALL,
+        name="output_grad",
+    )(meta, context, grad)
+
+
+def joint_grad_kernel(meta, first, dq, dkv_own, dk_got, dv_got, give, keep, dkv, dw, sem):
+    width = first.shape[1]
+    for part, got in enumerate((dk_got, dv_got)):
+        cols = slice(part * width, (part + 1) * width)
+        more = jnp.where(meta[2] == 1, 0.0, got[...].astype(F32))
+        dkv[:, cols] = (dkv_own[:, cols] + more).astype(BF)
+    rights = (lambda: dq[...], lambda: dkv[:, :width], lambda: dkv[:, width:])
+    shard = width // (2 * CHIPS)
+    leaving = []
+    for k in range(3):
+
+        def step(t, _, k=k):
+            cols = aligned(t, TILE)
+            dw[k, cols, :] = dot_tn(first[:, cols], rights[k]()).astype(BF)
+            return 0
+
+        lax.fori_loop(0, width // TILE, step, 0)
+        leaving += store_devices(
+            dw, k, 0, shard, k, (give, keep), k * CHIPS * shard, meta, sem, len(leaving)
+        )
+    finish(leaving)
+
+
+def joint_grad(meta, first, dq, dkv_own, dk_got, dv_got):
+    rows, width = first.shape
+    part = jax.ShapeDtypeStruct((3 * width // 2, width), BF)
+    return pl.pallas_call(
+        joint_grad_kernel,
+        in_specs=[SM] + [VM] * 5,
+        out_specs=[HB, HB, VM],
+        out_shape=[part, part, jax.ShapeDtypeStruct((rows, 2 * width), BF)],
+        scratch_shapes=[
+            pltpu.VMEM((3, width, width), BF),
+            pltpu.SemaphoreType.DMA((PAIR_COPIES,)),
+        ],
+        compiler_params=pltpu.CompilerParams(vmem_limit_bytes=60 * MIB),
+        cost_estimate=SMALL,
+        name="joint_grad",
+    )(meta, first, dq, dkv_own, dk_got, dv_got)
+
+
+def input_back_kernel(count, tables, meta, dq, dkv, dh, x, gains, *refs):
+    pieces = refs[:count]
+    out, dg1, w, dn, sem = refs[count:]
+    rows, width = x.shape
+    finish(load_joint(tables, pieces, w, meta, sem))
+
+    def step(t, _):
+        cols = aligned(t, TILE)
+        dn[:, cols] = dot_nt(dq[...], w[cols, :width]) + dot_nt(dkv[...], w[cols, width:])
+        return 0
+
+    lax.fori_loop(0, width // TILE, step, 0)
+    grad_in, dg1[...] = norm_back(x[...].astype(F32), gains[0:1, :], dn[...])
+    out[...] = (dh[...] + grad_in).astype(BF)
+
+
+def input_back(meta, dq, dkv, dh, x, gains, chains):
+    rows, width = x.shape
+    arrays, tables = operands(*chains)
+    return pl.pallas_call(
+        functools.partial(input_back_kernel, len(arrays), tables),
+        in_specs=[SM] + [VM] * 5 + [HB] * len(arrays),
+        out_specs=[VM, VM],
+        out_shape=[
+            jax.ShapeDtypeStruct((rows, width), BF),
+            jax.ShapeDtypeStruct((1, width), F32),
+        ],
+        scratch_shapes=[
+            pltpu.VMEM((width, 3 * width), BF),
+            pltpu.VMEM((rows, width), F32),
+            pltpu.SemaphoreType.DMA((PAIR_COPIES,)),
+        ],
+        compiler_params=pltpu.CompilerParams(vmem_limit_bytes=60 * MIB),
+        cost_estimate=SMALL,
+        name="input_back",
+    )(meta, dq, dkv, dh, x, gains, *arrays)
+
+
+def adam_expand_kernel(meta, factor, w, m, v, own_a, own_b, got_a, got_b, w_out, m_out, v_out):
+    core, group = meta[1], meta[2]
+    block = w.shape[1] // (2 * CHIPS)
+    k = factor[0]
+    turn = (pl.program_id(0) % 2) ^ (1 - group)
+    for q in range(2 * CHIPS):
+        cols = slice(q * block, (q + 1) * block)
+        near = slice((q // 2) * block, (q // 2 + 1) * block)
+        own = jnp.where(turn == 0, own_a[:, near], own_b[:, near])
+        got = jnp.where(turn == 0, got_a[:, near], got_b[:, near])
+        grad = jnp.where(core == q % 2, own, got)
+        w_new, m_new, v_new = adam_step(
+            w[:, cols], k * grad, m[:, cols], v[:, cols], MATRIX_RATE, MATRIX_DECAY
+        )
+        w_out[:, cols] = w_new
+        m_out[:, cols] = m_new
+        v_out[:, cols] = v_new
+
+
+def adam_expand(meta, factor, w, m, v, own, got):
+    rows, width = w.shape
+    wide = pl.BlockSpec((rows, width // 4), lambda i: (0, i))
+    grad = pl.BlockSpec((rows, width // 8), lambda i: (i // 2, 0))
+    return pl.pallas_call(
+        adam_expand_kernel,
+        grid=(4,),
+        in_specs=[SM, SM, wide, wide, wide] + [grad] * 4,
+        out_specs=[wide, wide, wide],
+        out_shape=[jax.ShapeDtypeStruct(w.shape, F32)] * 3,
+        compiler_params=pltpu.CompilerParams(vmem_limit_bytes=60 * MIB),
+        name="adam_expand",
+    )(meta, factor, w, m, v, *own, *got)
+
+
+def local_cube(
+    count,
+    tokens,
+    depth_count,
+    cotangent,
+    joint_weight,
+    output_weight,
+    expand_weight,
+    shrink_weight,
+    norm_gains,
+    joint_mean,
+    joint_square,
+    output_mean,
+    output_square,
+    expand_mean,
+    expand_square,
+    shrink_mean,
+    shrink_square,
+    gains_mean,
+    gains_square,
+):
+    cube = Cube(count)
+    frames, positions, width = tokens.shape
+    run = positions // SETS
+    group = cube.bit(cube.top)
+    core = cube.bit(0)
+    upper = group == 1
+    second_core = core == 1
+    all_frames = 2 * frames
+    rows = all_frames * run
+    chip = (cube.index >> 1) & (CHIPS - 1)
+    meta = jnp.stack([chip, core, group]).astype(jnp.int32)
+
+    def halves(own, other):
+        return jnp.concatenate([jnp.where(upper, other, own), jnp.where(upper, own, other)], axis=0)
+
+    def parted(value):
+        first, second = value[:, :run], value[:, run:]
+        own, other = jnp.where(upper, second, first), jnp.where(upper, first, second)
+        return own.reshape(rows // 2, width), other.reshape(rows // 2, width)
+
+    def from_sets(value):
+        value = value.reshape(2, frames, run, width)
+        own = jnp.where(upper, value[1], value[0])
+        other = cube.swap(jnp.where(upper, value[0], value[1]), cube.top)
+        first = jnp.where(upper, other, own)
+        second = jnp.where(upper, own, other)
+        return jnp.concatenate([first, second], axis=1)
+
+    shard_rows = joint_weight.shape[0]
+    lane = norm_gains.shape[1]
+    small = jnp.concatenate([norm_gains.astype(BF).reshape(-1), depth_count.astype(BF)])
+    small_other = cube.swap(small.reshape(1, -1), cube.top)[0]
+    depth_all = halves(small[2 * lane :], small_other[2 * lane :]).astype(jnp.int32)
+    gain_pair = halves(small[None, : 2 * lane], small_other[None, : 2 * lane])
+    gain_pair = gain_pair.reshape(2, 2, lane).transpose(1, 0, 2)
+    spread = jnp.broadcast_to(gain_pair[:, :, None, :], (2, 2, 2 * CHIPS, lane)).reshape(2, width)
+    mine = (jnp.arange(width) // lane) % (2 * CHIPS) == (cube.index & (2 * CHIPS - 1))
+    gain_rows = jnp.pad(jnp.where(mine[None, :], spread, 0), ((0, 14), (0, 0)))
+    shards = list(first_shards(joint_weight))
+    shards[2] = lax.dynamic_update_slice(shards[2], gain_rows, (shard_rows, 0))
+    joint = [Blocks(shard) for shard in shards]
+    x_own, x_give = parted(tokens)
+    x_got = cube.swap(x_give, cube.top)
+    x_rows = halves(x_own, x_got)
+
+    def begin(name):
+        return Round(cube, meta, width, name)
+
+    one = begin("pack_one").gather(joint, 0).run(x_give)
+    own_cols, give_cols, shrink_keep, shrink_give, out_a, out_b = split_weights(
+        meta, expand_weight, shrink_weight, output_weight
+    )
+    output = [None, Blocks(out_a), Blocks(out_b)]
+    joint_other = [Blocks(rows=blocks.rows) for blocks in joint]
+    output_other = [None] + [Blocks(rows=blocks.rows) for blocks in output[1:]]
+    two = begin("pack_two").gather(joint, 1).gather(output, 0).run(one.got, give_cols)
+    shrink_other = cube.swap(after(shrink_give, two.got, x_got), cube.top)
+    got_cols = cube.swap(after(give_cols, two.got, x_got), 0)
+    three = begin("pack_three").gather(joint, 2).gather(output, 1)
+    three = three.core(joint, joint_other, 0, 4).run(two.got, x_got)
+    units = Jobs(width)
+    unit_rows = 2 * shard_rows
+    for kind in range(2):
+        target = units.output(2 * unit_rows)
+        for turn_index in range(2):
+            unit = turn_index * 2 + kind
+            base = turn_index * unit_rows
+            low, high = (base, base + shard_rows), (base + shard_rows, base)
+            units.copy(own_cols, unit * shard_rows, target, low, shard_rows)
+            units.copy(got_cols, unit * shard_rows, target, high, shard_rows)
+    target = units.output(2 * unit_rows)
+    units.copy(shrink_other, 0, target, 0, unit_rows)
+    units.copy(shrink_keep, 0, target, unit_rows, unit_rows)
+    units = units.run(meta, "expand_units", three.packed)
+    part_a = [Blocks(unit, unit_rows) for unit in units]
+    part_b = [Blocks(rows=unit_rows) for unit in units]
+    for blocks, unit in zip(part_b, units):
+        blocks.arrived(unit, unit_rows, 1)
+
+    cot_own, cot_give = parted(cotangent)
+    cot_got = cube.swap(after(cot_give, three.packed, shrink_other), cube.top)
+    late = begin("pack_late").core(joint, joint_other, 4, 8).run(three.got, three.core_got, units)
+    first_units = after(units, three.got, three.core_got)
+    got_four = [cube.swap(unit, 1 + axis) for axis, unit in enumerate(first_units)]
+    for k in range(3):
+        part_a[k].arrived(got_four[k], 0, 1)
+        part_b[k].arrived(got_four[k], unit_rows, 1)
+
+    position = group * run + jnp.arange(run)
+    live = (position[None, :] < depth_all[:, None]).astype(F32).reshape(rows, 1)
+
+    first, query, key, value, gains_all = joint_forward(meta, x_rows, joint + joint_other)
+    five = begin("pack_five").gather(part_a, 1).gather(part_b, 1).gather(output, 2)
+    five = five.run(got_four, key, cot_got)
+    key_other = cube.swap(after(key, cot_got), cube.top)
+    value_other = cube.swap(after(value, cot_got), cube.top)
+    seven = begin("pack_seven").gather(part_a, 2).core(output, output_other, 0, 8)
+    seven = seven.run(five.got, key_other, value_other)
+    cot_live = (halves(cot_own, after(cot_got, key)).astype(F32) * live).astype(BF)
+    cot_other = cube.swap(after(cot_live, five.got, key_other), 0)
+    output_chains = output[1:] + output_other[1:]
+    context, middle, second = context_forward(
+        run,
+        meta,
+        query,
+        key,
+        value,
+        key_other,
+        value_other,
+        x_rows,
+        live,
+        gains_all,
+        output_chains,
+    )
+    eight = begin("pack_eight").gather(part_b, 2).run(
+        seven.packed, seven.core_got, cot_other, gate=(seven.got, second)
+    )
+    second_other = cube.swap(second, 0)
+    row_args = (meta, second, second_other, cot_live, cot_other)
+    dn_a, *kept_a = ffn_rows(*row_args, part_a, None)
+    f_a, *grad_a = ffn_weights(*row_args, *kept_a, part_a[2], None)
+    dn_own, dn_send, *kept_b = ffn_rows(*row_args, part_b, after(dn_a, f_a))
+    dn_got = cube.swap(dn_send, 0)
+    f_own, f_send, *grad_b = ffn_weights(*row_args, *kept_b, part_b[2], f_a)
+
+    outcome = {}
+
+    def expand_final(key, kind):
+        def final(jobs, got, keep, count):
+            if key not in outcome:
+                outcome[key] = (jobs.output(2 * shard_rows, F32), jobs.output(2 * shard_rows, F32))
+            own, give = outcome[key]
+            half = count // 2
+            for target, offset in ((own, (0, half)), (give, (half, 0))):
+                got_at = tuple(got[1] + o for o in offset)
+                keep_at = tuple(keep[1] + o for o in offset)
+                jobs.add(got[0], got_at, keep[0], keep_at, target, kind * shard_rows, half)
+
+        return final
+
+    def plain_final(key):
+        def final(jobs, got, keep, count):
+            outcome[key] = jobs.output(count, F32)
+            jobs.add(got[0], got[1], keep[0], keep[1], outcome[key], 0, count)
+
+        return final
+
+    def ffn_sums(grads, name):
+        finals = (expand_final(name, 0), expand_final(name, 1), plain_final(name + "_shrink"))
+        block = grads[0].shape[0] // 4
+        return [Sums((grads[2 * k], 0), (grads[2 * k + 1], 0), block, finals[k]) for k in range(3)]
+
+    def turn(name, work, *earlier, squares=False, gate=()):
+        return reduce_round(cube, meta, width, name, work, *earlier, squares=squares, gate=gate)
+
+    def core_sum(name, give, keep, chains, *earlier):
+        got = cube.swap(after(give, *earlier) if earlier else give, 0)
+        jobs = Jobs(width)
+        row, sums = 0, [None] * 3
+        targets = []
+        for k, count in chains:
+            send, own = jobs.output(4 * count), jobs.output(4 * count)
+            jobs.add(got, row + 4 * count, keep, row + 4 * count, send, 0, 4 * count)
+            jobs.add(got, row, keep, row, own, 0, 4 * count)
+            targets.append((k, count, own, send))
+            row += CHIPS * count
+        out = jobs.run(meta, name)
+        for k, count, own, send in targets:
+            sums[k] = Sums((out[own], 0), (out[send], 0), count, plain_final((name, k)))
+        return sums
+
+    sums_a = ffn_sums(grad_a, "a")
+    sums_b = ffn_sums(grad_b, "b")
+    turn_one, _ = turn("turn_one", [(sums_a, 0)], eight.got)
+    turn_two, _ = turn("turn_two", [(sums_b, 0)], turn_one)
+
+    grad_middle, grad_gain_two, grad_branch, d_query, dkv_own, k_give, v_give = context_back(
+        run,
+        meta,
+        after(dn_own, f_own, turn_one),
+        dn_got,
+        middle,
+        cot_live,
+        live,
+        gains_all,
+        query,
+        key,
+        value,
+        key_other,
+        value_other,
+        output_chains,
+    )
+    turn_three, _ = turn("turn_three", [(sums_a, 1), (sums_b, 1)], turn_two, k_give)
+    dk_got = cube.swap(k_give, cube.top)
+    dv_got = cube.swap(v_give, cube.top)
+    output_give, output_keep = output_grad(meta, context, after(grad_branch, turn_two))
+    half_shard = shard_rows // 2
+    sums_o = core_sum(
+        "output_core", output_give, output_keep, [(k, half_shard) for k in OUTPUT_CHAINS]
+    )
+    turn_four, packed_four = turn("turn_four", [(sums_a, 2), (sums_b, 2), (sums_o, 0)], turn_three, dk_got, dv_got)
+    shrunk_got = cube.swap(after(f_send, turn_three, packed_four), 0)
+    shrunk = f_own + shrunk_got.astype(F32)
+    result = (middle + live * shrunk).astype(BF)
+    joint_give, joint_keep, dkv = joint_grad(
+        meta, first, d_query, dkv_own, dk_got, after(dv_got, packed_four)
+    )
+    sums_j = core_sum("joint_core", joint_give, joint_keep, [(k, shard_rows) for k in range(3)])
+    result = from_sets(after(result, packed_four))
+    turn_seven, out_seven = turn(
+        "turn_seven",
+        [(sums_a, 3), (sums_b, 3), (sums_o, 1), (sums_j, 0)],
+        turn_four,
+        result,
+        squares=True,
+    )
+    expand_own_a, expand_give_a = (out_seven[i] for i in outcome["a"])
+    expand_own_b, expand_give_b = (out_seven[i] for i in outcome["b"])
+    shrink_first = out_seven[outcome["a_shrink"]]
+    shrink_mine = out_seven[outcome["b_shrink"]]
+
+    expand_give = jnp.concatenate([expand_give_a, expand_give_b])
+    expand_got = cube.swap(expand_give, 0)
+    expand_got_a, expand_got_b = expand_got[: 2 * shard_rows], expand_got[2 * shard_rows :]
+    shrink_got = cube.swap(shrink_first.astype(BF), cube.top).astype(F32)
+    grad_inputs, grad_gain_one = input_back(
+        meta,
+        d_query,
+        after(dkv, sums_j[0].send[0]),
+        grad_middle,
+        x_rows,
+        gains_all,
+        joint + joint_other,
+    )
+    turn_nine, out_nine = turn(
+        "turn_nine", [(sums_o, 2), (sums_j, 1)], turn_seven, shrink_got, expand_got
+    )
+    gains_term = jnp.concatenate([grad_gain_one, grad_gain_two]).reshape(2, count, -1)
+    gains_term = gains_term.transpose(1, 0, 2).reshape(count, -1)
+    gains_parts = lax.all_to_all(after(gains_term, out_nine), "fsdp", 0, 0, tiled=True)
+    grad_gains = jnp.sum(gains_parts, axis=0).reshape(2, -1)
+    grad_inputs = from_sets(after(grad_inputs, turn_seven))
+    turn_ten, out_ten = turn(
+        "turn_ten", [(sums_o, 3), (sums_j, 2)], turn_nine, grad_inputs, squares=True
+    )
+    grad_output = jnp.concatenate([out_ten[outcome[("output_core", k)]] for k in OUTPUT_CHAINS])
+    _, out_last = turn("turn_last", [(sums_j, 3)], turn_ten, squares=True)
+    grad_joint = [out_last[outcome[("joint_core", k)]] for k in range(3)]
+
+    grad_shrink = jnp.stack(
+        [jnp.where(upper, shrink_got, shrink_mine), jnp.where(upper, shrink_mine, shrink_got)]
+    )
+    grad_joint = jnp.concatenate(grad_joint, axis=1)
+
+    local_sq = sum(jnp.sum(out[-1]) for out in (out_seven, out_ten, out_last))
+    local_sq = local_sq + jnp.sum(grad_gains * grad_gains)
+    squares = lax.all_to_all(jnp.broadcast_to(local_sq, (count, 128)), "fsdp", 0, 0, tiled=True)
+    total_sq = jnp.sum(squares[:, 0])
+    grad_norm_value = jnp.sqrt(total_sq)
+    factor = CLIP_LIMIT / jnp.maximum(grad_norm_value, CLIP_LIMIT)
+    joint_new = adam_step(
+        joint_weight, factor * grad_joint, joint_mean, joint_square, MATRIX_RATE, MATRIX_DECAY
+    )
+    output_new = adam_step(
+        output_weight, factor * grad_output, output_mean, output_square, MATRIX_RATE, MATRIX_DECAY
+    )
+    expand_new = adam_expand(
+        meta,
+        factor.reshape(1),
+        expand_weight,
+        expand_mean,
+        expand_square,
+        (expand_own_a, expand_own_b),
+        (expand_got_a, expand_got_b),
+    )
+    shrink_new = adam_step(
+        shrink_weight, factor * grad_shrink, shrink_mean, shrink_square, MATRIX_RATE, MATRIX_DECAY
+    )
+    gains_new = adam_step(norm_gains, factor * grad_gains, gains_mean, gains_square, GAIN_RATE, 0.0)
+    return (
+        result,
+        grad_inputs,
+        grad_norm_value,
+        *joint_new,
+        *output_new,
+        *expand_new,
+        *shrink_new,
+        *gains_new,
+    )
+
+
 def solution(mesh):
     rows = P("fsdp", None)
     cube = P("fsdp", None, None)
@@ -377,7 +1718,7 @@
     count = mesh.shape["fsdp"]
 
     def body(*args):
-        return local(count, *args)
+        return (local_cube if count == 4 * CHIPS else local_general)(count, *args)
 
     return jax.shard_map(
         body,

time: 685 us -> 488 us (0.71); the launches traced: 675 us -> 487 us
  Pallas kernels: 0 us -> 198 us
  waiting for transfers between devices: 278 us -> 161 us
  other arithmetic: 123 us -> 30.8 us
  matrix products: 88.4 us -> 0 us
  local copies, waits for them, and re-layouts: 101 us -> 17.9 us
    pallas_call x0 -> x28, Pallas kernels: none -> 198 us  [the longest x15 66 us: run(): pl.pallas_call(functools.partial(jobs_kernel, self.work, len(inputs), sel...]
    ppermute x100 -> x64, waiting for transfers between devices: 278 us -> 155 us  [swap(): return lax.ppermute(value, 'fsdp', pairs)]
    dot_general x38 -> x0, matrix products: 83.1 us -> none  [the longest x13 28.1 us: dot(): lax.dot_general(a, b, (((1,), (0,)), ((), ())), preferred_element_type=F32)]
    another operation x80 -> x2, other arithmetic: 57.3 us -> 1.71 us  [the longest x1 1.12 us: local_cube(): jnp.stack([jnp.where(upper, shrink_got, shrink_mine), jnp.where(upper, sh...]
    convert_element_type x44 -> x7, other arithmetic: 31.1 us -> 2.6 us  [the longest x1 0.74 us: local_cube(): shrink_got = cube.swap(shrink_first.astype(BF), cube.top).astype(F32)]
    dynamic_slice x25 -> x0, local copies, waits for them, and re-layouts: 23.4 us -> none  [the longest x10 11.8 us: reduce(): keep = lax.dynamic_index_in_dim(value, mine, axis, keepdims=False)]
    reshape x10 -> x6, local copies, waits for them, and re-layouts: 21.9 us -> 1.06 us  [the longest x1 0.69 us: local_cube(): gains_term = gains_term.transpose(1, 0, 2).reshape(count, -1)]
    unnamed x364 -> x134, local copies, waits for them, and re-layouts: 23.9 us -> 13.5 us
  transfers between devices with their start and end apart: 100 -> 66, of which waited for: 47 -> 25; matrix products, arithmetic and copies ran while one was open for 32% -> 4% of each run, Pallas kernels for 0% -> 29%
where the time goes in v2:
time: 488 us; the launch traced here: 487 us
  Pallas kernels  198 us (41%)
  waiting for transfers between devices  161 us (33%)
  starting transfers between devices  72.4 us (15%)
  other arithmetic  30.8 us (6%)
  local copies, waits for them, and re-layouts  17.9 us (4%)
  between operations  6.14 us (1%)
    ppermute x64, waiting for transfers between devices, swap(): return lax.ppermute(value, 'fsdp', pairs)  155 us
    pallas_call x15, Pallas kernels, run(): pl.pallas_call(functools.partial(jobs_kernel, self.work, len(inputs), sel...  66 us
    ppermute x64, starting transfers between devices, swap(): return lax.ppermute(value, 'fsdp', pairs)  65.7 us
    pallas_call x2, Pallas kernels, ffn_rows(): pl.pallas_call(functools.partial(ffn_rows_kernel, first, len(arrays), tab...  27.3 us
    pallas_call x2, Pallas kernels, ffn_weights(): pl.pallas_call(functools.partial(ffn_weights_kernel, first, len(arrays),...  24.4 us
    pallas_call x1, Pallas kernels, context_back(): pl.pallas_call(functools.partial(context_back_kernel, run, width // HEADS...  19.7 us
    unnamed x134, local copies, waits for them, and re-layouts  13.5 us
    pallas_call x1, Pallas kernels, context_forward(): pl.pallas_call(functools.partial(context_kernel, run, width // HEADS, len...  13.1 us
  transfers between devices with their start and end apart: 66, of which 25 were waited for; matrix products, arithmetic and copies ran while one was open for 4% of the time, Pallas kernels for 29%

profile of v2, /device:TPU:0, one launch (start us, length us, event | category | flops | bytes accessed | tf_op | source)
XLA Modules:
  0.0 486.8 jit_solution(932860795003958142)
XLA Ops:
  2.2 4.0 collective-permute-start.1
  15.3 3.4 split_weights.1
  19.5 2.8 pack_two.1
  25.8 8.9 %collective-permute-done = bf16[128,1024]{1,0:T(8,128)(2,1)S(1)} collective-permute-done((bf16[128,1024]{1,0:T(8,128)(2,1)S(1)}, bf16[128,1024]{1,0:T(8,128)(2,1)S(1)}, u32[]{:S(2)}, u32[]{:S(2)}) %collective-permute-start) | collective-permute-done | bytes 262176 | tf_op jit(solution)/shard_map/ppermute | solution.py:65
  38.2 5.0 %pack_three.1 = (bf16[320,1024]{1,0:T(8,128)(2,1)}, bf16[320,1024]{1,0:T(8,128)(2,1)}, bf16[320,1024]{1,0:T(8,128)(2,1)}, bf16[832,1024]{1,0:T(8,128)(2,1)}) custom-call(s32[3]{0:T(128)} %pad_add_fusion.meta, bf16[64,1024]{1,0:T(8,128)(2,1)} %get-tuple-element.329.refs_5_.refs_0_.refs_4_, bf16[64,1024]{1,0:T(8,128)(2,1)} %copy-done.26, ...), custom_call_target="tpu_custom_call" | custom-call | flops 1 | bytes 1 | tf_op jit(solution)/shard_map/pack_three/pallas_call | solution.py:435
  43.3 2.2 collective-permute-start.13
  49.6 9.1 %collective-permute-done.13.refs_2_ = bf16[128,1024]{1,0:T(8,128)(2,1)S(1)} collective-permute-done((bf16[128,1024]{1,0:T(8,128)(2,1)S(1)}, bf16[128,1024]{1,0:T(8,128)(2,1)S(1)}, u32[]{:S(2)}, u32[]{:S(2)}) %collective-permute-start.13) | collective-permute-done | bytes 262176 | tf_op jit(solution)/shard_map/ppermute | solution.py:65
  61.4 3.1 expand_units.1
  64.5 2.9 collective-permute-done.8.refs_0_.refs_3_.refs_4_.refs_11_.refs_2_.refs_6_
  68.8 3.1 pack_late.1
  80.9 10.4 %joint_forward.1 = (bf16[256,1024]{1,0:T(8,128)(2,1)}, bf16[256,1024]{1,0:T(8,128)(2,1)}, bf16[256,1024]{1,0:T(8,128)(2,1)}, bf16[256,1024]{1,0:T(8,128)(2,1)}, f32[8,1024]{1,0:T(8,128)}) custom-call(s32[3]{0:T(128)} %pad_add_fusion.meta, bf16[256,1024]{1,0:T(8,128)(2,1)} %pad_maximum_fusion.1.x, ...), custom_call_target="tpu_custom_call" | custom-call | flops 1 | bytes 1 | tf_op jit(solution)/shard_map/joint_forward/pallas_call | solution.py:1014
  93.0 4.3 pack_five.1
  104.1 32.0 %collective-permute-done.16.k_other.refs_2_ = bf16[256,1024]{1,0:T(8,128)(2,1)} collective-permute-done((bf16[256,1024]{1,0:T(8,128)(2,1)S(1)}, bf16[256,1024]{1,0:T(8,128)(2,1)}, u32[]{:S(2)}, u32[]{:S(2)}) %collective-permute-start.16) | collective-permute-done | bytes 524320 | tf_op jit(solution)/shard_map/ppermute | solution.py:65
  136.2 12.5 %collective-permute-done.17.v_other.refs_3_ = bf16[256,1024]{1,0:T(8,128)(2,1)} collective-permute-done((bf16[256,1024]{1,0:T(8,128)(2,1)}, bf16[256,1024]{1,0:T(8,128)(2,1)}, u32[]{:S(2)}, u32[]{:S(2)}) %collective-permute-start.17) | collective-permute-done | bytes 524320 | tf_op jit(solution)/shard_map/ppermute | solution.py:65
  150.8 4.7 pack_seven.1
  160.7 3.6 pack_eight.1
  164.4 13.1 %context_forward.1 = (bf16[256,1024]{1,0:T(8,128)(2,1)}, f32[256,1024]{1,0:T(8,128)}, bf16[256,1024]{1,0:T(8,128)(2,1)}) custom-call(s32[3]{0:T(128)} %pad_add_fusion.meta, bf16[256,1024]{1,0:T(8,128)(2,1)} %get-tuple-element.359.query, bf16[256,1024]{1,0:T(8,128)(2,1)} %get-tuple-element.363.k_own.refs_0_, ...), custom_call_target="tpu_custom_call" | custom-call | flops 1 | bytes 1 | tf_op jit(solution)/shard_map/context_forward/pallas_call | solution.py:1106
  177.5 4.0 collective-permute-done.27.refs_7_
  188.3 13.3 %ffn_rows.2 = (f32[512,1024]{1,0:T(8,128)}, bf16[512,1024]{1,0:T(8,128)(2,1)}, bf16[512,1024]{1,0:T(8,128)(2,1)}, bf16[512,1024]{1,0:T(8,128)(2,1)}) custom-call(s32[3]{0:T(128)} %pad_add_fusion.meta, bf16[256,1024]{1,0:T(8,128)(2,1)} %get-tuple-element.401.n2m, bf16[256,1024]{1,0:T(8,128)(2,1)} %copy-done.14, bf16[256,1024]{1,0:T(8,128)(2,1)} %copy-done.6, ...), custom_call_target="tpu_custom_call" | custom-call | flops 1 | bytes 1 | tf_op jit(solution)/shard_map/ffn_rows/pallas_call | solution.py:837
  201.6 11.8 %ffn_weights.2 = (f32[512,1024]{1,0:T(8,128)}, bf16[512,1024]{1,0:T(8,128)(2,1)}, bf16[512,1024]{1,0:T(8,128)(2,1)}, bf16[512,1024]{1,0:T(8,128)(2,1)}, bf16[512...) custom-call(s32[3]{0:T(128)} %pad_add_fusion.meta, ...), custom_call_target="tpu_custom_call" | custom-call | flops 1 | bytes 1 | tf_op jit(solution)/shard_map/ffn_weights/pallas_call | solution.py:908
  217.6 14.0 %ffn_rows.3 = (f32[256,1024]{1,0:T(8,128)}, f32[256,1024]{1,0:T(8,128)}, bf16[512,1024]{1,0:T(8,128)(2,1)}, bf16[512,1024]{1,0:T(8,128)(2,1)}, bf16[512,1024]{1,0:T(8,128)(2,1)}) custom-call(s32[3]{0:T(128)} %pad_add_fusion.meta, bf16[256,1024]{1,0:T(8,128)(2,1)} %get-tuple-element.401.n2m, bf16[256,1024]{1,0:T(8,128)(2,1)} %copy-done.14, ...), custom_call_target="tpu_custom_call" | custom-call | flops 1 | bytes 1 | tf_op jit(solution)/shard_map/ffn_rows/pallas_call | solution.py:837
  231.7 12.6 %ffn_weights.3 = (f32[256,1024]{1,0:T(8,128)}, bf16[256,1024]{1,0:T(8,128)(2,1)}, bf16[512,1024]{1,0:T(8,128)(2,1)}, bf16[512,1024]{1,0:T(8,128)(2,1)}, bf16[512...) custom-call(s32[3]{0:T(128)} %pad_add_fusion.meta, ...), custom_call_target="tpu_custom_call" | custom-call | flops 1 | bytes 1 | tf_op jit(solution)/shard_map/ffn_weights/pallas_call | solution.py:908
  247.4 19.7 %context_back.1 = (f32[256,1024]{1,0:T(8,128)}, f32[1,1024]{1,0:T(1,128)}, bf16[256,1024]{1,0:T(8,128)(2,1)}, bf16[256,1024]{1,0:T(8,128)(2,1)}, f32[256,2048]{1...) custom-call(s32[3]{0:T(128)} %pad_add_fusion.meta, f32[256,1024]{1,0:T(8,128)} %get-tuple-element.452.dn_own, ...), custom_call_target="tpu_custom_call" | custom-call | flops 1 | bytes 1 | tf_op jit(solution)/shard_map/context_back/pallas_call | solution.py:1188
  267.1 3.1 collective-permute-done.36.refs_2_
  271.5 5.0 %output_grad.1 = (bf16[512,1024]{1,0:T(8,128)(2,1)}, bf16[512,1024]{1,0:T(8,128)(2,1)}) custom-call(s32[3]{0:T(128)} %pad_add_fusion.meta, bf16[256,1024]{1,0:T(8,128)(2,1)} %get-tuple-element.472.context, bf16[256,1024]{1,0:T(8,128)(2,1)} %get-tuple-element.474.grad), custom_call_target="tpu_custom_call" | custom-call | flops 1 | bytes 1 | tf_op jit(solution)/shard_map/output_grad/pallas_call | solution.py:1273
  276.6 8.2 %turn_three.1 = (bf16[512,1024]{1,0:T(8,128)(2,1)}, bf16[512,1024]{1,0:T(8,128)(2,1)}, bf16[512,1024]{1,0:T(8,128)(2,1)}, bf16[256,1024]{1,0:T(8,128)(2,1)}, bf1...) custom-call(s32[3]{0:T(128)} %pad_add_fusion.meta, ...), custom_call_target="tpu_custom_call" | custom-call | flops 1 | bytes 1 | tf_op jit(solution)/shard_map/turn_three/pallas_call | solution.py:435
  291.1 3.0 output_core.1
  294.1 29.2 %collective-permute-done.45.dv_got = bf16[256,1024]{1,0:T(8,128)(2,1)S(1)} collective-permute-done((bf16[256,1024]{1,0:T(8,128)(2,1)}, bf16[256,1024]{1,0:T(8,128)(2,1)S(1)}, u32[]{:S(2)}, u32[]{:S(2)}) %collective-permute-start.45) | collective-permute-done | bytes 524320 | tf_op jit(solution)/shard_map/ppermute | solution.py:65
  323.3 13.3 %collective-permute-done.44.dk_got = bf16[256,1024]{1,0:T(8,128)(2,1)} collective-permute-done((bf16[256,1024]{1,0:T(8,128)(2,1)}, bf16[256,1024]{1,0:T(8,128)(2,1)}, u32[]{:S(2)}, u32[]{:S(2)}) %collective-permute-start.44) | collective-permute-done | bytes 524320 | tf_op jit(solution)/shard_map/ppermute | solution.py:65
  337.9 5.6 %turn_four.1 = (bf16[384,1024]{1,0:T(8,128)(2,1)}, bf16[384,1024]{1,0:T(8,128)(2,1)}, bf16[256,1024]{1,0:T(8,128)(2,1)}, bf16[128,1024]{1,0:T(8,128)(2,1)}, bf16...) custom-call(s32[3]{0:T(128)} %pad_add_fusion.meta, ...), custom_call_target="tpu_custom_call" | custom-call | flops 1 | bytes 1 | tf_op jit(solution)/shard_map/turn_four/pallas_call | solution.py:435
  343.5 10.1 %joint_grad.1 = (bf16[1536,1024]{1,0:T(8,128)(2,1)}, bf16[1536,1024]{1,0:T(8,128)(2,1)}, bf16[256,2048]{1,0:T(8,128)(2,1)}) custom-call(s32[3]{0:T(128)} %pad_add_fusion.meta, bf16[256,1024]{1,0:T(8,128)(2,1)} %get-tuple-element.507.first, bf16[256,1024]{1,0:T(8,128)(2,1)} %get-tuple-element.506.dq, f32[256,2048]{1,0:T(8,128)} %get-tuple-element.508.dkv_own, ...), custom_call_target="tpu_custom_call" | custom-call | flops 1 | bytes 1 | tf_op jit(solution)/shard_map/joint_grad/pallas_call | solution.py:1314
  356.7 3.2 collective-permute-done.46
  360.6 2.6 collective-permute-start.51
  363.2 12.0 %collective-permute-done.47 = bf16[16,8,1024]{2,1,0:T(8,128)(2,1)S(1)} collective-permute-done((bf16[16,8,1024]{2,1,0:T(8,128)(2,1)S(1)}, bf16[16,8,1024]{2,1,0:T(8,128)(2,1)S(1)}, u32[]{:S(2)}, u32[]{:S(2)}) %collective-permute-start.47) | collective-permute-done | bytes 262176 | tf_op jit(solution)/shard_map/ppermute | solution.py:65
  376.1 5.3 %joint_core.1 = (bf16[256,1024]{1,0:T(8,128)(2,1)}, bf16[256,1024]{1,0:T(8,128)(2,1)}, bf16[256,1024]{1,0:T(8,128)(2,1)}, bf16[256,1024]{1,0:T(8,128)(2,1)}, bf1...) custom-call(s32[3]{0:T(128)} %pad_add_fusion.meta, bf16[1536,1024]{1,0:T(8,128)(2,1)} %collective-permute-done.48.refs_0_, ...), custom_call_target="tpu_custom_call" | custom-call | flops 1 | bytes 1 | tf_op jit(solution)/shard_map/joint_core/pallas_call | solution.py:435
  382.8 6.7 %turn_seven.1 = (bf16[320,1024]{1,0:T(8,128)(2,1)}, bf16[256,1024]{1,0:T(8,128)(2,1)}, bf16[320,1024]{1,0:T(8,128)(2,1)}, bf16[64,1024]{1,0:T(8,128)(2,1)}, bf16...) custom-call(s32[3]{0:T(128)} %pad_add_fusion.meta, ...), custom_call_target="tpu_custom_call" | custom-call | flops 1 | bytes 1 | tf_op jit(solution)/shard_map/turn_seven/pallas_call | solution.py:435
  393.2 9.9 %input_back.1 = (bf16[256,1024]{1,0:T(8,128)(2,1)}, f32[1,1024]{1,0:T(1,128)}) custom-call(s32[3]{0:T(128)} %pad_add_fusion.meta, bf16[256,1024]{1,0:T(8,128)(2,1)} %get-tuple-element.506.dq, bf16[256,2048]{1,0:T(8,128)(2,1)} %get-tuple-element.514.dkv, f32[256,1024]{1,0:T(8,128)} %get-tuple-element.515.dh, bf16[256,1024]{1,0:T(8,128)(2,1)} %pad_maximum_fusion.1.x, ...), custom_call_target="tpu_custom_call" | custom-call | flops 1 | bytes 1 | tf_op jit(solution)/shard_map/input_back/pallas_call | solution.py:1348
  403.1 3.0 collective-permute-done.53.refs_0_
  414.5 3.7 turn_nine.1
  422.1 7.8 %collective-permute-done.55 = bf16[16,8,1024]{2,1,0:T(8,128)(2,1)} collective-permute-done((bf16[16,8,1024]{2,1,0:T(8,128)(2,1)}, bf16[16,8,1024]{2,1,0:T(8,128)(2,1)}, u32[]{:S(2)}, u32[]{:S(2)}) %collective-permute-start.55) | collective-permute-done | bytes 262176 | tf_op jit(solution)/shard_map/ppermute | solution.py:65
  431.7 3.5 all-to-all-start
  435.3 3.1 collective-permute-done.59.refs_2_
  439.2 3.7 turn_ten.1
  450.4 3.3 turn_last.1
  457.1 3.2 all-to-all-start.1
  461.4 6.0 %all-to-all-done.1 = f32[32,1,128]{2,1,0:T(1,128)S(1)} async-done(((f32[32,1,128]{2,1,0:T(1,128)}), f32[32,1,128]{2,1,0:T(1,128)S(1)}, u32[]{:S(2)}, u32[]{:S(2)}) %all-to-all-start.1) | async-done | bytes 16416 | tf_op jit(solution)/shard_map/all_to_all | solution.py:1678
  473.0 3.6 multiply_subtract_fusion
  478.4 7.2 %adam_expand.1 = (f32[64,8192]{1,0:T(8,128)}, f32[64,8192]{1,0:T(8,128)}, f32[64,8192]{1,0:T(8,128)}) custom-call(s32[3]{0:T(128)} %pad_add_fusion.meta, f32[1]{0:T(128)} %bitcast.18.factor, f32[64,8192]{1,0:T(8,128)} %w.1, f32[64,8192]{1,0:T(8,128)} %m.1, f32[64,8192]{1,0:T(8,128)} %v.1, f32[128,1024]{1,0:T(8,128)} %get-tuple-element.594.own_a, ...), custom_call_target="tpu_custom_call" | custom-call | tf_op jit(solution)/shard_map/adam_expand/pallas_call | solution.py:1390
  (301 shorter events, 114.7 us)
Async XLA Ops:
  23.4 13.3 %collective-permute-start.6 = (bf16[160,1024]{1,0:T(8,128)(2,1)}, bf16[160,1024]{1,0:T(8,128)(2,1)S(1)}, u32[]{:S(2)}, u32[]{:S(2)}) collective-permute-start(bf16[160,1024]{1,0:T(8,128)(2,1)} %get-tuple-element.327), channel_id=1, source_target_pairs={{0,8},{1,9},{2,10},{3,11},{4,12},{5,13},{6,14},{7,15},{8,0},{9,1},... | collective-permute-start | bytes 983048 | tf_op jit(solution)/shard_map/ppermute | solution.py:65
  43.2 24.2 %collective-permute-start.11 = (bf16[832,1024]{1,0:T(8,128)(2,1)}, bf16[832,1024]{1,0:T(8,128)(2,1)}, u32[]{:S(2)}, u32[]{:S(2)}) collective-permute-start(bf16[832,1024]{1,0:T(8,128)(2,1)} %get-tuple-element.343), channel_id=1, source_target_pairs={{0,1},{1,0},{2,3},{3,2},{4,5},{5,4},{6,7},{7,6},{8,9},{9,8},{10,11... | collective-permute-start | bytes 5111816 | tf_op jit(solution)/shard_map/ppermute | solution.py:65
  43.3 15.3 %collective-permute-start.13 = (bf16[128,1024]{1,0:T(8,128)(2,1)S(1)}, bf16[128,1024]{1,0:T(8,128)(2,1)S(1)}, u32[]{:S(2)}, u32[]{:S(2)}) collective-permute-start(bf16[128,1024]{1,0:T(8,128)(2,1)S(1)} %copy-done.66), channel_id=1, source_target_pairs={{0,16},{1,17},{2,18},{3,19},{4,20},{5,21},{6,22},{7,23},{8,24},{9,... | collective-permute-start | bytes 786440 | tf_op jit(solution)/shard_map/ppermute | solution.py:65
  45.5 21.9 %collective-permute-start.8 = (bf16[320,1024]{1,0:T(8,128)(2,1)}, bf16[320,1024]{1,0:T(8,128)(2,1)S(1)}, u32[]{:S(2)}, u32[]{:S(2)}) collective-permute-start(bf16[320,1024]{1,0:T(8,128)(2,1)} %get-tuple-element.340), channel_id=1, source_target_pairs={{0,8},{1,9},{2,10},{3,11},{4,12},{5,13},{6,14},{7,15},{8,0},{9,1},... | collective-permute-start | bytes 1966088 | tf_op jit(solution)/shard_map/ppermute | solution.py:65
  47.1 20.3 %collective-permute-start.9 = (bf16[320,1024]{1,0:T(8,128)(2,1)}, bf16[320,1024]{1,0:T(8,128)(2,1)S(1)}, u32[]{:S(2)}, u32[]{:S(2)}) collective-permute-start(bf16[320,1024]{1,0:T(8,128)(2,1)} %get-tuple-element.341), channel_id=1, source_target_pairs={{0,2},{1,3},{2,0},{3,1},{4,6},{5,7},{6,4},{7,5},{8,10},{9,11},{10,... | collective-permute-start | bytes 1966088 | tf_op jit(solution)/shard_map/ppermute | solution.py:65
  48.3 19.1 %collective-permute-start.10 = (bf16[320,1024]{1,0:T(8,128)(2,1)}, bf16[320,1024]{1,0:T(8,128)(2,1)S(1)}, u32[]{:S(2)}, u32[]{:S(2)}) collective-permute-start(bf16[320,1024]{1,0:T(8,128)(2,1)} %get-tuple-element.342), channel_id=1, source_target_pairs={{0,4},{1,5},{2,6},{3,7},{4,0},{5,1},{6,2},{7,3},{8,12},{9,13},{10,... | collective-permute-start | bytes 1966088 | tf_op jit(solution)/shard_map/ppermute | solution.py:65
  72.0 19.9 %collective-permute-start.18 = (bf16[256,1024]{1,0:T(8,128)(2,1)S(1)}, bf16[256,1024]{1,0:T(8,128)(2,1)S(1)}, u32[]{:S(2)}, u32[]{:S(2)}) collective-permute-start(bf16[256,1024]{1,0:T(8,128)(2,1)S(1)} %copy-done.4), channel_id=1, source_target_pairs={{0,8},{1,9},{2,10},{3,11},{4,12},{5,13},{6,14},{7,15},{8,0},{9,1},... | collective-permute-start | bytes 1572872 | tf_op jit(solution)/shard_map/ppermute | solution.py:65
  72.9 19.0 %collective-permute-start.19 = (bf16[256,1024]{1,0:T(8,128)(2,1)S(1)}, bf16[256,1024]{1,0:T(8,128)(2,1)S(1)}, u32[]{:S(2)}, u32[]{:S(2)}) collective-permute-start(bf16[256,1024]{1,0:T(8,128)(2,1)S(1)} %copy-done.9), channel_id=1, source_target_pairs={{0,2},{1,3},{2,0},{3,1},{4,6},{5,7},{6,4},{7,5},{8,10},{9,11},{10,... | collective-permute-start | bytes 1572872 | tf_op jit(solution)/shard_map/ppermute | solution.py:65
  73.9 18.1 %collective-permute-start.20 = (bf16[256,1024]{1,0:T(8,128)(2,1)S(1)}, bf16[256,1024]{1,0:T(8,128)(2,1)S(1)}, u32[]{:S(2)}, u32[]{:S(2)}) collective-permute-start(bf16[256,1024]{1,0:T(8,128)(2,1)S(1)} %copy-done.10), channel_id=1, source_target_pairs={{0,4},{1,5},{2,6},{3,7},{4,0},{5,1},{6,2},{7,3},{8,12},{9,13},{10,... | collective-permute-start | bytes 1572872 | tf_op jit(solution)/shard_map/ppermute | solution.py:65
  77.0 14.4 %collective-permute-start.15 = (bf16[128,1024]{1,0:T(8,128)(2,1)}, bf16[128,1024]{1,0:T(8,128)(2,1)}, u32[]{:S(2)}, u32[]{:S(2)}) collective-permute-start(bf16[128,1024]{1,0:T(8,128)(2,1)} %select_bitcast_fusion.4), channel_id=1, source_target_pairs={{0,16},{1,17},{2,18},{3,19},{4,20},{5,21},{6,22},{7,23},{8,24},{9,... | collective-permute-start | bytes 786440 | tf_op jit(solution)/shard_map/ppermute | solution.py:65
  97.3 51.3 %collective-permute-start.21 = (bf16[640,1024]{1,0:T(8,128)(2,1)}, bf16[640,1024]{1,0:T(8,128)(2,1)S(1)}, u32[]{:S(2)}, u32[]{:S(2)}) collective-permute-start(bf16[640,1024]{1,0:T(8,128)(2,1)} %get-tuple-element.381), channel_id=1, source_target_pairs={{0,2},{1,3},{2,0},{3,1},{4,6},{5,7},{6,4},{7,5},{8,10},{9,11},{10,... | collective-permute-start | bytes 3932168 | tf_op jit(solution)/shard_map/ppermute | solution.py:65
  99.1 49.5 %collective-permute-start.22 = (bf16[640,1024]{1,0:T(8,128)(2,1)}, bf16[640,1024]{1,0:T(8,128)(2,1)S(1)}, u32[]{:S(2)}, u32[]{:S(2)}) collective-permute-start(bf16[640,1024]{1,0:T(8,128)(2,1)} %get-tuple-element.382), channel_id=1, source_target_pairs={{0,4},{1,5},{2,6},{3,7},{4,0},{5,1},{6,2},{7,3},{8,12},{9,13},{10,... | collective-permute-start | bytes 3932168 | tf_op jit(solution)/shard_map/ppermute | solution.py:65
  100.5 48.1 %collective-permute-start.23 = (bf16[512,1024]{1,0:T(8,128)(2,1)}, bf16[512,1024]{1,0:T(8,128)(2,1)}, u32[]{:S(2)}, u32[]{:S(2)}) collective-permute-start(bf16[512,1024]{1,0:T(8,128)(2,1)} %get-tuple-element.383), channel_id=1, source_target_pairs={{0,8},{1,9},{2,10},{3,11},{4,12},{5,13},{6,14},{7,15},{8,0},{9,1},... | collective-permute-start | bytes 3145736 | tf_op jit(solution)/shard_map/ppermute | solution.py:65
  101.0 35.1 %collective-permute-start.16 = (bf16[256,1024]{1,0:T(8,128)(2,1)S(1)}, bf16[256,1024]{1,0:T(8,128)(2,1)}, u32[]{:S(2)}, u32[]{:S(2)}) collective-permute-start(bf16[256,1024]{1,0:T(8,128)(2,1)S(1)} %copy-done.24), channel_id=1, source_target_pairs={{0,16},{1,17},{2,18},{3,19},{4,20},{5,21},{6,22},{7,23},{8,24},{9,... | collective-permute-start | bytes 1572872 | tf_op jit(solution)/shard_map/ppermute | solution.py:65
  102.7 45.9 %collective-permute-start.17 = (bf16[256,1024]{1,0:T(8,128)(2,1)}, bf16[256,1024]{1,0:T(8,128)(2,1)}, u32[]{:S(2)}, u32[]{:S(2)}) collective-permute-start(bf16[256,1024]{1,0:T(8,128)(2,1)} %get-tuple-element.364.v_own.refs_1_), channel_id=1, source_target_pairs={{0,16},{1,17},{2,18},{3,19},{4,20},{5,21},{6,22},{7,23},{8,24},{9,... | collective-permute-start | bytes 1572872 | tf_op jit(solution)/shard_map/ppermute | solution.py:65
  155.6 25.9 %collective-permute-start.27 = (bf16[512,1024]{1,0:T(8,128)(2,1)}, bf16[512,1024]{1,0:T(8,128)(2,1)}, u32[]{:S(2)}, u32[]{:S(2)}) collective-permute-start(bf16[512,1024]{1,0:T(8,128)(2,1)} %get-tuple-element.404), channel_id=1, source_target_pairs={{0,2},{1,3},{2,0},{3,1},{4,6},{5,7},{6,4},{7,5},{8,10},{9,11},{10,... | collective-permute-start | bytes 3145736 | tf_op jit(solution)/shard_map/ppermute | solution.py:65
  156.7 25.4 %collective-permute-start.28 = (bf16[512,1024]{1,0:T(8,128)(2,1)}, bf16[512,1024]{1,0:T(8,128)(2,1)S(1)}, u32[]{:S(2)}, u32[]{:S(2)}) collective-permute-start(bf16[512,1024]{1,0:T(8,128)(2,1)} %get-tuple-element.405), channel_id=1, source_target_pairs={{0,4},{1,5},{2,6},{3,7},{4,0},{5,1},{6,2},{7,3},{8,12},{9,13},{10,... | collective-permute-start | bytes 3145736 | tf_op jit(solution)/shard_map/ppermute | solution.py:65
  157.2 25.3 %collective-permute-start.29 = (bf16[512,1024]{1,0:T(8,128)(2,1)}, bf16[512,1024]{1,0:T(8,128)(2,1)}, u32[]{:S(2)}, u32[]{:S(2)}) collective-permute-start(bf16[512,1024]{1,0:T(8,128)(2,1)} %get-tuple-element.406), channel_id=1, source_target_pairs={{0,8},{1,9},{2,10},{3,11},{4,12},{5,13},{6,14},{7,15},{8,0},{9,1},... | collective-permute-start | bytes 3145736 | tf_op jit(solution)/shard_map/ppermute | solution.py:65
  182.4 31.0 %collective-permute-start.30 = (bf16[512,1024]{1,0:T(8,128)(2,1)}, bf16[512,1024]{1,0:T(8,128)(2,1)S(1)}, u32[]{:S(2)}, u32[]{:S(2)}) collective-permute-start(bf16[512,1024]{1,0:T(8,128)(2,1)} %get-tuple-element.419), channel_id=1, source_target_pairs={{0,8},{1,9},{2,10},{3,11},{4,12},{5,13},{6,14},{7,15},{8,0},{9,1},... | collective-permute-start | bytes 3145736 | tf_op jit(solution)/shard_map/ppermute | solution.py:65
  182.7 30.8 %collective-permute-start.31 = (bf16[512,1024]{1,0:T(8,128)(2,1)}, bf16[512,1024]{1,0:T(8,128)(2,1)}, u32[]{:S(2)}, u32[]{:S(2)}) collective-permute-start(bf16[512,1024]{1,0:T(8,128)(2,1)} %get-tuple-element.420), channel_id=1, source_target_pairs={{0,2},{1,3},{2,0},{3,1},{4,6},{5,7},{6,4},{7,5},{8,10},{9,11},{10,... | collective-permute-start | bytes 3145736 | tf_op jit(solution)/shard_map/ppermute | solution.py:65
  184.0 29.5 %collective-permute-start.32 = (bf16[512,1024]{1,0:T(8,128)(2,1)}, bf16[512,1024]{1,0:T(8,128)(2,1)S(1)}, u32[]{:S(2)}, u32[]{:S(2)}) collective-permute-start(bf16[512,1024]{1,0:T(8,128)(2,1)} %get-tuple-element.421), channel_id=1, source_target_pairs={{0,4},{1,5},{2,6},{3,7},{4,0},{5,1},{6,2},{7,3},{8,12},{9,13},{10,... | collective-permute-start | bytes 3145736 | tf_op jit(solution)/shard_map/ppermute | solution.py:65
  214.5 29.9 %collective-permute-start.33 = (bf16[512,1024]{1,0:T(8,128)(2,1)}, bf16[512,1024]{1,0:T(8,128)(2,1)S(1)}, u32[]{:S(2)}, u32[]{:S(2)}) collective-permute-start(bf16[512,1024]{1,0:T(8,128)(2,1)} %get-tuple-element.436), channel_id=1, source_target_pairs={{0,4},{1,5},{2,6},{3,7},{4,0},{5,1},{6,2},{7,3},{8,12},{9,13},{10,... | collective-permute-start | bytes 3145736 | tf_op jit(solution)/shard_map/ppermute | solution.py:65
  215.1 29.2 %collective-permute-start.34 = (bf16[512,1024]{1,0:T(8,128)(2,1)}, bf16[512,1024]{1,0:T(8,128)(2,1)S(1)}, u32[]{:S(2)}, u32[]{:S(2)}) collective-permute-start(bf16[512,1024]{1,0:T(8,128)(2,1)} %get-tuple-element.441), channel_id=1, source_target_pairs={{0,2},{1,3},{2,0},{3,1},{4,6},{5,7},{6,4},{7,5},{8,10},{9,11},{10,... | collective-permute-start | bytes 3145736 | tf_op jit(solution)/shard_map/ppermute | solution.py:65
  215.9 28.5 %collective-permute-start.35 = (bf16[512,1024]{1,0:T(8,128)(2,1)}, bf16[512,1024]{1,0:T(8,128)(2,1)}, u32[]{:S(2)}, u32[]{:S(2)}) collective-permute-start(bf16[512,1024]{1,0:T(8,128)(2,1)} %get-tuple-element.442), channel_id=1, source_target_pairs={{0,8},{1,9},{2,10},{3,11},{4,12},{5,13},{6,14},{7,15},{8,0},{9,1},... | collective-permute-start | bytes 3145736 | tf_op jit(solution)/shard_map/ppermute | solution.py:65
  231.7 15.7 %collective-permute-start.39 = (f32[256,1024]{1,0:T(8,128)}, f32[256,1024]{1,0:T(8,128)}, u32[]{:S(2)}, u32[]{:S(2)}) collective-permute-start(f32[256,1024]{1,0:T(8,128)} %get-tuple-element.453), channel_id=1, source_target_pairs={{0,1},{1,0},{2,3},{3,2},{4,5},{5,4},{6,7},{7,6},{8,9},{9,8},{10,11... | collective-permute-start | bytes 3145736 | tf_op jit(solution)/shard_map/ppermute | solution.py:65
  244.4 25.8 %collective-permute-start.36 = (bf16[512,1024]{1,0:T(8,128)(2,1)}, bf16[512,1024]{1,0:T(8,128)(2,1)S(1)}, u32[]{:S(2)}, u32[]{:S(2)}) collective-permute-start(bf16[512,1024]{1,0:T(8,128)(2,1)} %get-tuple-element.443), channel_id=1, source_target_pairs={{0,4},{1,5},{2,6},{3,7},{4,0},{5,1},{6,2},{7,3},{8,12},{9,13},{10,... | collective-permute-start | bytes 3145736 | tf_op jit(solution)/shard_map/ppermute | solution.py:65
  245.9 25.6 %collective-permute-start.37 = (bf16[512,1024]{1,0:T(8,128)(2,1)}, bf16[512,1024]{1,0:T(8,128)(2,1)}, u32[]{:S(2)}, u32[]{:S(2)}) collective-permute-start(bf16[512,1024]{1,0:T(8,128)(2,1)} %get-tuple-element.446), channel_id=1, source_target_pairs={{0,8},{1,9},{2,10},{3,11},{4,12},{5,13},{6,14},{7,15},{8,0},{9,1},... | collective-permute-start | bytes 3145736 | tf_op jit(solution)/shard_map/ppermute | solution.py:65
  246.2 25.3 %collective-permute-start.38 = (bf16[512,1024]{1,0:T(8,128)(2,1)}, bf16[512,1024]{1,0:T(8,128)(2,1)}, u32[]{:S(2)}, u32[]{:S(2)}) collective-permute-start(bf16[512,1024]{1,0:T(8,128)(2,1)} %get-tuple-element.449), channel_id=1, source_target_pairs={{0,2},{1,3},{2,0},{3,1},{4,6},{5,7},{6,4},{7,5},{8,10},{9,11},{10,... | collective-permute-start | bytes 3145736 | tf_op jit(solution)/shard_map/ppermute | solution.py:65
  284.8 51.8 %collective-permute-start.40 = (bf16[512,1024]{1,0:T(8,128)(2,1)}, bf16[512,1024]{1,0:T(8,128)(2,1)S(1)}, u32[]{:S(2)}, u32[]{:S(2)}) collective-permute-start(bf16[512,1024]{1,0:T(8,128)(2,1)} %get-tuple-element.467), channel_id=1, source_target_pairs={{0,2},{1,3},{2,0},{3,1},{4,6},{5,7},{6,4},{7,5},{8,10},{9,11},{10,... | collective-permute-start | bytes 3145736 | tf_op jit(solution)/shard_map/ppermute | solution.py:65
  286.0 50.6 %collective-permute-start.41 = (bf16[512,1024]{1,0:T(8,128)(2,1)}, bf16[512,1024]{1,0:T(8,128)(2,1)S(1)}, u32[]{:S(2)}, u32[]{:S(2)}) collective-permute-start(bf16[512,1024]{1,0:T(8,128)(2,1)} %get-tuple-element.468), channel_id=1, source_target_pairs={{0,4},{1,5},{2,6},{3,7},{4,0},{5,1},{6,2},{7,3},{8,12},{9,13},{10,... | collective-permute-start | bytes 3145736 | tf_op jit(solution)/shard_map/ppermute | solution.py:65
  286.7 49.9 %collective-permute-start.42 = (bf16[512,1024]{1,0:T(8,128)(2,1)}, bf16[512,1024]{1,0:T(8,128)(2,1)}, u32[]{:S(2)}, u32[]{:S(2)}) collective-permute-start(bf16[512,1024]{1,0:T(8,128)(2,1)} %get-tuple-element.469), channel_id=1, source_target_pairs={{0,8},{1,9},{2,10},{3,11},{4,12},{5,13},{6,14},{7,15},{8,0},{9,1},... | collective-permute-start | bytes 3145736 | tf_op jit(solution)/shard_map/ppermute | solution.py:65
  288.2 35.2 %collective-permute-start.45 = (bf16[256,1024]{1,0:T(8,128)(2,1)}, bf16[256,1024]{1,0:T(8,128)(2,1)S(1)}, u32[]{:S(2)}, u32[]{:S(2)}) collective-permute-start(bf16[256,1024]{1,0:T(8,128)(2,1)} %get-tuple-element.483), channel_id=1, source_target_pairs={{0,16},{1,17},{2,18},{3,19},{4,20},{5,21},{6,22},{7,23},{8,24},{9,... | collective-permute-start | bytes 1572872 | tf_op jit(solution)/shard_map/ppermute | solution.py:65
  289.4 47.2 %collective-permute-start.44 = (bf16[256,1024]{1,0:T(8,128)(2,1)}, bf16[256,1024]{1,0:T(8,128)(2,1)}, u32[]{:S(2)}, u32[]{:S(2)}) collective-permute-start(bf16[256,1024]{1,0:T(8,128)(2,1)} %get-tuple-element.454), channel_id=1, source_target_pairs={{0,16},{1,17},{2,18},{3,19},{4,20},{5,21},{6,22},{7,23},{8,24},{9,... | collective-permute-start | bytes 1572872 | tf_op jit(solution)/shard_map/ppermute | solution.py:65
  353.6 22.5 %collective-permute-start.48 = (bf16[1536,1024]{1,0:T(8,128)(2,1)}, bf16[1536,1024]{1,0:T(8,128)(2,1)}, u32[]{:S(2)}, u32[]{:S(2)}) collective-permute-start(bf16[1536,1024]{1,0:T(8,128)(2,1)} %get-tuple-element.511), channel_id=1, source_target_pairs={{0,1},{1,0},{2,3},{3,2},{4,5},{5,4},{6,7},{7,6},{8,9},{9,8},{10,11... | collective-permute-start | bytes 9437192 | tf_op jit(solution)/shard_map/ppermute | solution.py:65
  354.2 27.3 %collective-permute-start.50 = (bf16[384,1024]{1,0:T(8,128)(2,1)}, bf16[384,1024]{1,0:T(8,128)(2,1)S(1)}, u32[]{:S(2)}, u32[]{:S(2)}) collective-permute-start(bf16[384,1024]{1,0:T(8,128)(2,1)} %get-tuple-element.495), channel_id=1, source_target_pairs={{0,2},{1,3},{2,0},{3,1},{4,6},{5,7},{6,4},{7,5},{8,10},{9,11},{10,... | collective-permute-start | bytes 2359304 | tf_op jit(solution)/shard_map/ppermute | solution.py:65
  355.2 26.3 %collective-permute-start.49 = (bf16[384,1024]{1,0:T(8,128)(2,1)}, bf16[384,1024]{1,0:T(8,128)(2,1)S(1)}, u32[]{:S(2)}, u32[]{:S(2)}) collective-permute-start(bf16[384,1024]{1,0:T(8,128)(2,1)} %get-tuple-element.496), channel_id=1, source_target_pairs={{0,4},{1,5},{2,6},{3,7},{4,0},{5,1},{6,2},{7,3},{8,12},{9,13},{10,... | collective-permute-start | bytes 2359304 | tf_op jit(solution)/shard_map/ppermute | solution.py:65
  360.2 15.0 %collective-permute-start.47 = (bf16[16,8,1024]{2,1,0:T(8,128)(2,1)S(1)}, bf16[16,8,1024]{2,1,0:T(8,128)(2,1)S(1)}, u32[]{:S(2)}, u32[]{:S(2)}) collective-permute-start(bf16[16,8,1024]{2,1,0:T(8,128)(2,1)S(1)} %select_bitcast_fusion.3), channel_id=1, source_target_pairs={{0,16},{1,17},{2,18},{3,19},{4,20},{5,21},{6,22},{7,23},{8,24},{9,... | collective-permute-start | bytes 786440 | tf_op jit(solution)/shard_map/ppermute | solution.py:65
  360.6 20.8 %collective-permute-start.51 = (bf16[256,1024]{1,0:T(8,128)(2,1)}, bf16[256,1024]{1,0:T(8,128)(2,1)S(1)}, u32[]{:S(2)}, u32[]{:S(2)}) collective-permute-start(bf16[256,1024]{1,0:T(8,128)(2,1)} %get-tuple-element.497), channel_id=1, source_target_pairs={{0,8},{1,9},{2,10},{3,11},{4,12},{5,13},{6,14},{7,15},{8,0},{9,1},... | collective-permute-start | bytes 1572872 | tf_op jit(solution)/shard_map/ppermute | solution.py:65
  389.5 17.0 %collective-permute-start.52 = (bf16[320,1024]{1,0:T(8,128)(2,1)}, bf16[320,1024]{1,0:T(8,128)(2,1)}, u32[]{:S(2)}, u32[]{:S(2)}) collective-permute-start(bf16[320,1024]{1,0:T(8,128)(2,1)} %get-tuple-element.535), channel_id=1, source_target_pairs={{0,2},{1,3},{2,0},{3,1},{4,6},{5,7},{6,4},{7,5},{8,10},{9,11},{10,... | collective-permute-start | bytes 1966088 | tf_op jit(solution)/shard_map/ppermute | solution.py:65
  390.3 16.7 %collective-permute-start.54 = (bf16[320,1024]{1,0:T(8,128)(2,1)}, bf16[320,1024]{1,0:T(8,128)(2,1)}, u32[]{:S(2)}, u32[]{:S(2)}) collective-permute-start(bf16[320,1024]{1,0:T(8,128)(2,1)} %get-tuple-element.537), channel_id=1, source_target_pairs={{0,8},{1,9},{2,10},{3,11},{4,12},{5,13},{6,14},{7,15},{8,0},{9,1},... | collective-permute-start | bytes 1966088 | tf_op jit(solution)/shard_map/ppermute | solution.py:65
  391.6 22.9 %collective-permute-start.57 = (f32[256,1024]{1,0:T(8,128)S(1)}, f32[256,1024]{1,0:T(8,128)S(1)}, u32[]{:S(2)}, u32[]{:S(2)}) collective-permute-start(f32[256,1024]{1,0:T(8,128)S(1)} %pad_maximum_fusion), channel_id=1, source_target_pairs={{0,1},{1,0},{2,3},{3,2},{4,5},{5,4},{6,7},{7,6},{8,9},{9,8},{10,11... | collective-permute-start | bytes 3145736 | tf_op jit(solution)/shard_map/ppermute | solution.py:65
  391.7 14.4 %collective-permute-start.53 = (bf16[256,1024]{1,0:T(8,128)(2,1)S(1)}, bf16[256,1024]{1,0:T(8,128)(2,1)}, u32[]{:S(2)}, u32[]{:S(2)}) collective-permute-start(bf16[256,1024]{1,0:T(8,128)(2,1)S(1)} %copy-done.65), channel_id=1, source_target_pairs={{0,4},{1,5},{2,6},{3,7},{4,0},{5,1},{6,2},{7,3},{8,12},{9,13},{10,... | collective-permute-start | bytes 1572872 | tf_op jit(solution)/shard_map/ppermute | solution.py:65
  408.7 21.2 %collective-permute-start.55 = (bf16[16,8,1024]{2,1,0:T(8,128)(2,1)}, bf16[16,8,1024]{2,1,0:T(8,128)(2,1)}, u32[]{:S(2)}, u32[]{:S(2)}) collective-permute-start(bf16[16,8,1024]{2,1,0:T(8,128)(2,1)} %select_bitcast_fusion.2), channel_id=1, source_target_pairs={{0,16},{1,17},{2,18},{3,19},{4,20},{5,21},{6,22},{7,23},{8,24},{9,... | collective-permute-start | bytes 786440 | tf_op jit(solution)/shard_map/ppermute | solution.py:65
  412.5 32.8 %collective-permute-start.56 = (bf16[128,1024]{1,0:T(8,128)(2,1)}, bf16[128,1024]{1,0:T(8,128)(2,1)}, u32[]{:S(2)}, u32[]{:S(2)}) collective-permute-start(bf16[128,1024]{1,0:T(8,128)(2,1)} %convert_element_type.65), channel_id=1, source_target_pairs={{0,16},{1,17},{2,18},{3,19},{4,20},{5,21},{6,22},{7,23},{8,24},{9,... | collective-permute-start | bytes 786440 | tf_op jit(solution)/shard_map/ppermute | solution.py:65
  418.2 17.1 %collective-permute-start.60 = (bf16[128,1024]{1,0:T(8,128)(2,1)}, bf16[128,1024]{1,0:T(8,128)(2,1)}, u32[]{:S(2)}, u32[]{:S(2)}) collective-permute-start(bf16[128,1024]{1,0:T(8,128)(2,1)} %get-tuple-element.560), channel_id=1, source_target_pairs={{0,2},{1,3},{2,0},{3,1},{4,6},{5,7},{6,4},{7,5},{8,10},{9,11},{10,... | collective-permute-start | bytes 786440 | tf_op jit(solution)/shard_map/ppermute | solution.py:65
  419.6 15.7 %collective-permute-start.58 = (bf16[160,1024]{1,0:T(8,128)(2,1)}, bf16[160,1024]{1,0:T(8,128)(2,1)S(1)}, u32[]{:S(2)}, u32[]{:S(2)}) collective-permute-start(bf16[160,1024]{1,0:T(8,128)(2,1)} %get-tuple-element.556), channel_id=1, source_target_pairs={{0,4},{1,5},{2,6},{3,7},{4,0},{5,1},{6,2},{7,3},{8,12},{9,13},{10,... | collective-permute-start | bytes 983048 | tf_op jit(solution)/shard_map/ppermute | solution.py:65
  420.9 17.5 %collective-permute-start.59 = (bf16[160,1024]{1,0:T(8,128)(2,1)}, bf16[160,1024]{1,0:T(8,128)(2,1)S(1)}, u32[]{:S(2)}, u32[]{:S(2)}) collective-permute-start(bf16[160,1024]{1,0:T(8,128)(2,1)} %get-tuple-element.558), channel_id=1, source_target_pairs={{0,8},{1,9},{2,10},{3,11},{4,12},{5,13},{6,14},{7,15},{8,0},{9,1},... | collective-permute-start | bytes 983048 | tf_op jit(solution)/shard_map/ppermute | solution.py:65
  431.7 14.6 %all-to-all-start = ((f32[32,1,64]{2,1,0:T(1,128)}), f32[32,1,64]{2,1,0:T(1,128)S(1)}, u32[]{:S(2)}, u32[]{:S(2)}) async-start(f32[32,1,64]{2,1,0:T(1,128)} %bitcast.16), calls=%async_computation | async-start | bytes 32768 | tf_op jit(solution)/shard_map/all_to_all | solution.py:1661
  (85 other events, 641.0 us)

commit v3 on v2

--- a/solution.py
+++ b/solution.py
@@ -419,7 +419,7 @@
     def add(self, a, a_row, b, b_row, target, target_row, count):
         self.work.append((self.source(a), a_row, self.source(b), b_row, target, target_row, count))
 
-    def run(self, meta, name, *earlier, squares=False):
+    def run(self, meta, name, *earlier, squares=False, norm=(), waits=()):
         inputs = after(self.inputs, *earlier) if earlier else self.inputs
         adds = [w for w in self.work if w[2] is not None]
         rows = sum(w[6] for w in adds)
@@ -431,25 +431,32 @@
             scratch += [pltpu.VMEM((rows, self.width), F32)]
         shapes = list(self.outputs)
         if squares:
-            shapes.append(jax.ShapeDtypeStruct((8, self.width), F32))
+            shape = (norm[0], 128) if norm else (8, self.width)
+            shapes.append(jax.ShapeDtypeStruct(shape, F32))
+        more = list(norm[1:])
+        scratch += [pltpu.VMEM((8, self.width), F32)] if squares else []
         return pl.pallas_call(
-            functools.partial(jobs_kernel, self.work, len(inputs), self.outputs, squares),
-            in_specs=[SM] + [HB] * len(inputs),
+            functools.partial(
+                jobs_kernel, self.work, len(inputs), self.outputs, squares, len(more), len(waits)
+            ),
+            in_specs=[SM] + [HB] * len(inputs) + [VM] * len(more) + [HB] * len(waits),
             out_specs=[HB] * len(self.outputs) + ([VM] if squares else []),
             out_shape=shapes,
             scratch_shapes=scratch,
             compiler_params=pltpu.CompilerParams(vmem_limit_bytes=60 * MIB),
             cost_estimate=SMALL,
             name=name,
-        )(meta, *inputs)
-
-
-def jobs_kernel(work, count, outputs, squares, meta, *refs):
-    sources, targets = refs[:count], refs[count : count + len(outputs)]
-    refs = refs[count + len(outputs) :]
+        )(meta, *inputs, *more, *waits)
+
+
+def jobs_kernel(work, count, outputs, squares, more, waits, meta, *refs):
+    sources, norm = refs[:count], refs[count : count + more]
+    refs = refs[count + more + waits :]
+    targets = refs[: len(outputs)]
+    refs = refs[len(outputs) :]
     if squares:
-        square_ref = refs[0]
-        refs = refs[1:]
+        square_out, square_ref = refs[0], refs[-1]
+        refs = refs[1:-1]
     sem = refs[0]
     core = meta[1]
 
@@ -507,6 +514,14 @@
         )
         copy.start()
         leaving.append(copy)
+    if squares and not norm:
+        square_out[...] = square_ref[...]
+    if norm:
+        total = jnp.sum(square_ref[...])
+        for i, ref in enumerate(norm):
+            value = ref[...]
+            total = total + jnp.sum(value if i == 0 else value * value)
+        square_out[...] = jnp.full(square_out.shape, total, F32)
     finish(leaving)
 
 
@@ -629,7 +644,7 @@
         self.keep, self.send, self.rows, self.count, self.final = keep, send, rows, 4, final
 
 
-def reduce_round(cube, meta, width, name, work, *earlier, squares=False, gate=()):
+def reduce_round(cube, meta, width, name, work, *earlier, squares=False, gate=(), norm=(), waits=()):
     jobs = Jobs(width)
     filled = []
     direct = all(step == 0 for _, step in work) and len(work) == 1
@@ -675,7 +690,7 @@
                 for chain in chains:
                     if chain is not None:
                         chain.final(jobs, chain.got, chain.keep, chain.rows)
-        out = jobs.run(meta, name, *earlier, squares=squares)
+        out = jobs.run(meta, name, *earlier, squares=squares, norm=norm, waits=waits)
         for own, chain in kept.items():
             chain.keep = (out[own], 0)
         payloads = [out[target] for target, _ in layout]
@@ -971,11 +986,12 @@
 
 
 PAIR_COPIES = 128
+PAD = 16
 
 
 def joint_kernel(count, tables, meta, x, *refs):
     pieces = refs[:count]
-    first, query, key, value_out, gains, w, gain_rows, sem, gain_sem = refs[count:]
+    first, query, pair, gains, w, gain_rows, sem, gain_sem = refs[count:]
     width = x.shape[1]
     coming = load_joint(tables, pieces, w, meta, sem)
     shard = width // (2 * CHIPS)
@@ -997,11 +1013,13 @@
     first[...] = (value * inverse * whole[0:1]).astype(BF)
     finish(coming)
     tiles = width // TILE
-    for part, out in enumerate((query, key, value_out)):
-
-        def step(t, _, part=part, out=out):
+    rows = x.shape[0]
+    pair[2 * rows :] = jnp.zeros((PAD, width), BF)
+    for part, (out, low) in enumerate(((query, 0), (pair, 0), (pair, rows))):
+
+        def step(t, _, part=part, out=out, low=low):
             weight = w[:, aligned(t + part * tiles, TILE)]
-            out[:, aligned(t, TILE)] = dot(first[...], weight).astype(BF)
+            out[low : low + rows, aligned(t, TILE)] = dot(first[...], weight).astype(BF)
             return 0
 
         lax.fori_loop(0, tiles, step, 0)
@@ -1014,12 +1032,11 @@
     return pl.pallas_call(
         functools.partial(joint_kernel, len(arrays), tables),
         in_specs=[SM, VM] + [HB] * len(arrays),
-        out_specs=[VM] * 5,
+        out_specs=[VM] * 4,
         out_shape=[
             low,
             low,
-            low,
-            low,
+            jax.ShapeDtypeStruct((2 * rows + PAD, width), BF),
             jax.ShapeDtypeStruct((8, width), F32),
         ],
         scratch_shapes=[
@@ -1061,7 +1078,7 @@
     return exp_scores / jnp.sum(exp_scores, axis=-1, keepdims=True)
 
 
-def context_kernel(run, head_dim, count, tables, meta, query, k_own, v_own, k_other, v_other, x, live, gains, *refs):
+def context_kernel(run, head_dim, count, tables, meta, query, own, other, x, live, gains, *refs):
     pieces = refs[:count]
     ctx, h_out, n2, wo, bias, sem = refs[count:]
     rows, width = x.shape
@@ -1075,9 +1092,10 @@
         cols = aligned(p, lanes)
         for chunk in range(rows // CHUNK):
             r = slice(chunk * CHUNK, (chunk + 1) * CHUNK)
+            r_v = slice(rows + chunk * CHUNK, rows + (chunk + 1) * CHUNK)
             q_st = stacked(query[r, cols], left)
-            k_all = jnp.concatenate([k_own[r, cols], k_other[r, cols]], axis=0)
-            v_all = jnp.concatenate([v_own[r, cols], v_other[r, cols]], axis=0)
+            k_all = jnp.concatenate([own[r, cols], other[r, cols]], axis=0)
+            v_all = jnp.concatenate([own[r_v, cols], other[r_v, cols]], axis=0)
             prob = probabilities(q_st, k_all, bias, scale)
             out = dot(prob.astype(BF), v_all)
             ctx[r, cols] = jnp.where(left, out[:CHUNK], out[CHUNK:]).astype(BF)
@@ -1098,14 +1116,14 @@
 
 
 def context_forward(
-    run, meta, query, k_own, v_own, k_other, v_other, x, live, gains, chains
+    run, meta, query, own, other, x, live, gains, chains
 ):
     rows, width = x.shape
     arrays, tables = operands(*chains)
     low = jax.ShapeDtypeStruct((rows, width), BF)
     return pl.pallas_call(
         functools.partial(context_kernel, run, width // HEADS, len(arrays), tables),
-        in_specs=[SM] + [VM] * 8 + [HB] * len(arrays),
+        in_specs=[SM] + [VM] * 6 + [HB] * len(arrays),
         out_specs=[VM] * 3,
         out_shape=[low, jax.ShapeDtypeStruct((rows, width), F32), low],
         scratch_shapes=[
@@ -1116,7 +1134,7 @@
         compiler_params=pltpu.CompilerParams(vmem_limit_bytes=60 * MIB),
         cost_estimate=SMALL,
         name="context_forward",
-    )(meta, query, k_own, v_own, k_other, v_other, x, live, gains, *arrays)
+    )(meta, query, own, other, x, live, gains, *arrays)
 
 
 def norm_back(value, gain, grad):
@@ -1130,12 +1148,13 @@
 def context_back_kernel(
     run, head_dim, count, tables, meta, dn_own, dn_got, h, cot, live, gains, query, *refs
 ):
-    k_own, v_own, k_other, v_other = refs[:4]
-    pieces = refs[4 : 4 + count]
-    dh, dg2, da, dq, dkv, k_give, v_give, wo, bias, dctx, sem = refs[4 + count :]
+    own, other = refs[:2]
+    pieces = refs[2 : 2 + count]
+    dh, dg2, da, dq, dkv, give, wo, bias, dctx, sem = refs[2 + count :]
     rows, width = h.shape
     coming = load_output(tables, pieces, wo, meta, sem)
     bias_into(bias, run, meta[2] == 1)
+    give[2 * rows :] = jnp.zeros((PAD, width), BF)
     grad_in, dg2[...] = norm_back(h[...], gains[1:2, :], dn_own[...] + dn_got[...])
     grad = cot[...].astype(F32) + grad_in
     dh[...] = grad
@@ -1158,10 +1177,11 @@
         v_cols = aligned(p + pairs, lanes)
         for chunk in range(rows // CHUNK):
             r = slice(chunk * CHUNK, (chunk + 1) * CHUNK)
+            r_v = slice(rows + chunk * CHUNK, rows + (chunk + 1) * CHUNK)
             q_st = stacked(query[r, cols], left)
             g_st = stacked(dctx[r, cols], left)
-            k_all = jnp.concatenate([k_own[r, cols], k_other[r, cols]], axis=0)
-            v_all = jnp.concatenate([v_own[r, cols], v_other[r, cols]], axis=0)
+            k_all = jnp.concatenate([own[r, cols], other[r, cols]], axis=0)
+            v_all = jnp.concatenate([own[r_v, cols], other[r_v, cols]], axis=0)
             prob = probabilities(q_st, k_all, bias, scale)
             d_prob = dot_nt(g_st, v_all)
             d_score = prob * (d_prob - jnp.sum(d_prob * prob, axis=-1, keepdims=True))
@@ -1172,31 +1192,30 @@
             dq[r, cols] = jnp.where(left, d_query[:CHUNK], d_query[CHUNK:]).astype(BF)
             dkv[r, cols] = d_key[:CHUNK]
             dkv[r, v_cols] = d_value[:CHUNK]
-            k_give[r, cols] = d_key[CHUNK:].astype(BF)
-            v_give[r, cols] = d_value[CHUNK:].astype(BF)
+            give[r, cols] = d_key[CHUNK:].astype(BF)
+            give[r_v, cols] = d_value[CHUNK:].astype(BF)
         return 0
 
     lax.fori_loop(0, pairs, pair, 0)
 
 
 def context_back(
-    run, meta, dn_own, dn_got, h, cot, live, gains, query, k_own, v_own, k_other, v_other, chains
+    run, meta, dn_own, dn_got, h, cot, live, gains, query, own, other, chains
 ):
     rows, width = h.shape
     arrays, tables = operands(*chains)
     low = jax.ShapeDtypeStruct((rows, width), BF)
     return pl.pallas_call(
         functools.partial(context_back_kernel, run, width // HEADS, len(arrays), tables),
-        in_specs=[SM] + [VM] * 11 + [HB] * len(arrays),
-        out_specs=[VM] * 7,
+        in_specs=[SM] + [VM] * 9 + [HB] * len(arrays),
+        out_specs=[VM] * 6,
         out_shape=[
             jax.ShapeDtypeStruct((rows, width), F32),
             jax.ShapeDtypeStruct((1, width), F32),
             low,
             low,
             jax.ShapeDtypeStruct((rows, 2 * width), F32),
-            low,
-            low,
+            jax.ShapeDtypeStruct((2 * rows + PAD, width), BF),
         ],
         scratch_shapes=[
             pltpu.VMEM((width, width), BF),
@@ -1216,10 +1235,8 @@
         live,
         gains,
         query,
-        k_own,
-        v_own,
-        k_other,
-        v_other,
+        own,
+        other,
         *arrays,
     )
 
@@ -1285,11 +1302,13 @@
     )(meta, context, grad)
 
 
-def joint_grad_kernel(meta, first, dq, dkv_own, dk_got, dv_got, give, keep, dkv, dw, sem):
+def joint_grad_kernel(meta, first, dq, dkv_own, dkv_got, give, keep, dkv, dw, sem):
     width = first.shape[1]
-    for part, got in enumerate((dk_got, dv_got)):
+    rows = first.shape[0]
+    for part in range(2):
         cols = slice(part * width, (part + 1) * width)
-        more = jnp.where(meta[2] == 1, 0.0, got[...].astype(F32))
+        got = dkv_got[part * rows : (part + 1) * rows, :]
+        more = jnp.where(meta[2] == 1, 0.0, got.astype(F32))
         dkv[:, cols] = (dkv_own[:, cols] + more).astype(BF)
     rights = (lambda: dq[...], lambda: dkv[:, :width], lambda: dkv[:, width:])
     shard = width // (2 * CHIPS)
@@ -1308,12 +1327,12 @@
     finish(leaving)
 
 
-def joint_grad(meta, first, dq, dkv_own, dk_got, dv_got):
+def joint_grad(meta, first, dq, dkv_own, dkv_got):
     rows, width = first.shape
     part = jax.ShapeDtypeStruct((3 * width // 2, width), BF)
     return pl.pallas_call(
         joint_grad_kernel,
-        in_specs=[SM] + [VM] * 5,
+        in_specs=[SM] + [VM] * 4,
         out_specs=[HB, HB, VM],
         out_shape=[part, part, jax.ShapeDtypeStruct((rows, 2 * width), BF)],
         scratch_shapes=[
@@ -1323,7 +1342,7 @@
         compiler_params=pltpu.CompilerParams(vmem_limit_bytes=60 * MIB),
         cost_estimate=SMALL,
         name="joint_grad",
-    )(meta, first, dq, dkv_own, dk_got, dv_got)
+    )(meta, first, dq, dkv_own, dkv_got)
 
 
 def input_back_kernel(count, tables, meta, dq, dkv, dh, x, gains, *refs):
@@ -1364,38 +1383,84 @@
     )(meta, dq, dkv, dh, x, gains, *arrays)
 
 
-def adam_expand_kernel(meta, factor, w, m, v, own_a, own_b, got_a, got_b, w_out, m_out, v_out):
+def adam_rows(k, w, m, v, grad, outs, where, rate, decay):
+    new = adam_step(w[where], k * grad, m[where], v[where], rate, decay)
+    for out, value in zip(outs, new):
+        out[where] = value
+
+
+def adam_kernel(meta, squares, *refs):
+    (ew, em, ev, own_a, own_b, got_a, got_b, jw, jm, jv, jg, ow, om, ov, og_a, og_b) = refs[:16]
+    (sw, sm, sv, sg_mine, sg_got) = refs[16:21]
+    e_out, j_out, o_out, s_out = refs[21:24], refs[24:27], refs[27:30], refs[30:33]
     core, group = meta[1], meta[2]
-    block = w.shape[1] // (2 * CHIPS)
-    k = factor[0]
-    turn = (pl.program_id(0) % 2) ^ (1 - group)
-    for q in range(2 * CHIPS):
-        cols = slice(q * block, (q + 1) * block)
+    step = pl.program_id(0)
+    total = jnp.sum(squares[...], axis=0, keepdims=True)[0:1, 0:1]
+    k = CLIP_LIMIT / jnp.maximum(jnp.sqrt(total), CLIP_LIMIT)
+    block = 128
+    turn = ((step // 2) % 2) ^ (1 - group)
+    for q in range(ew.shape[1] // block):
+        cols = (slice(None), slice(q * block, (q + 1) * block))
         near = slice((q // 2) * block, (q // 2 + 1) * block)
         own = jnp.where(turn == 0, own_a[:, near], own_b[:, near])
         got = jnp.where(turn == 0, got_a[:, near], got_b[:, near])
         grad = jnp.where(core == q % 2, own, got)
-        w_new, m_new, v_new = adam_step(
-            w[:, cols], k * grad, m[:, cols], v[:, cols], MATRIX_RATE, MATRIX_DECAY
-        )
-        w_out[:, cols] = w_new
-        m_out[:, cols] = m_new
-        v_out[:, cols] = v_new
-
-
-def adam_expand(meta, factor, w, m, v, own, got):
-    rows, width = w.shape
-    wide = pl.BlockSpec((rows, width // 4), lambda i: (0, i))
-    grad = pl.BlockSpec((rows, width // 8), lambda i: (i // 2, 0))
+        adam_rows(k, ew, em, ev, grad, e_out, cols, MATRIX_RATE, MATRIX_DECAY)
+    everything = (slice(None), slice(None))
+
+    @pl.when(step < 3)
+    def _():
+        adam_rows(k, jw, jm, jv, jg[0], j_out, everything, MATRIX_RATE, MATRIX_DECAY)
+
+    @pl.when((step >= 3) & (step < 5))
+    def _():
+        grad = jnp.where(step == 3, og_a[...], og_b[...])
+        adam_rows(k, ow, om, ov, grad, o_out, everything, MATRIX_RATE, MATRIX_DECAY)
+
+    @pl.when(step >= 4)
+    def _():
+        mine = ((step - 4) // 2) == group
+        grad = jnp.where(mine, sg_mine[...], sg_got[...].astype(F32))
+        adam_rows(k, sw, sm, sv, grad, s_out, (0,), MATRIX_RATE, MATRIX_DECAY)
+
+
+def adam_matrices(meta, squares, expand, joint, output, shrink):
+    rows, wide = expand[0].shape
+    width = wide // 8
+    shrink_rows = shrink[0].shape[1] // 2
+
+    def half(i):
+        return (i // 4, i % 2)
+
+    e_spec = pl.BlockSpec((rows, width), lambda i: (0, i))
+    e_grad = pl.BlockSpec((rows, width // 2), half)
+    j_spec = pl.BlockSpec((rows, width), lambda i: (0, jnp.minimum(i, 2)))
+    j_grad = pl.BlockSpec((1, rows, width), lambda i: (jnp.minimum(i, 2), 0, 0))
+    o_spec = pl.BlockSpec((rows // 2, width), lambda i: (jnp.clip(i - 3, 0, 1), 0))
+    o_grad = pl.BlockSpec((rows // 2, width), lambda i: (0, 0))
+    s_spec = pl.BlockSpec(
+        (1, shrink_rows, width), lambda i: (jnp.maximum(i - 4, 0) // 2, jnp.maximum(i - 4, 0) % 2, 0)
+    )
+    s_grad = pl.BlockSpec((shrink_rows, width), lambda i: (jnp.maximum(i - 4, 0) % 2, 0))
+    whole = pl.BlockSpec(squares.shape, lambda i: (0, 0))
+    shapes = [jax.ShapeDtypeStruct(p[0].shape, F32) for p in (expand, joint, output, shrink)]
     return pl.pallas_call(
-        adam_expand_kernel,
-        grid=(4,),
-        in_specs=[SM, SM, wide, wide, wide] + [grad] * 4,
-        out_specs=[wide, wide, wide],
-        out_shape=[jax.ShapeDtypeStruct(w.shape, F32)] * 3,
+        adam_kernel,
+        grid=(8,),
+        in_specs=[SM, whole]
+        + [e_spec] * 3
+        + [e_grad] * 4
+        + [j_spec] * 3
+        + [j_grad]
+        + [o_spec] * 3
+        + [o_grad] * 2
+        + [s_spec] * 3
+        + [s_grad] * 2,
+        out_specs=[e_spec] * 3 + [j_spec] * 3 + [o_spec] * 3 + [s_spec] * 3,
+        out_shape=[s for s in shapes for _ in range(3)],
         compiler_params=pltpu.CompilerParams(vmem_limit_bytes=60 * MIB),
-        name="adam_expand",
-    )(meta, factor, w, m, v, *own, *got)
+        name="adam_matrices",
+    )(meta, squares, *expand, *joint, *output, *shrink)
 
 
 def local_cube(
@@ -1500,7 +1565,8 @@
 
     cot_own, cot_give = parted(cotangent)
     cot_got = cube.swap(after(cot_give, three.packed, shrink_other), cube.top)
-    late = begin("pack_late").core(joint, joint_other, 4, 8).run(three.got, three.core_got, units)
+    late = begin("pack_late").core(joint, joint_other, 4, 8)
+    late = late.run(three.got, three.core_got, units)
     first_units = after(units, three.got, three.core_got)
     got_four = [cube.swap(unit, 1 + axis) for axis, unit in enumerate(first_units)]
     for k in range(3):
@@ -1510,24 +1576,22 @@
     position = group * run + jnp.arange(run)
     live = (position[None, :] < depth_all[:, None]).astype(F32).reshape(rows, 1)
 
-    first, query, key, value, gains_all = joint_forward(meta, x_rows, joint + joint_other)
-    five = begin("pack_five").gather(part_a, 1).gather(part_b, 1).gather(output, 2)
-    five = five.run(got_four, key, cot_got)
-    key_other = cube.swap(after(key, cot_got), cube.top)
-    value_other = cube.swap(after(value, cot_got), cube.top)
+    first, query, key_value, gains_all = joint_forward(meta, x_rows, joint + joint_other)
+    key_value_other = cube.swap(after(key_value, cot_got), cube.top)
+    five = begin("pack_five").gather(part_a, 1).gather(part_b, 1).run(got_four, key_value, cot_got)
+    last = begin("pack_output").gather(output, 2).run(five.packed)
     seven = begin("pack_seven").gather(part_a, 2).core(output, output_other, 0, 8)
-    seven = seven.run(five.got, key_other, value_other)
-    cot_live = (halves(cot_own, after(cot_got, key)).astype(F32) * live).astype(BF)
-    cot_other = cube.swap(after(cot_live, five.got, key_other), 0)
+    seven = seven.run(five.got, key_value_other, last.got)
+    cot_live = (halves(cot_own, after(cot_got, key_value)).astype(F32) * live).astype(BF)
+    cot_other = cube.swap(after(cot_live, five.got, key_value_other), 0)
+
     output_chains = output[1:] + output_other[1:]
     context, middle, second = context_forward(
         run,
         meta,
         query,
-        key,
-        value,
-        key_other,
-        value_other,
+        key_value,
+        key_value_other,
         x_rows,
         live,
         gains_all,
@@ -1571,132 +1635,168 @@
         block = grads[0].shape[0] // 4
         return [Sums((grads[2 * k], 0), (grads[2 * k + 1], 0), block, finals[k]) for k in range(3)]
 
-    def turn(name, work, *earlier, squares=False, gate=()):
-        return reduce_round(cube, meta, width, name, work, *earlier, squares=squares, gate=gate)
-
-    def core_sum(name, give, keep, chains, *earlier):
-        got = cube.swap(after(give, *earlier) if earlier else give, 0)
+    def turn(name, work, *earlier, **options):
+        return reduce_round(cube, meta, width, name, work, *earlier, **options)
+
+    def core_sums(name, tensors, *waits):
         jobs = Jobs(width)
-        row, sums = 0, [None] * 3
-        targets = []
-        for k, count in chains:
-            send, own = jobs.output(4 * count), jobs.output(4 * count)
-            jobs.add(got, row + 4 * count, keep, row + 4 * count, send, 0, 4 * count)
-            jobs.add(got, row, keep, row, own, 0, 4 * count)
-            targets.append((k, count, own, send))
-            row += CHIPS * count
-        out = jobs.run(meta, name)
-        for k, count, own, send in targets:
-            sums[k] = Sums((out[own], 0), (out[send], 0), count, plain_final((name, k)))
-        return sums
-
+        result = []
+        payload = []
+        for k in range(3):
+            rows_out = sum(4 * c for *_, chains in tensors for kk, c in chains if kk == k)
+            payload.append(jobs.output(rows_out))
+        filled_rows = [0, 0, 0]
+        for key, got, keep, chains in tensors:
+            row, sums = 0, [None] * 3
+            for k, c in chains:
+                own = jobs.output(4 * c)
+                send_row = filled_rows[k]
+                jobs.add(got, row + 4 * c, keep, row + 4 * c, payload[k], send_row, 4 * c)
+                jobs.add(got, row, keep, row, own, 0, 4 * c)
+                filled_rows[k] += 4 * c
+                sums[k] = (own, send_row, c)
+                row += CHIPS * c
+            result.append((key, sums))
+        out = jobs.run(meta, name, waits=waits)
+        made = []
+        for key, sums in result:
+            made.append(
+                [
+                    None
+                    if s is None
+                    else Sums((out[s[0]], 0), (out[payload[k]], s[1]), s[2], plain_final((key, k)))
+                    for k, s in enumerate(sums)
+                ]
+            )
+        return made, [out[p] for p in payload]
+
+    shrunk_got = cube.swap(f_send, 0)
+    shrunk = f_own + shrunk_got.astype(F32)
+    result_rows = (middle + live * shrunk).astype(BF).reshape(2, frames, run, width)
+    result_own = jnp.where(upper, result_rows[1], result_rows[0])
+    result_give = jnp.where(upper, result_rows[0], result_rows[1])
+    result_got = cube.swap(result_give, cube.top)
+    result = jnp.concatenate(
+        [jnp.where(upper, result_got, result_own), jnp.where(upper, result_own, result_got)], axis=1
+    )
     sums_a = ffn_sums(grad_a, "a")
     sums_b = ffn_sums(grad_b, "b")
     turn_one, _ = turn("turn_one", [(sums_a, 0)], eight.got)
     turn_two, _ = turn("turn_two", [(sums_b, 0)], turn_one)
 
-    grad_middle, grad_gain_two, grad_branch, d_query, dkv_own, k_give, v_give = context_back(
+    grad_middle, grad_gain_two, grad_branch, d_query, dkv_own, dkv_give = context_back(
         run,
         meta,
-        after(dn_own, f_own, turn_one),
+        after(dn_own, result_give, turn_one),
         dn_got,
         middle,
         cot_live,
         live,
         gains_all,
         query,
-        key,
-        value,
-        key_other,
-        value_other,
+        key_value,
+        key_value_other,
         output_chains,
     )
-    turn_three, _ = turn("turn_three", [(sums_a, 1), (sums_b, 1)], turn_two, k_give)
-    dk_got = cube.swap(k_give, cube.top)
-    dv_got = cube.swap(v_give, cube.top)
-    output_give, output_keep = output_grad(meta, context, after(grad_branch, turn_two))
-    half_shard = shard_rows // 2
-    sums_o = core_sum(
-        "output_core", output_give, output_keep, [(k, half_shard) for k in OUTPUT_CHAINS]
-    )
-    turn_four, packed_four = turn("turn_four", [(sums_a, 2), (sums_b, 2), (sums_o, 0)], turn_three, dk_got, dv_got)
-    shrunk_got = cube.swap(after(f_send, turn_three, packed_four), 0)
-    shrunk = f_own + shrunk_got.astype(F32)
-    result = (middle + live * shrunk).astype(BF)
+    turn_three, packed_three = turn(
+        "turn_three", [(sums_a, 1), (sums_b, 1)], turn_two, dkv_give, result_got
+    )
+    dkv_got = cube.swap(dkv_give, cube.top)
+    output_give, output_keep = output_grad(meta, context, after(grad_branch, packed_three))
     joint_give, joint_keep, dkv = joint_grad(
-        meta, first, d_query, dkv_own, dk_got, after(dv_got, packed_four)
-    )
-    sums_j = core_sum("joint_core", joint_give, joint_keep, [(k, shard_rows) for k in range(3)])
-    result = from_sets(after(result, packed_four))
-    turn_seven, out_seven = turn(
-        "turn_seven",
-        [(sums_a, 3), (sums_b, 3), (sums_o, 1), (sums_j, 0)],
-        turn_four,
-        result,
-        squares=True,
-    )
-    expand_own_a, expand_give_a = (out_seven[i] for i in outcome["a"])
-    expand_own_b, expand_give_b = (out_seven[i] for i in outcome["b"])
-    shrink_first = out_seven[outcome["a_shrink"]]
-    shrink_mine = out_seven[outcome["b_shrink"]]
-
-    expand_give = jnp.concatenate([expand_give_a, expand_give_b])
-    expand_got = cube.swap(expand_give, 0)
-    expand_got_a, expand_got_b = expand_got[: 2 * shard_rows], expand_got[2 * shard_rows :]
-    shrink_got = cube.swap(shrink_first.astype(BF), cube.top).astype(F32)
+        meta, first, d_query, dkv_own, after(dkv_got, output_give)
+    )
+    turn_four, packed_four = turn(
+        "turn_four", [(sums_a, 2), (sums_b, 2)], turn_three, dkv_got, waits=(joint_give,)
+    )
+    joint_got = cube.swap(after(joint_give, packed_four), 0)
+    output_got = cube.swap(after(output_give, packed_four), 0)
     grad_inputs, grad_gain_one = input_back(
         meta,
         d_query,
-        after(dkv, sums_j[0].send[0]),
+        after(dkv, packed_four),
         grad_middle,
         x_rows,
         gains_all,
         joint + joint_other,
     )
-    turn_nine, out_nine = turn(
-        "turn_nine", [(sums_o, 2), (sums_j, 1)], turn_seven, shrink_got, expand_got
-    )
+    half_shard = shard_rows // 2
+    (sums_j, sums_o), sends = core_sums(
+        "joint_core",
+        [
+            ("joint", joint_got, joint_keep, [(k, shard_rows) for k in range(3)]),
+            ("output", output_got, output_keep, [(k, half_shard) for k in OUTPUT_CHAINS]),
+        ],
+        grad_inputs,
+    )
+    turn_seven = []
+    for axis in range(3):
+        k = (axis - 2) % 3
+        array = cube.swap(sends[k], 1 + axis)
+        turn_seven.append(array)
+        for sums in (sums_j, sums_o):
+            if sums[k] is not None:
+                sums[k].got = (array, sums[k].send[1])
     gains_term = jnp.concatenate([grad_gain_one, grad_gain_two]).reshape(2, count, -1)
     gains_term = gains_term.transpose(1, 0, 2).reshape(count, -1)
-    gains_parts = lax.all_to_all(after(gains_term, out_nine), "fsdp", 0, 0, tiled=True)
+    gains_parts = lax.all_to_all(after(gains_term, sends[0]), "fsdp", 0, 0, tiled=True)
     grad_gains = jnp.sum(gains_parts, axis=0).reshape(2, -1)
-    grad_inputs = from_sets(after(grad_inputs, turn_seven))
+    grad_inputs = from_sets(after(grad_inputs, sends[0]))
+    _, out_five = turn(
+        "turn_five",
+        [(sums_a, 3), (sums_b, 3)],
+        turn_four,
+        sends[0],
+        squares=True,
+    )
+    expand_own_a, expand_give_a = (out_five[i] for i in outcome["a"])
+    expand_own_b, expand_give_b = (out_five[i] for i in outcome["b"])
+    shrink_first = out_five[outcome["a_shrink"]]
+    shrink_mine = out_five[outcome["b_shrink"]]
+    expand_got_a = cube.swap(after(expand_give_a, sends[0]), 0)
+    expand_got_b = cube.swap(after(expand_give_b, expand_got_a), 0)
+    turn_nine, out_nine = turn(
+        "turn_nine",
+        [(sums_o, 1), (sums_j, 1)],
+        turn_seven,
+        grad_inputs,
+        waits=(grad_gains, out_five[-1]),
+    )
+    shrink_got = cube.swap(after(shrink_first.astype(BF), out_nine[0]), cube.top)
     turn_ten, out_ten = turn(
-        "turn_ten", [(sums_o, 3), (sums_j, 2)], turn_nine, grad_inputs, squares=True
-    )
-    grad_output = jnp.concatenate([out_ten[outcome[("output_core", k)]] for k in OUTPUT_CHAINS])
-    _, out_last = turn("turn_last", [(sums_j, 3)], turn_ten, squares=True)
-    grad_joint = [out_last[outcome[("joint_core", k)]] for k in range(3)]
-
-    grad_shrink = jnp.stack(
-        [jnp.where(upper, shrink_got, shrink_mine), jnp.where(upper, shrink_mine, shrink_got)]
-    )
-    grad_joint = jnp.concatenate(grad_joint, axis=1)
-
-    local_sq = sum(jnp.sum(out[-1]) for out in (out_seven, out_ten, out_last))
-    local_sq = local_sq + jnp.sum(grad_gains * grad_gains)
-    squares = lax.all_to_all(jnp.broadcast_to(local_sq, (count, 128)), "fsdp", 0, 0, tiled=True)
+        "turn_ten", [(sums_o, 2), (sums_j, 2)], turn_nine, shrink_got
+    )
+    _, out_last = turn(
+        "turn_last",
+        [(sums_o, 3), (sums_j, 3)],
+        turn_ten,
+        squares=True,
+        norm=(count, out_five[-1], grad_gains),
+    )
+    grad_output = [out_last[outcome[("output", k)]] for k in OUTPUT_CHAINS]
+    grad_joint = jnp.stack([out_last[outcome[("joint", k)]] for k in range(3)])
+
+    squares = lax.all_to_all(out_last[-1], "fsdp", 0, 0, tiled=True)
     total_sq = jnp.sum(squares[:, 0])
     grad_norm_value = jnp.sqrt(total_sq)
     factor = CLIP_LIMIT / jnp.maximum(grad_norm_value, CLIP_LIMIT)
-    joint_new = adam_step(
-        joint_weight, factor * grad_joint, joint_mean, joint_square, MATRIX_RATE, MATRIX_DECAY
-    )
-    output_new = adam_step(
-        output_weight, factor * grad_output, output_mean, output_square, MATRIX_RATE, MATRIX_DECAY
-    )
-    expand_new = adam_expand(
+    new = adam_matrices(
         meta,
-        factor.reshape(1),
-        expand_weight,
-        expand_mean,
-        expand_square,
-        (expand_own_a, expand_own_b),
-        (expand_got_a, expand_got_b),
-    )
-    shrink_new = adam_step(
-        shrink_weight, factor * grad_shrink, shrink_mean, shrink_square, MATRIX_RATE, MATRIX_DECAY
-    )
+        squares,
+        (
+            expand_weight,
+            expand_mean,
+            expand_square,
+            expand_own_a,
+            expand_own_b,
+            expand_got_a,
+            expand_got_b,
+        ),
+        (joint_weight, joint_mean, joint_square, grad_joint),
+        (output_weight, output_mean, output_square, *grad_output),
+        (shrink_weight, shrink_mean, shrink_square, shrink_mine, shrink_got),
+    )
+    expand_new, joint_new, output_new, shrink_new = (new[i : i + 3] for i in (0, 3, 6, 9))
     gains_new = adam_step(norm_gains, factor * grad_gains, gains_mean, gains_square, GAIN_RATE, 0.0)
     return (
         result,

time: 488 us -> 454 us (0.930)
  waiting for transfers between devices: 161 us -> 138 us
  other arithmetic: 30.8 us -> 16.7 us
  Pallas kernels: 198 us -> 203 us
    ppermute x64 -> x65, waiting for transfers between devices: 155 us -> 123 us  [swap(): return lax.ppermute(value, 'fsdp', pairs)]
    all_to_all x2, waiting for transfers between devices: 6.02 us -> 15 us  [the longest x1 9.99 us: local_cube(): lax.all_to_all(after(gains_term, sends[0]), 'fsdp', 0, 0, tiled=True)]
    sub x4 -> x1, other arithmetic: 8.83 us -> 0.59 us  [adam_step(): weight - learn_rate * (mean_hat / (jnp.sqrt(square_hat) + ADAM_EPS) + wei...]
    pallas_call x2, Pallas kernels: 17.3 us -> 24.7 us  [the longest x1 14.7 us: adam_matrices(): pl.pallas_call(adam_kernel, grid=(8,), in_specs=[SM, whole] + [e_spec] *...]
    unnamed x134 -> x126, local copies, waits for them, and re-layouts: 13.5 us -> 15.2 us
    ppermute x64 -> x65, starting transfers between devices: 65.7 us -> 66.1 us  [swap(): return lax.ppermute(value, 'fsdp', pairs)]
  transfers between devices with their start and end apart: 66 -> 67, of which waited for: 25 -> 24; matrix products, arithmetic and copies ran while one was open for 4% -> 4% of each run, Pallas kernels for 29% -> 36%
where the time goes in v3:
time: 454 us; the launch traced here: 452 us
  Pallas kernels  203 us (45%)
  waiting for transfers between devices  138 us (30%)
  starting transfers between devices  72.9 us (16%)
  local copies, waits for them, and re-layouts  18.4 us (4%)
  other arithmetic  16.7 us (4%)
    ppermute x65, waiting for transfers between devices, swap(): return lax.ppermute(value, 'fsdp', pairs)  123 us
    ppermute x65, starting transfers between devices, swap(): return lax.ppermute(value, 'fsdp', pairs)  66.1 us
    pallas_call x15, Pallas kernels, run(): pl.pallas_call(functools.partial(jobs_kernel, self.work, len(inputs), sel...  63.4 us
    pallas_call x2, Pallas kernels, ffn_rows(): pl.pallas_call(functools.partial(ffn_rows_kernel, first, len(arrays), tab...  27.3 us
    pallas_call x2, Pallas kernels, ffn_weights(): pl.pallas_call(functools.partial(ffn_weights_kernel, first, len(arrays),...  24.5 us
    pallas_call x1, Pallas kernels, context_back(): pl.pallas_call(functools.partial(context_back_kernel, run, width // HEADS...  19.4 us
    unnamed x126, local copies, waits for them, and re-layouts  15.2 us
    pallas_call x1, Pallas kernels, adam_matrices(): pl.pallas_call(adam_kernel, grid=(8,), in_specs=[SM, whole] + [e_spec] *...  14.7 us
  transfers between devices with their start and end apart: 67, of which 24 were waited for; matrix products, arithmetic and copies ran while one was open for 4% of the time, Pallas kernels for 36%

profile of v3, /device:TPU:0, one launch (start us, length us, event | category | flops | bytes accessed | tf_op | source)
XLA Modules:
  0.0 452.3 jit_solution(1700816557564810420)
XLA Ops:
  2.2 4.0 collective-permute-start.1
  15.4 3.4 split_weights.1
  19.5 2.8 pack_two.1
  25.8 9.0 %collective-permute-done = bf16[128,1024]{1,0:T(8,128)(2,1)S(1)} collective-permute-done((bf16[128,1024]{1,0:T(8,128)(2,1)S(1)}, bf16[128,1024]{1,0:T(8,128)(2,1)S(1)}, u32[]{:S(2)}, u32[]{:S(2)}) %collective-permute-start) | collective-permute-done | bytes 262176 | tf_op jit(solution)/shard_map/ppermute | solution.py:65
  38.3 4.9 %pack_three.1 = (bf16[320,1024]{1,0:T(8,128)(2,1)}, bf16[320,1024]{1,0:T(8,128)(2,1)}, bf16[320,1024]{1,0:T(8,128)(2,1)}, bf16[832,1024]{1,0:T(8,128)(2,1)}) custom-call(s32[3]{0:T(128)} %pad_add_fusion.meta, bf16[64,1024]{1,0:T(8,128)(2,1)} %get-tuple-element.331.refs_5_.refs_0_.refs_4_, bf16[64,1024]{1,0:T(8,128)(2,1)} %copy-done.27, ...), custom_call_target="tpu_custom_call" | custom-call | flops 1 | bytes 1 | tf_op jit(solution)/shard_map/pack_three/pallas_call | solution.py:438
  43.3 2.2 collective-permute-start.13
  49.6 9.1 %collective-permute-done.13.refs_2_ = bf16[128,1024]{1,0:T(8,128)(2,1)S(1)} collective-permute-done((bf16[128,1024]{1,0:T(8,128)(2,1)S(1)}, bf16[128,1024]{1,0:T(8,128)(2,1)S(1)}, u32[]{:S(2)}, u32[]{:S(2)}) %collective-permute-start.13) | collective-permute-done | bytes 262176 | tf_op jit(solution)/shard_map/ppermute | solution.py:65
  61.3 3.1 expand_units.1
  64.5 2.9 collective-permute-done.8.refs_0_.refs_3_.refs_2_.refs_11_.refs_4_
  68.7 3.1 pack_late.1
  76.8 2.1 collective-permute-start.15
  80.8 10.4 %joint_forward.1 = (bf16[256,1024]{1,0:T(8,128)(2,1)}, bf16[256,1024]{1,0:T(8,128)(2,1)}, bf16[528,1024]{1,0:T(8,128)(2,1)}, f32[8,1024]{1,0:T(8,128)}) custom-call(s32[3]{0:T(128)} %pad_add_fusion.meta, bf16[256,1024]{1,0:T(8,128)(2,1)} %pad_maximum_fusion.1.x, bf16[64,1024]{1,0:T(8,128)(2,1)} %get-tuple-element.338.refs_2_.refs_7_.refs_0_, ...), custom_call_target="tpu_custom_call" | custom-call | flops 1 | bytes 1 | tf_op jit(solution)/shard_map/joint_forward/pallas_call | solution.py:1032
  91.3 2.4 collective-permute-start.16
  95.5 3.6 pack_five.1
  101.6 2.6 pack_output.1
  105.3 24.1 %collective-permute-done.20.refs_12_.refs_3_.refs_5_ = bf16[128,1024]{1,0:T(8,128)(2,1)S(1)} collective-permute-done((bf16[128,1024]{1,0:T(8,128)(2,1)}, bf16[128,1024]{1,0:T(8,128)(2,1)S(1)}, u32[]{:S(2)}, u32[]{:S(2)}) %collective-permute-start.20) | collective-permute-done | bytes 262176 | tf_op jit(solution)/shard_map/ppermute | solution.py:65
  131.1 5.3 %collective-permute-done.21.refs_16_.refs_7_.refs_9_ = bf16[128,1024]{1,0:T(8,128)(2,1)S(1)} collective-permute-done((bf16[128,1024]{1,0:T(8,128)(2,1)}, bf16[128,1024]{1,0:T(8,128)(2,1)S(1)}, u32[]{:S(2)}, u32[]{:S(2)}) %collective-permute-start.21) | collective-permute-done | bytes 262176 | tf_op jit(solution)/shard_map/ppermute | solution.py:65
  136.4 11.1 %collective-permute-done.22.refs_2_.refs_6_ = bf16[512,1024]{1,0:T(8,128)(2,1)S(1)} collective-permute-done((bf16[512,1024]{1,0:T(8,128)(2,1)}, bf16[512,1024]{1,0:T(8,128)(2,1)S(1)}, u32[]{:S(2)}, u32[]{:S(2)}) %collective-permute-start.22) | collective-permute-done | bytes 1048608 | tf_op jit(solution)/shard_map/ppermute | solution.py:65
  148.4 4.7 %pack_seven.1 = (bf16[512,1024]{1,0:T(8,128)(2,1)}, bf16[512,1024]{1,0:T(8,128)(2,1)}, bf16[512,1024]{1,0:T(8,128)(2,1)}, bf16[512,1024]{1,0:T(8,128)(2,1)}) custom-call(s32[3]{0:T(128)} %pad_add_fusion.meta, bf16[256,1024]{1,0:T(8,128)(2,1)} %get-tuple-element.411.refs_4_.refs_0_, bf16[256,1024]{1,0:T(8,128)(2,1)} %copy-done.13, ...), custom_call_target="tpu_custom_call" | custom-call | flops 1 | bytes 1 | tf_op jit(solution)/shard_map/pack_seven/pallas_call | solution.py:438
  158.3 3.6 pack_eight.1
  161.9 13.1 %context_forward.1 = (bf16[256,1024]{1,0:T(8,128)(2,1)}, f32[256,1024]{1,0:T(8,128)}, bf16[256,1024]{1,0:T(8,128)(2,1)}) custom-call(s32[3]{0:T(128)} %pad_add_fusion.meta, bf16[256,1024]{1,0:T(8,128)(2,1)} %get-tuple-element.361.query, bf16[528,1024]{1,0:T(8,128)(2,1)} %get-tuple-element.364.own.refs_0_, ...), custom_call_target="tpu_custom_call" | custom-call | flops 1 | bytes 1 | tf_op jit(solution)/shard_map/context_forward/pallas_call | solution.py:1124
  175.1 4.0 collective-permute-done.28.refs_7_
  182.9 2.1 collective-permute-done.26.n2o
  185.8 13.3 %ffn_rows.2 = (f32[512,1024]{1,0:T(8,128)}, bf16[512,1024]{1,0:T(8,128)(2,1)}, bf16[512,1024]{1,0:T(8,128)(2,1)}, bf16[512,1024]{1,0:T(8,128)(2,1)}) custom-call(s32[3]{0:T(128)} %pad_add_fusion.meta, bf16[256,1024]{1,0:T(8,128)(2,1)} %get-tuple-element.405.n2m, bf16[256,1024]{1,0:T(8,128)(2,1)} %copy-done.15, bf16[256,1024]{1,0:T(8,128)(2,1)} %copy-done.5, ...), custom_call_target="tpu_custom_call" | custom-call | flops 1 | bytes 1 | tf_op jit(solution)/shard_map/ffn_rows/pallas_call | solution.py:852
  199.1 11.8 %ffn_weights.2 = (f32[512,1024]{1,0:T(8,128)}, bf16[512,1024]{1,0:T(8,128)(2,1)}, bf16[512,1024]{1,0:T(8,128)(2,1)}, bf16[512,1024]{1,0:T(8,128)(2,1)}, bf16[512...) custom-call(s32[3]{0:T(128)} %pad_add_fusion.meta, ...), custom_call_target="tpu_custom_call" | custom-call | flops 1 | bytes 1 | tf_op jit(solution)/shard_map/ffn_weights/pallas_call | solution.py:923
  215.2 14.0 %ffn_rows.3 = (f32[256,1024]{1,0:T(8,128)}, f32[256,1024]{1,0:T(8,128)}, bf16[512,1024]{1,0:T(8,128)(2,1)}, bf16[512,1024]{1,0:T(8,128)(2,1)}, bf16[512,1024]{1,0:T(8,128)(2,1)}) custom-call(s32[3]{0:T(128)} %pad_add_fusion.meta, bf16[256,1024]{1,0:T(8,128)(2,1)} %get-tuple-element.405.n2m, bf16[256,1024]{1,0:T(8,128)(2,1)} %copy-done.15, ...), custom_call_target="tpu_custom_call" | custom-call | flops 1 | bytes 1 | tf_op jit(solution)/shard_map/ffn_rows/pallas_call | solution.py:852
  229.2 12.6 %ffn_weights.3 = (f32[256,1024]{1,0:T(8,128)}, bf16[256,1024]{1,0:T(8,128)(2,1)}, bf16[512,1024]{1,0:T(8,128)(2,1)}, bf16[512,1024]{1,0:T(8,128)(2,1)}, bf16[512...) custom-call(s32[3]{0:T(128)} %pad_add_fusion.meta, ...), custom_call_target="tpu_custom_call" | custom-call | flops 1 | bytes 1 | tf_op jit(solution)/shard_map/ffn_weights/pallas_call | solution.py:923
  248.9 19.4 %context_back.1 = (f32[256,1024]{1,0:T(8,128)}, f32[1,1024]{1,0:T(1,128)}, bf16[256,1024]{1,0:T(8,128)(2,1)}, bf16[256,1024]{1,0:T(8,128)(2,1)}, f32[256,2048]{1,0:T(8,128)}, /*index=5*/bf16[528,1024]{1,0:T(8,128)(2,1)}) custom-call(s32[3]{0:T(128)} %pad_add_fusion.meta, f32[256,1024]{1,0:T(8,128)} %get-tuple-element.444.dn_own, ...), custom_call_target="tpu_custom_call" | custom-call | flops 1 | bytes 1 | tf_op jit(solution)/shard_map/context_back/pallas_call | solution.py:1208
  269.4 4.5 collective-permute-done.35
  275.0 8.2 %turn_three.1 = (bf16[512,1024]{1,0:T(8,128)(2,1)}, bf16[512,1024]{1,0:T(8,128)(2,1)}, bf16[512,1024]{1,0:T(8,128)(2,1)}, bf16[256,1024]{1,0:T(8,128)(2,1)}, bf1...) custom-call(s32[3]{0:T(128)} %pad_add_fusion.meta, ...), custom_call_target="tpu_custom_call" | custom-call | flops 1 | bytes 1 | tf_op jit(solution)/shard_map/turn_three/pallas_call | solution.py:438
  286.1 5.0 %output_grad.1 = (bf16[512,1024]{1,0:T(8,128)(2,1)}, bf16[512,1024]{1,0:T(8,128)(2,1)}) custom-call(s32[3]{0:T(128)} %pad_add_fusion.meta, bf16[256,1024]{1,0:T(8,128)(2,1)} %get-tuple-element.450.context, bf16[256,1024]{1,0:T(8,128)(2,1)} %get-tuple-element.485.grad), custom_call_target="tpu_custom_call" | custom-call | flops 1 | bytes 1 | tf_op jit(solution)/shard_map/output_grad/pallas_call | solution.py:1290
  291.1 29.4 %collective-permute-done.40.dkv_got = bf16[528,1024]{1,0:T(8,128)(2,1)S(1)} collective-permute-done((bf16[528,1024]{1,0:T(8,128)(2,1)}, bf16[528,1024]{1,0:T(8,128)(2,1)S(1)}, u32[]{:S(2)}, u32[]{:S(2)}) %collective-permute-start.40) | collective-permute-done | bytes 1081376 | tf_op jit(solution)/shard_map/ppermute | solution.py:65
  321.5 10.0 %joint_grad.1 = (bf16[1536,1024]{1,0:T(8,128)(2,1)}, bf16[1536,1024]{1,0:T(8,128)(2,1)}, bf16[256,2048]{1,0:T(8,128)(2,1)}) custom-call(s32[3]{0:T(128)} %pad_add_fusion.meta, bf16[256,1024]{1,0:T(8,128)(2,1)} %get-tuple-element.447.first, bf16[256,1024]{1,0:T(8,128)(2,1)} %get-tuple-element.446.dq, f32[256,2048]{1,0:T(8,128)} %get-tuple-element.448.dkv_own, ...), custom_call_target="tpu_custom_call" | custom-call | flops 1 | bytes 1 | tf_op jit(solution)/shard_map/joint_grad/pallas_call | solution.py:1333
  332.5 5.3 %turn_four.1 = (bf16[256,1024]{1,0:T(8,128)(2,1)}, bf16[256,1024]{1,0:T(8,128)(2,1)}, bf16[256,1024]{1,0:T(8,128)(2,1)}, bf16[128,1024]{1,0:T(8,128)(2,1)}, bf16...) custom-call(s32[3]{0:T(128)} %pad_add_fusion.meta, ...), custom_call_target="tpu_custom_call" | custom-call | flops 1 | bytes 1 | tf_op jit(solution)/shard_map/turn_four/pallas_call | solution.py:438
  340.4 9.6 %input_back.1 = (bf16[256,1024]{1,0:T(8,128)(2,1)}, f32[1,1024]{1,0:T(1,128)}) custom-call(s32[3]{0:T(128)} %pad_add_fusion.meta, bf16[256,1024]{1,0:T(8,128)(2,1)} %get-tuple-element.446.dq, bf16[256,2048]{1,0:T(8,128)(2,1)} %get-tuple-element.508.dkv, f32[256,1024]{1,0:T(8,128)} %get-tuple-element.509.dh, bf16[256,1024]{1,0:T(8,128)(2,1)} %pad_maximum_fusion.1.x, ...), custom_call_target="tpu_custom_call" | custom-call | flops 1 | bytes 1 | tf_op jit(solution)/shard_map/input_back/pallas_call | solution.py:1367
  351.0 6.1 %joint_core.1 = (bf16[256,1024]{1,0:T(8,128)(2,1)}, bf16[384,1024]{1,0:T(8,128)(2,1)}, bf16[384,1024]{1,0:T(8,128)(2,1)}, bf16[256,1024]{1,0:T(8,128)(2,1)}, bf1...) custom-call(s32[3]{0:T(128)} %pad_add_fusion.meta, ...), custom_call_target="tpu_custom_call" | custom-call | flops 1 | bytes 1 | tf_op jit(solution)/shard_map/joint_core/pallas_call | solution.py:438
  359.9 3.3 collective-permute-start.49
  364.1 3.3 all-to-all-start
  367.5 4.4 turn_five.1
  371.9 10.0 %all-to-all-done = f32[32,1,64]{2,1,0:T(1,128)S(1)} async-done(((f32[32,1,64]{2,1,0:T(1,128)}), f32[32,1,64]{2,1,0:T(1,128)S(1)}, u32[]{:S(2)}, u32[]{:S(2)}) %all-to-all-start) | async-done | bytes 8224 | tf_op jit(solution)/shard_map/all_to_all | solution.py:1742
  385.7 4.3 turn_nine.1
  391.6 2.5 collective-permute-start.59
  395.4 9.5 %collective-permute-done.59.refs_20_ = bf16[128,1024]{1,0:T(8,128)(2,1)S(1)} collective-permute-done((bf16[128,1024]{1,0:T(8,128)(2,1)S(1)}, bf16[128,1024]{1,0:T(8,128)(2,1)S(1)}, u32[]{:S(2)}, u32[]{:S(2)}) %collective-permute-start.59) | collective-permute-done | bytes 262176 | tf_op jit(solution)/shard_map/ppermute | solution.py:65
  407.7 3.2 turn_ten.1
  419.6 3.6 turn_last.1
  423.2 3.4 all-to-all-start.1
  428.7 5.0 %all-to-all-done.1 = f32[32,1,128]{2,1,0:T(1,128)S(1)} async-done(((f32[32,1,128]{2,1,0:T(1,128)}), f32[32,1,128]{2,1,0:T(1,128)S(1)}, u32[]{:S(2)}, u32[]{:S(2)}) %all-to-all-start.1) | async-done | bytes 16416 | tf_op jit(solution)/shard_map/all_to_all | solution.py:1779
  436.5 14.7 %adam_matrices.1 = (f32[64,8192]{1,0:T(8,128)}, f32[64,8192]{1,0:T(8,128)}, f32[64,8192]{1,0:T(8,128)}, f32[64,3072]{1,0:T(8,128)}, f32[64,3072]{1,0:T(8,128)}, ...) custom-call(s32[3]{0:T(128)} %pad_add_fusion.meta, ...), custom_call_target="tpu_custom_call" | custom-call | tf_op jit(solution)/shard_map/adam_matrices/pallas_call | solution.py:1447
  (284 shorter events, 98.7 us)
Async XLA Ops:
  22.4 12.5 %collective-permute-start.5 = (bf16[160,1024]{1,0:T(8,128)(2,1)}, bf16[160,1024]{1,0:T(8,128)(2,1)S(1)}, u32[]{:S(2)}, u32[]{:S(2)}) collective-permute-start(bf16[160,1024]{1,0:T(8,128)(2,1)} %get-tuple-element.328), channel_id=1, source_target_pairs={{0,4},{1,5},{2,6},{3,7},{4,0},{5,1},{6,2},{7,3},{8,12},{9,13},{10,... | collective-permute-start | bytes 983048 | tf_op jit(solution)/shard_map/ppermute | solution.py:65
  23.5 13.3 %collective-permute-start.6 = (bf16[160,1024]{1,0:T(8,128)(2,1)}, bf16[160,1024]{1,0:T(8,128)(2,1)S(1)}, u32[]{:S(2)}, u32[]{:S(2)}) collective-permute-start(bf16[160,1024]{1,0:T(8,128)(2,1)} %get-tuple-element.329), channel_id=1, source_target_pairs={{0,8},{1,9},{2,10},{3,11},{4,12},{5,13},{6,14},{7,15},{8,0},{9,1},... | collective-permute-start | bytes 983048 | tf_op jit(solution)/shard_map/ppermute | solution.py:65
  23.9 12.9 %collective-permute-start.7 = (bf16[160,1024]{1,0:T(8,128)(2,1)}, bf16[160,1024]{1,0:T(8,128)(2,1)S(1)}, u32[]{:S(2)}, u32[]{:S(2)}) collective-permute-start(bf16[160,1024]{1,0:T(8,128)(2,1)} %get-tuple-element.330), channel_id=1, source_target_pairs={{0,2},{1,3},{2,0},{3,1},{4,6},{5,7},{6,4},{7,5},{8,10},{9,11},{10,... | collective-permute-start | bytes 983048 | tf_op jit(solution)/shard_map/ppermute | solution.py:65
  43.2 24.2 %collective-permute-start.11 = (bf16[832,1024]{1,0:T(8,128)(2,1)}, bf16[832,1024]{1,0:T(8,128)(2,1)}, u32[]{:S(2)}, u32[]{:S(2)}) collective-permute-start(bf16[832,1024]{1,0:T(8,128)(2,1)} %get-tuple-element.345), channel_id=1, source_target_pairs={{0,1},{1,0},{2,3},{3,2},{4,5},{5,4},{6,7},{7,6},{8,9},{9,8},{10,11... | collective-permute-start | bytes 5111816 | tf_op jit(solution)/shard_map/ppermute | solution.py:65
  43.3 15.3 %collective-permute-start.13 = (bf16[128,1024]{1,0:T(8,128)(2,1)S(1)}, bf16[128,1024]{1,0:T(8,128)(2,1)S(1)}, u32[]{:S(2)}, u32[]{:S(2)}) collective-permute-start(bf16[128,1024]{1,0:T(8,128)(2,1)S(1)} %copy-done.62), channel_id=1, source_target_pairs={{0,16},{1,17},{2,18},{3,19},{4,20},{5,21},{6,22},{7,23},{8,24},{9,... | collective-permute-start | bytes 786440 | tf_op jit(solution)/shard_map/ppermute | solution.py:65
  45.5 21.9 %collective-permute-start.8 = (bf16[320,1024]{1,0:T(8,128)(2,1)}, bf16[320,1024]{1,0:T(8,128)(2,1)S(1)}, u32[]{:S(2)}, u32[]{:S(2)}) collective-permute-start(bf16[320,1024]{1,0:T(8,128)(2,1)} %get-tuple-element.342), channel_id=1, source_target_pairs={{0,8},{1,9},{2,10},{3,11},{4,12},{5,13},{6,14},{7,15},{8,0},{9,1},... | collective-permute-start | bytes 1966088 | tf_op jit(solution)/shard_map/ppermute | solution.py:65
  47.0 20.4 %collective-permute-start.9 = (bf16[320,1024]{1,0:T(8,128)(2,1)}, bf16[320,1024]{1,0:T(8,128)(2,1)S(1)}, u32[]{:S(2)}, u32[]{:S(2)}) collective-permute-start(bf16[320,1024]{1,0:T(8,128)(2,1)} %get-tuple-element.343), channel_id=1, source_target_pairs={{0,2},{1,3},{2,0},{3,1},{4,6},{5,7},{6,4},{7,5},{8,10},{9,11},{10,... | collective-permute-start | bytes 1966088 | tf_op jit(solution)/shard_map/ppermute | solution.py:65
  48.2 19.2 %collective-permute-start.10 = (bf16[320,1024]{1,0:T(8,128)(2,1)}, bf16[320,1024]{1,0:T(8,128)(2,1)S(1)}, u32[]{:S(2)}, u32[]{:S(2)}) collective-permute-start(bf16[320,1024]{1,0:T(8,128)(2,1)} %get-tuple-element.344), channel_id=1, source_target_pairs={{0,4},{1,5},{2,6},{3,7},{4,0},{5,1},{6,2},{7,3},{8,12},{9,13},{10,... | collective-permute-start | bytes 1966088 | tf_op jit(solution)/shard_map/ppermute | solution.py:65
  71.9 21.8 %collective-permute-start.17 = (bf16[256,1024]{1,0:T(8,128)(2,1)S(1)}, bf16[256,1024]{1,0:T(8,128)(2,1)S(1)}, u32[]{:S(2)}, u32[]{:S(2)}) collective-permute-start(bf16[256,1024]{1,0:T(8,128)(2,1)S(1)} %copy-done.3), channel_id=1, source_target_pairs={{0,8},{1,9},{2,10},{3,11},{4,12},{5,13},{6,14},{7,15},{8,0},{9,1},... | collective-permute-start | bytes 1572872 | tf_op jit(solution)/shard_map/ppermute | solution.py:65
  72.8 20.9 %collective-permute-start.18 = (bf16[256,1024]{1,0:T(8,128)(2,1)S(1)}, bf16[256,1024]{1,0:T(8,128)(2,1)S(1)}, u32[]{:S(2)}, u32[]{:S(2)}) collective-permute-start(bf16[256,1024]{1,0:T(8,128)(2,1)S(1)} %copy-done.10), channel_id=1, source_target_pairs={{0,2},{1,3},{2,0},{3,1},{4,6},{5,7},{6,4},{7,5},{8,10},{9,11},{10,... | collective-permute-start | bytes 1572872 | tf_op jit(solution)/shard_map/ppermute | solution.py:65
  73.7 20.0 %collective-permute-start.19 = (bf16[256,1024]{1,0:T(8,128)(2,1)S(1)}, bf16[256,1024]{1,0:T(8,128)(2,1)S(1)}, u32[]{:S(2)}, u32[]{:S(2)}) collective-permute-start(bf16[256,1024]{1,0:T(8,128)(2,1)S(1)} %copy-done.11), channel_id=1, source_target_pairs={{0,4},{1,5},{2,6},{3,7},{4,0},{5,1},{6,2},{7,3},{8,12},{9,13},{10,... | collective-permute-start | bytes 1572872 | tf_op jit(solution)/shard_map/ppermute | solution.py:65
  76.8 14.4 %collective-permute-start.15 = (bf16[128,1024]{1,0:T(8,128)(2,1)}, bf16[128,1024]{1,0:T(8,128)(2,1)}, u32[]{:S(2)}, u32[]{:S(2)}) collective-permute-start(bf16[128,1024]{1,0:T(8,128)(2,1)} %select_bitcast_fusion.2), channel_id=1, source_target_pairs={{0,16},{1,17},{2,18},{3,19},{4,20},{5,21},{6,22},{7,23},{8,24},{9,... | collective-permute-start | bytes 786440 | tf_op jit(solution)/shard_map/ppermute | solution.py:65
  91.3 56.2 %collective-permute-start.16 = (bf16[528,1024]{1,0:T(8,128)(2,1)}, bf16[528,1024]{1,0:T(8,128)(2,1)}, u32[]{:S(2)}, u32[]{:S(2)}) collective-permute-start(bf16[528,1024]{1,0:T(8,128)(2,1)} %get-tuple-element.364.own.refs_0_), channel_id=1, source_target_pairs={{0,16},{1,17},{2,18},{3,19},{4,20},{5,21},{6,22},{7,23},{8,24},{9,... | collective-permute-start | bytes 3244040 | tf_op jit(solution)/shard_map/ppermute | solution.py:65
  99.1 37.3 %collective-permute-start.23 = (bf16[512,1024]{1,0:T(8,128)(2,1)}, bf16[512,1024]{1,0:T(8,128)(2,1)S(1)}, u32[]{:S(2)}, u32[]{:S(2)}) collective-permute-start(bf16[512,1024]{1,0:T(8,128)(2,1)} %get-tuple-element.375), channel_id=1, source_target_pairs={{0,2},{1,3},{2,0},{3,1},{4,6},{5,7},{6,4},{7,5},{8,10},{9,11},{10,... | collective-permute-start | bytes 3145736 | tf_op jit(solution)/shard_map/ppermute | solution.py:65
  100.2 36.2 %collective-permute-start.24 = (bf16[512,1024]{1,0:T(8,128)(2,1)}, bf16[512,1024]{1,0:T(8,128)(2,1)S(1)}, u32[]{:S(2)}, u32[]{:S(2)}) collective-permute-start(bf16[512,1024]{1,0:T(8,128)(2,1)} %get-tuple-element.376), channel_id=1, source_target_pairs={{0,4},{1,5},{2,6},{3,7},{4,0},{5,1},{6,2},{7,3},{8,12},{9,13},{10,... | collective-permute-start | bytes 3145736 | tf_op jit(solution)/shard_map/ppermute | solution.py:65
  101.6 45.9 %collective-permute-start.22 = (bf16[512,1024]{1,0:T(8,128)(2,1)}, bf16[512,1024]{1,0:T(8,128)(2,1)S(1)}, u32[]{:S(2)}, u32[]{:S(2)}) collective-permute-start(bf16[512,1024]{1,0:T(8,128)(2,1)} %get-tuple-element.377), channel_id=1, source_target_pairs={{0,8},{1,9},{2,10},{3,11},{4,12},{5,13},{6,14},{7,15},{8,0},{9,1},... | collective-permute-start | bytes 3145736 | tf_op jit(solution)/shard_map/ppermute | solution.py:65
  104.2 25.2 %collective-permute-start.20 = (bf16[128,1024]{1,0:T(8,128)(2,1)}, bf16[128,1024]{1,0:T(8,128)(2,1)S(1)}, u32[]{:S(2)}, u32[]{:S(2)}) collective-permute-start(bf16[128,1024]{1,0:T(8,128)(2,1)} %get-tuple-element.384), channel_id=1, source_target_pairs={{0,2},{1,3},{2,0},{3,1},{4,6},{5,7},{6,4},{7,5},{8,10},{9,11},{10,... | collective-permute-start | bytes 786440 | tf_op jit(solution)/shard_map/ppermute | solution.py:65
  153.2 25.9 %collective-permute-start.28 = (bf16[512,1024]{1,0:T(8,128)(2,1)}, bf16[512,1024]{1,0:T(8,128)(2,1)}, u32[]{:S(2)}, u32[]{:S(2)}) collective-permute-start(bf16[512,1024]{1,0:T(8,128)(2,1)} %get-tuple-element.408), channel_id=1, source_target_pairs={{0,2},{1,3},{2,0},{3,1},{4,6},{5,7},{6,4},{7,5},{8,10},{9,11},{10,... | collective-permute-start | bytes 3145736 | tf_op jit(solution)/shard_map/ppermute | solution.py:65
  154.4 25.4 %collective-permute-start.29 = (bf16[512,1024]{1,0:T(8,128)(2,1)}, bf16[512,1024]{1,0:T(8,128)(2,1)S(1)}, u32[]{:S(2)}, u32[]{:S(2)}) collective-permute-start(bf16[512,1024]{1,0:T(8,128)(2,1)} %get-tuple-element.409), channel_id=1, source_target_pairs={{0,4},{1,5},{2,6},{3,7},{4,0},{5,1},{6,2},{7,3},{8,12},{9,13},{10,... | collective-permute-start | bytes 3145736 | tf_op jit(solution)/shard_map/ppermute | solution.py:65
  154.8 25.3 %collective-permute-start.30 = (bf16[512,1024]{1,0:T(8,128)(2,1)}, bf16[512,1024]{1,0:T(8,128)(2,1)}, u32[]{:S(2)}, u32[]{:S(2)}) collective-permute-start(bf16[512,1024]{1,0:T(8,128)(2,1)} %get-tuple-element.410), channel_id=1, source_target_pairs={{0,8},{1,9},{2,10},{3,11},{4,12},{5,13},{6,14},{7,15},{8,0},{9,1},... | collective-permute-start | bytes 3145736 | tf_op jit(solution)/shard_map/ppermute | solution.py:65
  180.1 30.9 %collective-permute-start.31 = (bf16[512,1024]{1,0:T(8,128)(2,1)}, bf16[512,1024]{1,0:T(8,128)(2,1)S(1)}, u32[]{:S(2)}, u32[]{:S(2)}) collective-permute-start(bf16[512,1024]{1,0:T(8,128)(2,1)} %get-tuple-element.423), channel_id=1, source_target_pairs={{0,8},{1,9},{2,10},{3,11},{4,12},{5,13},{6,14},{7,15},{8,0},{9,1},... | collective-permute-start | bytes 3145736 | tf_op jit(solution)/shard_map/ppermute | solution.py:65
  180.3 30.7 %collective-permute-start.32 = (bf16[512,1024]{1,0:T(8,128)(2,1)}, bf16[512,1024]{1,0:T(8,128)(2,1)}, u32[]{:S(2)}, u32[]{:S(2)}) collective-permute-start(bf16[512,1024]{1,0:T(8,128)(2,1)} %get-tuple-element.424), channel_id=1, source_target_pairs={{0,2},{1,3},{2,0},{3,1},{4,6},{5,7},{6,4},{7,5},{8,10},{9,11},{10,... | collective-permute-start | bytes 3145736 | tf_op jit(solution)/shard_map/ppermute | solution.py:65
  181.5 29.5 %collective-permute-start.33 = (bf16[512,1024]{1,0:T(8,128)(2,1)}, bf16[512,1024]{1,0:T(8,128)(2,1)S(1)}, u32[]{:S(2)}, u32[]{:S(2)}) collective-permute-start(bf16[512,1024]{1,0:T(8,128)(2,1)} %get-tuple-element.425), channel_id=1, source_target_pairs={{0,4},{1,5},{2,6},{3,7},{4,0},{5,1},{6,2},{7,3},{8,12},{9,13},{10,... | collective-permute-start | bytes 3145736 | tf_op jit(solution)/shard_map/ppermute | solution.py:65
  212.0 30.4 %collective-permute-start.36 = (bf16[512,1024]{1,0:T(8,128)(2,1)}, bf16[512,1024]{1,0:T(8,128)(2,1)S(1)}, u32[]{:S(2)}, u32[]{:S(2)}) collective-permute-start(bf16[512,1024]{1,0:T(8,128)(2,1)} %get-tuple-element.441), channel_id=1, source_target_pairs={{0,2},{1,3},{2,0},{3,1},{4,6},{5,7},{6,4},{7,5},{8,10},{9,11},{10,... | collective-permute-start | bytes 3145736 | tf_op jit(solution)/shard_map/ppermute | solution.py:65
  213.0 29.4 %collective-permute-start.37 = (bf16[512,1024]{1,0:T(8,128)(2,1)}, bf16[512,1024]{1,0:T(8,128)(2,1)S(1)}, u32[]{:S(2)}, u32[]{:S(2)}) collective-permute-start(bf16[512,1024]{1,0:T(8,128)(2,1)} %get-tuple-element.442), channel_id=1, source_target_pairs={{0,4},{1,5},{2,6},{3,7},{4,0},{5,1},{6,2},{7,3},{8,12},{9,13},{10,... | collective-permute-start | bytes 3145736 | tf_op jit(solution)/shard_map/ppermute | solution.py:65
  213.5 29.0 %collective-permute-start.38 = (bf16[512,1024]{1,0:T(8,128)(2,1)}, bf16[512,1024]{1,0:T(8,128)(2,1)}, u32[]{:S(2)}, u32[]{:S(2)}) collective-permute-start(bf16[512,1024]{1,0:T(8,128)(2,1)} %get-tuple-element.443), channel_id=1, source_target_pairs={{0,8},{1,9},{2,10},{3,11},{4,12},{5,13},{6,14},{7,15},{8,0},{9,1},... | collective-permute-start | bytes 3145736 | tf_op jit(solution)/shard_map/ppermute | solution.py:65
  242.5 31.4 %collective-permute-start.41 = (bf16[512,1024]{1,0:T(8,128)(2,1)}, bf16[512,1024]{1,0:T(8,128)(2,1)}, u32[]{:S(2)}, u32[]{:S(2)}) collective-permute-start(bf16[512,1024]{1,0:T(8,128)(2,1)} %get-tuple-element.456), channel_id=1, source_target_pairs={{0,4},{1,5},{2,6},{3,7},{4,0},{5,1},{6,2},{7,3},{8,12},{9,13},{10,... | collective-permute-start | bytes 3145736 | tf_op jit(solution)/shard_map/ppermute | solution.py:65
  244.1 30.9 %collective-permute-start.42 = (bf16[512,1024]{1,0:T(8,128)(2,1)}, bf16[512,1024]{1,0:T(8,128)(2,1)}, u32[]{:S(2)}, u32[]{:S(2)}) collective-permute-start(bf16[512,1024]{1,0:T(8,128)(2,1)} %get-tuple-element.459), channel_id=1, source_target_pairs={{0,8},{1,9},{2,10},{3,11},{4,12},{5,13},{6,14},{7,15},{8,0},{9,1},... | collective-permute-start | bytes 3145736 | tf_op jit(solution)/shard_map/ppermute | solution.py:65
  244.4 30.6 %collective-permute-start.43 = (bf16[512,1024]{1,0:T(8,128)(2,1)}, bf16[512,1024]{1,0:T(8,128)(2,1)}, u32[]{:S(2)}, u32[]{:S(2)}) collective-permute-start(bf16[512,1024]{1,0:T(8,128)(2,1)} %get-tuple-element.462), channel_id=1, source_target_pairs={{0,2},{1,3},{2,0},{3,1},{4,6},{5,7},{6,4},{7,5},{8,10},{9,11},{10,... | collective-permute-start | bytes 3145736 | tf_op jit(solution)/shard_map/ppermute | solution.py:65
  246.8 27.0 %collective-permute-start.35 = (bf16[16,8,1024]{2,1,0:T(8,128)(2,1)S(1)}, bf16[16,8,1024]{2,1,0:T(8,128)(2,1)S(1)}, u32[]{:S(2)}, u32[]{:S(2)}) collective-permute-start(bf16[16,8,1024]{2,1,0:T(8,128)(2,1)S(1)} %select_bitcast_fusion.1), channel_id=1, source_target_pairs={{0,16},{1,17},{2,18},{3,19},{4,20},{5,21},{6,22},{7,23},{8,24},{9,... | collective-permute-start | bytes 786440 | tf_op jit(solution)/shard_map/ppermute | solution.py:65
  268.4 52.2 %collective-permute-start.40 = (bf16[528,1024]{1,0:T(8,128)(2,1)}, bf16[528,1024]{1,0:T(8,128)(2,1)S(1)}, u32[]{:S(2)}, u32[]{:S(2)}) collective-permute-start(bf16[528,1024]{1,0:T(8,128)(2,1)} %get-tuple-element.449), channel_id=1, source_target_pairs={{0,16},{1,17},{2,18},{3,19},{4,20},{5,21},{6,22},{7,23},{8,24},{9,... | collective-permute-start | bytes 3244040 | tf_op jit(solution)/shard_map/ppermute | solution.py:65
  283.2 48.4 %collective-permute-start.46 = (bf16[512,1024]{1,0:T(8,128)(2,1)}, bf16[512,1024]{1,0:T(8,128)(2,1)S(1)}, u32[]{:S(2)}, u32[]{:S(2)}) collective-permute-start(bf16[512,1024]{1,0:T(8,128)(2,1)} %get-tuple-element.476), channel_id=1, source_target_pairs={{0,2},{1,3},{2,0},{3,1},{4,6},{5,7},{6,4},{7,5},{8,10},{9,11},{10,... | collective-permute-start | bytes 3145736 | tf_op jit(solution)/shard_map/ppermute | solution.py:65
  284.2 47.4 %collective-permute-start.44 = (bf16[512,1024]{1,0:T(8,128)(2,1)}, bf16[512,1024]{1,0:T(8,128)(2,1)}, u32[]{:S(2)}, u32[]{:S(2)}) collective-permute-start(bf16[512,1024]{1,0:T(8,128)(2,1)} %get-tuple-element.477), channel_id=1, source_target_pairs={{0,4},{1,5},{2,6},{3,7},{4,0},{5,1},{6,2},{7,3},{8,12},{9,13},{10,... | collective-permute-start | bytes 3145736 | tf_op jit(solution)/shard_map/ppermute | solution.py:65
  284.8 46.8 %collective-permute-start.45 = (bf16[512,1024]{1,0:T(8,128)(2,1)}, bf16[512,1024]{1,0:T(8,128)(2,1)}, u32[]{:S(2)}, u32[]{:S(2)}) collective-permute-start(bf16[512,1024]{1,0:T(8,128)(2,1)} %get-tuple-element.478), channel_id=1, source_target_pairs={{0,8},{1,9},{2,10},{3,11},{4,12},{5,13},{6,14},{7,15},{8,0},{9,1},... | collective-permute-start | bytes 3145736 | tf_op jit(solution)/shard_map/ppermute | solution.py:65
  337.8 12.2 %collective-permute-start.47 = (bf16[1536,1024]{1,0:T(8,128)(2,1)}, bf16[1536,1024]{1,0:T(8,128)(2,1)}, u32[]{:S(2)}, u32[]{:S(2)}) collective-permute-start(bf16[1536,1024]{1,0:T(8,128)(2,1)} %get-tuple-element.511.refs_9_), channel_id=1, source_target_pairs={{0,1},{1,0},{2,3},{3,2},{4,5},{5,4},{6,7},{7,6},{8,9},{9,8},{10,11... | collective-permute-start | bytes 9437192 | tf_op jit(solution)/shard_map/ppermute | solution.py:65
  338.4 21.6 %collective-permute-start.53 = (bf16[256,1024]{1,0:T(8,128)(2,1)}, bf16[256,1024]{1,0:T(8,128)(2,1)S(1)}, u32[]{:S(2)}, u32[]{:S(2)}) collective-permute-start(bf16[256,1024]{1,0:T(8,128)(2,1)} %get-tuple-element.499), channel_id=1, source_target_pairs={{0,2},{1,3},{2,0},{3,1},{4,6},{5,7},{6,4},{7,5},{8,10},{9,11},{10,... | collective-permute-start | bytes 1572872 | tf_op jit(solution)/shard_map/ppermute | solution.py:65
  340.0 23.3 %collective-permute-start.54 = (bf16[256,1024]{1,0:T(8,128)(2,1)}, bf16[256,1024]{1,0:T(8,128)(2,1)}, u32[]{:S(2)}, u32[]{:S(2)}) collective-permute-start(bf16[256,1024]{1,0:T(8,128)(2,1)} %get-tuple-element.500), channel_id=1, source_target_pairs={{0,4},{1,5},{2,6},{3,7},{4,0},{5,1},{6,2},{7,3},{8,12},{9,13},{10,... | collective-permute-start | bytes 1572872 | tf_op jit(solution)/shard_map/ppermute | solution.py:65
  340.4 27.1 %collective-permute-start.55 = (bf16[256,1024]{1,0:T(8,128)(2,1)}, bf16[256,1024]{1,0:T(8,128)(2,1)}, u32[]{:S(2)}, u32[]{:S(2)}) collective-permute-start(bf16[256,1024]{1,0:T(8,128)(2,1)} %get-tuple-element.501), channel_id=1, source_target_pairs={{0,8},{1,9},{2,10},{3,11},{4,12},{5,13},{6,14},{7,15},{8,0},{9,1},... | collective-permute-start | bytes 1572872 | tf_op jit(solution)/shard_map/ppermute | solution.py:65
  357.1 27.3 %collective-permute-start.50 = (bf16[384,1024]{1,0:T(8,128)(2,1)}, bf16[384,1024]{1,0:T(8,128)(2,1)S(1)}, u32[]{:S(2)}, u32[]{:S(2)}) collective-permute-start(bf16[384,1024]{1,0:T(8,128)(2,1)} %get-tuple-element.517), channel_id=1, source_target_pairs={{0,4},{1,5},{2,6},{3,7},{4,0},{5,1},{6,2},{7,3},{8,12},{9,13},{10,... | collective-permute-start | bytes 2359304 | tf_op jit(solution)/shard_map/ppermute | solution.py:65
  358.8 25.6 %collective-permute-start.52 = (bf16[384,1024]{1,0:T(8,128)(2,1)}, bf16[384,1024]{1,0:T(8,128)(2,1)S(1)}, u32[]{:S(2)}, u32[]{:S(2)}) collective-permute-start(bf16[384,1024]{1,0:T(8,128)(2,1)} %get-tuple-element.521), channel_id=1, source_target_pairs={{0,2},{1,3},{2,0},{3,1},{4,6},{5,7},{6,4},{7,5},{8,10},{9,11},{10,... | collective-permute-start | bytes 2359304 | tf_op jit(solution)/shard_map/ppermute | solution.py:65
  359.9 22.6 %collective-permute-start.49 = (bf16[16,8,1024]{2,1,0:T(8,128)(2,1)}, bf16[16,8,1024]{2,1,0:T(8,128)(2,1)}, u32[]{:S(2)}, u32[]{:S(2)}) collective-permute-start(bf16[16,8,1024]{2,1,0:T(8,128)(2,1)} %select_bitcast_fusion), channel_id=1, source_target_pairs={{0,16},{1,17},{2,18},{3,19},{4,20},{5,21},{6,22},{7,23},{8,24},{9,... | collective-permute-start | bytes 786440 | tf_op jit(solution)/shard_map/ppermute | solution.py:65
  363.3 21.1 %collective-permute-start.51 = (bf16[256,1024]{1,0:T(8,128)(2,1)}, bf16[256,1024]{1,0:T(8,128)(2,1)S(1)}, u32[]{:S(2)}, u32[]{:S(2)}) collective-permute-start(bf16[256,1024]{1,0:T(8,128)(2,1)} %get-tuple-element.515), channel_id=1, source_target_pairs={{0,8},{1,9},{2,10},{3,11},{4,12},{5,13},{6,14},{7,15},{8,0},{9,1},... | collective-permute-start | bytes 1572872 | tf_op jit(solution)/shard_map/ppermute | solution.py:65
  364.1 17.7 %all-to-all-start = ((f32[32,1,64]{2,1,0:T(1,128)}), f32[32,1,64]{2,1,0:T(1,128)S(1)}, u32[]{:S(2)}, u32[]{:S(2)}) async-start(f32[32,1,64]{2,1,0:T(1,128)} %bitcast.16), calls=%async_computation | async-start | bytes 32768 | tf_op jit(solution)/shard_map/all_to_all | solution.py:1742
  390.0 16.8 %collective-permute-start.57 = (bf16[192,1024]{1,0:T(8,128)(2,1)}, bf16[192,1024]{1,0:T(8,128)(2,1)S(1)}, u32[]{:S(2)}, u32[]{:S(2)}) collective-permute-start(bf16[192,1024]{1,0:T(8,128)(2,1)} %get-tuple-element.547), channel_id=1, source_target_pairs={{0,8},{1,9},{2,10},{3,11},{4,12},{5,13},{6,14},{7,15},{8,0},{9,1},... | collective-permute-start | bytes 1179656 | tf_op jit(solution)/shard_map/ppermute | solution.py:65
  390.7 16.1 %collective-permute-start.58 = (bf16[192,1024]{1,0:T(8,128)(2,1)}, bf16[192,1024]{1,0:T(8,128)(2,1)S(1)}, u32[]{:S(2)}, u32[]{:S(2)}) collective-permute-start(bf16[192,1024]{1,0:T(8,128)(2,1)} %get-tuple-element.550), channel_id=1, source_target_pairs={{0,2},{1,3},{2,0},{3,1},{4,6},{5,7},{6,4},{7,5},{8,10},{9,11},{10,... | collective-permute-start | bytes 1179656 | tf_op jit(solution)/shard_map/ppermute | solution.py:65
  391.5 23.5 %collective-permute-start.63 = (f32[128,1024]{1,0:T(8,128)}, f32[128,1024]{1,0:T(8,128)S(1)}, u32[]{:S(2)}, u32[]{:S(2)}) collective-permute-start(f32[128,1024]{1,0:T(8,128)} %get-tuple-element.583), channel_id=1, source_target_pairs={{0,1},{1,0},{2,3},{3,2},{4,5},{5,4},{6,7},{7,6},{8,9},{9,8},{10,11... | collective-permute-start | bytes 1572872 | tf_op jit(solution)/shard_map/ppermute | solution.py:65
  391.6 13.4 %collective-permute-start.59 = (bf16[128,1024]{1,0:T(8,128)(2,1)S(1)}, bf16[128,1024]{1,0:T(8,128)(2,1)S(1)}, u32[]{:S(2)}, u32[]{:S(2)}) collective-permute-start(bf16[128,1024]{1,0:T(8,128)(2,1)S(1)} %convert_element_type.62), channel_id=1, source_target_pairs={{0,16},{1,17},{2,18},{3,19},{4,20},{5,21},{6,22},{7,23},{8,24},{9,... | collective-permute-start | bytes 786440 | tf_op jit(solution)/shard_map/ppermute | solution.py:65
  415.0 20.7 %collective-permute-start.64 = (f32[128,1024]{1,0:T(8,128)S(1)}, f32[128,1024]{1,0:T(8,128)S(1)}, u32[]{:S(2)}, u32[]{:S(2)}) collective-permute-start(f32[128,1024]{1,0:T(8,128)S(1)} %copy-done.60), channel_id=1, source_target_pairs={{0,1},{1,0},{2,3},{3,2},{4,5},{5,4},{6,7},{7,6},{8,9},{9,8},{10,11... | collective-permute-start | bytes 1572872 | tf_op jit(solution)/shard_map/ppermute | solution.py:65
  (82 other events, 618.5 us)

commit v4 on v3

--- a/solution.py
+++ b/solution.py
@@ -431,7 +431,7 @@
             scratch += [pltpu.VMEM((rows, self.width), F32)]
         shapes = list(self.outputs)
         if squares:
-            shape = (norm[0], 128) if norm else (8, self.width)
+            shape = (norm[0], 128 + self.width * (len(norm) - 2)) if norm else (8, self.width)
             shapes.append(jax.ShapeDtypeStruct(shape, F32))
         more = list(norm[1:])
         scratch += [pltpu.VMEM((8, self.width), F32)] if squares else []
@@ -517,11 +517,12 @@
     if squares and not norm:
         square_out[...] = square_ref[...]
     if norm:
-        total = jnp.sum(square_ref[...])
-        for i, ref in enumerate(norm):
-            value = ref[...]
-            total = total + jnp.sum(value if i == 0 else value * value)
-        square_out[...] = jnp.full(square_out.shape, total, F32)
+        total = jnp.sum(square_ref[...]) + jnp.sum(norm[0][...])
+        square_out[:, :128] = jnp.full((square_out.shape[0], 128), total, F32)
+        for i, ref in enumerate(norm[1:]):
+            width = ref.shape[1]
+            spot = slice(128 + i * width, 128 + (i + 1) * width)
+            square_out[:, spot] = jnp.broadcast_to(ref[...], (square_out.shape[0], width))
     finish(leaving)
 
 
@@ -828,7 +829,7 @@
         dg[:, cols] = (dh * u * sig * (1.0 + g * (1.0 - sig))).astype(BF)
         return 0
 
-    lax.fori_loop(0, width // TILE, gates, 0)
+    lax.fori_loop(0, width // TILE, gates, 0, unroll=True)
 
     def back(t, _):
         cols = aligned(t, TILE)
@@ -841,7 +842,7 @@
             dn_send[:, cols] = d[rows:]
         return 0
 
-    lax.fori_loop(0, width // TILE, back, 0)
+    lax.fori_loop(0, width // TILE, back, 0, unroll=True)
 
 
 def ffn_rows(meta, n2m, n2o, cm, co, chains, carried):
@@ -896,7 +897,7 @@
             dw[cols, :] = dot_tn(lhs[:, cols], rhs[...]).astype(BF)
             return 0
 
-        lax.fori_loop(0, width // TILE, step, 0)
+        lax.fori_loop(0, width // TILE, step, 0, unroll=True)
         leaving += store_blocks(dw, outs[2 * k : 2 * k + 2], table[0], k, chip, out_sem.at[k])
     finish(coming)
 
@@ -911,7 +912,7 @@
             f_send[:, cols] = f[rows:].astype(BF)
         return 0
 
-    lax.fori_loop(0, width // TILE, down, 0)
+    lax.fori_loop(0, width // TILE, down, 0, unroll=True)
     finish(leaving)
 
 
@@ -1022,7 +1023,7 @@
             out[low : low + rows, aligned(t, TILE)] = dot(first[...], weight).astype(BF)
             return 0
 
-        lax.fori_loop(0, tiles, step, 0)
+        lax.fori_loop(0, tiles, step, 0, unroll=True)
 
 
 def joint_forward(meta, x, chains):
@@ -1109,7 +1110,7 @@
         h_out[:, cols] = x[:, cols].astype(F32) + live[...] * dot(ctx[...], wo[:, cols])
         return 0
 
-    lax.fori_loop(0, width // TILE, project, 0)
+    lax.fori_loop(0, width // TILE, project, 0, unroll=True)
     h = h_out[...]
     inverse = lax.rsqrt(jnp.mean(h * h, axis=-1, keepdims=True) + NORM_EPS)
     n2[...] = (h * inverse * gains[1:2, :]).astype(BF)
@@ -1166,7 +1167,7 @@
         dctx[:, cols] = dot_nt(da[...], wo[cols, :]).astype(BF)
         return 0
 
-    lax.fori_loop(0, width // TILE, project, 0)
+    lax.fori_loop(0, width // TILE, project, 0, unroll=True)
     scale = head_dim ** (-0.5)
     lanes = 2 * head_dim
     pairs = width // lanes
@@ -1250,7 +1251,7 @@
             dw[i, cols, :] = dot_tn(lhs[:, cols], rhs()).astype(BF)
             return 0
 
-        lax.fori_loop(0, width // TILE, step, 0)
+        lax.fori_loop(0, width // TILE, step, 0, unroll=True)
 
 
 def store_devices(dw, matrix, row, count, k, targets, base, meta, sem, used):
@@ -1302,9 +1303,10 @@
     )(meta, context, grad)
 
 
-def joint_grad_kernel(meta, first, dq, dkv_own, dkv_got, give, keep, dkv, dw, sem):
+def joint_grad_kernel(meta, first, dq, dkv_own, dkv_got, give, keep, dkv):
     width = first.shape[1]
     rows = first.shape[0]
+    chip, core = meta[0], meta[1]
     for part in range(2):
         cols = slice(part * width, (part + 1) * width)
         got = dkv_got[part * rows : (part + 1) * rows, :]
@@ -1312,19 +1314,13 @@
         dkv[:, cols] = (dkv_own[:, cols] + more).astype(BF)
     rights = (lambda: dq[...], lambda: dkv[:, :width], lambda: dkv[:, width:])
     shard = width // (2 * CHIPS)
-    leaving = []
     for k in range(3):
-
-        def step(t, _, k=k):
-            cols = aligned(t, TILE)
-            dw[k, cols, :] = dot_tn(first[:, cols], rights[k]()).astype(BF)
-            return 0
-
-        lax.fori_loop(0, width // TILE, step, 0)
-        leaving += store_devices(
-            dw, k, 0, shard, k, (give, keep), k * CHIPS * shard, meta, sem, len(leaving)
-        )
-    finish(leaving)
+        for j in range(CHIPS):
+            grad = dot_tn(first[:, aligned(chip ^ CHAIN_MASKS[k][j], 2 * shard)], rights[k]())
+            low, high = grad[:shard].astype(BF), grad[shard:].astype(BF)
+            at = slice((k * CHIPS + j) * shard, (k * CHIPS + j + 1) * shard)
+            give[at] = jnp.where(core == 0, high, low)
+            keep[at] = jnp.where(core == 0, low, high)
 
 
 def joint_grad(meta, first, dq, dkv_own, dkv_got):
@@ -1333,12 +1329,8 @@
     return pl.pallas_call(
         joint_grad_kernel,
         in_specs=[SM] + [VM] * 4,
-        out_specs=[HB, HB, VM],
+        out_specs=[VM] * 3,
         out_shape=[part, part, jax.ShapeDtypeStruct((rows, 2 * width), BF)],
-        scratch_shapes=[
-            pltpu.VMEM((3, width, width), BF),
-            pltpu.SemaphoreType.DMA((PAIR_COPIES,)),
-        ],
         compiler_params=pltpu.CompilerParams(vmem_limit_bytes=60 * MIB),
         cost_estimate=SMALL,
         name="joint_grad",
@@ -1356,7 +1348,7 @@
         dn[:, cols] = dot_nt(dq[...], w[cols, :width]) + dot_nt(dkv[...], w[cols, width:])
         return 0
 
-    lax.fori_loop(0, width // TILE, step, 0)
+    lax.fori_loop(0, width // TILE, step, 0, unroll=True)
     grad_in, dg1[...] = norm_back(x[...].astype(F32), gains[0:1, :], dn[...])
     out[...] = (dh[...] + grad_in).astype(BF)
 
@@ -1383,84 +1375,116 @@
     )(meta, dq, dkv, dh, x, gains, *arrays)
 
 
-def adam_rows(k, w, m, v, grad, outs, where, rate, decay):
-    new = adam_step(w[where], k * grad, m[where], v[where], rate, decay)
-    for out, value in zip(outs, new):
-        out[where] = value
+def adam_in_place(k, w, m, v, grad, where, rate, decay):
+    grad = k * grad
+    mean = BETA_ONE * m[where] + (1.0 - BETA_ONE) * grad
+    square = BETA_TWO * v[where] + (1.0 - BETA_TWO) * grad * grad
+    root = jnp.sqrt(square * (1.0 / (1.0 - BETA_TWO**STEP))) + ADAM_EPS
+    old = w[where]
+    move = mean * (rate / (1.0 - BETA_ONE**STEP)) / root
+    w[where] = old - (move + (rate * decay) * old)
+    m[where] = mean
+    v[where] = square
 
 
 def adam_kernel(meta, squares, *refs):
-    (ew, em, ev, own_a, own_b, got_a, got_b, jw, jm, jv, jg, ow, om, ov, og_a, og_b) = refs[:16]
-    (sw, sm, sv, sg_mine, sg_got) = refs[16:21]
-    e_out, j_out, o_out, s_out = refs[21:24], refs[24:27], refs[27:30], refs[30:33]
+    sources, targets, held = refs[:21], refs[21:33], refs[33:54]
+    in_sem, out_sem = refs[54:]
     core, group = meta[1], meta[2]
-    step = pl.program_id(0)
-    total = jnp.sum(squares[...], axis=0, keepdims=True)[0:1, 0:1]
+    (ew, em, ev, own_a, own_b, got_a, got_b, jw, jm, jv, jg, ow, om, ov, og_a, og_b) = held[:16]
+    (sw, sm, sv, sg_mine, sg_got) = held[16:]
+    width = own_a.shape[1]
+    rows = ew.shape[0]
+    started = []
+
+    def load(index, where):
+        copy = pltpu.make_async_copy(
+            sources[index].at[where], held[index].at[where], in_sem.at[len(started)]
+        )
+        copy.start()
+        started.append(copy)
+        return copy
+
+    def whole(ref):
+        return (slice(None),) * len(ref.shape)
+
+    pieces = []
+    gradients = [load(i, whole(held[i])) for i in (3, 4, 5, 6)]
+    for c in range(ew.shape[1] // width):
+        where = (slice(None), slice(c * width, (c + 1) * width))
+        pieces.append(("expand", c, where, [load(i, where) for i in (0, 1, 2)]))
+    for c in range(jw.shape[1] // width):
+        where = (slice(None), slice(c * width, (c + 1) * width))
+        copies = [load(10, (c,))] + [load(i, where) for i in (7, 8, 9)]
+        pieces.append(("joint", c, where, copies))
+    copies = [load(i, whole(held[i])) for i in (14, 15, 11, 12, 13)]
+    pieces.append(("output", 0, None, copies))
+    more = [load(i, whole(held[i])) for i in (19, 20)]
+    for c in range(sw.shape[0]):
+        pieces.append(("shrink", c, (c,), (more if c == 0 else []) + [load(i, (c,)) for i in (16, 17, 18)]))
+
+    sums = jnp.sum(squares[...], axis=0, keepdims=True)
+    total = sums[:, 0:1] + jnp.sum(sums[:, 128:] * sums[:, 128:], axis=1, keepdims=True)
     k = CLIP_LIMIT / jnp.maximum(jnp.sqrt(total), CLIP_LIMIT)
-    block = 128
-    turn = ((step // 2) % 2) ^ (1 - group)
-    for q in range(ew.shape[1] // block):
-        cols = (slice(None), slice(q * block, (q + 1) * block))
-        near = slice((q // 2) * block, (q // 2 + 1) * block)
-        own = jnp.where(turn == 0, own_a[:, near], own_b[:, near])
-        got = jnp.where(turn == 0, got_a[:, near], got_b[:, near])
-        grad = jnp.where(core == q % 2, own, got)
-        adam_rows(k, ew, em, ev, grad, e_out, cols, MATRIX_RATE, MATRIX_DECAY)
-    everything = (slice(None), slice(None))
-
-    @pl.when(step < 3)
-    def _():
-        adam_rows(k, jw, jm, jv, jg[0], j_out, everything, MATRIX_RATE, MATRIX_DECAY)
-
-    @pl.when((step >= 3) & (step < 5))
-    def _():
-        grad = jnp.where(step == 3, og_a[...], og_b[...])
-        adam_rows(k, ow, om, ov, grad, o_out, everything, MATRIX_RATE, MATRIX_DECAY)
-
-    @pl.when(step >= 4)
-    def _():
-        mine = ((step - 4) // 2) == group
-        grad = jnp.where(mine, sg_mine[...], sg_got[...].astype(F32))
-        adam_rows(k, sw, sm, sv, grad, s_out, (0,), MATRIX_RATE, MATRIX_DECAY)
+    finish(gradients)
+    leaving = []
+
+    def store(target, index, where):
+        copy = pltpu.make_async_copy(
+            held[index].at[where], targets[target].at[where], out_sem.at[len(leaving)]
+        )
+        copy.start()
+        leaving.append(copy)
+
+    block = width // CHIPS
+    for kind, c, where, copies in pieces:
+        finish(copies)
+        if kind == "expand":
+            turn = ((c // 2) % 2) ^ (1 - group)
+            r = slice((c // 4) * rows, (c // 4 + 1) * rows)
+            for q in range(CHIPS):
+                near = (c % 2) * (CHIPS // 2) + q // 2
+                near = (r, slice(near * block, (near + 1) * block))
+                own = jnp.where(turn == 0, own_a[near], own_b[near])
+                got = jnp.where(turn == 0, got_a[near], got_b[near])
+                grad = jnp.where(core == q % 2, own, got)
+                cols = (slice(None), slice(c * width + q * block, c * width + (q + 1) * block))
+                adam_in_place(k, ew, em, ev, grad, cols, MATRIX_RATE, MATRIX_DECAY)
+            for i in range(3):
+                store(i, i, where)
+        elif kind == "joint":
+            adam_in_place(k, jw, jm, jv, jg[c], where, MATRIX_RATE, MATRIX_DECAY)
+            for i in range(3):
+                store(3 + i, 7 + i, where)
+        elif kind == "output":
+            half = og_a.shape[0]
+            for part, grad in enumerate((og_a, og_b)):
+                at = (slice(part * half, (part + 1) * half),)
+                adam_in_place(k, ow, om, ov, grad[...], at, MATRIX_RATE, MATRIX_DECAY)
+            for i in range(3):
+                store(6 + i, 11 + i, whole(ow))
+        else:
+            grad = jnp.where(group == c, sg_mine[...], sg_got[...].astype(F32))
+            adam_in_place(k, sw, sm, sv, grad, where, MATRIX_RATE, MATRIX_DECAY)
+            for i in range(3):
+                store(9 + i, 16 + i, where)
+    finish(leaving)
 
 
 def adam_matrices(meta, squares, expand, joint, output, shrink):
-    rows, wide = expand[0].shape
-    width = wide // 8
-    shrink_rows = shrink[0].shape[1] // 2
-
-    def half(i):
-        return (i // 4, i % 2)
-
-    e_spec = pl.BlockSpec((rows, width), lambda i: (0, i))
-    e_grad = pl.BlockSpec((rows, width // 2), half)
-    j_spec = pl.BlockSpec((rows, width), lambda i: (0, jnp.minimum(i, 2)))
-    j_grad = pl.BlockSpec((1, rows, width), lambda i: (jnp.minimum(i, 2), 0, 0))
-    o_spec = pl.BlockSpec((rows // 2, width), lambda i: (jnp.clip(i - 3, 0, 1), 0))
-    o_grad = pl.BlockSpec((rows // 2, width), lambda i: (0, 0))
-    s_spec = pl.BlockSpec(
-        (1, shrink_rows, width), lambda i: (jnp.maximum(i - 4, 0) // 2, jnp.maximum(i - 4, 0) % 2, 0)
-    )
-    s_grad = pl.BlockSpec((shrink_rows, width), lambda i: (jnp.maximum(i - 4, 0) % 2, 0))
-    whole = pl.BlockSpec(squares.shape, lambda i: (0, 0))
+    arrays = (*expand, *joint, *output, *shrink)
     shapes = [jax.ShapeDtypeStruct(p[0].shape, F32) for p in (expand, joint, output, shrink)]
     return pl.pallas_call(
         adam_kernel,
-        grid=(8,),
-        in_specs=[SM, whole]
-        + [e_spec] * 3
-        + [e_grad] * 4
-        + [j_spec] * 3
-        + [j_grad]
-        + [o_spec] * 3
-        + [o_grad] * 2
-        + [s_spec] * 3
-        + [s_grad] * 2,
-        out_specs=[e_spec] * 3 + [j_spec] * 3 + [o_spec] * 3 + [s_spec] * 3,
+        in_specs=[SM, VM] + [HB] * len(arrays),
+        out_specs=[HB] * 12,
         out_shape=[s for s in shapes for _ in range(3)],
+        scratch_shapes=[pltpu.VMEM(a.shape, a.dtype) for a in arrays]
+        + [pltpu.SemaphoreType.DMA((64,)), pltpu.SemaphoreType.DMA((64,))],
         compiler_params=pltpu.CompilerParams(vmem_limit_bytes=60 * MIB),
+        cost_estimate=SMALL,
         name="adam_matrices",
-    )(meta, squares, *expand, *joint, *output, *shrink)
+    )(meta, squares, *arrays)
 
 
 def local_cube(
@@ -1566,7 +1590,7 @@
     cot_own, cot_give = parted(cotangent)
     cot_got = cube.swap(after(cot_give, three.packed, shrink_other), cube.top)
     late = begin("pack_late").core(joint, joint_other, 4, 8)
-    late = late.run(three.got, three.core_got, units)
+    late = late.run(three.got, three.core_got, units, x_rows)
     first_units = after(units, three.got, three.core_got)
     got_four = [cube.swap(unit, 1 + axis) for axis, unit in enumerate(first_units)]
     for k in range(3):
@@ -1577,11 +1601,12 @@
     live = (position[None, :] < depth_all[:, None]).astype(F32).reshape(rows, 1)
 
     first, query, key_value, gains_all = joint_forward(meta, x_rows, joint + joint_other)
-    key_value_other = cube.swap(after(key_value, cot_got), cube.top)
+    key_value_other = cube.swap(key_value, cube.top)
     five = begin("pack_five").gather(part_a, 1).gather(part_b, 1).run(got_four, key_value, cot_got)
     last = begin("pack_output").gather(output, 2).run(five.packed)
-    seven = begin("pack_seven").gather(part_a, 2).core(output, output_other, 0, 8)
-    seven = seven.run(five.got, key_value_other, last.got)
+    output_core = begin("pack_core").core(output, output_other, 0, 8).run(last.got)
+    seven = begin("pack_seven").gather(part_a, 2)
+    seven = seven.run(five.got, key_value_other, output_core.packed)
     cot_live = (halves(cot_own, after(cot_got, key_value)).astype(F32) * live).astype(BF)
     cot_other = cube.swap(after(cot_live, five.got, key_value_other), 0)
 
@@ -1598,7 +1623,7 @@
         output_chains,
     )
     eight = begin("pack_eight").gather(part_b, 2).run(
-        seven.packed, seven.core_got, cot_other, gate=(seven.got, second)
+        seven.packed, cot_other, gate=(seven.got, second)
     )
     second_other = cube.swap(second, 0)
     row_args = (meta, second, second_other, cot_live, cot_other)
@@ -1737,10 +1762,6 @@
         for sums in (sums_j, sums_o):
             if sums[k] is not None:
                 sums[k].got = (array, sums[k].send[1])
-    gains_term = jnp.concatenate([grad_gain_one, grad_gain_two]).reshape(2, count, -1)
-    gains_term = gains_term.transpose(1, 0, 2).reshape(count, -1)
-    gains_parts = lax.all_to_all(after(gains_term, sends[0]), "fsdp", 0, 0, tiled=True)
-    grad_gains = jnp.sum(gains_parts, axis=0).reshape(2, -1)
     grad_inputs = from_sets(after(grad_inputs, sends[0]))
     _, out_five = turn(
         "turn_five",
@@ -1760,7 +1781,7 @@
         [(sums_o, 1), (sums_j, 1)],
         turn_seven,
         grad_inputs,
-        waits=(grad_gains, out_five[-1]),
+        waits=(out_five[-1],),
     )
     shrink_got = cube.swap(after(shrink_first.astype(BF), out_nine[0]), cube.top)
     turn_ten, out_ten = turn(
@@ -1771,13 +1792,17 @@
         [(sums_o, 3), (sums_j, 3)],
         turn_ten,
         squares=True,
-        norm=(count, out_five[-1], grad_gains),
+        norm=(count, out_five[-1], grad_gain_one, grad_gain_two),
     )
     grad_output = [out_last[outcome[("output", k)]] for k in OUTPUT_CHAINS]
     grad_joint = jnp.stack([out_last[outcome[("joint", k)]] for k in range(3)])
 
     squares = lax.all_to_all(out_last[-1], "fsdp", 0, 0, tiled=True)
-    total_sq = jnp.sum(squares[:, 0])
+    gains_sum = jnp.sum(squares[:, 128:], axis=0)
+    total_sq = jnp.sum(squares[:, 0]) + jnp.sum(gains_sum * gains_sum)
+    grad_gains = lax.dynamic_index_in_dim(
+        gains_sum.reshape(2, count, lane), cube.index, 1, keepdims=False
+    )
     grad_norm_value = jnp.sqrt(total_sq)
     factor = CLIP_LIMIT / jnp.maximum(grad_norm_value, CLIP_LIMIT)
     new = adam_matrices(

time: 454 us -> 446 us (0.982); the launches traced: 452 us -> 439 us
  Pallas kernels: 203 us -> 190 us
  waiting for transfers between devices: 138 us -> 147 us
  starting transfers between devices: 72.9 us -> 65.3 us
    ppermute x65, waiting for transfers between devices: 123 us -> 138 us  [swap(): return lax.ppermute(value, 'fsdp', pairs)]
    all_to_all x1 -> x0, waiting for transfers between devices: 9.99 us -> none  [local_cube(): lax.all_to_all(after(gains_term, sends[0]), 'fsdp', 0, 0, tiled=True)]
    pallas_call x15 -> x16, Pallas kernels: 63.4 us -> 65.4 us  [run(): pl.pallas_call(functools.partial(jobs_kernel, self.work, len(inputs), sel...]
    unnamed x126 -> x127, local copies, waits for them, and re-layouts: 15.2 us -> 14.3 us
  transfers between devices with their start and end apart: 67 -> 66, of which waited for: 24 -> 24; matrix products, arithmetic and copies ran while one was open for 4% -> 4% of each run, Pallas kernels for 36% -> 35%
where the time goes in v4:
time: 446 us; the launch traced here: 439 us
  Pallas kernels  190 us (43%)
  waiting for transfers between devices  147 us (33%)
  starting transfers between devices  65.3 us (15%)
  local copies, waits for them, and re-layouts  18.2 us (4%)
  other arithmetic  13.9 us (3%)
  between operations  4.54 us (1%)
    ppermute x65, waiting for transfers between devices, swap(): return lax.ppermute(value, 'fsdp', pairs)  138 us
    pallas_call x16, Pallas kernels, run(): pl.pallas_call(functools.partial(jobs_kernel, self.work, len(inputs), sel...  65.4 us
    ppermute x65, starting transfers between devices, swap(): return lax.ppermute(value, 'fsdp', pairs)  62.8 us
    pallas_call x2, Pallas kernels, ffn_rows(): pl.pallas_call(functools.partial(ffn_rows_kernel, first, len(arrays), tab...  24.5 us
    pallas_call x2, Pallas kernels, ffn_weights(): pl.pallas_call(functools.partial(ffn_weights_kernel, first, len(arrays),...  21.7 us
    pallas_call x1, Pallas kernels, context_back(): pl.pallas_call(functools.partial(context_back_kernel, run, width // HEADS...  18.8 us
    unnamed x127, local copies, waits for them, and re-layouts  14.3 us
    pallas_call x1, Pallas kernels, context_forward(): pl.pallas_call(functools.partial(context_kernel, run, width // HEADS, len...  12.9 us
  transfers between devices with their start and end apart: 66, of which 24 were waited for; matrix products, arithmetic and copies ran while one was open for 4% of the time, Pallas kernels for 35%

profile of v4, /device:TPU:0, one launch (start us, length us, event | category | flops | bytes accessed | tf_op | source)
XLA Modules:
  0.0 439.4 jit_solution(18139667597988672016)
XLA Ops:
  2.2 4.0 collective-permute-start.1
  15.3 3.4 split_weights.1
  19.5 2.8 pack_two.1
  25.9 8.9 %collective-permute-done = bf16[128,1024]{1,0:T(8,128)(2,1)S(1)} collective-permute-done((bf16[128,1024]{1,0:T(8,128)(2,1)S(1)}, bf16[128,1024]{1,0:T(8,128)(2,1)S(1)}, u32[]{:S(2)}, u32[]{:S(2)}) %collective-permute-start) | collective-permute-done | bytes 262176 | tf_op jit(solution)/shard_map/ppermute | solution.py:65
  38.3 5.0 %pack_three.1 = (bf16[320,1024]{1,0:T(8,128)(2,1)}, bf16[320,1024]{1,0:T(8,128)(2,1)}, bf16[320,1024]{1,0:T(8,128)(2,1)}, bf16[832,1024]{1,0:T(8,128)(2,1)}) custom-call(s32[3]{0:T(128)} %pad_add_fusion.meta, bf16[64,1024]{1,0:T(8,128)(2,1)} %get-tuple-element.328.refs_5_.refs_0_.refs_4_, bf16[64,1024]{1,0:T(8,128)(2,1)} %copy-done.28, ...), custom_call_target="tpu_custom_call" | custom-call | flops 1 | bytes 1 | tf_op jit(solution)/shard_map/pack_three/pallas_call | solution.py:438
  49.1 9.6 %collective-permute-done.13.refs_2_ = bf16[128,1024]{1,0:T(8,128)(2,1)S(1)} collective-permute-done((bf16[128,1024]{1,0:T(8,128)(2,1)S(1)}, bf16[128,1024]{1,0:T(8,128)(2,1)S(1)}, u32[]{:S(2)}, u32[]{:S(2)}) %collective-permute-start.13) | collective-permute-done | bytes 262176 | tf_op jit(solution)/shard_map/ppermute | solution.py:65
  61.7 3.1 expand_units.1
  64.8 2.7 collective-permute-done.8.refs_0_.refs_3_.refs_2_.refs_4_
  68.8 3.0 pack_late.1
  75.2 2.1 collective-permute-start.19
  77.3 8.2 %joint_forward.1 = (bf16[256,1024]{1,0:T(8,128)(2,1)}, bf16[256,1024]{1,0:T(8,128)(2,1)}, bf16[528,1024]{1,0:T(8,128)(2,1)}, f32[8,1024]{1,0:T(8,128)}) custom-call(s32[3]{0:T(128)} %pad_add_fusion.meta, bf16[256,1024]{1,0:T(8,128)(2,1)} %pad_maximum_fusion.1.x, bf16[64,1024]{1,0:T(8,128)(2,1)} %get-tuple-element.335.refs_2_.refs_7_.refs_0_, ...), custom_call_target="tpu_custom_call" | custom-call | flops 1 | bytes 1 | tf_op jit(solution)/shard_map/joint_forward/pallas_call | solution.py:1033
  86.4 3.8 collective-permute-done.19
  93.7 3.6 pack_five.1
  100.6 2.6 pack_output.1
  104.2 23.6 %collective-permute-done.20.refs_3_.refs_5_ = bf16[128,1024]{1,0:T(8,128)(2,1)S(1)} collective-permute-done((bf16[128,1024]{1,0:T(8,128)(2,1)}, bf16[128,1024]{1,0:T(8,128)(2,1)S(1)}, u32[]{:S(2)}, u32[]{:S(2)}) %collective-permute-start.20) | collective-permute-done | bytes 262176 | tf_op jit(solution)/shard_map/ppermute | solution.py:65
  129.5 5.6 %collective-permute-done.21.refs_7_.refs_9_ = bf16[128,1024]{1,0:T(8,128)(2,1)S(1)} collective-permute-done((bf16[128,1024]{1,0:T(8,128)(2,1)}, bf16[128,1024]{1,0:T(8,128)(2,1)S(1)}, u32[]{:S(2)}, u32[]{:S(2)}) %collective-permute-start.21) | collective-permute-done | bytes 262176 | tf_op jit(solution)/shard_map/ppermute | solution.py:65
  135.8 2.8 pack_core.1
  138.8 8.4 %collective-permute-done.26.refs_2_.refs_6_ = bf16[512,1024]{1,0:T(8,128)(2,1)S(1)} collective-permute-done((bf16[512,1024]{1,0:T(8,128)(2,1)}, bf16[512,1024]{1,0:T(8,128)(2,1)S(1)}, u32[]{:S(2)}, u32[]{:S(2)}) %collective-permute-start.26) | collective-permute-done | bytes 1048608 | tf_op jit(solution)/shard_map/ppermute | solution.py:65
  148.2 3.6 pack_seven.1
  155.7 12.9 %context_forward.1 = (bf16[256,1024]{1,0:T(8,128)(2,1)}, f32[256,1024]{1,0:T(8,128)}, bf16[256,1024]{1,0:T(8,128)(2,1)}) custom-call(s32[3]{0:T(128)} %pad_add_fusion.meta, bf16[256,1024]{1,0:T(8,128)(2,1)} %get-tuple-element.358.query, bf16[528,1024]{1,0:T(8,128)(2,1)} %get-tuple-element.359.own.refs_0_, ...), custom_call_target="tpu_custom_call" | custom-call | flops 1 | bytes 1 | tf_op jit(solution)/shard_map/context_forward/pallas_call | solution.py:1125
  168.7 3.7 pack_eight.1
  172.5 2.9 collective-permute-done.28.refs_7_
  181.9 11.7 %ffn_rows.2 = (f32[512,1024]{1,0:T(8,128)}, bf16[512,1024]{1,0:T(8,128)(2,1)}, bf16[512,1024]{1,0:T(8,128)(2,1)}, bf16[512,1024]{1,0:T(8,128)(2,1)}) custom-call(s32[3]{0:T(128)} %pad_add_fusion.meta, bf16[256,1024]{1,0:T(8,128)(2,1)} %get-tuple-element.391.n2m, bf16[256,1024]{1,0:T(8,128)(2,1)} %copy-done.16, bf16[256,1024]{1,0:T(8,128)(2,1)} %copy-done.5, ...), custom_call_target="tpu_custom_call" | custom-call | flops 1 | bytes 1 | tf_op jit(solution)/shard_map/ffn_rows/pallas_call | solution.py:853
  193.6 10.4 %ffn_weights.2 = (f32[512,1024]{1,0:T(8,128)}, bf16[512,1024]{1,0:T(8,128)(2,1)}, bf16[512,1024]{1,0:T(8,128)(2,1)}, bf16[512,1024]{1,0:T(8,128)(2,1)}, bf16[512...) custom-call(s32[3]{0:T(128)} %pad_add_fusion.meta, ...), custom_call_target="tpu_custom_call" | custom-call | flops 1 | bytes 1 | tf_op jit(solution)/shard_map/ffn_weights/pallas_call | solution.py:924
  207.6 12.9 %ffn_rows.3 = (f32[256,1024]{1,0:T(8,128)}, f32[256,1024]{1,0:T(8,128)}, bf16[512,1024]{1,0:T(8,128)(2,1)}, bf16[512,1024]{1,0:T(8,128)(2,1)}, bf16[512,1024]{1,0:T(8,128)(2,1)}) custom-call(s32[3]{0:T(128)} %pad_add_fusion.meta, bf16[256,1024]{1,0:T(8,128)(2,1)} %get-tuple-element.391.n2m, bf16[256,1024]{1,0:T(8,128)(2,1)} %copy-done.16, ...), custom_call_target="tpu_custom_call" | custom-call | flops 1 | bytes 1 | tf_op jit(solution)/shard_map/ffn_rows/pallas_call | solution.py:853
  220.4 11.3 %ffn_weights.3 = (f32[256,1024]{1,0:T(8,128)}, bf16[256,1024]{1,0:T(8,128)(2,1)}, bf16[512,1024]{1,0:T(8,128)(2,1)}, bf16[512,1024]{1,0:T(8,128)(2,1)}, bf16[512...) custom-call(s32[3]{0:T(128)} %pad_add_fusion.meta, ...), custom_call_target="tpu_custom_call" | custom-call | flops 1 | bytes 1 | tf_op jit(solution)/shard_map/ffn_weights/pallas_call | solution.py:924
  236.5 2.1 collective-permute-start.35
  238.6 18.8 %context_back.1 = (f32[256,1024]{1,0:T(8,128)}, f32[1,1024]{1,0:T(1,128)}, bf16[256,1024]{1,0:T(8,128)(2,1)}, bf16[256,1024]{1,0:T(8,128)(2,1)}, f32[256,2048]{1,0:T(8,128)}, /*index=5*/bf16[528,1024]{1,0:T(8,128)(2,1)}) custom-call(s32[3]{0:T(128)} %pad_add_fusion.meta, f32[256,1024]{1,0:T(8,128)} %get-tuple-element.439.dn_own, ...), custom_call_target="tpu_custom_call" | custom-call | flops 1 | bytes 1 | tf_op jit(solution)/shard_map/context_back/pallas_call | solution.py:1209
  258.4 5.1 %collective-permute-done.35 = bf16[16,8,1024]{2,1,0:T(8,128)(2,1)S(1)} collective-permute-done((bf16[16,8,1024]{2,1,0:T(8,128)(2,1)S(1)}, bf16[16,8,1024]{2,1,0:T(8,128)(2,1)S(1)}, u32[]{:S(2)}, u32[]{:S(2)}) %collective-permute-start.35) | collective-permute-done | bytes 262176 | tf_op jit(solution)/shard_map/ppermute | solution.py:65
  264.8 8.2 %turn_three.1 = (bf16[512,1024]{1,0:T(8,128)(2,1)}, bf16[512,1024]{1,0:T(8,128)(2,1)}, bf16[512,1024]{1,0:T(8,128)(2,1)}, bf16[256,1024]{1,0:T(8,128)(2,1)}, bf1...) custom-call(s32[3]{0:T(128)} %pad_add_fusion.meta, ...), custom_call_target="tpu_custom_call" | custom-call | flops 1 | bytes 1 | tf_op jit(solution)/shard_map/turn_three/pallas_call | solution.py:438
  276.1 4.4 output_grad.1
  280.4 30.5 %collective-permute-done.40.dkv_got = bf16[528,1024]{1,0:T(8,128)(2,1)S(1)} collective-permute-done((bf16[528,1024]{1,0:T(8,128)(2,1)}, bf16[528,1024]{1,0:T(8,128)(2,1)S(1)}, u32[]{:S(2)}, u32[]{:S(2)}) %collective-permute-start.40) | collective-permute-done | bytes 1081376 | tf_op jit(solution)/shard_map/ppermute | solution.py:65
  311.9 7.5 %joint_grad.1 = (bf16[1536,1024]{1,0:T(8,128)(2,1)}, bf16[1536,1024]{1,0:T(8,128)(2,1)}, bf16[256,2048]{1,0:T(8,128)(2,1)}) custom-call(s32[3]{0:T(128)} %pad_add_fusion.meta, bf16[256,1024]{1,0:T(8,128)(2,1)} %get-tuple-element.442.first, bf16[256,1024]{1,0:T(8,128)(2,1)} %get-tuple-element.441.dq, f32[256,2048]{1,0:T(8,128)} %get-tuple-element.443.dkv_own, ...), custom_call_target="tpu_custom_call" | custom-call | flops 1 | bytes 1 | tf_op jit(solution)/shard_map/joint_grad/pallas_call | solution.py:1329
  321.5 5.3 %turn_four.1 = (bf16[256,1024]{1,0:T(8,128)(2,1)}, bf16[256,1024]{1,0:T(8,128)(2,1)}, bf16[256,1024]{1,0:T(8,128)(2,1)}, bf16[128,1024]{1,0:T(8,128)(2,1)}, bf16...) custom-call(s32[3]{0:T(128)} %pad_add_fusion.meta, ...), custom_call_target="tpu_custom_call" | custom-call | flops 1 | bytes 1 | tf_op jit(solution)/shard_map/turn_four/pallas_call | solution.py:438
  329.8 8.8 %input_back.1 = (bf16[256,1024]{1,0:T(8,128)(2,1)}, f32[1,1024]{1,0:T(1,128)}) custom-call(s32[3]{0:T(128)} %pad_add_fusion.meta, bf16[256,1024]{1,0:T(8,128)(2,1)} %get-tuple-element.441.dq, bf16[256,2048]{1,0:T(8,128)(2,1)} %get-tuple-element.503.dkv, f32[256,1024]{1,0:T(8,128)} %get-tuple-element.504.dh, bf16[256,1024]{1,0:T(8,128)(2,1)} %pad_maximum_fusion.1.x, ...), custom_call_target="tpu_custom_call" | custom-call | flops 1 | bytes 1 | tf_op jit(solution)/shard_map/input_back/pallas_call | solution.py:1359
  339.6 6.1 %joint_core.1 = (bf16[256,1024]{1,0:T(8,128)(2,1)}, bf16[384,1024]{1,0:T(8,128)(2,1)}, bf16[384,1024]{1,0:T(8,128)(2,1)}, bf16[256,1024]{1,0:T(8,128)(2,1)}, bf1...) custom-call(s32[3]{0:T(128)} %pad_add_fusion.meta, ...), custom_call_target="tpu_custom_call" | custom-call | flops 1 | bytes 1 | tf_op jit(solution)/shard_map/joint_core/pallas_call | solution.py:438
  348.1 2.1 collective-permute-start.49
  350.3 4.4 %turn_five.1 = (f32[128,1024]{1,0:T(8,128)}, f32[128,1024]{1,0:T(8,128)}, f32[128,1024]{1,0:T(8,128)}, f32[128,1024]{1,0:T(8,128)}, f32[128,1024]{1,0:T(8,128)}, /*index=5*/f32[128,1024]{1,0:T(8,128)}, f32[8,1024]{1,0:T(8,128)}) custom-call(s32[3]{0:T(128)} %pad_add_fusion.meta, bf16[256,1024]{1,0:T(8,128)(2,1)} %copy-done.44, ...), custom_call_target="tpu_custom_call" | custom-call | flops 1 | bytes 1 | tf_op jit(solution)/shard_map/turn_five/pallas_call | solution.py:438
  354.7 7.5 %collective-permute-done.49 = bf16[16,8,1024]{2,1,0:T(8,128)(2,1)} collective-permute-done((bf16[16,8,1024]{2,1,0:T(8,128)(2,1)}, bf16[16,8,1024]{2,1,0:T(8,128)(2,1)}, u32[]{:S(2)}, u32[]{:S(2)}) %collective-permute-start.49) | collective-permute-done | bytes 262176 | tf_op jit(solution)/shard_map/ppermute | solution.py:65
  364.1 3.6 collective-permute-done.51.refs_3_
  369.0 4.3 turn_nine.1
  378.1 8.4 %collective-permute-done.59.refs_20_ = bf16[128,1024]{1,0:T(8,128)(2,1)S(1)} collective-permute-done((bf16[128,1024]{1,0:T(8,128)(2,1)S(1)}, bf16[128,1024]{1,0:T(8,128)(2,1)S(1)}, u32[]{:S(2)}, u32[]{:S(2)}) %collective-permute-start.59) | collective-permute-done | bytes 262176 | tf_op jit(solution)/shard_map/ppermute | solution.py:65
  389.1 3.2 turn_ten.1
  396.5 4.1 collective-permute-done.62.refs_4_
  401.4 3.7 turn_last.1
  407.2 2.6 all-to-all-start
  411.8 9.1 %all-to-all-done = f32[32,1,2176]{2,1,0:T(1,128)S(1)} async-done(((f32[32,1,2176]{2,1,0:T(1,128)}), f32[32,1,2176]{2,1,0:T(1,128)S(1)}, u32[]{:S(2)}, u32[]{:S(2)}) %all-to-all-start) | async-done | bytes 278560 | tf_op jit(solution)/shard_map/all_to_all | solution.py:1800
  425.1 12.8 %adam_matrices.1 = (f32[64,8192]{1,0:T(8,128)}, f32[64,8192]{1,0:T(8,128)}, f32[64,8192]{1,0:T(8,128)}, f32[64,3072]{1,0:T(8,128)}, f32[64,3072]{1,0:T(8,128)}, ...) custom-call(s32[3]{0:T(128)} %pad_add_fusion.meta, ...), custom_call_target="tpu_custom_call" | custom-call | flops 1 | bytes 1 | tf_op jit(solution)/shard_map/adam_matrices/pallas_call | solution.py:1477
  (283 shorter events, 99.7 us)
Async XLA Ops:
  22.4 12.5 %collective-permute-start.5 = (bf16[160,1024]{1,0:T(8,128)(2,1)}, bf16[160,1024]{1,0:T(8,128)(2,1)S(1)}, u32[]{:S(2)}, u32[]{:S(2)}) collective-permute-start(bf16[160,1024]{1,0:T(8,128)(2,1)} %get-tuple-element.325), channel_id=1, source_target_pairs={{0,4},{1,5},{2,6},{3,7},{4,0},{5,1},{6,2},{7,3},{8,12},{9,13},{10,... | collective-permute-start | bytes 983048 | tf_op jit(solution)/shard_map/ppermute | solution.py:65
  23.5 13.3 %collective-permute-start.6 = (bf16[160,1024]{1,0:T(8,128)(2,1)}, bf16[160,1024]{1,0:T(8,128)(2,1)S(1)}, u32[]{:S(2)}, u32[]{:S(2)}) collective-permute-start(bf16[160,1024]{1,0:T(8,128)(2,1)} %get-tuple-element.326), channel_id=1, source_target_pairs={{0,8},{1,9},{2,10},{3,11},{4,12},{5,13},{6,14},{7,15},{8,0},{9,1},... | collective-permute-start | bytes 983048 | tf_op jit(solution)/shard_map/ppermute | solution.py:65
  23.9 12.9 %collective-permute-start.7 = (bf16[160,1024]{1,0:T(8,128)(2,1)}, bf16[160,1024]{1,0:T(8,128)(2,1)S(1)}, u32[]{:S(2)}, u32[]{:S(2)}) collective-permute-start(bf16[160,1024]{1,0:T(8,128)(2,1)} %get-tuple-element.327), channel_id=1, source_target_pairs={{0,2},{1,3},{2,0},{3,1},{4,6},{5,7},{6,4},{7,5},{8,10},{9,11},{10,... | collective-permute-start | bytes 983048 | tf_op jit(solution)/shard_map/ppermute | solution.py:65
  43.3 24.2 %collective-permute-start.11 = (bf16[832,1024]{1,0:T(8,128)(2,1)}, bf16[832,1024]{1,0:T(8,128)(2,1)}, u32[]{:S(2)}, u32[]{:S(2)}) collective-permute-start(bf16[832,1024]{1,0:T(8,128)(2,1)} %get-tuple-element.342), channel_id=1, source_target_pairs={{0,1},{1,0},{2,3},{3,2},{4,5},{5,4},{6,7},{7,6},{8,9},{9,8},{10,11... | collective-permute-start | bytes 5111816 | tf_op jit(solution)/shard_map/ppermute | solution.py:65
  43.4 15.3 %collective-permute-start.13 = (bf16[128,1024]{1,0:T(8,128)(2,1)S(1)}, bf16[128,1024]{1,0:T(8,128)(2,1)S(1)}, u32[]{:S(2)}, u32[]{:S(2)}) collective-permute-start(bf16[128,1024]{1,0:T(8,128)(2,1)S(1)} %copy-done.62), channel_id=1, source_target_pairs={{0,16},{1,17},{2,18},{3,19},{4,20},{5,21},{6,22},{7,23},{8,24},{9,... | collective-permute-start | bytes 786440 | tf_op jit(solution)/shard_map/ppermute | solution.py:65
  45.0 22.5 %collective-permute-start.8 = (bf16[320,1024]{1,0:T(8,128)(2,1)}, bf16[320,1024]{1,0:T(8,128)(2,1)S(1)}, u32[]{:S(2)}, u32[]{:S(2)}) collective-permute-start(bf16[320,1024]{1,0:T(8,128)(2,1)} %get-tuple-element.339), channel_id=1, source_target_pairs={{0,8},{1,9},{2,10},{3,11},{4,12},{5,13},{6,14},{7,15},{8,0},{9,1},... | collective-permute-start | bytes 1966088 | tf_op jit(solution)/shard_map/ppermute | solution.py:65
  46.6 20.9 %collective-permute-start.9 = (bf16[320,1024]{1,0:T(8,128)(2,1)}, bf16[320,1024]{1,0:T(8,128)(2,1)S(1)}, u32[]{:S(2)}, u32[]{:S(2)}) collective-permute-start(bf16[320,1024]{1,0:T(8,128)(2,1)} %get-tuple-element.340), channel_id=1, source_target_pairs={{0,2},{1,3},{2,0},{3,1},{4,6},{5,7},{6,4},{7,5},{8,10},{9,11},{10,... | collective-permute-start | bytes 1966088 | tf_op jit(solution)/shard_map/ppermute | solution.py:65
  47.7 19.8 %collective-permute-start.10 = (bf16[320,1024]{1,0:T(8,128)(2,1)}, bf16[320,1024]{1,0:T(8,128)(2,1)S(1)}, u32[]{:S(2)}, u32[]{:S(2)}) collective-permute-start(bf16[320,1024]{1,0:T(8,128)(2,1)} %get-tuple-element.341), channel_id=1, source_target_pairs={{0,4},{1,5},{2,6},{3,7},{4,0},{5,1},{6,2},{7,3},{8,12},{9,13},{10,... | collective-permute-start | bytes 1966088 | tf_op jit(solution)/shard_map/ppermute | solution.py:65
  71.8 20.0 %collective-permute-start.16 = (bf16[256,1024]{1,0:T(8,128)(2,1)S(1)}, bf16[256,1024]{1,0:T(8,128)(2,1)S(1)}, u32[]{:S(2)}, u32[]{:S(2)}) collective-permute-start(bf16[256,1024]{1,0:T(8,128)(2,1)S(1)} %copy-done.3), channel_id=1, source_target_pairs={{0,8},{1,9},{2,10},{3,11},{4,12},{5,13},{6,14},{7,15},{8,0},{9,1},... | collective-permute-start | bytes 1572872 | tf_op jit(solution)/shard_map/ppermute | solution.py:65
  72.2 19.7 %collective-permute-start.17 = (bf16[256,1024]{1,0:T(8,128)(2,1)S(1)}, bf16[256,1024]{1,0:T(8,128)(2,1)S(1)}, u32[]{:S(2)}, u32[]{:S(2)}) collective-permute-start(bf16[256,1024]{1,0:T(8,128)(2,1)S(1)} %copy-done.10), channel_id=1, source_target_pairs={{0,2},{1,3},{2,0},{3,1},{4,6},{5,7},{6,4},{7,5},{8,10},{9,11},{10,... | collective-permute-start | bytes 1572872 | tf_op jit(solution)/shard_map/ppermute | solution.py:65
  73.1 18.8 %collective-permute-start.18 = (bf16[256,1024]{1,0:T(8,128)(2,1)S(1)}, bf16[256,1024]{1,0:T(8,128)(2,1)S(1)}, u32[]{:S(2)}, u32[]{:S(2)}) collective-permute-start(bf16[256,1024]{1,0:T(8,128)(2,1)S(1)} %copy-done.11), channel_id=1, source_target_pairs={{0,4},{1,5},{2,6},{3,7},{4,0},{5,1},{6,2},{7,3},{8,12},{9,13},{10,... | collective-permute-start | bytes 1572872 | tf_op jit(solution)/shard_map/ppermute | solution.py:65
  75.2 15.0 %collective-permute-start.19 = (bf16[128,1024]{1,0:T(8,128)(2,1)}, bf16[128,1024]{1,0:T(8,128)(2,1)S(1)}, u32[]{:S(2)}, u32[]{:S(2)}) collective-permute-start(bf16[128,1024]{1,0:T(8,128)(2,1)} %select_bitcast_fusion.2), channel_id=1, source_target_pairs={{0,16},{1,17},{2,18},{3,19},{4,20},{5,21},{6,22},{7,23},{8,24},{9,... | collective-permute-start | bytes 786440 | tf_op jit(solution)/shard_map/ppermute | solution.py:65
  85.5 61.7 %collective-permute-start.15 = (bf16[528,1024]{1,0:T(8,128)(2,1)}, bf16[528,1024]{1,0:T(8,128)(2,1)}, u32[]{:S(2)}, u32[]{:S(2)}) collective-permute-start(bf16[528,1024]{1,0:T(8,128)(2,1)} %get-tuple-element.359.own.refs_0_), channel_id=1, source_target_pairs={{0,16},{1,17},{2,18},{3,19},{4,20},{5,21},{6,22},{7,23},{8,24},{9,... | collective-permute-start | bytes 3244040 | tf_op jit(solution)/shard_map/ppermute | solution.py:65
  97.3 41.5 %collective-permute-start.24 = (bf16[512,1024]{1,0:T(8,128)(2,1)}, bf16[512,1024]{1,0:T(8,128)(2,1)S(1)}, u32[]{:S(2)}, u32[]{:S(2)}) collective-permute-start(bf16[512,1024]{1,0:T(8,128)(2,1)} %get-tuple-element.371), channel_id=1, source_target_pairs={{0,2},{1,3},{2,0},{3,1},{4,6},{5,7},{6,4},{7,5},{8,10},{9,11},{10,... | collective-permute-start | bytes 3145736 | tf_op jit(solution)/shard_map/ppermute | solution.py:65
  98.4 40.4 %collective-permute-start.25 = (bf16[512,1024]{1,0:T(8,128)(2,1)}, bf16[512,1024]{1,0:T(8,128)(2,1)S(1)}, u32[]{:S(2)}, u32[]{:S(2)}) collective-permute-start(bf16[512,1024]{1,0:T(8,128)(2,1)} %get-tuple-element.372), channel_id=1, source_target_pairs={{0,4},{1,5},{2,6},{3,7},{4,0},{5,1},{6,2},{7,3},{8,12},{9,13},{10,... | collective-permute-start | bytes 3145736 | tf_op jit(solution)/shard_map/ppermute | solution.py:65
  99.8 47.4 %collective-permute-start.26 = (bf16[512,1024]{1,0:T(8,128)(2,1)}, bf16[512,1024]{1,0:T(8,128)(2,1)S(1)}, u32[]{:S(2)}, u32[]{:S(2)}) collective-permute-start(bf16[512,1024]{1,0:T(8,128)(2,1)} %get-tuple-element.373), channel_id=1, source_target_pairs={{0,8},{1,9},{2,10},{3,11},{4,12},{5,13},{6,14},{7,15},{8,0},{9,1},... | collective-permute-start | bytes 3145736 | tf_op jit(solution)/shard_map/ppermute | solution.py:65
  103.1 24.7 %collective-permute-start.20 = (bf16[128,1024]{1,0:T(8,128)(2,1)}, bf16[128,1024]{1,0:T(8,128)(2,1)S(1)}, u32[]{:S(2)}, u32[]{:S(2)}) collective-permute-start(bf16[128,1024]{1,0:T(8,128)(2,1)} %get-tuple-element.380), channel_id=1, source_target_pairs={{0,2},{1,3},{2,0},{3,1},{4,6},{5,7},{6,4},{7,5},{8,10},{9,11},{10,... | collective-permute-start | bytes 786440 | tf_op jit(solution)/shard_map/ppermute | solution.py:65
  138.7 17.0 %collective-permute-start.22 = (bf16[512,1024]{1,0:T(8,128)(2,1)}, bf16[512,1024]{1,0:T(8,128)(2,1)}, u32[]{:S(2)}, u32[]{:S(2)}) collective-permute-start(bf16[512,1024]{1,0:T(8,128)(2,1)} %pack_core.1), channel_id=1, source_target_pairs={{0,1},{1,0},{2,3},{3,2},{4,5},{5,4},{6,7},{7,6},{8,9},{9,8},{10,11... | collective-permute-start | bytes 3145736 | tf_op jit(solution)/shard_map/ppermute | solution.py:65
  151.8 23.5 %collective-permute-start.28 = (bf16[512,1024]{1,0:T(8,128)(2,1)}, bf16[512,1024]{1,0:T(8,128)(2,1)S(1)}, u32[]{:S(2)}, u32[]{:S(2)}) collective-permute-start(bf16[512,1024]{1,0:T(8,128)(2,1)} %get-tuple-element.403), channel_id=1, source_target_pairs={{0,2},{1,3},{2,0},{3,1},{4,6},{5,7},{6,4},{7,5},{8,10},{9,11},{10,... | collective-permute-start | bytes 3145736 | tf_op jit(solution)/shard_map/ppermute | solution.py:65
  152.9 23.2 %collective-permute-start.29 = (bf16[512,1024]{1,0:T(8,128)(2,1)}, bf16[512,1024]{1,0:T(8,128)(2,1)S(1)}, u32[]{:S(2)}, u32[]{:S(2)}) collective-permute-start(bf16[512,1024]{1,0:T(8,128)(2,1)} %get-tuple-element.404), channel_id=1, source_target_pairs={{0,4},{1,5},{2,6},{3,7},{4,0},{5,1},{6,2},{7,3},{8,12},{9,13},{10,... | collective-permute-start | bytes 3145736 | tf_op jit(solution)/shard_map/ppermute | solution.py:65
  153.4 23.1 %collective-permute-start.30 = (bf16[512,1024]{1,0:T(8,128)(2,1)}, bf16[512,1024]{1,0:T(8,128)(2,1)}, u32[]{:S(2)}, u32[]{:S(2)}) collective-permute-start(bf16[512,1024]{1,0:T(8,128)(2,1)} %get-tuple-element.405), channel_id=1, source_target_pairs={{0,8},{1,9},{2,10},{3,11},{4,12},{5,13},{6,14},{7,15},{8,0},{9,1},... | collective-permute-start | bytes 3145736 | tf_op jit(solution)/shard_map/ppermute | solution.py:65
  154.9 13.8 %collective-permute-start.27 = (bf16[256,1024]{1,0:T(8,128)(2,1)S(1)}, bf16[256,1024]{1,0:T(8,128)(2,1)S(1)}, u32[]{:S(2)}, u32[]{:S(2)}) collective-permute-start(bf16[256,1024]{1,0:T(8,128)(2,1)S(1)} %multiply_convert_fusion.cm.cot), channel_id=1, source_target_pairs={{0,1},{1,0},{2,3},{3,2},{4,5},{5,4},{6,7},{7,6},{8,9},{9,8},{10,11... | collective-permute-start | bytes 1572872 | tf_op jit(solution)/shard_map/ppermute | solution.py:65
  176.5 27.5 %collective-permute-start.31 = (bf16[512,1024]{1,0:T(8,128)(2,1)}, bf16[512,1024]{1,0:T(8,128)(2,1)}, u32[]{:S(2)}, u32[]{:S(2)}) collective-permute-start(bf16[512,1024]{1,0:T(8,128)(2,1)} %get-tuple-element.418), channel_id=1, source_target_pairs={{0,8},{1,9},{2,10},{3,11},{4,12},{5,13},{6,14},{7,15},{8,0},{9,1},... | collective-permute-start | bytes 3145736 | tf_op jit(solution)/shard_map/ppermute | solution.py:65
  176.7 27.3 %collective-permute-start.32 = (bf16[512,1024]{1,0:T(8,128)(2,1)}, bf16[512,1024]{1,0:T(8,128)(2,1)}, u32[]{:S(2)}, u32[]{:S(2)}) collective-permute-start(bf16[512,1024]{1,0:T(8,128)(2,1)} %get-tuple-element.419), channel_id=1, source_target_pairs={{0,2},{1,3},{2,0},{3,1},{4,6},{5,7},{6,4},{7,5},{8,10},{9,11},{10,... | collective-permute-start | bytes 3145736 | tf_op jit(solution)/shard_map/ppermute | solution.py:65
  177.8 26.3 %collective-permute-start.33 = (bf16[512,1024]{1,0:T(8,128)(2,1)}, bf16[512,1024]{1,0:T(8,128)(2,1)S(1)}, u32[]{:S(2)}, u32[]{:S(2)}) collective-permute-start(bf16[512,1024]{1,0:T(8,128)(2,1)} %get-tuple-element.420), channel_id=1, source_target_pairs={{0,4},{1,5},{2,6},{3,7},{4,0},{5,1},{6,2},{7,3},{8,12},{9,13},{10,... | collective-permute-start | bytes 3145736 | tf_op jit(solution)/shard_map/ppermute | solution.py:65
  204.1 28.2 %collective-permute-start.36 = (bf16[512,1024]{1,0:T(8,128)(2,1)}, bf16[512,1024]{1,0:T(8,128)(2,1)S(1)}, u32[]{:S(2)}, u32[]{:S(2)}) collective-permute-start(bf16[512,1024]{1,0:T(8,128)(2,1)} %get-tuple-element.436), channel_id=1, source_target_pairs={{0,2},{1,3},{2,0},{3,1},{4,6},{5,7},{6,4},{7,5},{8,10},{9,11},{10,... | collective-permute-start | bytes 3145736 | tf_op jit(solution)/shard_map/ppermute | solution.py:65
  205.2 27.1 %collective-permute-start.37 = (bf16[512,1024]{1,0:T(8,128)(2,1)}, bf16[512,1024]{1,0:T(8,128)(2,1)S(1)}, u32[]{:S(2)}, u32[]{:S(2)}) collective-permute-start(bf16[512,1024]{1,0:T(8,128)(2,1)} %get-tuple-element.437), channel_id=1, source_target_pairs={{0,4},{1,5},{2,6},{3,7},{4,0},{5,1},{6,2},{7,3},{8,12},{9,13},{10,... | collective-permute-start | bytes 3145736 | tf_op jit(solution)/shard_map/ppermute | solution.py:65
  205.7 26.6 %collective-permute-start.38 = (bf16[512,1024]{1,0:T(8,128)(2,1)}, bf16[512,1024]{1,0:T(8,128)(2,1)}, u32[]{:S(2)}, u32[]{:S(2)}) collective-permute-start(bf16[512,1024]{1,0:T(8,128)(2,1)} %get-tuple-element.438), channel_id=1, source_target_pairs={{0,8},{1,9},{2,10},{3,11},{4,12},{5,13},{6,14},{7,15},{8,0},{9,1},... | collective-permute-start | bytes 3145736 | tf_op jit(solution)/shard_map/ppermute | solution.py:65
  232.3 31.2 %collective-permute-start.41 = (bf16[512,1024]{1,0:T(8,128)(2,1)}, bf16[512,1024]{1,0:T(8,128)(2,1)}, u32[]{:S(2)}, u32[]{:S(2)}) collective-permute-start(bf16[512,1024]{1,0:T(8,128)(2,1)} %get-tuple-element.451), channel_id=1, source_target_pairs={{0,4},{1,5},{2,6},{3,7},{4,0},{5,1},{6,2},{7,3},{8,12},{9,13},{10,... | collective-permute-start | bytes 3145736 | tf_op jit(solution)/shard_map/ppermute | solution.py:65
  233.9 30.9 %collective-permute-start.42 = (bf16[512,1024]{1,0:T(8,128)(2,1)}, bf16[512,1024]{1,0:T(8,128)(2,1)}, u32[]{:S(2)}, u32[]{:S(2)}) collective-permute-start(bf16[512,1024]{1,0:T(8,128)(2,1)} %get-tuple-element.454), channel_id=1, source_target_pairs={{0,8},{1,9},{2,10},{3,11},{4,12},{5,13},{6,14},{7,15},{8,0},{9,1},... | collective-permute-start | bytes 3145736 | tf_op jit(solution)/shard_map/ppermute | solution.py:65
  234.1 30.7 %collective-permute-start.43 = (bf16[512,1024]{1,0:T(8,128)(2,1)}, bf16[512,1024]{1,0:T(8,128)(2,1)}, u32[]{:S(2)}, u32[]{:S(2)}) collective-permute-start(bf16[512,1024]{1,0:T(8,128)(2,1)} %get-tuple-element.457), channel_id=1, source_target_pairs={{0,2},{1,3},{2,0},{3,1},{4,6},{5,7},{6,4},{7,5},{8,10},{9,11},{10,... | collective-permute-start | bytes 3145736 | tf_op jit(solution)/shard_map/ppermute | solution.py:65
  236.5 27.0 %collective-permute-start.35 = (bf16[16,8,1024]{2,1,0:T(8,128)(2,1)S(1)}, bf16[16,8,1024]{2,1,0:T(8,128)(2,1)S(1)}, u32[]{:S(2)}, u32[]{:S(2)}) collective-permute-start(bf16[16,8,1024]{2,1,0:T(8,128)(2,1)S(1)} %select_bitcast_fusion.1), channel_id=1, source_target_pairs={{0,16},{1,17},{2,18},{3,19},{4,20},{5,21},{6,22},{7,23},{8,24},{9,... | collective-permute-start | bytes 786440 | tf_op jit(solution)/shard_map/ppermute | solution.py:65
  257.5 53.4 %collective-permute-start.40 = (bf16[528,1024]{1,0:T(8,128)(2,1)}, bf16[528,1024]{1,0:T(8,128)(2,1)S(1)}, u32[]{:S(2)}, u32[]{:S(2)}) collective-permute-start(bf16[528,1024]{1,0:T(8,128)(2,1)} %get-tuple-element.444), channel_id=1, source_target_pairs={{0,16},{1,17},{2,18},{3,19},{4,20},{5,21},{6,22},{7,23},{8,24},{9,... | collective-permute-start | bytes 3244040 | tf_op jit(solution)/shard_map/ppermute | solution.py:65
  273.0 46.4 %collective-permute-start.46 = (bf16[512,1024]{1,0:T(8,128)(2,1)}, bf16[512,1024]{1,0:T(8,128)(2,1)S(1)}, u32[]{:S(2)}, u32[]{:S(2)}) collective-permute-start(bf16[512,1024]{1,0:T(8,128)(2,1)} %get-tuple-element.471), channel_id=1, source_target_pairs={{0,2},{1,3},{2,0},{3,1},{4,6},{5,7},{6,4},{7,5},{8,10},{9,11},{10,... | collective-permute-start | bytes 3145736 | tf_op jit(solution)/shard_map/ppermute | solution.py:65
  274.1 45.4 %collective-permute-start.44 = (bf16[512,1024]{1,0:T(8,128)(2,1)}, bf16[512,1024]{1,0:T(8,128)(2,1)}, u32[]{:S(2)}, u32[]{:S(2)}) collective-permute-start(bf16[512,1024]{1,0:T(8,128)(2,1)} %get-tuple-element.472), channel_id=1, source_target_pairs={{0,4},{1,5},{2,6},{3,7},{4,0},{5,1},{6,2},{7,3},{8,12},{9,13},{10,... | collective-permute-start | bytes 3145736 | tf_op jit(solution)/shard_map/ppermute | solution.py:65
  274.7 46.8 %collective-permute-start.45 = (bf16[512,1024]{1,0:T(8,128)(2,1)}, bf16[512,1024]{1,0:T(8,128)(2,1)}, u32[]{:S(2)}, u32[]{:S(2)}) collective-permute-start(bf16[512,1024]{1,0:T(8,128)(2,1)} %get-tuple-element.473), channel_id=1, source_target_pairs={{0,8},{1,9},{2,10},{3,11},{4,12},{5,13},{6,14},{7,15},{8,0},{9,1},... | collective-permute-start | bytes 3145736 | tf_op jit(solution)/shard_map/ppermute | solution.py:65
  327.4 20.8 %collective-permute-start.53 = (bf16[256,1024]{1,0:T(8,128)(2,1)}, bf16[256,1024]{1,0:T(8,128)(2,1)S(1)}, u32[]{:S(2)}, u32[]{:S(2)}) collective-permute-start(bf16[256,1024]{1,0:T(8,128)(2,1)} %get-tuple-element.494), channel_id=1, source_target_pairs={{0,2},{1,3},{2,0},{3,1},{4,6},{5,7},{6,4},{7,5},{8,10},{9,11},{10,... | collective-permute-start | bytes 1572872 | tf_op jit(solution)/shard_map/ppermute | solution.py:65
  328.3 22.0 %collective-permute-start.54 = (bf16[256,1024]{1,0:T(8,128)(2,1)}, bf16[256,1024]{1,0:T(8,128)(2,1)}, u32[]{:S(2)}, u32[]{:S(2)}) collective-permute-start(bf16[256,1024]{1,0:T(8,128)(2,1)} %get-tuple-element.495), channel_id=1, source_target_pairs={{0,4},{1,5},{2,6},{3,7},{4,0},{5,1},{6,2},{7,3},{8,12},{9,13},{10,... | collective-permute-start | bytes 1572872 | tf_op jit(solution)/shard_map/ppermute | solution.py:65
  329.8 20.5 %collective-permute-start.55 = (bf16[256,1024]{1,0:T(8,128)(2,1)}, bf16[256,1024]{1,0:T(8,128)(2,1)}, u32[]{:S(2)}, u32[]{:S(2)}) collective-permute-start(bf16[256,1024]{1,0:T(8,128)(2,1)} %get-tuple-element.496), channel_id=1, source_target_pairs={{0,8},{1,9},{2,10},{3,11},{4,12},{5,13},{6,14},{7,15},{8,0},{9,1},... | collective-permute-start | bytes 1572872 | tf_op jit(solution)/shard_map/ppermute | solution.py:65
  345.7 21.9 %collective-permute-start.50 = (bf16[384,1024]{1,0:T(8,128)(2,1)}, bf16[384,1024]{1,0:T(8,128)(2,1)S(1)}, u32[]{:S(2)}, u32[]{:S(2)}) collective-permute-start(bf16[384,1024]{1,0:T(8,128)(2,1)} %get-tuple-element.512), channel_id=1, source_target_pairs={{0,4},{1,5},{2,6},{3,7},{4,0},{5,1},{6,2},{7,3},{8,12},{9,13},{10,... | collective-permute-start | bytes 2359304 | tf_op jit(solution)/shard_map/ppermute | solution.py:65
  346.3 21.4 %collective-permute-start.52 = (bf16[384,1024]{1,0:T(8,128)(2,1)}, bf16[384,1024]{1,0:T(8,128)(2,1)S(1)}, u32[]{:S(2)}, u32[]{:S(2)}) collective-permute-start(bf16[384,1024]{1,0:T(8,128)(2,1)} %get-tuple-element.516), channel_id=1, source_target_pairs={{0,2},{1,3},{2,0},{3,1},{4,6},{5,7},{6,4},{7,5},{8,10},{9,11},{10,... | collective-permute-start | bytes 2359304 | tf_op jit(solution)/shard_map/ppermute | solution.py:65
  348.1 14.1 %collective-permute-start.49 = (bf16[16,8,1024]{2,1,0:T(8,128)(2,1)}, bf16[16,8,1024]{2,1,0:T(8,128)(2,1)}, u32[]{:S(2)}, u32[]{:S(2)}) collective-permute-start(bf16[16,8,1024]{2,1,0:T(8,128)(2,1)} %select_bitcast_fusion), channel_id=1, source_target_pairs={{0,16},{1,17},{2,18},{3,19},{4,20},{5,21},{6,22},{7,23},{8,24},{9,... | collective-permute-start | bytes 786440 | tf_op jit(solution)/shard_map/ppermute | solution.py:65
  350.3 17.4 %collective-permute-start.51 = (bf16[256,1024]{1,0:T(8,128)(2,1)}, bf16[256,1024]{1,0:T(8,128)(2,1)S(1)}, u32[]{:S(2)}, u32[]{:S(2)}) collective-permute-start(bf16[256,1024]{1,0:T(8,128)(2,1)} %get-tuple-element.510), channel_id=1, source_target_pairs={{0,8},{1,9},{2,10},{3,11},{4,12},{5,13},{6,14},{7,15},{8,0},{9,1},... | collective-permute-start | bytes 1572872 | tf_op jit(solution)/shard_map/ppermute | solution.py:65
  373.3 15.0 %collective-permute-start.57 = (bf16[192,1024]{1,0:T(8,128)(2,1)}, bf16[192,1024]{1,0:T(8,128)(2,1)S(1)}, u32[]{:S(2)}, u32[]{:S(2)}) collective-permute-start(bf16[192,1024]{1,0:T(8,128)(2,1)} %get-tuple-element.539), channel_id=1, source_target_pairs={{0,8},{1,9},{2,10},{3,11},{4,12},{5,13},{6,14},{7,15},{8,0},{9,1},... | collective-permute-start | bytes 1179656 | tf_op jit(solution)/shard_map/ppermute | solution.py:65
  374.3 13.9 %collective-permute-start.58 = (bf16[192,1024]{1,0:T(8,128)(2,1)}, bf16[192,1024]{1,0:T(8,128)(2,1)S(1)}, u32[]{:S(2)}, u32[]{:S(2)}) collective-permute-start(bf16[192,1024]{1,0:T(8,128)(2,1)} %get-tuple-element.542), channel_id=1, source_target_pairs={{0,2},{1,3},{2,0},{3,1},{4,6},{5,7},{6,4},{7,5},{8,10},{9,11},{10,... | collective-permute-start | bytes 1179656 | tf_op jit(solution)/shard_map/ppermute | solution.py:65
  396.5 14.2 %collective-permute-start.63 = (f32[128,1024]{1,0:T(8,128)}, f32[128,1024]{1,0:T(8,128)S(1)}, u32[]{:S(2)}, u32[]{:S(2)}) collective-permute-start(f32[128,1024]{1,0:T(8,128)} %get-tuple-element.577), channel_id=1, source_target_pairs={{0,1},{1,0},{2,3},{3,2},{4,5},{5,4},{6,7},{7,6},{8,9},{9,8},{10,11... | collective-permute-start | bytes 1572872 | tf_op jit(solution)/shard_map/ppermute | solution.py:65
  407.2 13.7 %all-to-all-start = ((f32[32,1,2176]{2,1,0:T(1,128)}), f32[32,1,2176]{2,1,0:T(1,128)S(1)}, u32[]{:S(2)}, u32[]{:S(2)}) async-start(f32[32,1,2176]{2,1,0:T(1,128)} %copy.43), calls=%async_computation | async-start | bytes 557056 | tf_op jit(solution)/shard_map/all_to_all | solution.py:1800
  410.7 13.5 %collective-permute-start.64 = (f32[128,1024]{1,0:T(8,128)}, f32[128,1024]{1,0:T(8,128)S(1)}, u32[]{:S(2)}, u32[]{:S(2)}) collective-permute-start(f32[128,1024]{1,0:T(8,128)} %get-tuple-element.579), channel_id=1, source_target_pairs={{0,1},{1,0},{2,3},{3,2},{4,5},{5,4},{6,7},{7,6},{8,9},{9,8},{10,11... | collective-permute-start | bytes 1572872 | tf_op jit(solution)/shard_map/ppermute | solution.py:65
  (81 other events, 559.4 us)

commit v5 on v4

--- a/solution.py
+++ b/solution.py
@@ -1410,13 +1410,11 @@
 
     pieces = []
     gradients = [load(i, whole(held[i])) for i in (3, 4, 5, 6)]
-    for c in range(ew.shape[1] // width):
-        where = (slice(None), slice(c * width, (c + 1) * width))
+    for c in range(4):
+        where = (slice(None), slice(2 * c * width, 2 * (c + 1) * width))
         pieces.append(("expand", c, where, [load(i, where) for i in (0, 1, 2)]))
-    for c in range(jw.shape[1] // width):
-        where = (slice(None), slice(c * width, (c + 1) * width))
-        copies = [load(10, (c,))] + [load(i, where) for i in (7, 8, 9)]
-        pieces.append(("joint", c, where, copies))
+    copies = [load(i, whole(held[i])) for i in (10, 7, 8, 9)]
+    pieces.append(("joint", 0, whole(jw), copies))
     copies = [load(i, whole(held[i])) for i in (14, 15, 11, 12, 13)]
     pieces.append(("output", 0, None, copies))
     more = [load(i, whole(held[i])) for i in (19, 20)]
@@ -1440,20 +1438,22 @@
     for kind, c, where, copies in pieces:
         finish(copies)
         if kind == "expand":
-            turn = ((c // 2) % 2) ^ (1 - group)
-            r = slice((c // 4) * rows, (c // 4 + 1) * rows)
-            for q in range(CHIPS):
-                near = (c % 2) * (CHIPS // 2) + q // 2
-                near = (r, slice(near * block, (near + 1) * block))
+            turn = (c % 2) ^ (1 - group)
+            r = slice((c // 2) * rows, (c // 2 + 1) * rows)
+            for q in range(2 * CHIPS):
+                near = (r, slice((q // 2) * block, (q // 2 + 1) * block))
                 own = jnp.where(turn == 0, own_a[near], own_b[near])
                 got = jnp.where(turn == 0, got_a[near], got_b[near])
                 grad = jnp.where(core == q % 2, own, got)
-                cols = (slice(None), slice(c * width + q * block, c * width + (q + 1) * block))
+                low = 2 * c * width + q * block
+                cols = (slice(None), slice(low, low + block))
                 adam_in_place(k, ew, em, ev, grad, cols, MATRIX_RATE, MATRIX_DECAY)
             for i in range(3):
                 store(i, i, where)
         elif kind == "joint":
-            adam_in_place(k, jw, jm, jv, jg[c], where, MATRIX_RATE, MATRIX_DECAY)
+            for part in range(jg.shape[0]):
+                cols = (slice(None), slice(part * width, (part + 1) * width))
+                adam_in_place(k, jw, jm, jv, jg[part], cols, MATRIX_RATE, MATRIX_DECAY)
             for i in range(3):
                 store(3 + i, 7 + i, where)
         elif kind == "output":
@@ -1622,10 +1622,10 @@
         gains_all,
         output_chains,
     )
+    second_other = cube.swap(second, 0)
     eight = begin("pack_eight").gather(part_b, 2).run(
-        seven.packed, cot_other, gate=(seven.got, second)
-    )
-    second_other = cube.swap(second, 0)
+        seven.packed, cot_other, gate=(seven.got, second_other)
+    )
     row_args = (meta, second, second_other, cot_live, cot_other)
     dn_a, *kept_a = ffn_rows(*row_args, part_a, None)
     f_a, *grad_a = ffn_weights(*row_args, *kept_a, part_a[2], None)

time: 446 us -> 443 us (level)
    unnamed x127 -> x123, local copies, waits for them, and re-layouts: 14.3 us -> 12.8 us
  transfers between devices with their start and end apart: 66 -> 66, of which waited for: 24 -> 23; matrix products, arithmetic and copies ran while one was open for 4% -> 4% of each run, Pallas kernels for 35% -> 35%
where the time goes in v5:
time: 443 us; the launch traced here: 436 us
  Pallas kernels  189 us (43%)
  waiting for transfers between devices  145 us (33%)
  starting transfers between devices  65.9 us (15%)
  local copies, waits for them, and re-layouts  16.7 us (4%)
  other arithmetic  13.9 us (3%)
  between operations  4.51 us (1%)
    ppermute x65, waiting for transfers between devices, swap(): return lax.ppermute(value, 'fsdp', pairs)  136 us
    pallas_call x16, Pallas kernels, run(): pl.pallas_call(functools.partial(jobs_kernel, self.work, len(inputs), sel...  65.1 us
    ppermute x65, starting transfers between devices, swap(): return lax.ppermute(value, 'fsdp', pairs)  63.3 us
    pallas_call x2, Pallas kernels, ffn_rows(): pl.pallas_call(functools.partial(ffn_rows_kernel, first, len(arrays), tab...  24.6 us
    pallas_call x2, Pallas kernels, ffn_weights(): pl.pallas_call(functools.partial(ffn_weights_kernel, first, len(arrays),...  21.7 us
    pallas_call x1, Pallas kernels, context_back(): pl.pallas_call(functools.partial(context_back_kernel, run, width // HEADS...  18.8 us
    pallas_call x1, Pallas kernels, context_forward(): pl.pallas_call(functools.partial(context_kernel, run, width // HEADS, len...  12.9 us
    unnamed x123, local copies, waits for them, and re-layouts  12.8 us
  transfers between devices with their start and end apart: 66, of which 23 were waited for; matrix products, arithmetic and copies ran while one was open for 4% of the time, Pallas kernels for 35%

profile of v5, /device:TPU:0, one launch (start us, length us, event | category | flops | bytes accessed | tf_op | source)
XLA Modules:
  0.0 435.9 jit_solution(12444826872000483312)
XLA Ops:
  2.2 4.0 collective-permute-start.1
  15.3 3.4 split_weights.1
  19.5 2.8 pack_two.1
  25.8 9.0 %collective-permute-done = bf16[128,1024]{1,0:T(8,128)(2,1)S(1)} collective-permute-done((bf16[128,1024]{1,0:T(8,128)(2,1)S(1)}, bf16[128,1024]{1,0:T(8,128)(2,1)S(1)}, u32[]{:S(2)}, u32[]{:S(2)}) %collective-permute-start) | collective-permute-done | bytes 262176 | tf_op jit(solution)/shard_map/ppermute | solution.py:65
  38.3 4.9 %pack_three.1 = (bf16[320,1024]{1,0:T(8,128)(2,1)}, bf16[320,1024]{1,0:T(8,128)(2,1)}, bf16[320,1024]{1,0:T(8,128)(2,1)}, bf16[832,1024]{1,0:T(8,128)(2,1)}) custom-call(s32[3]{0:T(128)} %pad_add_fusion.meta, bf16[64,1024]{1,0:T(8,128)(2,1)} %get-tuple-element.328.refs_5_.refs_0_.refs_4_, bf16[64,1024]{1,0:T(8,128)(2,1)} %copy-done.26, ...), custom_call_target="tpu_custom_call" | custom-call | flops 1 | bytes 1 | tf_op jit(solution)/shard_map/pack_three/pallas_call | solution.py:438
  49.0 9.6 %collective-permute-done.13.refs_2_ = bf16[128,1024]{1,0:T(8,128)(2,1)S(1)} collective-permute-done((bf16[128,1024]{1,0:T(8,128)(2,1)S(1)}, bf16[128,1024]{1,0:T(8,128)(2,1)S(1)}, u32[]{:S(2)}, u32[]{:S(2)}) %collective-permute-start.13) | collective-permute-done | bytes 262176 | tf_op jit(solution)/shard_map/ppermute | solution.py:65
  61.6 3.1 expand_units.1
  64.7 2.7 collective-permute-done.8.refs_0_.refs_3_.refs_2_.refs_4_
  68.7 3.0 pack_late.1
  75.1 2.1 collective-permute-start.19
  77.2 8.2 %joint_forward.1 = (bf16[256,1024]{1,0:T(8,128)(2,1)}, bf16[256,1024]{1,0:T(8,128)(2,1)}, bf16[528,1024]{1,0:T(8,128)(2,1)}, f32[8,1024]{1,0:T(8,128)}) custom-call(s32[3]{0:T(128)} %pad_add_fusion.meta, bf16[256,1024]{1,0:T(8,128)(2,1)} %pad_maximum_fusion.1.x, bf16[64,1024]{1,0:T(8,128)(2,1)} %get-tuple-element.335.refs_2_.refs_7_.refs_0_, ...), custom_call_target="tpu_custom_call" | custom-call | flops 1 | bytes 1 | tf_op jit(solution)/shard_map/joint_forward/pallas_call | solution.py:1033
  86.3 3.8 collective-permute-done.19
  93.6 3.6 pack_five.1
  100.5 2.6 pack_output.1
  104.1 23.6 %collective-permute-done.20.refs_3_.refs_5_ = bf16[128,1024]{1,0:T(8,128)(2,1)S(1)} collective-permute-done((bf16[128,1024]{1,0:T(8,128)(2,1)}, bf16[128,1024]{1,0:T(8,128)(2,1)S(1)}, u32[]{:S(2)}, u32[]{:S(2)}) %collective-permute-start.20) | collective-permute-done | bytes 262176 | tf_op jit(solution)/shard_map/ppermute | solution.py:65
  129.3 5.8 %collective-permute-done.21.refs_7_.refs_9_ = bf16[128,1024]{1,0:T(8,128)(2,1)} collective-permute-done((bf16[128,1024]{1,0:T(8,128)(2,1)}, bf16[128,1024]{1,0:T(8,128)(2,1)}, u32[]{:S(2)}, u32[]{:S(2)}) %collective-permute-start.21) | collective-permute-done | bytes 262176 | tf_op jit(solution)/shard_map/ppermute | solution.py:65
  135.1 2.8 pack_core.1
  138.3 8.9 %collective-permute-done.26.refs_2_.refs_6_ = bf16[512,1024]{1,0:T(8,128)(2,1)S(1)} collective-permute-done((bf16[512,1024]{1,0:T(8,128)(2,1)}, bf16[512,1024]{1,0:T(8,128)(2,1)S(1)}, u32[]{:S(2)}, u32[]{:S(2)}) %collective-permute-start.26) | collective-permute-done | bytes 1048608 | tf_op jit(solution)/shard_map/ppermute | solution.py:65
  148.1 3.6 pack_seven.1
  155.6 12.9 %context_forward.1 = (bf16[256,1024]{1,0:T(8,128)(2,1)}, f32[256,1024]{1,0:T(8,128)}, bf16[256,1024]{1,0:T(8,128)(2,1)}) custom-call(s32[3]{0:T(128)} %pad_add_fusion.meta, bf16[256,1024]{1,0:T(8,128)(2,1)} %get-tuple-element.358.query, bf16[528,1024]{1,0:T(8,128)(2,1)} %get-tuple-element.359.own.refs_0_, ...), custom_call_target="tpu_custom_call" | custom-call | flops 1 | bytes 1 | tf_op jit(solution)/shard_map/context_forward/pallas_call | solution.py:1125
  169.1 3.6 pack_eight.1
  172.8 2.4 collective-permute-done.28.refs_7_
  179.1 11.7 %ffn_rows.2 = (f32[512,1024]{1,0:T(8,128)}, bf16[512,1024]{1,0:T(8,128)(2,1)}, bf16[512,1024]{1,0:T(8,128)(2,1)}, bf16[512,1024]{1,0:T(8,128)(2,1)}) custom-call(s32[3]{0:T(128)} %pad_add_fusion.meta, bf16[256,1024]{1,0:T(8,128)(2,1)} %get-tuple-element.391.n2m, bf16[256,1024]{1,0:T(8,128)(2,1)} %copy-done.15, bf16[256,1024]{1,0:T(8,128)(2,1)} %copy-done.5, ...), custom_call_target="tpu_custom_call" | custom-call | flops 1 | bytes 1 | tf_op jit(solution)/shard_map/ffn_rows/pallas_call | solution.py:853
  190.8 10.4 %ffn_weights.2 = (f32[512,1024]{1,0:T(8,128)}, bf16[512,1024]{1,0:T(8,128)(2,1)}, bf16[512,1024]{1,0:T(8,128)(2,1)}, bf16[512,1024]{1,0:T(8,128)(2,1)}, bf16[512...) custom-call(s32[3]{0:T(128)} %pad_add_fusion.meta, ...), custom_call_target="tpu_custom_call" | custom-call | flops 1 | bytes 1 | tf_op jit(solution)/shard_map/ffn_weights/pallas_call | solution.py:924
  204.8 13.0 %ffn_rows.3 = (f32[256,1024]{1,0:T(8,128)}, f32[256,1024]{1,0:T(8,128)}, bf16[512,1024]{1,0:T(8,128)(2,1)}, bf16[512,1024]{1,0:T(8,128)(2,1)}, bf16[512,1024]{1,0:T(8,128)(2,1)}) custom-call(s32[3]{0:T(128)} %pad_add_fusion.meta, bf16[256,1024]{1,0:T(8,128)(2,1)} %get-tuple-element.391.n2m, bf16[256,1024]{1,0:T(8,128)(2,1)} %copy-done.15, ...), custom_call_target="tpu_custom_call" | custom-call | flops 1 | bytes 1 | tf_op jit(solution)/shard_map/ffn_rows/pallas_call | solution.py:853
  217.8 11.3 %ffn_weights.3 = (f32[256,1024]{1,0:T(8,128)}, bf16[256,1024]{1,0:T(8,128)(2,1)}, bf16[512,1024]{1,0:T(8,128)(2,1)}, bf16[512,1024]{1,0:T(8,128)(2,1)}, bf16[512...) custom-call(s32[3]{0:T(128)} %pad_add_fusion.meta, ...), custom_call_target="tpu_custom_call" | custom-call | flops 1 | bytes 1 | tf_op jit(solution)/shard_map/ffn_weights/pallas_call | solution.py:924
  233.8 2.1 collective-permute-start.35
  236.0 18.8 %context_back.1 = (f32[256,1024]{1,0:T(8,128)}, f32[1,1024]{1,0:T(1,128)}, bf16[256,1024]{1,0:T(8,128)(2,1)}, bf16[256,1024]{1,0:T(8,128)(2,1)}, f32[256,2048]{1,0:T(8,128)}, /*index=5*/bf16[528,1024]{1,0:T(8,128)(2,1)}) custom-call(s32[3]{0:T(128)} %pad_add_fusion.meta, f32[256,1024]{1,0:T(8,128)} %get-tuple-element.439.dn_own, ...), custom_call_target="tpu_custom_call" | custom-call | flops 1 | bytes 1 | tf_op jit(solution)/shard_map/context_back/pallas_call | solution.py:1209
  255.7 5.1 %collective-permute-done.35 = bf16[16,8,1024]{2,1,0:T(8,128)(2,1)S(1)} collective-permute-done((bf16[16,8,1024]{2,1,0:T(8,128)(2,1)S(1)}, bf16[16,8,1024]{2,1,0:T(8,128)(2,1)S(1)}, u32[]{:S(2)}, u32[]{:S(2)}) %collective-permute-start.35) | collective-permute-done | bytes 262176 | tf_op jit(solution)/shard_map/ppermute | solution.py:65
  262.2 8.2 %turn_three.1 = (bf16[512,1024]{1,0:T(8,128)(2,1)}, bf16[512,1024]{1,0:T(8,128)(2,1)}, bf16[512,1024]{1,0:T(8,128)(2,1)}, bf16[256,1024]{1,0:T(8,128)(2,1)}, bf1...) custom-call(s32[3]{0:T(128)} %pad_add_fusion.meta, ...), custom_call_target="tpu_custom_call" | custom-call | flops 1 | bytes 1 | tf_op jit(solution)/shard_map/turn_three/pallas_call | solution.py:438
  273.6 4.4 %output_grad.1 = (bf16[512,1024]{1,0:T(8,128)(2,1)}, bf16[512,1024]{1,0:T(8,128)(2,1)}) custom-call(s32[3]{0:T(128)} %pad_add_fusion.meta, bf16[256,1024]{1,0:T(8,128)(2,1)} %get-tuple-element.445.context, bf16[256,1024]{1,0:T(8,128)(2,1)} %get-tuple-element.480.grad), custom_call_target="tpu_custom_call" | custom-call | flops 1 | bytes 1 | tf_op jit(solution)/shard_map/output_grad/pallas_call | solution.py:1291
  278.0 30.3 %collective-permute-done.40.dkv_got = bf16[528,1024]{1,0:T(8,128)(2,1)S(1)} collective-permute-done((bf16[528,1024]{1,0:T(8,128)(2,1)}, bf16[528,1024]{1,0:T(8,128)(2,1)S(1)}, u32[]{:S(2)}, u32[]{:S(2)}) %collective-permute-start.40) | collective-permute-done | bytes 1081376 | tf_op jit(solution)/shard_map/ppermute | solution.py:65
  309.2 7.5 %joint_grad.1 = (bf16[1536,1024]{1,0:T(8,128)(2,1)}, bf16[1536,1024]{1,0:T(8,128)(2,1)}, bf16[256,2048]{1,0:T(8,128)(2,1)}) custom-call(s32[3]{0:T(128)} %pad_add_fusion.meta, bf16[256,1024]{1,0:T(8,128)(2,1)} %get-tuple-element.442.first, bf16[256,1024]{1,0:T(8,128)(2,1)} %get-tuple-element.441.dq, f32[256,2048]{1,0:T(8,128)} %get-tuple-element.443.dkv_own, ...), custom_call_target="tpu_custom_call" | custom-call | flops 1 | bytes 1 | tf_op jit(solution)/shard_map/joint_grad/pallas_call | solution.py:1329
  318.8 5.3 %turn_four.1 = (bf16[256,1024]{1,0:T(8,128)(2,1)}, bf16[256,1024]{1,0:T(8,128)(2,1)}, bf16[256,1024]{1,0:T(8,128)(2,1)}, bf16[128,1024]{1,0:T(8,128)(2,1)}, bf16...) custom-call(s32[3]{0:T(128)} %pad_add_fusion.meta, ...), custom_call_target="tpu_custom_call" | custom-call | flops 1 | bytes 1 | tf_op jit(solution)/shard_map/turn_four/pallas_call | solution.py:438
  327.1 8.8 %input_back.1 = (bf16[256,1024]{1,0:T(8,128)(2,1)}, f32[1,1024]{1,0:T(1,128)}) custom-call(s32[3]{0:T(128)} %pad_add_fusion.meta, bf16[256,1024]{1,0:T(8,128)(2,1)} %get-tuple-element.441.dq, bf16[256,2048]{1,0:T(8,128)(2,1)} %get-tuple-element.503.dkv, f32[256,1024]{1,0:T(8,128)} %get-tuple-element.504.dh, bf16[256,1024]{1,0:T(8,128)(2,1)} %pad_maximum_fusion.1.x, ...), custom_call_target="tpu_custom_call" | custom-call | flops 1 | bytes 1 | tf_op jit(solution)/shard_map/input_back/pallas_call | solution.py:1359
  336.9 6.1 %joint_core.1 = (bf16[256,1024]{1,0:T(8,128)(2,1)}, bf16[384,1024]{1,0:T(8,128)(2,1)}, bf16[384,1024]{1,0:T(8,128)(2,1)}, bf16[256,1024]{1,0:T(8,128)(2,1)}, bf1...) custom-call(s32[3]{0:T(128)} %pad_add_fusion.meta, ...), custom_call_target="tpu_custom_call" | custom-call | flops 1 | bytes 1 | tf_op jit(solution)/shard_map/joint_core/pallas_call | solution.py:438
  345.5 2.1 collective-permute-start.49
  347.6 4.4 %turn_five.1 = (f32[128,1024]{1,0:T(8,128)}, f32[128,1024]{1,0:T(8,128)}, f32[128,1024]{1,0:T(8,128)}, f32[128,1024]{1,0:T(8,128)}, f32[128,1024]{1,0:T(8,128)}, /*index=5*/f32[128,1024]{1,0:T(8,128)}, f32[8,1024]{1,0:T(8,128)}) custom-call(s32[3]{0:T(128)} %pad_add_fusion.meta, bf16[256,1024]{1,0:T(8,128)(2,1)} %copy-done.42, ...), custom_call_target="tpu_custom_call" | custom-call | flops 1 | bytes 1 | tf_op jit(solution)/shard_map/turn_five/pallas_call | solution.py:438
  352.0 7.6 %collective-permute-done.49 = bf16[16,8,1024]{2,1,0:T(8,128)(2,1)} collective-permute-done((bf16[16,8,1024]{2,1,0:T(8,128)(2,1)}, bf16[16,8,1024]{2,1,0:T(8,128)(2,1)}, u32[]{:S(2)}, u32[]{:S(2)}) %collective-permute-start.49) | collective-permute-done | bytes 262176 | tf_op jit(solution)/shard_map/ppermute | solution.py:65
  361.4 3.6 collective-permute-done.51.refs_3_
  366.3 4.3 turn_nine.1
  375.4 8.4 %collective-permute-done.59.refs_20_ = bf16[128,1024]{1,0:T(8,128)(2,1)S(1)} collective-permute-done((bf16[128,1024]{1,0:T(8,128)(2,1)S(1)}, bf16[128,1024]{1,0:T(8,128)(2,1)S(1)}, u32[]{:S(2)}, u32[]{:S(2)}) %collective-permute-start.59) | collective-permute-done | bytes 262176 | tf_op jit(solution)/shard_map/ppermute | solution.py:65
  386.5 3.2 turn_ten.1
  393.8 4.1 collective-permute-done.62.refs_4_
  398.7 3.7 turn_last.1
  404.5 2.6 all-to-all-start
  409.1 9.1 %all-to-all-done = f32[32,1,2176]{2,1,0:T(1,128)S(1)} async-done(((f32[32,1,2176]{2,1,0:T(1,128)}), f32[32,1,2176]{2,1,0:T(1,128)S(1)}, u32[]{:S(2)}, u32[]{:S(2)}) %all-to-all-start) | async-done | bytes 278560 | tf_op jit(solution)/shard_map/all_to_all | solution.py:1800
  422.4 12.0 %adam_matrices.1 = (f32[64,8192]{1,0:T(8,128)}, f32[64,8192]{1,0:T(8,128)}, f32[64,8192]{1,0:T(8,128)}, f32[64,3072]{1,0:T(8,128)}, f32[64,3072]{1,0:T(8,128)}, ...) custom-call(s32[3]{0:T(128)} %pad_add_fusion.meta, ...), custom_call_target="tpu_custom_call" | custom-call | flops 1 | bytes 1 | tf_op jit(solution)/shard_map/adam_matrices/pallas_call | solution.py:1477
  (279 shorter events, 97.0 us)
Async XLA Ops:
  22.4 12.5 %collective-permute-start.5 = (bf16[160,1024]{1,0:T(8,128)(2,1)}, bf16[160,1024]{1,0:T(8,128)(2,1)S(1)}, u32[]{:S(2)}, u32[]{:S(2)}) collective-permute-start(bf16[160,1024]{1,0:T(8,128)(2,1)} %get-tuple-element.325), channel_id=1, source_target_pairs={{0,4},{1,5},{2,6},{3,7},{4,0},{5,1},{6,2},{7,3},{8,12},{9,13},{10,... | collective-permute-start | bytes 983048 | tf_op jit(solution)/shard_map/ppermute | solution.py:65
  23.5 13.3 %collective-permute-start.6 = (bf16[160,1024]{1,0:T(8,128)(2,1)}, bf16[160,1024]{1,0:T(8,128)(2,1)S(1)}, u32[]{:S(2)}, u32[]{:S(2)}) collective-permute-start(bf16[160,1024]{1,0:T(8,128)(2,1)} %get-tuple-element.326), channel_id=1, source_target_pairs={{0,8},{1,9},{2,10},{3,11},{4,12},{5,13},{6,14},{7,15},{8,0},{9,1},... | collective-permute-start | bytes 983048 | tf_op jit(solution)/shard_map/ppermute | solution.py:65
  23.9 12.9 %collective-permute-start.7 = (bf16[160,1024]{1,0:T(8,128)(2,1)}, bf16[160,1024]{1,0:T(8,128)(2,1)S(1)}, u32[]{:S(2)}, u32[]{:S(2)}) collective-permute-start(bf16[160,1024]{1,0:T(8,128)(2,1)} %get-tuple-element.327), channel_id=1, source_target_pairs={{0,2},{1,3},{2,0},{3,1},{4,6},{5,7},{6,4},{7,5},{8,10},{9,11},{10,... | collective-permute-start | bytes 983048 | tf_op jit(solution)/shard_map/ppermute | solution.py:65
  43.2 24.2 %collective-permute-start.11 = (bf16[832,1024]{1,0:T(8,128)(2,1)}, bf16[832,1024]{1,0:T(8,128)(2,1)}, u32[]{:S(2)}, u32[]{:S(2)}) collective-permute-start(bf16[832,1024]{1,0:T(8,128)(2,1)} %get-tuple-element.342), channel_id=1, source_target_pairs={{0,1},{1,0},{2,3},{3,2},{4,5},{5,4},{6,7},{7,6},{8,9},{9,8},{10,11... | collective-permute-start | bytes 5111816 | tf_op jit(solution)/shard_map/ppermute | solution.py:65
  43.3 15.3 %collective-permute-start.13 = (bf16[128,1024]{1,0:T(8,128)(2,1)S(1)}, bf16[128,1024]{1,0:T(8,128)(2,1)S(1)}, u32[]{:S(2)}, u32[]{:S(2)}) collective-permute-start(bf16[128,1024]{1,0:T(8,128)(2,1)S(1)} %copy-done.60), channel_id=1, source_target_pairs={{0,16},{1,17},{2,18},{3,19},{4,20},{5,21},{6,22},{7,23},{8,24},{9,... | collective-permute-start | bytes 786440 | tf_op jit(solution)/shard_map/ppermute | solution.py:65
  44.9 22.5 %collective-permute-start.8 = (bf16[320,1024]{1,0:T(8,128)(2,1)}, bf16[320,1024]{1,0:T(8,128)(2,1)S(1)}, u32[]{:S(2)}, u32[]{:S(2)}) collective-permute-start(bf16[320,1024]{1,0:T(8,128)(2,1)} %get-tuple-element.339), channel_id=1, source_target_pairs={{0,8},{1,9},{2,10},{3,11},{4,12},{5,13},{6,14},{7,15},{8,0},{9,1},... | collective-permute-start | bytes 1966088 | tf_op jit(solution)/shard_map/ppermute | solution.py:65
  46.5 20.9 %collective-permute-start.9 = (bf16[320,1024]{1,0:T(8,128)(2,1)}, bf16[320,1024]{1,0:T(8,128)(2,1)S(1)}, u32[]{:S(2)}, u32[]{:S(2)}) collective-permute-start(bf16[320,1024]{1,0:T(8,128)(2,1)} %get-tuple-element.340), channel_id=1, source_target_pairs={{0,2},{1,3},{2,0},{3,1},{4,6},{5,7},{6,4},{7,5},{8,10},{9,11},{10,... | collective-permute-start | bytes 1966088 | tf_op jit(solution)/shard_map/ppermute | solution.py:65
  47.6 19.8 %collective-permute-start.10 = (bf16[320,1024]{1,0:T(8,128)(2,1)}, bf16[320,1024]{1,0:T(8,128)(2,1)S(1)}, u32[]{:S(2)}, u32[]{:S(2)}) collective-permute-start(bf16[320,1024]{1,0:T(8,128)(2,1)} %get-tuple-element.341), channel_id=1, source_target_pairs={{0,4},{1,5},{2,6},{3,7},{4,0},{5,1},{6,2},{7,3},{8,12},{9,13},{10,... | collective-permute-start | bytes 1966088 | tf_op jit(solution)/shard_map/ppermute | solution.py:65
  71.7 20.0 %collective-permute-start.16 = (bf16[256,1024]{1,0:T(8,128)(2,1)S(1)}, bf16[256,1024]{1,0:T(8,128)(2,1)S(1)}, u32[]{:S(2)}, u32[]{:S(2)}) collective-permute-start(bf16[256,1024]{1,0:T(8,128)(2,1)S(1)} %copy-done.3), channel_id=1, source_target_pairs={{0,8},{1,9},{2,10},{3,11},{4,12},{5,13},{6,14},{7,15},{8,0},{9,1},... | collective-permute-start | bytes 1572872 | tf_op jit(solution)/shard_map/ppermute | solution.py:65
  72.1 19.7 %collective-permute-start.17 = (bf16[256,1024]{1,0:T(8,128)(2,1)S(1)}, bf16[256,1024]{1,0:T(8,128)(2,1)S(1)}, u32[]{:S(2)}, u32[]{:S(2)}) collective-permute-start(bf16[256,1024]{1,0:T(8,128)(2,1)S(1)} %copy-done.10), channel_id=1, source_target_pairs={{0,2},{1,3},{2,0},{3,1},{4,6},{5,7},{6,4},{7,5},{8,10},{9,11},{10,... | collective-permute-start | bytes 1572872 | tf_op jit(solution)/shard_map/ppermute | solution.py:65
  73.0 18.8 %collective-permute-start.18 = (bf16[256,1024]{1,0:T(8,128)(2,1)S(1)}, bf16[256,1024]{1,0:T(8,128)(2,1)S(1)}, u32[]{:S(2)}, u32[]{:S(2)}) collective-permute-start(bf16[256,1024]{1,0:T(8,128)(2,1)S(1)} %copy-done.11), channel_id=1, source_target_pairs={{0,4},{1,5},{2,6},{3,7},{4,0},{5,1},{6,2},{7,3},{8,12},{9,13},{10,... | collective-permute-start | bytes 1572872 | tf_op jit(solution)/shard_map/ppermute | solution.py:65
  75.1 15.0 %collective-permute-start.19 = (bf16[128,1024]{1,0:T(8,128)(2,1)}, bf16[128,1024]{1,0:T(8,128)(2,1)S(1)}, u32[]{:S(2)}, u32[]{:S(2)}) collective-permute-start(bf16[128,1024]{1,0:T(8,128)(2,1)} %select_bitcast_fusion.2), channel_id=1, source_target_pairs={{0,16},{1,17},{2,18},{3,19},{4,20},{5,21},{6,22},{7,23},{8,24},{9,... | collective-permute-start | bytes 786440 | tf_op jit(solution)/shard_map/ppermute | solution.py:65
  85.4 61.7 %collective-permute-start.15 = (bf16[528,1024]{1,0:T(8,128)(2,1)}, bf16[528,1024]{1,0:T(8,128)(2,1)}, u32[]{:S(2)}, u32[]{:S(2)}) collective-permute-start(bf16[528,1024]{1,0:T(8,128)(2,1)} %get-tuple-element.359.own.refs_0_), channel_id=1, source_target_pairs={{0,16},{1,17},{2,18},{3,19},{4,20},{5,21},{6,22},{7,23},{8,24},{9,... | collective-permute-start | bytes 3244040 | tf_op jit(solution)/shard_map/ppermute | solution.py:65
  97.2 41.1 %collective-permute-start.24 = (bf16[512,1024]{1,0:T(8,128)(2,1)}, bf16[512,1024]{1,0:T(8,128)(2,1)S(1)}, u32[]{:S(2)}, u32[]{:S(2)}) collective-permute-start(bf16[512,1024]{1,0:T(8,128)(2,1)} %get-tuple-element.371), channel_id=1, source_target_pairs={{0,2},{1,3},{2,0},{3,1},{4,6},{5,7},{6,4},{7,5},{8,10},{9,11},{10,... | collective-permute-start | bytes 3145736 | tf_op jit(solution)/shard_map/ppermute | solution.py:65
  98.3 39.9 %collective-permute-start.25 = (bf16[512,1024]{1,0:T(8,128)(2,1)}, bf16[512,1024]{1,0:T(8,128)(2,1)S(1)}, u32[]{:S(2)}, u32[]{:S(2)}) collective-permute-start(bf16[512,1024]{1,0:T(8,128)(2,1)} %get-tuple-element.372), channel_id=1, source_target_pairs={{0,4},{1,5},{2,6},{3,7},{4,0},{5,1},{6,2},{7,3},{8,12},{9,13},{10,... | collective-permute-start | bytes 3145736 | tf_op jit(solution)/shard_map/ppermute | solution.py:65
  99.7 47.4 %collective-permute-start.26 = (bf16[512,1024]{1,0:T(8,128)(2,1)}, bf16[512,1024]{1,0:T(8,128)(2,1)S(1)}, u32[]{:S(2)}, u32[]{:S(2)}) collective-permute-start(bf16[512,1024]{1,0:T(8,128)(2,1)} %get-tuple-element.373), channel_id=1, source_target_pairs={{0,8},{1,9},{2,10},{3,11},{4,12},{5,13},{6,14},{7,15},{8,0},{9,1},... | collective-permute-start | bytes 3145736 | tf_op jit(solution)/shard_map/ppermute | solution.py:65
  103.0 24.7 %collective-permute-start.20 = (bf16[128,1024]{1,0:T(8,128)(2,1)}, bf16[128,1024]{1,0:T(8,128)(2,1)S(1)}, u32[]{:S(2)}, u32[]{:S(2)}) collective-permute-start(bf16[128,1024]{1,0:T(8,128)(2,1)} %get-tuple-element.380), channel_id=1, source_target_pairs={{0,2},{1,3},{2,0},{3,1},{4,6},{5,7},{6,4},{7,5},{8,10},{9,11},{10,... | collective-permute-start | bytes 786440 | tf_op jit(solution)/shard_map/ppermute | solution.py:65
  138.0 17.6 %collective-permute-start.22 = (bf16[512,1024]{1,0:T(8,128)(2,1)}, bf16[512,1024]{1,0:T(8,128)(2,1)}, u32[]{:S(2)}, u32[]{:S(2)}) collective-permute-start(bf16[512,1024]{1,0:T(8,128)(2,1)} %pack_core.1), channel_id=1, source_target_pairs={{0,1},{1,0},{2,3},{3,2},{4,5},{5,4},{6,7},{7,6},{8,9},{9,8},{10,11... | collective-permute-start | bytes 3145736 | tf_op jit(solution)/shard_map/ppermute | solution.py:65
  151.7 23.5 %collective-permute-start.28 = (bf16[512,1024]{1,0:T(8,128)(2,1)}, bf16[512,1024]{1,0:T(8,128)(2,1)S(1)}, u32[]{:S(2)}, u32[]{:S(2)}) collective-permute-start(bf16[512,1024]{1,0:T(8,128)(2,1)} %get-tuple-element.403), channel_id=1, source_target_pairs={{0,2},{1,3},{2,0},{3,1},{4,6},{5,7},{6,4},{7,5},{8,10},{9,11},{10,... | collective-permute-start | bytes 3145736 | tf_op jit(solution)/shard_map/ppermute | solution.py:65
  152.8 23.2 %collective-permute-start.29 = (bf16[512,1024]{1,0:T(8,128)(2,1)}, bf16[512,1024]{1,0:T(8,128)(2,1)S(1)}, u32[]{:S(2)}, u32[]{:S(2)}) collective-permute-start(bf16[512,1024]{1,0:T(8,128)(2,1)} %get-tuple-element.404), channel_id=1, source_target_pairs={{0,4},{1,5},{2,6},{3,7},{4,0},{5,1},{6,2},{7,3},{8,12},{9,13},{10,... | collective-permute-start | bytes 3145736 | tf_op jit(solution)/shard_map/ppermute | solution.py:65
  153.3 23.1 %collective-permute-start.30 = (bf16[512,1024]{1,0:T(8,128)(2,1)}, bf16[512,1024]{1,0:T(8,128)(2,1)}, u32[]{:S(2)}, u32[]{:S(2)}) collective-permute-start(bf16[512,1024]{1,0:T(8,128)(2,1)} %get-tuple-element.405), channel_id=1, source_target_pairs={{0,8},{1,9},{2,10},{3,11},{4,12},{5,13},{6,14},{7,15},{8,0},{9,1},... | collective-permute-start | bytes 3145736 | tf_op jit(solution)/shard_map/ppermute | solution.py:65
  154.8 14.4 %collective-permute-start.27 = (bf16[256,1024]{1,0:T(8,128)(2,1)S(1)}, bf16[256,1024]{1,0:T(8,128)(2,1)S(1)}, u32[]{:S(2)}, u32[]{:S(2)}) collective-permute-start(bf16[256,1024]{1,0:T(8,128)(2,1)S(1)} %multiply_convert_fusion.cm.cot), channel_id=1, source_target_pairs={{0,1},{1,0},{2,3},{3,2},{4,5},{5,4},{6,7},{7,6},{8,9},{9,8},{10,11... | collective-permute-start | bytes 1572872 | tf_op jit(solution)/shard_map/ppermute | solution.py:65
  176.5 24.8 %collective-permute-start.31 = (bf16[512,1024]{1,0:T(8,128)(2,1)}, bf16[512,1024]{1,0:T(8,128)(2,1)}, u32[]{:S(2)}, u32[]{:S(2)}) collective-permute-start(bf16[512,1024]{1,0:T(8,128)(2,1)} %get-tuple-element.418), channel_id=1, source_target_pairs={{0,8},{1,9},{2,10},{3,11},{4,12},{5,13},{6,14},{7,15},{8,0},{9,1},... | collective-permute-start | bytes 3145736 | tf_op jit(solution)/shard_map/ppermute | solution.py:65
  176.6 24.7 %collective-permute-start.32 = (bf16[512,1024]{1,0:T(8,128)(2,1)}, bf16[512,1024]{1,0:T(8,128)(2,1)}, u32[]{:S(2)}, u32[]{:S(2)}) collective-permute-start(bf16[512,1024]{1,0:T(8,128)(2,1)} %get-tuple-element.419), channel_id=1, source_target_pairs={{0,2},{1,3},{2,0},{3,1},{4,6},{5,7},{6,4},{7,5},{8,10},{9,11},{10,... | collective-permute-start | bytes 3145736 | tf_op jit(solution)/shard_map/ppermute | solution.py:65
  177.7 23.6 %collective-permute-start.33 = (bf16[512,1024]{1,0:T(8,128)(2,1)}, bf16[512,1024]{1,0:T(8,128)(2,1)S(1)}, u32[]{:S(2)}, u32[]{:S(2)}) collective-permute-start(bf16[512,1024]{1,0:T(8,128)(2,1)} %get-tuple-element.420), channel_id=1, source_target_pairs={{0,4},{1,5},{2,6},{3,7},{4,0},{5,1},{6,2},{7,3},{8,12},{9,13},{10,... | collective-permute-start | bytes 3145736 | tf_op jit(solution)/shard_map/ppermute | solution.py:65
  201.3 28.4 %collective-permute-start.36 = (bf16[512,1024]{1,0:T(8,128)(2,1)}, bf16[512,1024]{1,0:T(8,128)(2,1)S(1)}, u32[]{:S(2)}, u32[]{:S(2)}) collective-permute-start(bf16[512,1024]{1,0:T(8,128)(2,1)} %get-tuple-element.436), channel_id=1, source_target_pairs={{0,2},{1,3},{2,0},{3,1},{4,6},{5,7},{6,4},{7,5},{8,10},{9,11},{10,... | collective-permute-start | bytes 3145736 | tf_op jit(solution)/shard_map/ppermute | solution.py:65
  202.4 27.2 %collective-permute-start.37 = (bf16[512,1024]{1,0:T(8,128)(2,1)}, bf16[512,1024]{1,0:T(8,128)(2,1)S(1)}, u32[]{:S(2)}, u32[]{:S(2)}) collective-permute-start(bf16[512,1024]{1,0:T(8,128)(2,1)} %get-tuple-element.437), channel_id=1, source_target_pairs={{0,4},{1,5},{2,6},{3,7},{4,0},{5,1},{6,2},{7,3},{8,12},{9,13},{10,... | collective-permute-start | bytes 3145736 | tf_op jit(solution)/shard_map/ppermute | solution.py:65
  203.2 26.5 %collective-permute-start.38 = (bf16[512,1024]{1,0:T(8,128)(2,1)}, bf16[512,1024]{1,0:T(8,128)(2,1)}, u32[]{:S(2)}, u32[]{:S(2)}) collective-permute-start(bf16[512,1024]{1,0:T(8,128)(2,1)} %get-tuple-element.438), channel_id=1, source_target_pairs={{0,8},{1,9},{2,10},{3,11},{4,12},{5,13},{6,14},{7,15},{8,0},{9,1},... | collective-permute-start | bytes 3145736 | tf_op jit(solution)/shard_map/ppermute | solution.py:65
  229.7 31.1 %collective-permute-start.41 = (bf16[512,1024]{1,0:T(8,128)(2,1)}, bf16[512,1024]{1,0:T(8,128)(2,1)}, u32[]{:S(2)}, u32[]{:S(2)}) collective-permute-start(bf16[512,1024]{1,0:T(8,128)(2,1)} %get-tuple-element.451), channel_id=1, source_target_pairs={{0,4},{1,5},{2,6},{3,7},{4,0},{5,1},{6,2},{7,3},{8,12},{9,13},{10,... | collective-permute-start | bytes 3145736 | tf_op jit(solution)/shard_map/ppermute | solution.py:65
  231.3 30.9 %collective-permute-start.42 = (bf16[512,1024]{1,0:T(8,128)(2,1)}, bf16[512,1024]{1,0:T(8,128)(2,1)}, u32[]{:S(2)}, u32[]{:S(2)}) collective-permute-start(bf16[512,1024]{1,0:T(8,128)(2,1)} %get-tuple-element.454), channel_id=1, source_target_pairs={{0,8},{1,9},{2,10},{3,11},{4,12},{5,13},{6,14},{7,15},{8,0},{9,1},... | collective-permute-start | bytes 3145736 | tf_op jit(solution)/shard_map/ppermute | solution.py:65
  231.4 30.8 %collective-permute-start.43 = (bf16[512,1024]{1,0:T(8,128)(2,1)}, bf16[512,1024]{1,0:T(8,128)(2,1)}, u32[]{:S(2)}, u32[]{:S(2)}) collective-permute-start(bf16[512,1024]{1,0:T(8,128)(2,1)} %get-tuple-element.457), channel_id=1, source_target_pairs={{0,2},{1,3},{2,0},{3,1},{4,6},{5,7},{6,4},{7,5},{8,10},{9,11},{10,... | collective-permute-start | bytes 3145736 | tf_op jit(solution)/shard_map/ppermute | solution.py:65
  233.8 27.0 %collective-permute-start.35 = (bf16[16,8,1024]{2,1,0:T(8,128)(2,1)S(1)}, bf16[16,8,1024]{2,1,0:T(8,128)(2,1)S(1)}, u32[]{:S(2)}, u32[]{:S(2)}) collective-permute-start(bf16[16,8,1024]{2,1,0:T(8,128)(2,1)S(1)} %select_bitcast_fusion.1), channel_id=1, source_target_pairs={{0,16},{1,17},{2,18},{3,19},{4,20},{5,21},{6,22},{7,23},{8,24},{9,... | collective-permute-start | bytes 786440 | tf_op jit(solution)/shard_map/ppermute | solution.py:65
  254.8 53.4 %collective-permute-start.40 = (bf16[528,1024]{1,0:T(8,128)(2,1)}, bf16[528,1024]{1,0:T(8,128)(2,1)S(1)}, u32[]{:S(2)}, u32[]{:S(2)}) collective-permute-start(bf16[528,1024]{1,0:T(8,128)(2,1)} %get-tuple-element.444), channel_id=1, source_target_pairs={{0,16},{1,17},{2,18},{3,19},{4,20},{5,21},{6,22},{7,23},{8,24},{9,... | collective-permute-start | bytes 3244040 | tf_op jit(solution)/shard_map/ppermute | solution.py:65
  270.3 46.4 %collective-permute-start.46 = (bf16[512,1024]{1,0:T(8,128)(2,1)}, bf16[512,1024]{1,0:T(8,128)(2,1)S(1)}, u32[]{:S(2)}, u32[]{:S(2)}) collective-permute-start(bf16[512,1024]{1,0:T(8,128)(2,1)} %get-tuple-element.471), channel_id=1, source_target_pairs={{0,2},{1,3},{2,0},{3,1},{4,6},{5,7},{6,4},{7,5},{8,10},{9,11},{10,... | collective-permute-start | bytes 3145736 | tf_op jit(solution)/shard_map/ppermute | solution.py:65
  271.3 45.4 %collective-permute-start.44 = (bf16[512,1024]{1,0:T(8,128)(2,1)}, bf16[512,1024]{1,0:T(8,128)(2,1)}, u32[]{:S(2)}, u32[]{:S(2)}) collective-permute-start(bf16[512,1024]{1,0:T(8,128)(2,1)} %get-tuple-element.472), channel_id=1, source_target_pairs={{0,4},{1,5},{2,6},{3,7},{4,0},{5,1},{6,2},{7,3},{8,12},{9,13},{10,... | collective-permute-start | bytes 3145736 | tf_op jit(solution)/shard_map/ppermute | solution.py:65
  272.0 46.8 %collective-permute-start.45 = (bf16[512,1024]{1,0:T(8,128)(2,1)}, bf16[512,1024]{1,0:T(8,128)(2,1)}, u32[]{:S(2)}, u32[]{:S(2)}) collective-permute-start(bf16[512,1024]{1,0:T(8,128)(2,1)} %get-tuple-element.473), channel_id=1, source_target_pairs={{0,8},{1,9},{2,10},{3,11},{4,12},{5,13},{6,14},{7,15},{8,0},{9,1},... | collective-permute-start | bytes 3145736 | tf_op jit(solution)/shard_map/ppermute | solution.py:65
  324.7 20.8 %collective-permute-start.53 = (bf16[256,1024]{1,0:T(8,128)(2,1)}, bf16[256,1024]{1,0:T(8,128)(2,1)S(1)}, u32[]{:S(2)}, u32[]{:S(2)}) collective-permute-start(bf16[256,1024]{1,0:T(8,128)(2,1)} %get-tuple-element.494), channel_id=1, source_target_pairs={{0,2},{1,3},{2,0},{3,1},{4,6},{5,7},{6,4},{7,5},{8,10},{9,11},{10,... | collective-permute-start | bytes 1572872 | tf_op jit(solution)/shard_map/ppermute | solution.py:65
  325.6 22.0 %collective-permute-start.54 = (bf16[256,1024]{1,0:T(8,128)(2,1)}, bf16[256,1024]{1,0:T(8,128)(2,1)}, u32[]{:S(2)}, u32[]{:S(2)}) collective-permute-start(bf16[256,1024]{1,0:T(8,128)(2,1)} %get-tuple-element.495), channel_id=1, source_target_pairs={{0,4},{1,5},{2,6},{3,7},{4,0},{5,1},{6,2},{7,3},{8,12},{9,13},{10,... | collective-permute-start | bytes 1572872 | tf_op jit(solution)/shard_map/ppermute | solution.py:65
  327.1 20.5 %collective-permute-start.55 = (bf16[256,1024]{1,0:T(8,128)(2,1)}, bf16[256,1024]{1,0:T(8,128)(2,1)}, u32[]{:S(2)}, u32[]{:S(2)}) collective-permute-start(bf16[256,1024]{1,0:T(8,128)(2,1)} %get-tuple-element.496), channel_id=1, source_target_pairs={{0,8},{1,9},{2,10},{3,11},{4,12},{5,13},{6,14},{7,15},{8,0},{9,1},... | collective-permute-start | bytes 1572872 | tf_op jit(solution)/shard_map/ppermute | solution.py:65
  343.1 21.9 %collective-permute-start.50 = (bf16[384,1024]{1,0:T(8,128)(2,1)}, bf16[384,1024]{1,0:T(8,128)(2,1)S(1)}, u32[]{:S(2)}, u32[]{:S(2)}) collective-permute-start(bf16[384,1024]{1,0:T(8,128)(2,1)} %get-tuple-element.512), channel_id=1, source_target_pairs={{0,4},{1,5},{2,6},{3,7},{4,0},{5,1},{6,2},{7,3},{8,12},{9,13},{10,... | collective-permute-start | bytes 2359304 | tf_op jit(solution)/shard_map/ppermute | solution.py:65
  343.6 21.4 %collective-permute-start.52 = (bf16[384,1024]{1,0:T(8,128)(2,1)}, bf16[384,1024]{1,0:T(8,128)(2,1)S(1)}, u32[]{:S(2)}, u32[]{:S(2)}) collective-permute-start(bf16[384,1024]{1,0:T(8,128)(2,1)} %get-tuple-element.516), channel_id=1, source_target_pairs={{0,2},{1,3},{2,0},{3,1},{4,6},{5,7},{6,4},{7,5},{8,10},{9,11},{10,... | collective-permute-start | bytes 2359304 | tf_op jit(solution)/shard_map/ppermute | solution.py:65
  345.5 14.1 %collective-permute-start.49 = (bf16[16,8,1024]{2,1,0:T(8,128)(2,1)}, bf16[16,8,1024]{2,1,0:T(8,128)(2,1)}, u32[]{:S(2)}, u32[]{:S(2)}) collective-permute-start(bf16[16,8,1024]{2,1,0:T(8,128)(2,1)} %select_bitcast_fusion), channel_id=1, source_target_pairs={{0,16},{1,17},{2,18},{3,19},{4,20},{5,21},{6,22},{7,23},{8,24},{9,... | collective-permute-start | bytes 786440 | tf_op jit(solution)/shard_map/ppermute | solution.py:65
  347.6 17.4 %collective-permute-start.51 = (bf16[256,1024]{1,0:T(8,128)(2,1)}, bf16[256,1024]{1,0:T(8,128)(2,1)S(1)}, u32[]{:S(2)}, u32[]{:S(2)}) collective-permute-start(bf16[256,1024]{1,0:T(8,128)(2,1)} %get-tuple-element.510), channel_id=1, source_target_pairs={{0,8},{1,9},{2,10},{3,11},{4,12},{5,13},{6,14},{7,15},{8,0},{9,1},... | collective-permute-start | bytes 1572872 | tf_op jit(solution)/shard_map/ppermute | solution.py:65
  370.6 15.0 %collective-permute-start.57 = (bf16[192,1024]{1,0:T(8,128)(2,1)}, bf16[192,1024]{1,0:T(8,128)(2,1)S(1)}, u32[]{:S(2)}, u32[]{:S(2)}) collective-permute-start(bf16[192,1024]{1,0:T(8,128)(2,1)} %get-tuple-element.539), channel_id=1, source_target_pairs={{0,8},{1,9},{2,10},{3,11},{4,12},{5,13},{6,14},{7,15},{8,0},{9,1},... | collective-permute-start | bytes 1179656 | tf_op jit(solution)/shard_map/ppermute | solution.py:65
  371.6 14.0 %collective-permute-start.58 = (bf16[192,1024]{1,0:T(8,128)(2,1)}, bf16[192,1024]{1,0:T(8,128)(2,1)S(1)}, u32[]{:S(2)}, u32[]{:S(2)}) collective-permute-start(bf16[192,1024]{1,0:T(8,128)(2,1)} %get-tuple-element.542), channel_id=1, source_target_pairs={{0,2},{1,3},{2,0},{3,1},{4,6},{5,7},{6,4},{7,5},{8,10},{9,11},{10,... | collective-permute-start | bytes 1179656 | tf_op jit(solution)/shard_map/ppermute | solution.py:65
  393.8 14.2 %collective-permute-start.63 = (f32[128,1024]{1,0:T(8,128)}, f32[128,1024]{1,0:T(8,128)S(1)}, u32[]{:S(2)}, u32[]{:S(2)}) collective-permute-start(f32[128,1024]{1,0:T(8,128)} %get-tuple-element.577), channel_id=1, source_target_pairs={{0,1},{1,0},{2,3},{3,2},{4,5},{5,4},{6,7},{7,6},{8,9},{9,8},{10,11... | collective-permute-start | bytes 1572872 | tf_op jit(solution)/shard_map/ppermute | solution.py:65
  404.5 13.7 %all-to-all-start = ((f32[32,1,2176]{2,1,0:T(1,128)}), f32[32,1,2176]{2,1,0:T(1,128)S(1)}, u32[]{:S(2)}, u32[]{:S(2)}) async-start(f32[32,1,2176]{2,1,0:T(1,128)} %copy.43), calls=%async_computation | async-start | bytes 557056 | tf_op jit(solution)/shard_map/all_to_all | solution.py:1800
  408.0 13.5 %collective-permute-start.64 = (f32[128,1024]{1,0:T(8,128)}, f32[128,1024]{1,0:T(8,128)S(1)}, u32[]{:S(2)}, u32[]{:S(2)}) collective-permute-start(f32[128,1024]{1,0:T(8,128)} %get-tuple-element.579), channel_id=1, source_target_pairs={{0,1},{1,0},{2,3},{3,2},{4,5},{5,4},{6,7},{7,6},{8,9},{9,8},{10,11... | collective-permute-start | bytes 1572872 | tf_op jit(solution)/shard_map/ppermute | solution.py:65
  (79 other events, 547.6 us)

commit v6 on v5

--- a/solution.py
+++ b/solution.py
@@ -431,7 +431,8 @@
             scratch += [pltpu.VMEM((rows, self.width), F32)]
         shapes = list(self.outputs)
         if squares:
-            shape = (norm[0], 128 + self.width * (len(norm) - 2)) if norm else (8, self.width)
+            lines = 1 + (len(norm) - 2) * self.width // 128
+            shape = (norm[0], (lines + 7) // 8 * 8, 128) if norm else (8, self.width)
             shapes.append(jax.ShapeDtypeStruct(shape, F32))
         more = list(norm[1:])
         scratch += [pltpu.VMEM((8, self.width), F32)] if squares else []
@@ -518,11 +519,14 @@
         square_out[...] = square_ref[...]
     if norm:
         total = jnp.sum(square_ref[...]) + jnp.sum(norm[0][...])
-        square_out[:, :128] = jnp.full((square_out.shape[0], 128), total, F32)
-        for i, ref in enumerate(norm[1:]):
-            width = ref.shape[1]
-            spot = slice(128 + i * width, 128 + (i + 1) * width)
-            square_out[:, spot] = jnp.broadcast_to(ref[...], (square_out.shape[0], width))
+        square_out[...] = jnp.zeros_like(square_out)
+        square_out[:, 0, :] = jnp.full((square_out.shape[0], 128), total, F32)
+        line = 1
+        for ref in norm[1:]:
+            for low in range(0, ref.shape[1], 128):
+                value = jnp.broadcast_to(ref[:, low : low + 128], (square_out.shape[0], 128))
+                square_out[:, line, :] = value
+                line += 1
     finish(leaving)
 
 
@@ -1197,7 +1201,7 @@
             give[r_v, cols] = d_value[CHUNK:].astype(BF)
         return 0
 
-    lax.fori_loop(0, pairs, pair, 0)
+    lax.fori_loop(0, pairs, pair, 0, unroll=2)
 
 
 def context_back(
@@ -1421,8 +1425,8 @@
     for c in range(sw.shape[0]):
         pieces.append(("shrink", c, (c,), (more if c == 0 else []) + [load(i, (c,)) for i in (16, 17, 18)]))
 
-    sums = jnp.sum(squares[...], axis=0, keepdims=True)
-    total = sums[:, 0:1] + jnp.sum(sums[:, 128:] * sums[:, 128:], axis=1, keepdims=True)
+    sums = jnp.sum(squares[...], axis=0)
+    total = sums[0:1, 0:1] + jnp.sum(sums[1:] * sums[1:])
     k = CLIP_LIMIT / jnp.maximum(jnp.sqrt(total), CLIP_LIMIT)
     finish(gradients)
     leaving = []
@@ -1798,8 +1802,8 @@
     grad_joint = jnp.stack([out_last[outcome[("joint", k)]] for k in range(3)])
 
     squares = lax.all_to_all(out_last[-1], "fsdp", 0, 0, tiled=True)
-    gains_sum = jnp.sum(squares[:, 128:], axis=0)
-    total_sq = jnp.sum(squares[:, 0]) + jnp.sum(gains_sum * gains_sum)
+    gains_sum = jnp.sum(squares[:, 1 : 1 + 2 * width // 128], axis=0)
+    total_sq = jnp.sum(squares[:, 0, 0]) + jnp.sum(gains_sum * gains_sum)
     grad_gains = lax.dynamic_index_in_dim(
         gains_sum.reshape(2, count, lane), cube.index, 1, keepdims=False
     )

time: 443 us -> 443 us (level)
    unnamed x123 -> x124, local copies, waits for them, and re-layouts: 12.8 us -> 12.8 us
  transfers between devices with their start and end apart: 66 -> 66, of which waited for: 23 -> 24; matrix products, arithmetic and copies ran while one was open for 4% -> 3% of each run, Pallas kernels for 35% -> 34%
where the time goes in v6:
time: 443 us; the launch traced here: 436 us
  Pallas kernels  189 us (43%)
  waiting for transfers between devices  149 us (34%)
  starting transfers between devices  65.6 us (15%)
  local copies, waits for them, and re-layouts  14.7 us (3%)
  other arithmetic  13.9 us (3%)
  between operations  4.46 us (1%)
    ppermute x65, waiting for transfers between devices, swap(): return lax.ppermute(value, 'fsdp', pairs)  139 us
    pallas_call x16, Pallas kernels, run(): pl.pallas_call(functools.partial(jobs_kernel, self.work, len(inputs), sel...  65.2 us
    ppermute x65, starting transfers between devices, swap(): return lax.ppermute(value, 'fsdp', pairs)  62.9 us
    pallas_call x2, Pallas kernels, ffn_rows(): pl.pallas_call(functools.partial(ffn_rows_kernel, first, len(arrays), tab...  24.6 us
    pallas_call x2, Pallas kernels, ffn_weights(): pl.pallas_call(functools.partial(ffn_weights_kernel, first, len(arrays),...  21.7 us
    pallas_call x1, Pallas kernels, context_back(): pl.pallas_call(functools.partial(context_back_kernel, run, width // HEADS...  18.1 us
    pallas_call x1, Pallas kernels, context_forward(): pl.pallas_call(functools.partial(context_kernel, run, width // HEADS, len...  12.9 us
    unnamed x124, local copies, waits for them, and re-layouts  12.8 us
  transfers between devices with their start and end apart: 66, of which 24 were waited for; matrix products, arithmetic and copies ran while one was open for 3% of the time, Pallas kernels for 34%

profile of v6, /device:TPU:0, one launch (start us, length us, event | category | flops | bytes accessed | tf_op | source)
XLA Modules:
  0.0 436.0 jit_solution(6526624821216113203)
XLA Ops:
  2.2 4.0 collective-permute-start.1
  15.3 3.4 split_weights.1
  19.5 2.8 pack_two.1
  25.9 9.0 %collective-permute-done = bf16[128,1024]{1,0:T(8,128)(2,1)S(1)} collective-permute-done((bf16[128,1024]{1,0:T(8,128)(2,1)S(1)}, bf16[128,1024]{1,0:T(8,128)(2,1)S(1)}, u32[]{:S(2)}, u32[]{:S(2)}) %collective-permute-start) | collective-permute-done | bytes 262176 | tf_op jit(solution)/shard_map/ppermute | solution.py:65
  38.3 5.0 %pack_three.1 = (bf16[320,1024]{1,0:T(8,128)(2,1)}, bf16[320,1024]{1,0:T(8,128)(2,1)}, bf16[320,1024]{1,0:T(8,128)(2,1)}, bf16[832,1024]{1,0:T(8,128)(2,1)}) custom-call(s32[3]{0:T(128)} %pad_add_fusion.meta, bf16[64,1024]{1,0:T(8,128)(2,1)} %get-tuple-element.328.refs_5_.refs_0_.refs_4_, bf16[64,1024]{1,0:T(8,128)(2,1)} %copy-done.26, ...), custom_call_target="tpu_custom_call" | custom-call | flops 1 | bytes 1 | tf_op jit(solution)/shard_map/pack_three/pallas_call | solution.py:439
  49.0 9.6 %collective-permute-done.13.refs_2_ = bf16[128,1024]{1,0:T(8,128)(2,1)S(1)} collective-permute-done((bf16[128,1024]{1,0:T(8,128)(2,1)S(1)}, bf16[128,1024]{1,0:T(8,128)(2,1)S(1)}, u32[]{:S(2)}, u32[]{:S(2)}) %collective-permute-start.13) | collective-permute-done | bytes 262176 | tf_op jit(solution)/shard_map/ppermute | solution.py:65
  61.6 3.1 expand_units.1
  64.7 2.7 collective-permute-done.8.refs_0_.refs_3_.refs_2_.refs_4_
  68.7 3.0 pack_late.1
  75.2 2.1 collective-permute-start.19
  77.3 8.2 %joint_forward.1 = (bf16[256,1024]{1,0:T(8,128)(2,1)}, bf16[256,1024]{1,0:T(8,128)(2,1)}, bf16[528,1024]{1,0:T(8,128)(2,1)}, f32[8,1024]{1,0:T(8,128)}) custom-call(s32[3]{0:T(128)} %pad_add_fusion.meta, bf16[256,1024]{1,0:T(8,128)(2,1)} %pad_maximum_fusion.1.x, bf16[64,1024]{1,0:T(8,128)(2,1)} %get-tuple-element.335.refs_2_.refs_7_.refs_0_, ...), custom_call_target="tpu_custom_call" | custom-call | flops 1 | bytes 1 | tf_op jit(solution)/shard_map/joint_forward/pallas_call | solution.py:1037
  86.3 3.8 collective-permute-done.19
  93.6 3.6 pack_five.1
  100.5 2.6 pack_output.1
  104.2 23.6 %collective-permute-done.20.refs_3_.refs_5_ = bf16[128,1024]{1,0:T(8,128)(2,1)S(1)} collective-permute-done((bf16[128,1024]{1,0:T(8,128)(2,1)}, bf16[128,1024]{1,0:T(8,128)(2,1)S(1)}, u32[]{:S(2)}, u32[]{:S(2)}) %collective-permute-start.20) | collective-permute-done | bytes 262176 | tf_op jit(solution)/shard_map/ppermute | solution.py:65
  129.3 5.8 %collective-permute-done.21.refs_7_.refs_9_ = bf16[128,1024]{1,0:T(8,128)(2,1)} collective-permute-done((bf16[128,1024]{1,0:T(8,128)(2,1)}, bf16[128,1024]{1,0:T(8,128)(2,1)}, u32[]{:S(2)}, u32[]{:S(2)}) %collective-permute-start.21) | collective-permute-done | bytes 262176 | tf_op jit(solution)/shard_map/ppermute | solution.py:65
  135.2 2.8 pack_core.1
  138.3 8.9 %collective-permute-done.26.refs_2_.refs_6_ = bf16[512,1024]{1,0:T(8,128)(2,1)S(1)} collective-permute-done((bf16[512,1024]{1,0:T(8,128)(2,1)}, bf16[512,1024]{1,0:T(8,128)(2,1)S(1)}, u32[]{:S(2)}, u32[]{:S(2)}) %collective-permute-start.26) | collective-permute-done | bytes 1048608 | tf_op jit(solution)/shard_map/ppermute | solution.py:65
  148.2 3.6 pack_seven.1
  155.7 12.9 %context_forward.1 = (bf16[256,1024]{1,0:T(8,128)(2,1)}, f32[256,1024]{1,0:T(8,128)}, bf16[256,1024]{1,0:T(8,128)(2,1)}) custom-call(s32[3]{0:T(128)} %pad_add_fusion.meta, bf16[256,1024]{1,0:T(8,128)(2,1)} %get-tuple-element.358.query, bf16[528,1024]{1,0:T(8,128)(2,1)} %get-tuple-element.359.own.refs_0_, ...), custom_call_target="tpu_custom_call" | custom-call | flops 1 | bytes 1 | tf_op jit(solution)/shard_map/context_forward/pallas_call | solution.py:1129
  169.2 3.6 pack_eight.1
  172.8 2.4 collective-permute-done.28.refs_7_
  179.2 11.7 %ffn_rows.2 = (f32[512,1024]{1,0:T(8,128)}, bf16[512,1024]{1,0:T(8,128)(2,1)}, bf16[512,1024]{1,0:T(8,128)(2,1)}, bf16[512,1024]{1,0:T(8,128)(2,1)}) custom-call(s32[3]{0:T(128)} %pad_add_fusion.meta, bf16[256,1024]{1,0:T(8,128)(2,1)} %get-tuple-element.391.n2m, bf16[256,1024]{1,0:T(8,128)(2,1)} %copy-done.15, bf16[256,1024]{1,0:T(8,128)(2,1)} %copy-done.5, ...), custom_call_target="tpu_custom_call" | custom-call | flops 1 | bytes 1 | tf_op jit(solution)/shard_map/ffn_rows/pallas_call | solution.py:857
  190.9 10.4 %ffn_weights.2 = (f32[512,1024]{1,0:T(8,128)}, bf16[512,1024]{1,0:T(8,128)(2,1)}, bf16[512,1024]{1,0:T(8,128)(2,1)}, bf16[512,1024]{1,0:T(8,128)(2,1)}, bf16[512...) custom-call(s32[3]{0:T(128)} %pad_add_fusion.meta, ...), custom_call_target="tpu_custom_call" | custom-call | flops 1 | bytes 1 | tf_op jit(solution)/shard_map/ffn_weights/pallas_call | solution.py:928
  204.9 12.9 %ffn_rows.3 = (f32[256,1024]{1,0:T(8,128)}, f32[256,1024]{1,0:T(8,128)}, bf16[512,1024]{1,0:T(8,128)(2,1)}, bf16[512,1024]{1,0:T(8,128)(2,1)}, bf16[512,1024]{1,0:T(8,128)(2,1)}) custom-call(s32[3]{0:T(128)} %pad_add_fusion.meta, bf16[256,1024]{1,0:T(8,128)(2,1)} %get-tuple-element.391.n2m, bf16[256,1024]{1,0:T(8,128)(2,1)} %copy-done.15, ...), custom_call_target="tpu_custom_call" | custom-call | flops 1 | bytes 1 | tf_op jit(solution)/shard_map/ffn_rows/pallas_call | solution.py:857
  217.8 11.3 %ffn_weights.3 = (f32[256,1024]{1,0:T(8,128)}, bf16[256,1024]{1,0:T(8,128)(2,1)}, bf16[512,1024]{1,0:T(8,128)(2,1)}, bf16[512,1024]{1,0:T(8,128)(2,1)}, bf16[512...) custom-call(s32[3]{0:T(128)} %pad_add_fusion.meta, ...), custom_call_target="tpu_custom_call" | custom-call | flops 1 | bytes 1 | tf_op jit(solution)/shard_map/ffn_weights/pallas_call | solution.py:928
  233.9 2.1 collective-permute-start.35
  236.0 18.1 %context_back.1 = (f32[256,1024]{1,0:T(8,128)}, f32[1,1024]{1,0:T(1,128)}, bf16[256,1024]{1,0:T(8,128)(2,1)}, bf16[256,1024]{1,0:T(8,128)(2,1)}, f32[256,2048]{1,0:T(8,128)}, /*index=5*/bf16[528,1024]{1,0:T(8,128)(2,1)}) custom-call(s32[3]{0:T(128)} %pad_add_fusion.meta, f32[256,1024]{1,0:T(8,128)} %get-tuple-element.439.dn_own, ...), custom_call_target="tpu_custom_call" | custom-call | flops 1 | bytes 1 | tf_op jit(solution)/shard_map/context_back/pallas_call | solution.py:1213
  255.1 5.8 %collective-permute-done.35 = bf16[16,8,1024]{2,1,0:T(8,128)(2,1)S(1)} collective-permute-done((bf16[16,8,1024]{2,1,0:T(8,128)(2,1)S(1)}, bf16[16,8,1024]{2,1,0:T(8,128)(2,1)S(1)}, u32[]{:S(2)}, u32[]{:S(2)}) %collective-permute-start.35) | collective-permute-done | bytes 262176 | tf_op jit(solution)/shard_map/ppermute | solution.py:65
  262.4 8.2 %turn_three.1 = (bf16[512,1024]{1,0:T(8,128)(2,1)}, bf16[512,1024]{1,0:T(8,128)(2,1)}, bf16[512,1024]{1,0:T(8,128)(2,1)}, bf16[256,1024]{1,0:T(8,128)(2,1)}, bf1...) custom-call(s32[3]{0:T(128)} %pad_add_fusion.meta, ...), custom_call_target="tpu_custom_call" | custom-call | flops 1 | bytes 1 | tf_op jit(solution)/shard_map/turn_three/pallas_call | solution.py:439
  273.6 4.4 %output_grad.1 = (bf16[512,1024]{1,0:T(8,128)(2,1)}, bf16[512,1024]{1,0:T(8,128)(2,1)}) custom-call(s32[3]{0:T(128)} %pad_add_fusion.meta, bf16[256,1024]{1,0:T(8,128)(2,1)} %get-tuple-element.445.context, bf16[256,1024]{1,0:T(8,128)(2,1)} %get-tuple-element.480.grad), custom_call_target="tpu_custom_call" | custom-call | flops 1 | bytes 1 | tf_op jit(solution)/shard_map/output_grad/pallas_call | solution.py:1295
  278.0 30.1 %collective-permute-done.40.dkv_got = bf16[528,1024]{1,0:T(8,128)(2,1)S(1)} collective-permute-done((bf16[528,1024]{1,0:T(8,128)(2,1)}, bf16[528,1024]{1,0:T(8,128)(2,1)S(1)}, u32[]{:S(2)}, u32[]{:S(2)}) %collective-permute-start.40) | collective-permute-done | bytes 1081376 | tf_op jit(solution)/shard_map/ppermute | solution.py:65
  309.1 7.5 %joint_grad.1 = (bf16[1536,1024]{1,0:T(8,128)(2,1)}, bf16[1536,1024]{1,0:T(8,128)(2,1)}, bf16[256,2048]{1,0:T(8,128)(2,1)}) custom-call(s32[3]{0:T(128)} %pad_add_fusion.meta, bf16[256,1024]{1,0:T(8,128)(2,1)} %get-tuple-element.442.first, bf16[256,1024]{1,0:T(8,128)(2,1)} %get-tuple-element.441.dq, f32[256,2048]{1,0:T(8,128)} %get-tuple-element.443.dkv_own, ...), custom_call_target="tpu_custom_call" | custom-call | flops 1 | bytes 1 | tf_op jit(solution)/shard_map/joint_grad/pallas_call | solution.py:1333
  316.6 2.4 collective-permute-done.45.refs_3_
  319.0 5.3 %turn_four.1 = (bf16[256,1024]{1,0:T(8,128)(2,1)}, bf16[256,1024]{1,0:T(8,128)(2,1)}, bf16[256,1024]{1,0:T(8,128)(2,1)}, bf16[128,1024]{1,0:T(8,128)(2,1)}, bf16...) custom-call(s32[3]{0:T(128)} %pad_add_fusion.meta, ...), custom_call_target="tpu_custom_call" | custom-call | flops 1 | bytes 1 | tf_op jit(solution)/shard_map/turn_four/pallas_call | solution.py:439
  327.0 8.8 %input_back.1 = (bf16[256,1024]{1,0:T(8,128)(2,1)}, f32[1,1024]{1,0:T(1,128)}) custom-call(s32[3]{0:T(128)} %pad_add_fusion.meta, bf16[256,1024]{1,0:T(8,128)(2,1)} %get-tuple-element.441.dq, bf16[256,2048]{1,0:T(8,128)(2,1)} %get-tuple-element.503.dkv, f32[256,1024]{1,0:T(8,128)} %get-tuple-element.504.dh, bf16[256,1024]{1,0:T(8,128)(2,1)} %pad_maximum_fusion.1.x, ...), custom_call_target="tpu_custom_call" | custom-call | flops 1 | bytes 1 | tf_op jit(solution)/shard_map/input_back/pallas_call | solution.py:1363
  336.8 6.1 %joint_core.1 = (bf16[256,1024]{1,0:T(8,128)(2,1)}, bf16[384,1024]{1,0:T(8,128)(2,1)}, bf16[384,1024]{1,0:T(8,128)(2,1)}, bf16[256,1024]{1,0:T(8,128)(2,1)}, bf1...) custom-call(s32[3]{0:T(128)} %pad_add_fusion.meta, ...), custom_call_target="tpu_custom_call" | custom-call | flops 1 | bytes 1 | tf_op jit(solution)/shard_map/joint_core/pallas_call | solution.py:439
  347.7 4.4 %turn_five.1 = (f32[128,1024]{1,0:T(8,128)}, f32[128,1024]{1,0:T(8,128)}, f32[128,1024]{1,0:T(8,128)}, f32[128,1024]{1,0:T(8,128)}, f32[128,1024]{1,0:T(8,128)}, /*index=5*/f32[128,1024]{1,0:T(8,128)}, f32[8,1024]{1,0:T(8,128)}) custom-call(s32[3]{0:T(128)} %pad_add_fusion.meta, bf16[256,1024]{1,0:T(8,128)(2,1)} %copy-done.42, ...), custom_call_target="tpu_custom_call" | custom-call | flops 1 | bytes 1 | tf_op jit(solution)/shard_map/turn_five/pallas_call | solution.py:439
  352.1 7.6 %collective-permute-done.49 = bf16[16,8,1024]{2,1,0:T(8,128)(2,1)} collective-permute-done((bf16[16,8,1024]{2,1,0:T(8,128)(2,1)}, bf16[16,8,1024]{2,1,0:T(8,128)(2,1)}, u32[]{:S(2)}, u32[]{:S(2)}) %collective-permute-start.49) | collective-permute-done | bytes 262176 | tf_op jit(solution)/shard_map/ppermute | solution.py:65
  361.6 3.6 collective-permute-done.51.refs_3_
  366.5 4.3 turn_nine.1
  375.3 8.6 %collective-permute-done.59.refs_20_ = bf16[128,1024]{1,0:T(8,128)(2,1)S(1)} collective-permute-done((bf16[128,1024]{1,0:T(8,128)(2,1)S(1)}, bf16[128,1024]{1,0:T(8,128)(2,1)S(1)}, u32[]{:S(2)}, u32[]{:S(2)}) %collective-permute-start.59) | collective-permute-done | bytes 262176 | tf_op jit(solution)/shard_map/ppermute | solution.py:65
  386.7 3.2 turn_ten.1
  393.7 4.1 collective-permute-done.62.refs_4_
  398.6 3.7 turn_last.1
  402.4 2.7 all-to-all-start
  408.5 9.9 %all-to-all-done.squares = f32[32,24,128]{2,1,0:T(8,128)S(1)} async-done(((f32[32,24,128]{2,1,0:T(8,128)}), f32[32,24,128]{2,1,0:T(8,128)S(1)}, u32[]{:S(2)}, u32[]{:S(2)}) %all-to-all-start) | async-done | bytes 393248 | tf_op jit(solution)/shard_map/all_to_all | solution.py:1804
  422.6 11.8 %adam_matrices.1 = (f32[64,8192]{1,0:T(8,128)}, f32[64,8192]{1,0:T(8,128)}, f32[64,8192]{1,0:T(8,128)}, f32[64,3072]{1,0:T(8,128)}, f32[64,3072]{1,0:T(8,128)}, ...) custom-call(s32[3]{0:T(128)} %pad_add_fusion.meta, ...), custom_call_target="tpu_custom_call" | custom-call | flops 1 | bytes 1 | tf_op jit(solution)/shard_map/adam_matrices/pallas_call | solution.py:1481
  (279 shorter events, 95.8 us)
Async XLA Ops:
  22.3 12.5 %collective-permute-start.5 = (bf16[160,1024]{1,0:T(8,128)(2,1)}, bf16[160,1024]{1,0:T(8,128)(2,1)S(1)}, u32[]{:S(2)}, u32[]{:S(2)}) collective-permute-start(bf16[160,1024]{1,0:T(8,128)(2,1)} %get-tuple-element.325), channel_id=1, source_target_pairs={{0,4},{1,5},{2,6},{3,7},{4,0},{5,1},{6,2},{7,3},{8,12},{9,13},{10,... | collective-permute-start | bytes 983048 | tf_op jit(solution)/shard_map/ppermute | solution.py:65
  23.5 13.3 %collective-permute-start.6 = (bf16[160,1024]{1,0:T(8,128)(2,1)}, bf16[160,1024]{1,0:T(8,128)(2,1)S(1)}, u32[]{:S(2)}, u32[]{:S(2)}) collective-permute-start(bf16[160,1024]{1,0:T(8,128)(2,1)} %get-tuple-element.326), channel_id=1, source_target_pairs={{0,8},{1,9},{2,10},{3,11},{4,12},{5,13},{6,14},{7,15},{8,0},{9,1},... | collective-permute-start | bytes 983048 | tf_op jit(solution)/shard_map/ppermute | solution.py:65
  23.9 12.9 %collective-permute-start.7 = (bf16[160,1024]{1,0:T(8,128)(2,1)}, bf16[160,1024]{1,0:T(8,128)(2,1)S(1)}, u32[]{:S(2)}, u32[]{:S(2)}) collective-permute-start(bf16[160,1024]{1,0:T(8,128)(2,1)} %get-tuple-element.327), channel_id=1, source_target_pairs={{0,2},{1,3},{2,0},{3,1},{4,6},{5,7},{6,4},{7,5},{8,10},{9,11},{10,... | collective-permute-start | bytes 983048 | tf_op jit(solution)/shard_map/ppermute | solution.py:65
  43.3 24.2 %collective-permute-start.11 = (bf16[832,1024]{1,0:T(8,128)(2,1)}, bf16[832,1024]{1,0:T(8,128)(2,1)}, u32[]{:S(2)}, u32[]{:S(2)}) collective-permute-start(bf16[832,1024]{1,0:T(8,128)(2,1)} %get-tuple-element.342), channel_id=1, source_target_pairs={{0,1},{1,0},{2,3},{3,2},{4,5},{5,4},{6,7},{7,6},{8,9},{9,8},{10,11... | collective-permute-start | bytes 5111816 | tf_op jit(solution)/shard_map/ppermute | solution.py:65
  43.3 15.3 %collective-permute-start.13 = (bf16[128,1024]{1,0:T(8,128)(2,1)S(1)}, bf16[128,1024]{1,0:T(8,128)(2,1)S(1)}, u32[]{:S(2)}, u32[]{:S(2)}) collective-permute-start(bf16[128,1024]{1,0:T(8,128)(2,1)S(1)} %copy-done.61), channel_id=1, source_target_pairs={{0,16},{1,17},{2,18},{3,19},{4,20},{5,21},{6,22},{7,23},{8,24},{9,... | collective-permute-start | bytes 786440 | tf_op jit(solution)/shard_map/ppermute | solution.py:65
  45.0 22.5 %collective-permute-start.8 = (bf16[320,1024]{1,0:T(8,128)(2,1)}, bf16[320,1024]{1,0:T(8,128)(2,1)S(1)}, u32[]{:S(2)}, u32[]{:S(2)}) collective-permute-start(bf16[320,1024]{1,0:T(8,128)(2,1)} %get-tuple-element.339), channel_id=1, source_target_pairs={{0,8},{1,9},{2,10},{3,11},{4,12},{5,13},{6,14},{7,15},{8,0},{9,1},... | collective-permute-start | bytes 1966088 | tf_op jit(solution)/shard_map/ppermute | solution.py:65
  46.5 20.9 %collective-permute-start.9 = (bf16[320,1024]{1,0:T(8,128)(2,1)}, bf16[320,1024]{1,0:T(8,128)(2,1)S(1)}, u32[]{:S(2)}, u32[]{:S(2)}) collective-permute-start(bf16[320,1024]{1,0:T(8,128)(2,1)} %get-tuple-element.340), channel_id=1, source_target_pairs={{0,2},{1,3},{2,0},{3,1},{4,6},{5,7},{6,4},{7,5},{8,10},{9,11},{10,... | collective-permute-start | bytes 1966088 | tf_op jit(solution)/shard_map/ppermute | solution.py:65
  47.7 19.8 %collective-permute-start.10 = (bf16[320,1024]{1,0:T(8,128)(2,1)}, bf16[320,1024]{1,0:T(8,128)(2,1)S(1)}, u32[]{:S(2)}, u32[]{:S(2)}) collective-permute-start(bf16[320,1024]{1,0:T(8,128)(2,1)} %get-tuple-element.341), channel_id=1, source_target_pairs={{0,4},{1,5},{2,6},{3,7},{4,0},{5,1},{6,2},{7,3},{8,12},{9,13},{10,... | collective-permute-start | bytes 1966088 | tf_op jit(solution)/shard_map/ppermute | solution.py:65
  71.8 20.0 %collective-permute-start.16 = (bf16[256,1024]{1,0:T(8,128)(2,1)S(1)}, bf16[256,1024]{1,0:T(8,128)(2,1)S(1)}, u32[]{:S(2)}, u32[]{:S(2)}) collective-permute-start(bf16[256,1024]{1,0:T(8,128)(2,1)S(1)} %copy-done.3), channel_id=1, source_target_pairs={{0,8},{1,9},{2,10},{3,11},{4,12},{5,13},{6,14},{7,15},{8,0},{9,1},... | collective-permute-start | bytes 1572872 | tf_op jit(solution)/shard_map/ppermute | solution.py:65
  72.1 19.7 %collective-permute-start.17 = (bf16[256,1024]{1,0:T(8,128)(2,1)S(1)}, bf16[256,1024]{1,0:T(8,128)(2,1)S(1)}, u32[]{:S(2)}, u32[]{:S(2)}) collective-permute-start(bf16[256,1024]{1,0:T(8,128)(2,1)S(1)} %copy-done.10), channel_id=1, source_target_pairs={{0,2},{1,3},{2,0},{3,1},{4,6},{5,7},{6,4},{7,5},{8,10},{9,11},{10,... | collective-permute-start | bytes 1572872 | tf_op jit(solution)/shard_map/ppermute | solution.py:65
  73.0 18.8 %collective-permute-start.18 = (bf16[256,1024]{1,0:T(8,128)(2,1)S(1)}, bf16[256,1024]{1,0:T(8,128)(2,1)S(1)}, u32[]{:S(2)}, u32[]{:S(2)}) collective-permute-start(bf16[256,1024]{1,0:T(8,128)(2,1)S(1)} %copy-done.11), channel_id=1, source_target_pairs={{0,4},{1,5},{2,6},{3,7},{4,0},{5,1},{6,2},{7,3},{8,12},{9,13},{10,... | collective-permute-start | bytes 1572872 | tf_op jit(solution)/shard_map/ppermute | solution.py:65
  75.2 15.0 %collective-permute-start.19 = (bf16[128,1024]{1,0:T(8,128)(2,1)}, bf16[128,1024]{1,0:T(8,128)(2,1)S(1)}, u32[]{:S(2)}, u32[]{:S(2)}) collective-permute-start(bf16[128,1024]{1,0:T(8,128)(2,1)} %select_bitcast_fusion.2), channel_id=1, source_target_pairs={{0,16},{1,17},{2,18},{3,19},{4,20},{5,21},{6,22},{7,23},{8,24},{9,... | collective-permute-start | bytes 786440 | tf_op jit(solution)/shard_map/ppermute | solution.py:65
  85.5 61.7 %collective-permute-start.15 = (bf16[528,1024]{1,0:T(8,128)(2,1)}, bf16[528,1024]{1,0:T(8,128)(2,1)}, u32[]{:S(2)}, u32[]{:S(2)}) collective-permute-start(bf16[528,1024]{1,0:T(8,128)(2,1)} %get-tuple-element.359.own.refs_0_), channel_id=1, source_target_pairs={{0,16},{1,17},{2,18},{3,19},{4,20},{5,21},{6,22},{7,23},{8,24},{9,... | collective-permute-start | bytes 3244040 | tf_op jit(solution)/shard_map/ppermute | solution.py:65
  97.2 41.1 %collective-permute-start.24 = (bf16[512,1024]{1,0:T(8,128)(2,1)}, bf16[512,1024]{1,0:T(8,128)(2,1)S(1)}, u32[]{:S(2)}, u32[]{:S(2)}) collective-permute-start(bf16[512,1024]{1,0:T(8,128)(2,1)} %get-tuple-element.371), channel_id=1, source_target_pairs={{0,2},{1,3},{2,0},{3,1},{4,6},{5,7},{6,4},{7,5},{8,10},{9,11},{10,... | collective-permute-start | bytes 3145736 | tf_op jit(solution)/shard_map/ppermute | solution.py:65
  98.4 39.9 %collective-permute-start.25 = (bf16[512,1024]{1,0:T(8,128)(2,1)}, bf16[512,1024]{1,0:T(8,128)(2,1)S(1)}, u32[]{:S(2)}, u32[]{:S(2)}) collective-permute-start(bf16[512,1024]{1,0:T(8,128)(2,1)} %get-tuple-element.372), channel_id=1, source_target_pairs={{0,4},{1,5},{2,6},{3,7},{4,0},{5,1},{6,2},{7,3},{8,12},{9,13},{10,... | collective-permute-start | bytes 3145736 | tf_op jit(solution)/shard_map/ppermute | solution.py:65
  99.8 47.4 %collective-permute-start.26 = (bf16[512,1024]{1,0:T(8,128)(2,1)}, bf16[512,1024]{1,0:T(8,128)(2,1)S(1)}, u32[]{:S(2)}, u32[]{:S(2)}) collective-permute-start(bf16[512,1024]{1,0:T(8,128)(2,1)} %get-tuple-element.373), channel_id=1, source_target_pairs={{0,8},{1,9},{2,10},{3,11},{4,12},{5,13},{6,14},{7,15},{8,0},{9,1},... | collective-permute-start | bytes 3145736 | tf_op jit(solution)/shard_map/ppermute | solution.py:65
  103.1 24.7 %collective-permute-start.20 = (bf16[128,1024]{1,0:T(8,128)(2,1)}, bf16[128,1024]{1,0:T(8,128)(2,1)S(1)}, u32[]{:S(2)}, u32[]{:S(2)}) collective-permute-start(bf16[128,1024]{1,0:T(8,128)(2,1)} %get-tuple-element.380), channel_id=1, source_target_pairs={{0,2},{1,3},{2,0},{3,1},{4,6},{5,7},{6,4},{7,5},{8,10},{9,11},{10,... | collective-permute-start | bytes 786440 | tf_op jit(solution)/shard_map/ppermute | solution.py:65
  138.0 17.6 %collective-permute-start.22 = (bf16[512,1024]{1,0:T(8,128)(2,1)}, bf16[512,1024]{1,0:T(8,128)(2,1)}, u32[]{:S(2)}, u32[]{:S(2)}) collective-permute-start(bf16[512,1024]{1,0:T(8,128)(2,1)} %pack_core.1), channel_id=1, source_target_pairs={{0,1},{1,0},{2,3},{3,2},{4,5},{5,4},{6,7},{7,6},{8,9},{9,8},{10,11... | collective-permute-start | bytes 3145736 | tf_op jit(solution)/shard_map/ppermute | solution.py:65
  151.8 23.5 %collective-permute-start.28 = (bf16[512,1024]{1,0:T(8,128)(2,1)}, bf16[512,1024]{1,0:T(8,128)(2,1)S(1)}, u32[]{:S(2)}, u32[]{:S(2)}) collective-permute-start(bf16[512,1024]{1,0:T(8,128)(2,1)} %get-tuple-element.403), channel_id=1, source_target_pairs={{0,2},{1,3},{2,0},{3,1},{4,6},{5,7},{6,4},{7,5},{8,10},{9,11},{10,... | collective-permute-start | bytes 3145736 | tf_op jit(solution)/shard_map/ppermute | solution.py:65
  152.9 23.2 %collective-permute-start.29 = (bf16[512,1024]{1,0:T(8,128)(2,1)}, bf16[512,1024]{1,0:T(8,128)(2,1)S(1)}, u32[]{:S(2)}, u32[]{:S(2)}) collective-permute-start(bf16[512,1024]{1,0:T(8,128)(2,1)} %get-tuple-element.404), channel_id=1, source_target_pairs={{0,4},{1,5},{2,6},{3,7},{4,0},{5,1},{6,2},{7,3},{8,12},{9,13},{10,... | collective-permute-start | bytes 3145736 | tf_op jit(solution)/shard_map/ppermute | solution.py:65
  153.4 23.1 %collective-permute-start.30 = (bf16[512,1024]{1,0:T(8,128)(2,1)}, bf16[512,1024]{1,0:T(8,128)(2,1)}, u32[]{:S(2)}, u32[]{:S(2)}) collective-permute-start(bf16[512,1024]{1,0:T(8,128)(2,1)} %get-tuple-element.405), channel_id=1, source_target_pairs={{0,8},{1,9},{2,10},{3,11},{4,12},{5,13},{6,14},{7,15},{8,0},{9,1},... | collective-permute-start | bytes 3145736 | tf_op jit(solution)/shard_map/ppermute | solution.py:65
  154.8 14.3 %collective-permute-start.27 = (bf16[256,1024]{1,0:T(8,128)(2,1)S(1)}, bf16[256,1024]{1,0:T(8,128)(2,1)S(1)}, u32[]{:S(2)}, u32[]{:S(2)}) collective-permute-start(bf16[256,1024]{1,0:T(8,128)(2,1)S(1)} %multiply_convert_fusion.cm.cot), channel_id=1, source_target_pairs={{0,1},{1,0},{2,3},{3,2},{4,5},{5,4},{6,7},{7,6},{8,9},{9,8},{10,11... | collective-permute-start | bytes 1572872 | tf_op jit(solution)/shard_map/ppermute | solution.py:65
  176.5 24.8 %collective-permute-start.31 = (bf16[512,1024]{1,0:T(8,128)(2,1)}, bf16[512,1024]{1,0:T(8,128)(2,1)}, u32[]{:S(2)}, u32[]{:S(2)}) collective-permute-start(bf16[512,1024]{1,0:T(8,128)(2,1)} %get-tuple-element.418), channel_id=1, source_target_pairs={{0,8},{1,9},{2,10},{3,11},{4,12},{5,13},{6,14},{7,15},{8,0},{9,1},... | collective-permute-start | bytes 3145736 | tf_op jit(solution)/shard_map/ppermute | solution.py:65
  176.7 24.7 %collective-permute-start.32 = (bf16[512,1024]{1,0:T(8,128)(2,1)}, bf16[512,1024]{1,0:T(8,128)(2,1)}, u32[]{:S(2)}, u32[]{:S(2)}) collective-permute-start(bf16[512,1024]{1,0:T(8,128)(2,1)} %get-tuple-element.419), channel_id=1, source_target_pairs={{0,2},{1,3},{2,0},{3,1},{4,6},{5,7},{6,4},{7,5},{8,10},{9,11},{10,... | collective-permute-start | bytes 3145736 | tf_op jit(solution)/shard_map/ppermute | solution.py:65
  177.8 23.6 %collective-permute-start.33 = (bf16[512,1024]{1,0:T(8,128)(2,1)}, bf16[512,1024]{1,0:T(8,128)(2,1)S(1)}, u32[]{:S(2)}, u32[]{:S(2)}) collective-permute-start(bf16[512,1024]{1,0:T(8,128)(2,1)} %get-tuple-element.420), channel_id=1, source_target_pairs={{0,4},{1,5},{2,6},{3,7},{4,0},{5,1},{6,2},{7,3},{8,12},{9,13},{10,... | collective-permute-start | bytes 3145736 | tf_op jit(solution)/shard_map/ppermute | solution.py:65
  201.3 28.3 %collective-permute-start.36 = (bf16[512,1024]{1,0:T(8,128)(2,1)}, bf16[512,1024]{1,0:T(8,128)(2,1)S(1)}, u32[]{:S(2)}, u32[]{:S(2)}) collective-permute-start(bf16[512,1024]{1,0:T(8,128)(2,1)} %get-tuple-element.436), channel_id=1, source_target_pairs={{0,2},{1,3},{2,0},{3,1},{4,6},{5,7},{6,4},{7,5},{8,10},{9,11},{10,... | collective-permute-start | bytes 3145736 | tf_op jit(solution)/shard_map/ppermute | solution.py:65
  202.5 27.2 %collective-permute-start.37 = (bf16[512,1024]{1,0:T(8,128)(2,1)}, bf16[512,1024]{1,0:T(8,128)(2,1)S(1)}, u32[]{:S(2)}, u32[]{:S(2)}) collective-permute-start(bf16[512,1024]{1,0:T(8,128)(2,1)} %get-tuple-element.437), channel_id=1, source_target_pairs={{0,4},{1,5},{2,6},{3,7},{4,0},{5,1},{6,2},{7,3},{8,12},{9,13},{10,... | collective-permute-start | bytes 3145736 | tf_op jit(solution)/shard_map/ppermute | solution.py:65
  203.3 26.4 %collective-permute-start.38 = (bf16[512,1024]{1,0:T(8,128)(2,1)}, bf16[512,1024]{1,0:T(8,128)(2,1)}, u32[]{:S(2)}, u32[]{:S(2)}) collective-permute-start(bf16[512,1024]{1,0:T(8,128)(2,1)} %get-tuple-element.438), channel_id=1, source_target_pairs={{0,8},{1,9},{2,10},{3,11},{4,12},{5,13},{6,14},{7,15},{8,0},{9,1},... | collective-permute-start | bytes 3145736 | tf_op jit(solution)/shard_map/ppermute | solution.py:65
  229.7 31.1 %collective-permute-start.41 = (bf16[512,1024]{1,0:T(8,128)(2,1)}, bf16[512,1024]{1,0:T(8,128)(2,1)}, u32[]{:S(2)}, u32[]{:S(2)}) collective-permute-start(bf16[512,1024]{1,0:T(8,128)(2,1)} %get-tuple-element.451), channel_id=1, source_target_pairs={{0,4},{1,5},{2,6},{3,7},{4,0},{5,1},{6,2},{7,3},{8,12},{9,13},{10,... | collective-permute-start | bytes 3145736 | tf_op jit(solution)/shard_map/ppermute | solution.py:65
  231.3 31.1 %collective-permute-start.42 = (bf16[512,1024]{1,0:T(8,128)(2,1)}, bf16[512,1024]{1,0:T(8,128)(2,1)}, u32[]{:S(2)}, u32[]{:S(2)}) collective-permute-start(bf16[512,1024]{1,0:T(8,128)(2,1)} %get-tuple-element.454), channel_id=1, source_target_pairs={{0,8},{1,9},{2,10},{3,11},{4,12},{5,13},{6,14},{7,15},{8,0},{9,1},... | collective-permute-start | bytes 3145736 | tf_op jit(solution)/shard_map/ppermute | solution.py:65
  231.4 31.0 %collective-permute-start.43 = (bf16[512,1024]{1,0:T(8,128)(2,1)}, bf16[512,1024]{1,0:T(8,128)(2,1)}, u32[]{:S(2)}, u32[]{:S(2)}) collective-permute-start(bf16[512,1024]{1,0:T(8,128)(2,1)} %get-tuple-element.457), channel_id=1, source_target_pairs={{0,2},{1,3},{2,0},{3,1},{4,6},{5,7},{6,4},{7,5},{8,10},{9,11},{10,... | collective-permute-start | bytes 3145736 | tf_op jit(solution)/shard_map/ppermute | solution.py:65
  233.9 27.0 %collective-permute-start.35 = (bf16[16,8,1024]{2,1,0:T(8,128)(2,1)S(1)}, bf16[16,8,1024]{2,1,0:T(8,128)(2,1)S(1)}, u32[]{:S(2)}, u32[]{:S(2)}) collective-permute-start(bf16[16,8,1024]{2,1,0:T(8,128)(2,1)S(1)} %select_bitcast_fusion.1), channel_id=1, source_target_pairs={{0,16},{1,17},{2,18},{3,19},{4,20},{5,21},{6,22},{7,23},{8,24},{9,... | collective-permute-start | bytes 786440 | tf_op jit(solution)/shard_map/ppermute | solution.py:65
  254.1 54.0 %collective-permute-start.40 = (bf16[528,1024]{1,0:T(8,128)(2,1)}, bf16[528,1024]{1,0:T(8,128)(2,1)S(1)}, u32[]{:S(2)}, u32[]{:S(2)}) collective-permute-start(bf16[528,1024]{1,0:T(8,128)(2,1)} %get-tuple-element.444), channel_id=1, source_target_pairs={{0,16},{1,17},{2,18},{3,19},{4,20},{5,21},{6,22},{7,23},{8,24},{9,... | collective-permute-start | bytes 3244040 | tf_op jit(solution)/shard_map/ppermute | solution.py:65
  270.6 46.0 %collective-permute-start.46 = (bf16[512,1024]{1,0:T(8,128)(2,1)}, bf16[512,1024]{1,0:T(8,128)(2,1)S(1)}, u32[]{:S(2)}, u32[]{:S(2)}) collective-permute-start(bf16[512,1024]{1,0:T(8,128)(2,1)} %get-tuple-element.471), channel_id=1, source_target_pairs={{0,2},{1,3},{2,0},{3,1},{4,6},{5,7},{6,4},{7,5},{8,10},{9,11},{10,... | collective-permute-start | bytes 3145736 | tf_op jit(solution)/shard_map/ppermute | solution.py:65
  271.6 45.0 %collective-permute-start.44 = (bf16[512,1024]{1,0:T(8,128)(2,1)}, bf16[512,1024]{1,0:T(8,128)(2,1)}, u32[]{:S(2)}, u32[]{:S(2)}) collective-permute-start(bf16[512,1024]{1,0:T(8,128)(2,1)} %get-tuple-element.472), channel_id=1, source_target_pairs={{0,4},{1,5},{2,6},{3,7},{4,0},{5,1},{6,2},{7,3},{8,12},{9,13},{10,... | collective-permute-start | bytes 3145736 | tf_op jit(solution)/shard_map/ppermute | solution.py:65
  272.4 46.6 %collective-permute-start.45 = (bf16[512,1024]{1,0:T(8,128)(2,1)}, bf16[512,1024]{1,0:T(8,128)(2,1)}, u32[]{:S(2)}, u32[]{:S(2)}) collective-permute-start(bf16[512,1024]{1,0:T(8,128)(2,1)} %get-tuple-element.473), channel_id=1, source_target_pairs={{0,8},{1,9},{2,10},{3,11},{4,12},{5,13},{6,14},{7,15},{8,0},{9,1},... | collective-permute-start | bytes 3145736 | tf_op jit(solution)/shard_map/ppermute | solution.py:65
  324.3 11.6 %collective-permute-start.47 = (bf16[1536,1024]{1,0:T(8,128)(2,1)}, bf16[1536,1024]{1,0:T(8,128)(2,1)}, u32[]{:S(2)}, u32[]{:S(2)}) collective-permute-start(bf16[1536,1024]{1,0:T(8,128)(2,1)} %get-tuple-element.506.refs_9_), channel_id=1, source_target_pairs={{0,1},{1,0},{2,3},{3,2},{4,5},{5,4},{6,7},{7,6},{8,9},{9,8},{10,11... | collective-permute-start | bytes 9437192 | tf_op jit(solution)/shard_map/ppermute | solution.py:65
  324.8 20.8 %collective-permute-start.53 = (bf16[256,1024]{1,0:T(8,128)(2,1)}, bf16[256,1024]{1,0:T(8,128)(2,1)S(1)}, u32[]{:S(2)}, u32[]{:S(2)}) collective-permute-start(bf16[256,1024]{1,0:T(8,128)(2,1)} %get-tuple-element.494), channel_id=1, source_target_pairs={{0,2},{1,3},{2,0},{3,1},{4,6},{5,7},{6,4},{7,5},{8,10},{9,11},{10,... | collective-permute-start | bytes 1572872 | tf_op jit(solution)/shard_map/ppermute | solution.py:65
  325.8 22.0 %collective-permute-start.54 = (bf16[256,1024]{1,0:T(8,128)(2,1)}, bf16[256,1024]{1,0:T(8,128)(2,1)}, u32[]{:S(2)}, u32[]{:S(2)}) collective-permute-start(bf16[256,1024]{1,0:T(8,128)(2,1)} %get-tuple-element.495), channel_id=1, source_target_pairs={{0,4},{1,5},{2,6},{3,7},{4,0},{5,1},{6,2},{7,3},{8,12},{9,13},{10,... | collective-permute-start | bytes 1572872 | tf_op jit(solution)/shard_map/ppermute | solution.py:65
  327.0 20.7 %collective-permute-start.55 = (bf16[256,1024]{1,0:T(8,128)(2,1)}, bf16[256,1024]{1,0:T(8,128)(2,1)}, u32[]{:S(2)}, u32[]{:S(2)}) collective-permute-start(bf16[256,1024]{1,0:T(8,128)(2,1)} %get-tuple-element.496), channel_id=1, source_target_pairs={{0,8},{1,9},{2,10},{3,11},{4,12},{5,13},{6,14},{7,15},{8,0},{9,1},... | collective-permute-start | bytes 1572872 | tf_op jit(solution)/shard_map/ppermute | solution.py:65
  342.9 22.2 %collective-permute-start.50 = (bf16[384,1024]{1,0:T(8,128)(2,1)}, bf16[384,1024]{1,0:T(8,128)(2,1)S(1)}, u32[]{:S(2)}, u32[]{:S(2)}) collective-permute-start(bf16[384,1024]{1,0:T(8,128)(2,1)} %get-tuple-element.512), channel_id=1, source_target_pairs={{0,4},{1,5},{2,6},{3,7},{4,0},{5,1},{6,2},{7,3},{8,12},{9,13},{10,... | collective-permute-start | bytes 2359304 | tf_op jit(solution)/shard_map/ppermute | solution.py:65
  343.8 21.4 %collective-permute-start.52 = (bf16[384,1024]{1,0:T(8,128)(2,1)}, bf16[384,1024]{1,0:T(8,128)(2,1)S(1)}, u32[]{:S(2)}, u32[]{:S(2)}) collective-permute-start(bf16[384,1024]{1,0:T(8,128)(2,1)} %get-tuple-element.516), channel_id=1, source_target_pairs={{0,2},{1,3},{2,0},{3,1},{4,6},{5,7},{6,4},{7,5},{8,10},{9,11},{10,... | collective-permute-start | bytes 2359304 | tf_op jit(solution)/shard_map/ppermute | solution.py:65
  345.6 14.1 %collective-permute-start.49 = (bf16[16,8,1024]{2,1,0:T(8,128)(2,1)}, bf16[16,8,1024]{2,1,0:T(8,128)(2,1)}, u32[]{:S(2)}, u32[]{:S(2)}) collective-permute-start(bf16[16,8,1024]{2,1,0:T(8,128)(2,1)} %select_bitcast_fusion), channel_id=1, source_target_pairs={{0,16},{1,17},{2,18},{3,19},{4,20},{5,21},{6,22},{7,23},{8,24},{9,... | collective-permute-start | bytes 786440 | tf_op jit(solution)/shard_map/ppermute | solution.py:65
  347.7 17.4 %collective-permute-start.51 = (bf16[256,1024]{1,0:T(8,128)(2,1)}, bf16[256,1024]{1,0:T(8,128)(2,1)S(1)}, u32[]{:S(2)}, u32[]{:S(2)}) collective-permute-start(bf16[256,1024]{1,0:T(8,128)(2,1)} %get-tuple-element.510), channel_id=1, source_target_pairs={{0,8},{1,9},{2,10},{3,11},{4,12},{5,13},{6,14},{7,15},{8,0},{9,1},... | collective-permute-start | bytes 1572872 | tf_op jit(solution)/shard_map/ppermute | solution.py:65
  370.7 15.0 %collective-permute-start.57 = (bf16[192,1024]{1,0:T(8,128)(2,1)}, bf16[192,1024]{1,0:T(8,128)(2,1)S(1)}, u32[]{:S(2)}, u32[]{:S(2)}) collective-permute-start(bf16[192,1024]{1,0:T(8,128)(2,1)} %get-tuple-element.539), channel_id=1, source_target_pairs={{0,8},{1,9},{2,10},{3,11},{4,12},{5,13},{6,14},{7,15},{8,0},{9,1},... | collective-permute-start | bytes 1179656 | tf_op jit(solution)/shard_map/ppermute | solution.py:65
  371.7 14.0 %collective-permute-start.58 = (bf16[192,1024]{1,0:T(8,128)(2,1)}, bf16[192,1024]{1,0:T(8,128)(2,1)S(1)}, u32[]{:S(2)}, u32[]{:S(2)}) collective-permute-start(bf16[192,1024]{1,0:T(8,128)(2,1)} %get-tuple-element.542), channel_id=1, source_target_pairs={{0,2},{1,3},{2,0},{3,1},{4,6},{5,7},{6,4},{7,5},{8,10},{9,11},{10,... | collective-permute-start | bytes 1179656 | tf_op jit(solution)/shard_map/ppermute | solution.py:65
  402.4 15.9 %all-to-all-start = ((f32[32,24,128]{2,1,0:T(8,128)}), f32[32,24,128]{2,1,0:T(8,128)S(1)}, u32[]{:S(2)}, u32[]{:S(2)}) async-start(f32[32,24,128]{2,1,0:T(8,128)} %get-tuple-element.573), calls=%async_computation | async-start | bytes 786432 | tf_op jit(solution)/shard_map/all_to_all | solution.py:1804
  407.4 14.4 %collective-permute-start.64 = (f32[128,1024]{1,0:T(8,128)S(1)}, f32[128,1024]{1,0:T(8,128)S(1)}, u32[]{:S(2)}, u32[]{:S(2)}) collective-permute-start(f32[128,1024]{1,0:T(8,128)S(1)} %copy-done.60), channel_id=1, source_target_pairs={{0,1},{1,0},{2,3},{3,2},{4,5},{5,4},{6,7},{7,6},{8,9},{9,8},{10,11... | collective-permute-start | bytes 1572872 | tf_op jit(solution)/shard_map/ppermute | solution.py:65
  (80 other events, 551.1 us)
